TPU v7x, 32 devices: a whole 2x2x4 slice. The times are simulated.
32 devices in a mesh: group: 2 (over x), req: 2 (over core), tensor: 8 (over z, y).
Axes of the slice: x: 2, y: 2, z: 4, core: 2. Of those that a mesh axis runs over, the one named last changes fastest.
Arguments:
- queries: bfloat16 [128, 8192], P(('group', 'req'), 'tensor'), parts along dimension 0, may hold values from -300 to 300
- prefix_kv: bfloat16 [16, 2, 8192, 128], P(('group', 'tensor')), parts along dimension 0, may hold values from -9 to 9, as said below
- suffix_kv: bfloat16 [128, 8, 2, 256, 128], P(('group', 'req'), 'tensor'), parts along dimension 0, may hold values from -9 to 9, as said below
- suffix_len: int32 [128], P(('group', 'req')), parts along dimension 0, may hold values from 1 to 256, 8192 in all
- residual: bfloat16 [128, 8192], P(('group', 'req')), parts along dimension 0, may hold values from -3 to 3
- out_weight: bfloat16 [8192, 8192], P('tensor'), may hold values from -0.0625 to 0.0625
- adapter_pages: bfloat16 [128, 2, 64, 8192], P('req', None, None, 'tensor'), may hold values from -1 to 1
- adapter_ids: int32 [128], P(('group', 'req')), parts along dimension 0, may hold values from 0 to 127, as said below
- pool_slot: int32 [128], replicated, may hold values from 0 to 127, each once
Outputs:
- updated: bfloat16 [128, 8192], P(('group', 'req')), parts along dimension 0
There are 2 independent parts, one for each index of `group`. A program takes and returns all parts, laid end to end along the dimension named above; an argument that names none is the same for every part. Nothing has to cross between parts.
Inputs may be any that keep to these rules, and one draw needn't show every extreme that they name: `adapter_ids`: the 32 requests of one index of req name exactly 8 different adapters. `prefix_kv`: the copies of one key head are equal. `suffix_kv`: the copies of one key head are equal.
All inputs are finite; a program needn't handle non-finite values. No bound on the sum of `suffix_len` on one device may be relied on, other than what follows from the above.
Results may differ from a plain program's by a relative error of at most 0.0053.
Values may be sent and summed in bfloat16 or wider, within the bound.
No kernel may reach another device: no remote copies, remote signals or barrier semaphores. Data moves between devices by JAX's collectives and lax.ppermute only.
A program may use at most 192 MiB of HBM per device.

v0:
```python
import jax
import jax.numpy as jnp
from jax import lax
from jax.sharding import PartitionSpec as P


def rank_total(shrink_part):
    shrink_all = lax.all_gather(shrink_part[None], "tensor", axis=0, tiled=True)
    return jnp.sum(shrink_all, 0).astype(jnp.bfloat16)


def body(
    queries,
    prefix_kv,
    suffix_kv,
    suffix_len,
    residual,
    out_weight,
    adapter_pages,
    adapter_ids,
    pool_slot,
):
    row_count = queries.shape[0]
    head_dim = prefix_kv.shape[3]
    heads_here = queries.shape[1] // head_dim
    suffix_span = suffix_kv.shape[3]
    score_scale = head_dim ** (-0.5)
    flat_query = queries.reshape(row_count * heads_here, head_dim)
    prefix_scores = (
        lax.dot_general(
            flat_query,
            prefix_kv[0, 0],
            (((1,), (1,)), ((), ())),
            preferred_element_type=jnp.float32,
        )
        * score_scale
    )
    grouped = queries.reshape(row_count, heads_here, head_dim)
    suffix_scores = (
        jnp.einsum("rhd,rsd->rhs", grouped, suffix_kv[:, 0, 0], preferred_element_type=jnp.float32)
        * score_scale
    )
    live_mask = (jnp.arange(suffix_span)[None, :] < suffix_len[:, None])[:, None, :]
    suffix_scores = jnp.where(live_mask, suffix_scores, jnp.float32(-1e30))
    peak = jnp.maximum(
        jnp.max(prefix_scores, 1).reshape(row_count, heads_here, 1),
        jnp.max(suffix_scores, 2, keepdims=True),
    )
    prefix_exp = jnp.exp(prefix_scores - peak.reshape(-1, 1))
    suffix_exp = jnp.where(live_mask, jnp.exp(suffix_scores - peak), jnp.float32(0.0))
    denominator = jnp.sum(prefix_exp, 1).reshape(row_count, heads_here, 1) + jnp.sum(
        suffix_exp, 2, keepdims=True
    )
    prefix_weight = (prefix_exp / denominator.reshape(-1, 1)).astype(jnp.bfloat16)
    suffix_weight = (suffix_exp / denominator).astype(jnp.bfloat16)
    mixed = jnp.dot(prefix_weight, prefix_kv[0, 1], preferred_element_type=jnp.float32).reshape(
        row_count, heads_here, head_dim
    )
    mixed = mixed + jnp.einsum(
        "rhs,rsd->rhd", suffix_weight, suffix_kv[:, 0, 1], preferred_element_type=jnp.float32
    )
    attended = mixed.reshape(row_count, heads_here * head_dim).astype(jnp.bfloat16)
    adapter_count = pool_slot.shape[0]
    pool_size = adapter_pages.shape[0]
    req_count = lax.axis_size("req")
    share_width = attended.shape[1]
    pool_pos = jnp.sum(
        jnp.where(
            adapter_ids[:, None] == jnp.arange(adapter_count)[None, :], pool_slot[None, :], 0
        ),
        1,
    )
    owner_index = pool_pos // pool_size
    local_slot = pool_pos % pool_size
    flat_pool = adapter_pages.reshape(pool_size, -1)
    owner_match = owner_index[None, :] == jnp.arange(req_count)[:, None]
    wanted = jnp.where(owner_match, local_slot[None, :], -1)
    serve_wanted = lax.all_to_all(wanted, "req", split_axis=0, concat_axis=0, tiled=True)
    onehot = (serve_wanted[..., None] == jnp.arange(pool_size)).astype(jnp.bfloat16)
    found = jnp.dot(onehot.reshape(-1, pool_size), flat_pool, preferred_element_type=jnp.bfloat16)
    received = lax.all_to_all(
        found.reshape(serve_wanted.shape + (flat_pool.shape[1],)),
        "req",
        split_axis=0,
        concat_axis=0,
        tiled=True,
    )
    page_rows = jnp.sum(
        jnp.where(owner_match[:, :, None], received, jnp.zeros((), jnp.bfloat16)), 0
    )
    page_rows = page_rows.reshape(row_count, 2, -1, share_width)
    shrink_part = jnp.einsum(
        "ri,rki->rk", attended, page_rows[:, 0], preferred_element_type=jnp.float32
    )
    low_rank = rank_total(shrink_part)
    expanded = jnp.einsum(
        "rk,rkc->rc", low_rank, page_rows[:, 1], preferred_element_type=jnp.float32
    )
    base_part = jnp.dot(attended, out_weight, preferred_element_type=jnp.float32)
    tensor_pos = lax.axis_index("tensor")
    start_column = tensor_pos * share_width
    own_block = lax.dynamic_slice_in_dim(base_part, start_column, share_width, 1) + expanded
    placed = lax.dynamic_update_slice_in_dim(base_part, own_block, start_column, 1)
    summed = lax.psum(placed, "tensor")
    updated = (residual.astype(jnp.float32) + summed).astype(jnp.bfloat16)
    return updated


def solution(mesh):
    return jax.shard_map(
        body,
        mesh=mesh,
        in_specs=(
            P(("group", "req"), "tensor"),
            P(("group", "tensor"), None, None, None),
            P(("group", "req"), "tensor", None, None, None),
            P(("group", "req")),
            P(("group", "req"), None),
            P("tensor", None),
            P("req", None, None, "tensor"),
            P(("group", "req")),
            P(),
        ),
        out_specs=P(("group", "req"), None),
        check_vma=False,
    )
```

profile of v0, /device:TPU:0, one launch (start us, length us, event | category | flops | bytes accessed | tf_op | source)
XLA Modules:
  0.0 232.9 jit_solution(16944775414492143987)
XLA Ops:
  6.5 0.8 select_reduce_fusion.1
  7.4 0.6 compare_select_fusion
  8.0 3.2 %all-to-all-start = ((s32[2,1,32]{2,1,0:T(1,128)}), s32[2,1,32]{2,1,0:T(1,128)S(1)}, u32[]{:S(2)}, u32[]{:S(2)}) async-start(s32[2,1,32]{2,1,0:T(1,128)} %compare_select_fusion), calls=%async_computation | async-start | bytes 2048 | tf_op jit(solution)/shard_map/all_to_all | solution.py:78
  11.2 17.0 %reshape.211 = bf16[64,131072,1]{1,0,2:T(8,128)(2,1)} reshape(bf16[64,2,64,1024]{3,2,1,0:T(8,128)(2,1)} %param.15) | data formatting | bytes 33554432 | tf_op jit(solution)/shard_map/reshape | solution.py:75
  28.2 0.0 all-to-all-done
  28.2 11.5 %fusion.37 = bf16[2,32,131072]{2,1,0:T(8,128)(2,1)} fusion(bf16[64,131072,1]{1,0,2:T(8,128)(2,1)} %reshape.211, s32[2,32]{1,0:T(2,128)S(1)} %bitcast.77), kind=kOutput, calls=%fused_computation.41 | convolution fusion | flops 1073745920 | bytes 33554688 | tf_op jit(solution)/shard_map/dot_general | solution.py:80
  39.7 9.8 %all-to-all-start.1 = ((bf16[2,32,131072]{2,1,0:T(8,128)(2,1)}), bf16[2,32,131072]{2,1,0:T(8,128)(2,1)}, u32[]{:S(2)}, u32[]{:S(2)}) async-start(bf16[2,32,131072]{2,1,0:T(8,128)(2,1)} %fusion.37), calls=%async_computation.1 | async-start | bytes 33554432 | tf_op jit(solution)/shard_map/all_to_all | solution.py:81
  49.5 0.0 all-reduce.2.cloned.1.call-start
  49.5 0.0 copy-done.4
  49.5 0.1 iota_compare_fusion.1
  49.7 6.0 %fusion.42 = (f32[256]{0:T(256)S(1)}, f32[256,8192]{1,0:T(8,128)}) fusion(bf16[256,128]{1,0:T(8,128)(2,1)S(1)} %reshape.203, bf16[1,2,8192,128]{3,2,1,0:T(8,128)(2,1)} %param.10), kind=kOutput, calls=%fused_computation.55 | convolution fusion | flops 541064960 | bytes 10552320 | tf_op jit(solution)/shard_map/dot_general | solution.py:30
  55.7 0.1 reshape.205
  55.8 2.3 fusion.43
  58.1 0.1 reduce_max.22
  58.3 0.2 fusion.27
  58.5 0.1 reduce_sum.52
  58.6 4.6 %fusion = f32[256]{0:T(256)S(1)} fusion(f32[256,8192]{1,0:T(8,128)} %get-tuple-element.8, f32[256]{0:T(256)S(1)} %max.14), kind=kLoop, calls=%fused_computation.4 | loop fusion | flops 4194048 | bytes 8390656 | tf_op jit(solution)/shard_map/reduce_sum | solution.py:51
  63.2 0.1 reshape.206
  63.3 0.0 copy-start.1
  63.3 5.4 %fusion.3 = f32[32,8,128]{2,1,0:T(8,128)S(1)} fusion(f32[256,8192]{1,0:T(8,128)} %get-tuple-element.8, f32[256]{0:T(256)S(1)} %add.44, f32[256]{0:T(256)S(1)} %max.14, bf16[1,2,8192,128]{3,2,1,0:T(8,128)(2,1)} %param.10), kind=kOutput, calls=%fused_computation.9 | convolution fusion | flops 543162368 | bytes 10618880 | tf_op jit(solution)/shard_map/dot_general | solution.py:56
  68.8 0.5 fusion.24
  69.3 0.0 all-to-all-done.1
  69.3 15.8 %select_reduce_fusion = bf16[32,131072]{1,0:T(8,128)(2,1)} fusion(bf16[2,32,131072]{2,1,0:T(8,128)(2,1)} %all-to-all-done.1, pred[2,32]{1,0:T(4,128)(4,1)S(1)} %iota_compare_fusion.3), kind=kLoop, calls=%fused_computation | loop fusion | flops 12582912 | bytes 25165888 | tf_op jit(solution)/shard_map/reduce_sum | solution.py:88
  85.1 11.4 %copy.26 = bf16[4,8,128,1024]{3,2,1,0:T(8,128)(2,1)} copy(bf16[4,8,128,1024]{3,1,2,0:T(8,128)(2,1)} %bitcast.69) | data formatting | bytes 16777216
  96.4 3.4 %fusion.2 = f32[32,1,64]{2,1,0:T(1,128)S(1)} fusion(bf16[32,1024,1]{1,2,0:T(2,128)(2,1)S(1)} %reshape.217, bf16[32,2,64,1024]{3,2,1,0:T(8,128)(2,1)} %bitcast.70), kind=kOutput, calls=%fused_computation.8 | convolution fusion | flops 4194304 | bytes 4268032 | tf_op jit(solution)/shard_map/ri,rki->rk/dot_general | solution.py:92
  99.8 32.4 %all-gather = f32[256,64]{1,0:T(8,128)S(1)} all-gather(f32[32,64]{1,0:T(8,128)S(1)} %bitcast.78), channel_id=2, replica_groups=mesh['group'=2,'req'=2,'tensor'=8] {'tensor'}, dimensions={0}, use_global_device_ids=true | all-gather | bytes 73728 | tf_op jit(solution)/shard_map/all_gather | solution.py:8
  132.3 2.8 %fusion.1 = f32[32,1,1024]{2,1,0:T(1,128)S(1)} fusion(bf16[32,2,64,1024]{3,2,1,0:T(8,128)(2,1)} %bitcast.71, bf16[32,64,1]{1,0,2:T(8,128)(2,1)S(1)} %bitcast.76), kind=kOutput, calls=%fused_computation.6 | convolution fusion | flops 4194304 | bytes 4329472 | tf_op jit(solution)/shard_map/rk,rkc->rc/dot_general | solution.py:96
  135.1 8.8 %fusion.33 = f32[32,8192]{1,0:T(8,128)S(1)} fusion(bf16[1024,8192]{1,0:T(8,128)(2,1)} %param.14, bf16[4,8,8,128]{3,2,1,0:T(8,128)(2,1)S(1)} %bitcast.73), kind=kOutput, calls=%fused_computation.35 | convolution fusion | flops 536870912 | bytes 17891328 | tf_op jit(solution)/shard_map/dot_general | solution.py:99
  144.0 1.0 copy-done
  145.0 0.0 all-reduce.2.cloned.1.call-update
  145.0 79.0 %all-reduce.2.cloned.1.call-done = f32[32,8192]{1,0:T(8,128)} async-done(((f32[32,8192]{1,0:T(8,128)}), f32[32,8192]{1,0:T(8,128)}) %all-reduce.2.cloned.1.call-update) | async-done | bytes 1048592 | tf_op jit(solution)/shard_map/psum | solution.py:104
  224.0 2.1 add_convert_fusion
  (18 shorter events, 0.2 us)
Async XLA Ops:
  8.0 20.2 %all-to-all-start = ((s32[2,1,32]{2,1,0:T(1,128)}), s32[2,1,32]{2,1,0:T(1,128)S(1)}, u32[]{:S(2)}, u32[]{:S(2)}) async-start(s32[2,1,32]{2,1,0:T(1,128)} %compare_select_fusion), calls=%async_computation | async-start | bytes 2048 | tf_op jit(solution)/shard_map/all_to_all | solution.py:78
  39.6 9.9 %copy-start.4 = (s32[32]{0:T(128)S(1)}, s32[32]{0:T(128)}, u32[]{:S(2)}) copy-start(s32[32]{0:T(128)} %param.12) | copy-start | bytes 388
  39.6 10.0 %copy-start.3 = (bf16[32,1024]{1,0:T(8,128)(2,1)S(1)}, bf16[32,1024]{1,0:T(8,128)(2,1)}, u32[]{:S(2)}) copy-start(bf16[32,1024]{1,0:T(8,128)(2,1)} %param.9) | copy-start | bytes 196612
  39.7 29.6 %all-to-all-start.1 = ((bf16[2,32,131072]{2,1,0:T(8,128)(2,1)}), bf16[2,32,131072]{2,1,0:T(8,128)(2,1)}, u32[]{:S(2)}, u32[]{:S(2)}) async-start(bf16[2,32,131072]{2,1,0:T(8,128)(2,1)} %fusion.37), calls=%async_computation.1 | async-start | bytes 33554432 | tf_op jit(solution)/shard_map/all_to_all | solution.py:81
  49.5 174.5 %all-reduce.2.cloned.1.call-start = ((), (), s32[]{:S(2)}) async-start(), calls=%async_computation.2 | async-start | bytes 2097152 | tf_op jit(solution)/shard_map/psum | solution.py:104
  63.3 5.5 %copy-start.1 = (bf16[32,1,2,256,128]{4,3,2,1,0:T(8,128)(2,1)S(1)}, bf16[32,1,2,256,128]{4,3,2,1,0:T(8,128)(2,1)}, u32[]{:S(2)}) copy-start(bf16[32,1,2,256,128]{4,3,2,1,0:T(8,128)(2,1)} %param.11) | copy-start | bytes 12582916
  135.1 88.9 %copy-start.2 = (bf16[32,8192]{1,0:T(8,128)(2,1)S(1)}, bf16[32,8192]{1,0:T(8,128)(2,1)}, u32[]{:S(2)}) copy-start(bf16[32,8192]{1,0:T(8,128)(2,1)} %param.13) | copy-start | bytes 1572868
  144.0 1.0 copy-start
Sparse Core Ops, SparseCore 0:
  145.1 78.7 all-reduce.1
where the time goes:
time: 234 us; the launch traced here: 233 us
  waiting for transfers between devices  79 us (34%)
  matrix products  40.8 us (17%)
  blocking collectives  32.4 us (14%)
  local copies, waits for them, and re-layouts  29.8 us (13%)
  other arithmetic  24.3 us (10%)
  between operations  13.6 us (6%)
  starting transfers between devices  13 us (6%)
    psum x1, waiting for transfers between devices, body(): summed = lax.psum(placed, 'tensor')  79 us
    all_gather x1, blocking collectives, rank_total(): shrink_all = lax.all_gather(shrink_part[None], 'tensor', axis=0, tiled=True)  32.4 us
    reshape x1, local copies, waits for them, and re-layouts, body(): flat_pool = adapter_pages.reshape(pool_size, -1)  17 us
    reduce_sum x1, other arithmetic, body(): jnp.sum(jnp.where(owner_match[:, :, None], received, jnp.zeros((), jnp.bf...  15.8 us
    unnamed x12, local copies, waits for them, and re-layouts  12.4 us
    dot_general x1, matrix products, body(): jnp.dot(onehot.reshape(-1, pool_size), flat_pool, preferred_element_type=...  11.5 us
    all_to_all x1, starting transfers between devices, body(): lax.all_to_all(found.reshape(serve_wanted.shape + (flat_pool.shape[1],)),...  9.81 us
    dot_general x1, matrix products, body(): jnp.dot(attended, out_weight, preferred_element_type=jnp.float32)  8.82 us
  transfers between devices with their start and end apart: 3, of which 1 were waited for; matrix products, arithmetic and copies ran while one was open for 16% of the time, Pallas kernels for 0%

commit v1 on v0

v1 whole, which is shorter than its diff:
```python
import functools
import math

import jax
import jax.numpy as jnp
from jax import lax
from jax.experimental import pallas as pl
from jax.experimental.pallas import tpu as pltpu
from jax.sharding import PartitionSpec as P

F32 = jnp.float32
BF16 = jnp.bfloat16
LOG2E = 1.4426950408889634
ANY = pl.BlockSpec(memory_space=pl.ANY)
VMEM = pl.BlockSpec(memory_space=pltpu.VMEM)
SMEM = pl.BlockSpec(memory_space=pltpu.SMEM)
MIB = 1 << 20
DISTINCT = 8


def nt_dot(a, b):
    return lax.dot_general(a, b, (((1,), (1,)), ((), ())), preferred_element_type=F32)


def nn_dot(a, b):
    return jnp.dot(a, b, preferred_element_type=F32)


def distinct_list(ids_ref, pool_slot_ref, seen, list_id, list_pos):
    rows = ids_ref.shape[0]
    count = pool_slot_ref.shape[0]

    @pl.loop(0, count)
    def _(i):
        seen[i] = 0

    for j in range(DISTINCT):
        list_id[j] = -1
        list_pos[j] = 0

    def step(r, found):
        one = ids_ref[r]
        fresh = (seen[one] == 0) & (found < DISTINCT)

        @pl.when(fresh)
        def _():
            seen[one] = 1
            list_id[found] = one
            list_pos[found] = pool_slot_ref[one]

        return found + fresh.astype(jnp.int32)

    lax.fori_loop(0, rows, step, jnp.int32(0))


def attend_kernel(
    n_z,
    len_ref,
    q_ref,
    prefix_ref,
    suffix_ref,
    weight_ref,
    att_ref,
    *rest,
):
    piece_refs = rest[:n_z]
    (kv, suf, wbuf, scores, tail, rowbuf, peak, total, acc, sem_kv, sem_suf, sem_w) = rest[n_z:]
    rows = q_ref.shape[0]
    head_dim = prefix_ref.shape[3]
    heads = q_ref.shape[1] // head_dim
    n_q = rows * heads
    tokens = prefix_ref.shape[2]
    span = suffix_ref.shape[3]
    width = piece_refs[0].shape[1]
    me = lax.axis_index("tensor")
    z, y = me // 2, me % 2
    scale2 = float(head_dim) ** -0.5 * LOG2E

    n_part = 4
    part = tokens // n_part
    kv_copies = [
        [
            pltpu.make_async_copy(
                prefix_ref.at[0, i, pl.ds(j * part, part)],
                kv.at[i, pl.ds(j * part, part)],
                sem_kv.at[i, j],
            )
            for j in range(n_part)
        ]
        for i in range(2)
    ]
    n_sgrp = 4
    sgrp = rows // n_sgrp
    suf_copies = [
        pltpu.make_async_copy(
            suffix_ref.at[pl.ds(j * sgrp, sgrp), 0], suf.at[pl.ds(j * sgrp, sgrp)], sem_suf.at[j]
        )
        for j in range(n_sgrp)
    ]
    w_copies = []
    for k in range(n_z):
        column = pl.multiple_of(((z ^ k) * 2 + (1 - y)) * width, width)
        w_copies.append(
            pltpu.make_async_copy(weight_ref.at[:, pl.ds(column, width)], wbuf.at[k], sem_w.at[k])
        )
    for c in kv_copies[0] + suf_copies + kv_copies[1]:
        c.start()

    for h in range(heads):
        rowbuf[pl.ds(h, rows, stride=heads), :] = q_ref[:, h * head_dim : (h + 1) * head_dim].astype(F32)
    query = rowbuf[...].astype(BF16)
    peak[...] = jnp.full(peak.shape, -3.0e38, F32)

    chunk = 1024
    for j in range(n_part):
        kv_copies[0][j].wait()
        if j == 0:
            for c in w_copies[:1]:
                c.start()

        @pl.loop(0, part // chunk)
        def _(i):
            base = pl.multiple_of(j * part + i * chunk, chunk)
            best = peak[...]
            for b in range(chunk // 256):
                block = nt_dot(query, kv[0, pl.ds(base + b * 256, 256), :])
                scores[:, pl.ds(base + b * 256, 256)] = block
                best = jnp.maximum(best, jnp.maximum(block[:, :128], block[:, 128:]))
            peak[...] = best

    for c in w_copies[1:]:
        c.start()

    lanes = lax.broadcasted_iota(jnp.int32, (heads, span), 1)
    for j in range(n_sgrp):
        suf_copies[j].wait()
        for i in range(j * sgrp // 2, (j + 1) * sgrp // 2):
            keys = suf[2 * i : 2 * i + 2, 0].reshape(2 * span, head_dim)
            both = nt_dot(query[2 * heads * i : 2 * heads * (i + 1)], keys)
            for a in range(2):
                mine = both[a * heads : (a + 1) * heads, a * span : (a + 1) * span]
                row = 2 * i + a
                tail[row * heads : (row + 1) * heads, :] = jnp.where(lanes < len_ref[row], mine, -1.0e30)
    best = peak[...]
    for b in range(span // 128):
        best = jnp.maximum(best, tail[:, b * 128 : (b + 1) * 128])
    top = jnp.max(best, axis=1, keepdims=True)
    peak[...] = jnp.broadcast_to(top, peak.shape)

    for j in range(n_part):
        kv_copies[1][j].wait()
    total[...] = jnp.zeros(total.shape, F32)
    acc[...] = jnp.zeros(acc.shape, F32)

    @pl.loop(0, tokens // chunk)
    def _(i):
        base = pl.multiple_of(i * chunk, chunk)
        high = peak[...]
        summed = total[...]
        parts = []
        for b in range(chunk // 128):
            e = jnp.exp2((scores[:, pl.ds(base + b * 128, 128)] - high) * scale2)
            summed = summed + e
            parts.append(e.astype(BF16))
        total[...] = summed
        acc[...] += nn_dot(jnp.concatenate(parts, axis=1), kv[1, pl.ds(base, chunk), :])

    zeros = jnp.zeros((heads, span), F32)
    for i in range(rows // 2):
        lo = 2 * heads * i
        high = jnp.concatenate([peak[lo : lo + 2 * heads, :]] * (span // 128), axis=1)
        e = jnp.exp2((tail[lo : lo + 2 * heads, :] - high) * scale2)
        part_sum = e[:, :128]
        for b in range(1, span // 128):
            part_sum = part_sum + e[:, b * 128 : (b + 1) * 128]
        total[lo : lo + 2 * heads, :] += part_sum
        diag = jnp.concatenate(
            [
                jnp.concatenate([e[:heads], zeros], axis=1),
                jnp.concatenate([zeros, e[heads:]], axis=1),
            ],
            axis=0,
        ).astype(BF16)
        vals = suf[2 * i : 2 * i + 2, 1].reshape(2 * span, head_dim)
        acc[lo : lo + 2 * heads, :] += nn_dot(diag, vals)

    norm = jnp.sum(total[...], axis=1, keepdims=True)
    rowbuf[...] = acc[...] / norm
    for h in range(heads):
        att_ref[:, h * head_dim : (h + 1) * head_dim] = rowbuf[pl.ds(h, rows, stride=heads), :].astype(BF16)
    attended = att_ref[...]
    for k in range(n_z):
        w_copies[k].wait()
        piece_refs[k][...] = nn_dot(attended, wbuf[k]).astype(BF16)


def attend(suffix_len, queries, prefix_kv, suffix_kv, out_weight, n_tensor):
    rows = queries.shape[0]
    n_z = n_tensor // 2
    width = out_weight.shape[1] // n_tensor
    tokens, head_dim = prefix_kv.shape[2:]
    n_q = rows * queries.shape[1] // head_dim
    span = suffix_kv.shape[3]
    return pl.pallas_call(
        functools.partial(attend_kernel, n_z),
        out_shape=[jax.ShapeDtypeStruct(queries.shape, BF16)]
        + [jax.ShapeDtypeStruct((rows, width), BF16)] * n_z,
        in_specs=[SMEM, VMEM, ANY, ANY, ANY],
        out_specs=[VMEM] * (1 + n_z),
        scratch_shapes=[
            pltpu.VMEM((2, tokens, head_dim), BF16),
            pltpu.VMEM((rows, 2, span, head_dim), BF16),
            pltpu.VMEM((n_z, out_weight.shape[0], width), BF16),
            pltpu.VMEM((n_q, tokens), F32),
            pltpu.VMEM((n_q, span), F32),
            pltpu.VMEM((n_q, head_dim), F32),
            pltpu.VMEM((n_q, 128), F32),
            pltpu.VMEM((n_q, 128), F32),
            pltpu.VMEM((n_q, head_dim), F32),
            pltpu.SemaphoreType.DMA((2, 4)),
            pltpu.SemaphoreType.DMA((4,)),
            pltpu.SemaphoreType.DMA((n_z,)),
        ],
        compiler_params=pltpu.CompilerParams(vmem_limit_bytes=48 * MIB),
        cost_estimate=pl.CostEstimate(
            flops=2 * 2 * n_q * tokens * head_dim,
            bytes_accessed=16 * MIB,
            transcendentals=n_q * tokens,
        ),
        name="attend",
    )(suffix_len, queries, prefix_kv, suffix_kv, out_weight)


def own_kernel(n_z, att_ref, weight_ref, *rest):
    piece_refs = rest[:n_z]
    wbuf, sem_w = rest[n_z:]
    width = piece_refs[0].shape[1]
    me = lax.axis_index("tensor")
    z, y = me // 2, me % 2
    copies = []
    for k in range(n_z):
        column = pl.multiple_of(((z ^ k) * 2 + y) * width, width)
        copies.append(
            pltpu.make_async_copy(weight_ref.at[:, pl.ds(column, width)], wbuf.at[k], sem_w.at[k])
        )
    order = list(range(1, n_z)) + [0]
    for k in order:
        copies[k].start()
    attended = att_ref[...]
    for k in order:
        copies[k].wait()
        piece_refs[k][...] = nn_dot(attended, wbuf[k])


def own_part(attended, out_weight, n_tensor):
    rows = attended.shape[0]
    n_z = n_tensor // 2
    width = out_weight.shape[1] // n_tensor
    return pl.pallas_call(
        functools.partial(own_kernel, n_z),
        out_shape=[jax.ShapeDtypeStruct((rows, width), F32)] * n_z,
        in_specs=[VMEM, ANY],
        out_specs=[VMEM] * n_z,
        scratch_shapes=[
            pltpu.VMEM((n_z, out_weight.shape[0], width), BF16),
            pltpu.SemaphoreType.DMA((n_z,)),
        ],
        compiler_params=pltpu.CompilerParams(vmem_limit_bytes=24 * MIB),
        cost_estimate=pl.CostEstimate(
            flops=2 * rows * out_weight.shape[0] * width * n_z,
            bytes_accessed=8 * MIB,
            transcendentals=0,
        ),
        name="own_part",
    )(attended, out_weight)


def collect_kernel(ids_ref, slot_ref, pages_ref, shrink_ref, expand_ref, seen, list_id, list_pos, sem):
    distinct_list(ids_ref, slot_ref, seen, list_id, list_pos)
    pool = pages_ref.shape[0]
    me = lax.axis_index("req")
    for wait in (False, True):
        for i, out in enumerate((shrink_ref, expand_ref)):
            for j in range(DISTINCT):
                pos = list_pos[j]

                @pl.when(pos // pool == me)
                def _():
                    copy = pltpu.make_async_copy(pages_ref.at[pos % pool, i], out.at[j], sem.at[i, j])
                    if wait:
                        copy.wait()
                    else:
                        copy.start()


def collect_pages(ids, pool_slot, pages):
    shape = jax.ShapeDtypeStruct((DISTINCT,) + pages.shape[2:], BF16)
    return pl.pallas_call(
        collect_kernel,
        out_shape=[shape, shape],
        in_specs=[SMEM, SMEM, ANY],
        out_specs=[ANY, ANY],
        scratch_shapes=[
            pltpu.SMEM((pool_slot.shape[0],), jnp.int32),
            pltpu.SMEM((DISTINCT,), jnp.int32),
            pltpu.SMEM((DISTINCT,), jnp.int32),
            pltpu.SemaphoreType.DMA((2, DISTINCT)),
        ],
        cost_estimate=pl.CostEstimate(flops=0, bytes_accessed=4 * MIB, transcendentals=0),
        name="collect_pages",
    )(ids, pool_slot, pages)


def load_pages(half, pages_ref, other_ref, buf, sem, list_pos):
    pool = pages_ref.shape[0]
    me = lax.axis_index("req")
    rank = pages_ref.shape[2]
    for wait in (False, True):
        for j in range(DISTINCT):
            pos = list_pos[j]
            for mine in (True, False):

                @pl.when((pos // pool == me) == mine)
                def _():
                    source = pages_ref.at[pos % pool, half] if mine else other_ref.at[j]
                    copy = pltpu.make_async_copy(source, buf.at[pl.ds(j * rank, rank)], sem.at[j])
                    if wait:
                        copy.wait()
                    else:
                        copy.start()


def shrink_kernel(
    ids_ref, slot_ref, column_ref, att_ref, pages_ref, other_ref, out_ref, buf, seen, list_id, list_pos, sem
):
    distinct_list(ids_ref, slot_ref, seen, list_id, list_pos)
    load_pages(0, pages_ref, other_ref, buf, sem, list_pos)
    rank = pages_ref.shape[2]
    low = nt_dot(att_ref[...], buf[...])
    column = column_ref[...]
    lane_slot = lax.broadcasted_iota(jnp.int32, (column.shape[0], 128), 1) // rank
    per_tile = 128 // rank
    picked = jnp.zeros((column.shape[0], 128), F32)
    for j in range(DISTINCT):
        tile, place = j // per_tile, j % per_tile
        hit = (column == list_id[j]) & (lane_slot == place)
        picked = jnp.where(hit, low[:, tile * 128 : (tile + 1) * 128], picked)
    out_ref[...] = picked


def expand_kernel(
    ids_ref,
    slot_ref,
    column_ref,
    low_ref,
    pages_ref,
    other_ref,
    own_ref,
    recv_ref,
    residual_ref,
    out_ref,
    buf,
    res,
    seen,
    list_id,
    list_pos,
    sem,
    sem_res,
):
    distinct_list(ids_ref, slot_ref, seen, list_id, list_pos)
    width = own_ref.shape[1]
    me = lax.axis_index("tensor")
    fetch = pltpu.make_async_copy(
        residual_ref.at[:, pl.ds(pl.multiple_of(me * width, width), width)], res, sem_res.at[0]
    )
    fetch.start()
    load_pages(1, pages_ref, other_ref, buf, sem, list_pos)
    rank = pages_ref.shape[2]
    column = column_ref[...]
    per_tile = 128 // rank
    lane_slot = lax.broadcasted_iota(jnp.int32, (column.shape[0], 128), 1) // rank
    low = low_ref[...]
    tiles = []
    for tile in range(DISTINCT // per_tile):
        hit = jnp.zeros(low.shape, jnp.bool_)
        for place in range(per_tile):
            hit = hit | ((column == list_id[tile * per_tile + place]) & (lane_slot == place))
        tiles.append(jnp.where(hit, low, 0.0).astype(BF16))
    expanded = nn_dot(jnp.concatenate(tiles, axis=1), buf[...])
    fetch.wait()
    out_ref[...] = expanded + own_ref[...] + recv_ref[...].astype(F32) + res[...].astype(F32)


def adapter_scratch(pages, pool_slot):
    return [
        pltpu.SMEM((pool_slot.shape[0],), jnp.int32),
        pltpu.SMEM((DISTINCT,), jnp.int32),
        pltpu.SMEM((DISTINCT,), jnp.int32),
        pltpu.SemaphoreType.DMA((DISTINCT,)),
    ]


def shrink_part(ids, pool_slot, column, attended, pages, other):
    rows = attended.shape[0]
    return pl.pallas_call(
        shrink_kernel,
        out_shape=jax.ShapeDtypeStruct((rows, 128), F32),
        in_specs=[SMEM, SMEM, VMEM, VMEM, ANY, ANY],
        out_specs=VMEM,
        scratch_shapes=[pltpu.VMEM((DISTINCT * pages.shape[2], pages.shape[3]), BF16)]
        + adapter_scratch(pages, pool_slot),
        cost_estimate=pl.CostEstimate(flops=1 << 25, bytes_accessed=1 * MIB, transcendentals=0),
        name="shrink_part",
    )(ids, pool_slot, column, attended, pages, other)


def expand_part(ids, pool_slot, column, low, pages, other, own, recv, residual):
    rows, width = own.shape
    return pl.pallas_call(
        expand_kernel,
        out_shape=jax.ShapeDtypeStruct((rows, width), F32),
        in_specs=[SMEM, SMEM, VMEM, VMEM, ANY, ANY, VMEM, VMEM, ANY],
        out_specs=VMEM,
        scratch_shapes=[
            pltpu.VMEM((DISTINCT * pages.shape[2], pages.shape[3]), BF16),
            pltpu.VMEM((rows, width), BF16),
        ]
        + adapter_scratch(pages, pool_slot)
        + [pltpu.SemaphoreType.DMA((1,))],
        cost_estimate=pl.CostEstimate(flops=1 << 25, bytes_accessed=1 * MIB, transcendentals=0),
        name="expand_part",
    )(ids, pool_slot, column, low, pages, other, own, recv, residual)


def place_kernel(n_z, *refs):
    blocks = refs[: 2 * n_z]
    out_ref, sem = refs[2 * n_z :]
    width = blocks[0].shape[1]
    me = lax.axis_index("tensor")
    z, y = me // 2, me % 2
    copies = []
    for k in range(n_z):
        for other in range(2):
            where = (z ^ k) * 2 + (y ^ other)
            copies.append(
                pltpu.make_async_copy(
                    blocks[2 * k + other],
                    out_ref.at[:, pl.ds(pl.multiple_of(where * width, width), width)],
                    sem.at[2 * k + other],
                )
            )
    for c in copies:
        c.start()
    for c in copies:
        c.wait()


def place(blocks, n_tensor):
    rows, width = blocks[0].shape
    return pl.pallas_call(
        functools.partial(place_kernel, n_tensor // 2),
        out_shape=jax.ShapeDtypeStruct((rows, width * n_tensor), BF16),
        in_specs=[ANY] * n_tensor,
        out_specs=ANY,
        scratch_shapes=[pltpu.SemaphoreType.DMA((n_tensor,))],
        cost_estimate=pl.CostEstimate(flops=0, bytes_accessed=1 * MIB, transcendentals=0),
        name="place",
    )(*blocks)


def body(
    n_tensor,
    queries,
    prefix_kv,
    suffix_kv,
    suffix_len,
    residual,
    out_weight,
    adapter_pages,
    adapter_ids,
    pool_slot,
):
    n_z = n_tensor // 2

    def along_y(x):
        return lax.ppermute(x, "tensor", [(t, t ^ 1) for t in range(n_tensor)])

    def along_z(x, k):
        return lax.ppermute(x, "tensor", [(t, t ^ (2 * k)) for t in range(n_tensor)])

    def across(x):
        return lax.ppermute(x, "req", [(0, 1), (1, 0)])

    column = jnp.broadcast_to(adapter_ids[:, None], (adapter_ids.shape[0], 128))
    other_ids = across(adapter_ids)
    attended, *pieces = attend(suffix_len, queries, prefix_kv, suffix_kv, out_weight, n_tensor)
    send_order = list(range(1, n_z)) + [0]
    got_y = {k: along_y(pieces[k]) for k in send_order}
    found_shrink, found_expand = collect_pages(other_ids, pool_slot, adapter_pages)
    other_shrink = across(found_shrink)
    other_expand = across(found_expand)
    own = own_part(attended, out_weight, n_tensor)
    got_z = []
    for k in range(1, n_z):
        both = (got_y[k].astype(F32) + own[k]).astype(BF16)
        got_z.append(along_z(both, k))
    low = shrink_part(adapter_ids, pool_slot, column, attended, adapter_pages, other_shrink)
    low = low + along_y(low)
    for bit in range(int(math.log2(n_z))):
        low = low + along_z(low, 1 << bit)
    local = expand_part(
        adapter_ids, pool_slot, column, low, adapter_pages, other_expand, own[0], got_y[0], residual
    )
    for g in got_z:
        local = local + g.astype(F32)
    result = local.astype(BF16)
    blocks = []
    held = [result] + [along_z(result, k) for k in range(1, n_z)]
    for k in range(n_z):
        blocks += [held[k], along_y(held[k])]
    return place(blocks, n_tensor)


def solution(mesh):
    return jax.shard_map(
        functools.partial(body, mesh.shape["tensor"]),
        mesh=mesh,
        in_specs=(
            P(("group", "req"), "tensor"),
            P(("group", "tensor"), None, None, None),
            P(("group", "req"), "tensor", None, None, None),
            P(("group", "req")),
            P(("group", "req"), None),
            P("tensor", None),
            P("req", None, None, "tensor"),
            P(("group", "req")),
            P(),
        ),
        out_specs=P(("group", "req"), None),
        check_vma=False,
    )
```

time: 234 us -> 136 us (0.58)
  Pallas kernels: 0 us -> 82.3 us
  waiting for transfers between devices: 79 us -> 14.8 us
  matrix products: 40.8 us -> 0 us
  blocking collectives: 32.4 us -> 0 us
  other arithmetic: 24.3 us -> 2.31 us
  local copies, waits for them, and re-layouts: 29.8 us -> 11.7 us
  between operations: 13.6 us -> 0.21 us
  starting transfers between devices: 13 us -> 24.3 us
    pallas_call x0 -> x6, Pallas kernels: none -> 82.3 us  [the longest x1 42.9 us: collect_pages(): pl.pallas_call(collect_kernel, out_shape=[shape, shape], in_specs=[SMEM,...]
    psum x1 -> x0, waiting for transfers between devices: 79 us -> none  [body(): summed = lax.psum(placed, 'tensor')]
    dot_general x8 -> x0, matrix products: 40.8 us -> none  [the longest x1 11.5 us: body(): jnp.dot(onehot.reshape(-1, pool_size), flat_pool, preferred_element_type=...]
    all_gather x1 -> x0, blocking collectives: 32.4 us -> none  [rank_total(): shrink_all = lax.all_gather(shrink_part[None], 'tensor', axis=0, tiled=True)]
    ppermute x0 -> x20, starting transfers between devices: none -> 24.3 us  [the longest x9 11.7 us: along_y(): return lax.ppermute(x, 'tensor', [(t, t ^ 1) for t in range(n_tensor)])]
    reduce_sum x5 -> x0, other arithmetic: 21.5 us -> none  [the longest x1 15.8 us: body(): jnp.sum(jnp.where(owner_match[:, :, None], received, jnp.zeros((), jnp.bf...]
    reshape x4 -> x0, local copies, waits for them, and re-layouts: 17.2 us -> none  [the longest x1 17 us: body(): flat_pool = adapter_pages.reshape(pool_size, -1)]
    ppermute x0 -> x20, waiting for transfers between devices: none -> 14.8 us  [the longest x8 8.64 us: along_z(): return lax.ppermute(x, 'tensor', [(t, t ^ 2 * k) for t in range(n_tensor)])]
  transfers between devices with their start and end apart: 3 -> 20, of which waited for: 1 -> 8; matrix products, arithmetic and copies ran while one was open for 16% -> 2% of each run, Pallas kernels for 0% -> 16%
where the time goes in v1:
time: 136 us
  Pallas kernels  82.3 us (61%)
  starting transfers between devices  24.3 us (18%)
  waiting for transfers between devices  14.8 us (11%)
  local copies, waits for them, and re-layouts  11.7 us (9%)
  other arithmetic  2.31 us (2%)
    pallas_call x1, Pallas kernels, collect_pages(): pl.pallas_call(collect_kernel, out_shape=[shape, shape], in_specs=[SMEM,...  42.9 us
    pallas_call x1, Pallas kernels, place(): pl.pallas_call(functools.partial(place_kernel, n_tensor // 2), out_shape=...  17.1 us
    ppermute x9, starting transfers between devices, along_y(): return lax.ppermute(x, 'tensor', [(t, t ^ 1) for t in range(n_tensor)])  11.7 us
    ppermute x8, starting transfers between devices, along_z(): return lax.ppermute(x, 'tensor', [(t, t ^ 2 * k) for t in range(n_tensor)])  11.5 us
    unnamed x38, local copies, waits for them, and re-layouts  10.9 us
    pallas_call x1, Pallas kernels, attend(): pl.pallas_call(functools.partial(attend_kernel, n_z), out_shape=[jax.Shap...  9.67 us
    ppermute x8, waiting for transfers between devices, along_z(): return lax.ppermute(x, 'tensor', [(t, t ^ 2 * k) for t in range(n_tensor)])  8.64 us
    ppermute x9, waiting for transfers between devices, along_y(): return lax.ppermute(x, 'tensor', [(t, t ^ 1) for t in range(n_tensor)])  5.19 us
  transfers between devices with their start and end apart: 20, of which 8 were waited for; matrix products, arithmetic and copies ran while one was open for 2% of the time, Pallas kernels for 16%

profile of v1, /device:TPU:0, one launch (start us, length us, event | category | flops | bytes accessed | tf_op | source)
XLA Modules:
  0.0 135.5 jit_solution(15850149323676101875)
XLA Ops:
  0.5 1.0 collective-permute-done.ids_ref
  1.9 42.9 %collect_pages.1 = (bf16[8,64,1024]{2,1,0:T(8,128)(2,1)}, bf16[8,64,1024]{2,1,0:T(8,128)(2,1)}) custom-call(s32[32]{0:T(128)} %copy-done.18, s32[128]{0:T(128)} %slot_ref.5, bf16[64,2,64,1024]{3,2,1,0:T(8,128)(2,1)} %pages_ref.5), custom_call_target="tpu_custom_call" | custom-call | bytes 4194304 | tf_op jit(solution)/shard_map/collect_pages/pallas_call | solution.py:298
  45.4 2.2 %copy-done.1 = bf16[1,2,8192,128]{3,2,1,0:T(8,128)(2,1)S(1)} copy-done((bf16[1,2,8192,128]{3,2,1,0:T(8,128)(2,1)S(1)}, bf16[1,2,8192,128]{3,2,1,0:T(8,128)(2,1)}, u32[]{:S(2)}) %copy-start.1) | copy-done | bytes 4194328
  47.6 9.7 %attend.1 = (bf16[32,1024]{1,0:T(8,128)(2,1)S(1)}, bf16[32,1024]{1,0:T(8,128)(2,1)S(1)}, bf16[32,1024]{1,0:T(8,128)(2,1)S(1)}, bf16[32,1024]{1,0:T(8,128)(2,1)S(1)}, bf16[32,1024]{1,0:T(8,128)(2,1)S(1)}) custom-call(s32[32]{0:T(128)S(1)} %copy-done.5, bf16[32,1024]{1,0:T(8,128)(2,1)S(1)} %copy-done.4, bf16[1,2,8192,128]{3,2,1,0:T(8,128)(2,1)S(1)} %copy-done.1, ...), custom_call_target="tpu_custom_call" | custom-call | flops 1073741824 | bytes 16777216 | tf_op jit(solution)/shard_map/attend/pallas_call | solution.py:204
  57.3 2.9 %collective-permute-start.7 = (bf16[32,1024]{1,0:T(8,128)(2,1)S(1)}, bf16[32,1024]{1,0:T(8,128)(2,1)S(1)}, u32[]{:S(2)}, u32[]{:S(2)}) collective-permute-start(bf16[32,1024]{1,0:T(8,128)(2,1)S(1)} %get-tuple-element.21), channel_id=1, source_target_pairs={{0,1},{1,0},{2,3},{3,2},{4,5},{5,4},{6,7},{7,6},{8,9},{9,8},{10,11... | collective-permute-start | bytes 196616 | tf_op jit(solution)/shard_map/ppermute | solution.py:486
  60.3 1.9 %collective-permute-start.9 = (bf16[32,1024]{1,0:T(8,128)(2,1)S(1)}, bf16[32,1024]{1,0:T(8,128)(2,1)S(1)}, u32[]{:S(2)}, u32[]{:S(2)}) collective-permute-start(bf16[32,1024]{1,0:T(8,128)(2,1)S(1)} %get-tuple-element.23), channel_id=1, source_target_pairs={{0,1},{1,0},{2,3},{3,2},{4,5},{5,4},{6,7},{7,6},{8,9},{9,8},{10,11... | collective-permute-start | bytes 196616 | tf_op jit(solution)/shard_map/ppermute | solution.py:486
  62.2 5.8 %copy-done = bf16[1024,8192]{1,0:T(8,128)(2,1)S(1)} copy-done((bf16[1024,8192]{1,0:T(8,128)(2,1)S(1)}, bf16[1024,8192]{1,0:T(8,128)(2,1)}, u32[]{:S(2)}) %copy-start) | copy-done | bytes 16777240
  68.0 3.5 %own_part.1 = (f32[32,1024]{1,0:T(8,128)S(1)}, f32[32,1024]{1,0:T(8,128)S(1)}, f32[32,1024]{1,0:T(8,128)S(1)}, f32[32,1024]{1,0:T(8,128)S(1)}) custom-call(bf16[32,1024]{1,0:T(8,128)(2,1)S(1)} %get-tuple-element.16.att_ref, bf16[1024,8192]{1,0:T(8,128)(2,1)S(1)} %copy-done), custom_call_target="tpu_custom_call" | custom-call | flops 268435456 | bytes 8388608 | tf_op jit(solution)/shard_map/own_part/pallas_call | solution.py:259
  71.5 0.6 copy-done.3
  72.2 0.8 broadcast_in_dim.2.column_ref
  73.1 4.5 %shrink_part.1 = f32[32,128]{1,0:T(8,128)} custom-call(s32[32]{0:T(128)} %ids_ref.3, s32[128]{0:T(128)} %slot_ref.5, s32[32,128]{1,0:T(8,128)} %broadcast_in_dim.2.column_ref, bf16[32,1024]{1,0:T(8,128)(2,1)} %copy-done.2, bf16[64,2,64,1024]{3,2,1,0:T(8,128)(2,1)} %pages_ref.5, bf16[8,64,1024]{2,1,0:T(8,128)(2,1)} %copy-done.7), custom_call_target="tpu_custom_call" | custom-call | flops 33554432 | bytes 1048576 | tf_op jit(solution)/shard_map/shrink_part/pallas_call | solution.py:405
  77.7 1.8 %collective-permute-start.2 = (f32[32,128]{1,0:T(8,128)}, f32[32,128]{1,0:T(8,128)S(1)}, u32[]{:S(2)}, u32[]{:S(2)}) collective-permute-start(f32[32,128]{1,0:T(8,128)} %shrink_part.1), channel_id=1, source_target_pairs={{0,1},{1,0},{2,3},{3,2},{4,5},{5,4},{6,7},{7,6},{8,9},{9,8},{10,11... | collective-permute-start | bytes 49160 | tf_op jit(solution)/shard_map/ppermute | solution.py:486
  79.5 2.2 %collective-permute-done.2 = f32[32,128]{1,0:T(8,128)S(1)} collective-permute-done((f32[32,128]{1,0:T(8,128)}, f32[32,128]{1,0:T(8,128)S(1)}, u32[]{:S(2)}, u32[]{:S(2)}) %collective-permute-start.2) | collective-permute-done | bytes 16416 | tf_op jit(solution)/shard_map/ppermute | solution.py:486
  81.7 1.8 %collective-permute-start.8 = (bf16[32,1024]{1,0:T(8,128)(2,1)S(1)}, bf16[32,1024]{1,0:T(8,128)(2,1)S(1)}, u32[]{:S(2)}, u32[]{:S(2)}) collective-permute-start(bf16[32,1024]{1,0:T(8,128)(2,1)S(1)} %add_convert_fusion.3), channel_id=1, source_target_pairs={{0,2},{1,3},{2,0},{3,1},{4,6},{5,7},{6,4},{7,5},{8,10},{9,11},{10,... | collective-permute-start | bytes 196616 | tf_op jit(solution)/shard_map/ppermute | solution.py:489
  83.5 0.7 add.27
  84.5 3.5 %collective-permute-done.3 = f32[32,128]{1,0:T(8,128)S(1)} collective-permute-done((f32[32,128]{1,0:T(8,128)S(1)}, f32[32,128]{1,0:T(8,128)S(1)}, u32[]{:S(2)}, u32[]{:S(2)}) %collective-permute-start.3) | collective-permute-done | bytes 16416 | tf_op jit(solution)/shard_map/ppermute | solution.py:489
  88.0 2.5 %collective-permute-start.10 = (bf16[32,1024]{1,0:T(8,128)(2,1)S(1)}, bf16[32,1024]{1,0:T(8,128)(2,1)S(1)}, u32[]{:S(2)}, u32[]{:S(2)}) collective-permute-start(bf16[32,1024]{1,0:T(8,128)(2,1)S(1)} %add_convert_fusion.2), channel_id=1, source_target_pairs={{0,4},{1,5},{2,6},{3,7},{4,0},{5,1},{6,2},{7,3},{8,12},{9,13},{10,... | collective-permute-start | bytes 196616 | tf_op jit(solution)/shard_map/ppermute | solution.py:489
  91.0 4.8 %collective-permute-done.4 = f32[32,128]{1,0:T(8,128)S(1)} collective-permute-done((f32[32,128]{1,0:T(8,128)S(1)}, f32[32,128]{1,0:T(8,128)S(1)}, u32[]{:S(2)}, u32[]{:S(2)}) %collective-permute-start.4) | collective-permute-done | bytes 16416 | tf_op jit(solution)/shard_map/ppermute | solution.py:489
  95.8 2.1 %collective-permute-start.12 = (bf16[32,1024]{1,0:T(8,128)(2,1)S(1)}, bf16[32,1024]{1,0:T(8,128)(2,1)S(1)}, u32[]{:S(2)}, u32[]{:S(2)}) collective-permute-start(bf16[32,1024]{1,0:T(8,128)(2,1)S(1)} %add_convert_fusion.1), channel_id=1, source_target_pairs={{0,6},{1,7},{2,4},{3,5},{4,2},{5,3},{6,0},{7,1},{8,14},{9,15},{10,... | collective-permute-start | bytes 196616 | tf_op jit(solution)/shard_map/ppermute | solution.py:489
  97.8 0.6 add.29.low_ref
  99.5 4.6 %expand_part.1 = f32[32,1024]{1,0:T(8,128)} custom-call(s32[32]{0:T(128)} %ids_ref.3, s32[128]{0:T(128)} %slot_ref.5, s32[32,128]{1,0:T(8,128)} %broadcast_in_dim.2.column_ref, f32[32,128]{1,0:T(8,128)} %add.29.low_ref, bf16[64,2,64,1024]{3,2,1,0:T(8,128)(2,1)} %pages_ref.5, bf16[8,64,1024]{2,1,0:T(8,128)(2,1)} %copy-done.6, f32[32,1024]{1,0:T(8,128)} %copy-done.3, ...), custom_call_target="tpu_custom_call" | custom-call | flops 33554432 | bytes 1048576 | tf_op jit(solution)/shard_map/expand_part/pallas_call | solution.py:419
  104.1 0.9 add_convert_fusion.refs_0_
  105.1 2.3 %collective-permute-start.16 = (bf16[32,1024]{1,0:T(8,128)(2,1)S(1)}, bf16[32,1024]{1,0:T(8,128)(2,1)S(1)}, u32[]{:S(2)}, u32[]{:S(2)}) collective-permute-start(bf16[32,1024]{1,0:T(8,128)(2,1)S(1)} %add_convert_fusion.refs_0_), channel_id=1, source_target_pairs={{0,4},{1,5},{2,6},{3,7},{4,0},{5,1},{6,2},{7,3},{8,12},{9,13},{10,... | collective-permute-start | bytes 196616 | tf_op jit(solution)/shard_map/ppermute | solution.py:489
  107.5 2.1 %collective-permute-start.18 = (bf16[32,1024]{1,0:T(8,128)(2,1)S(1)}, bf16[32,1024]{1,0:T(8,128)(2,1)S(1)}, u32[]{:S(2)}, u32[]{:S(2)}) collective-permute-start(bf16[32,1024]{1,0:T(8,128)(2,1)S(1)} %add_convert_fusion.refs_0_), channel_id=1, source_target_pairs={{0,6},{1,7},{2,4},{3,5},{4,2},{5,3},{6,0},{7,1},{8,14},{9,15},{10,... | collective-permute-start | bytes 196616 | tf_op jit(solution)/shard_map/ppermute | solution.py:489
  109.5 1.6 %collective-permute-start.13 = (bf16[32,1024]{1,0:T(8,128)(2,1)S(1)}, bf16[32,1024]{1,0:T(8,128)(2,1)S(1)}, u32[]{:S(2)}, u32[]{:S(2)}) collective-permute-start(bf16[32,1024]{1,0:T(8,128)(2,1)S(1)} %add_convert_fusion.refs_0_), channel_id=1, source_target_pairs={{0,1},{1,0},{2,3},{3,2},{4,5},{5,4},{6,7},{7,6},{8,9},{9,8},{10,11... | collective-permute-start | bytes 196616 | tf_op jit(solution)/shard_map/ppermute | solution.py:486
  111.6 1.6 %collective-permute-start.17 = (bf16[32,1024]{1,0:T(8,128)(2,1)S(1)}, bf16[32,1024]{1,0:T(8,128)(2,1)S(1)}, u32[]{:S(2)}, u32[]{:S(2)}) collective-permute-start(bf16[32,1024]{1,0:T(8,128)(2,1)S(1)} %collective-permute-done.16.refs_4_), channel_id=1, source_target_pairs={{0,1},{1,0},{2,3},{3,2},{4,5},{5,4},{6,7},{7,6},{8,9},{9,8},{10,11... | collective-permute-start | bytes 196616 | tf_op jit(solution)/shard_map/ppermute | solution.py:486
  113.5 1.3 collective-permute-start.19
  114.8 0.6 collective-permute-done.15.refs_3_
  115.4 0.7 collective-permute-done.17.refs_5_
  116.1 1.7 %collective-permute-done.19.refs_7_ = bf16[32,1024]{1,0:T(8,128)(2,1)S(1)} collective-permute-done((bf16[32,1024]{1,0:T(8,128)(2,1)S(1)}, bf16[32,1024]{1,0:T(8,128)(2,1)S(1)}, u32[]{:S(2)}, u32[]{:S(2)}) %collective-permute-start.19) | collective-permute-done | bytes 65568 | tf_op jit(solution)/shard_map/ppermute | solution.py:486
  117.9 0.6 copy-done.16
  118.5 17.1 %place.1 = bf16[32,8192]{1,0:T(8,128)(2,1)} custom-call(bf16[32,1024]{1,0:T(8,128)(2,1)} %copy-done.8, bf16[32,1024]{1,0:T(8,128)(2,1)} %copy-done.13, bf16[32,1024]{1,0:T(8,128)(2,1)} %copy-done.10, bf16[32,1024]{1,0:T(8,128)(2,1)} %copy-done.14, bf16[32,1024]{1,0:T(8,128)(2,1)} %copy-done.11, bf16[32,1024]{1,0:T(8,128)(2,1)} %copy-done.15, ...), custom_call_target="tpu_custom_call" | custom-call | bytes 1048576 | tf_op jit(solution)/shard_map/place/pallas_call | solution.py:460
  (60 shorter events, 4.4 us)
Async XLA Ops:
  0.0 45.4 %copy-start.5 = (s32[32]{0:T(128)S(1)}, s32[32]{0:T(128)}, u32[]{:S(2)}) copy-start(s32[32]{0:T(128)} %len_ref.1) | copy-start | bytes 388
  0.0 45.4 %copy-start.4 = (bf16[32,1024]{1,0:T(8,128)(2,1)S(1)}, bf16[32,1024]{1,0:T(8,128)(2,1)}, u32[]{:S(2)}) copy-start(bf16[32,1024]{1,0:T(8,128)(2,1)} %q_ref.1) | copy-start | bytes 196612
  0.0 1.4 %collective-permute-start = (s32[32]{0:T(128)}, s32[32]{0:T(128)S(1)}, u32[]{:S(2)}, u32[]{:S(2)}) collective-permute-start(s32[32]{0:T(128)} %ids_ref.3), channel_id=1, source_target_pairs={{0,8},{8,0},{1,9},{9,1},{2,10},{10,2},{3,11},{11,3},{4,12},{12,4},... | collective-permute-start | bytes 392 | tf_op jit(solution)/shard_map/ppermute | solution.py:492
  44.8 27.3 %collective-permute-start.1 = (bf16[8,64,1024]{2,1,0:T(8,128)(2,1)}, bf16[8,64,1024]{2,1,0:T(8,128)(2,1)S(1)}, u32[]{:S(2)}, u32[]{:S(2)}) collective-permute-start(bf16[8,64,1024]{2,1,0:T(8,128)(2,1)} %get-tuple-element.17), channel_id=1, source_target_pairs={{0,8},{8,0},{1,9},{9,1},{2,10},{10,2},{3,11},{11,3},{4,12},{12,4},... | collective-permute-start | bytes 3145736 | tf_op jit(solution)/shard_map/ppermute | solution.py:492
  44.9 53.5 %collective-permute-start.5 = (bf16[8,64,1024]{2,1,0:T(8,128)(2,1)}, bf16[8,64,1024]{2,1,0:T(8,128)(2,1)S(1)}, u32[]{:S(2)}, u32[]{:S(2)}) collective-permute-start(bf16[8,64,1024]{2,1,0:T(8,128)(2,1)} %get-tuple-element.18), channel_id=1, source_target_pairs={{0,8},{8,0},{1,9},{9,1},{2,10},{10,2},{3,11},{11,3},{4,12},{12,4},... | collective-permute-start | bytes 3145736 | tf_op jit(solution)/shard_map/ppermute | solution.py:492
  45.4 2.2 %copy-start.1 = (bf16[1,2,8192,128]{3,2,1,0:T(8,128)(2,1)S(1)}, bf16[1,2,8192,128]{3,2,1,0:T(8,128)(2,1)}, u32[]{:S(2)}) copy-start(bf16[1,2,8192,128]{3,2,1,0:T(8,128)(2,1)} %prefix_ref.1) | copy-start | bytes 12582916
  47.6 24.6 %copy-start.17 = (s32[32]{0:T(128)S(1)}, s32[32]{0:T(128)}, u32[]{:S(2)}) copy-start(s32[32]{0:T(128)} %ids_ref.3) | copy-start | bytes 388
  57.3 15.8 %copy-start.2 = (bf16[32,1024]{1,0:T(8,128)(2,1)}, bf16[32,1024]{1,0:T(8,128)(2,1)S(1)}, u32[]{:S(2)}) copy-start(bf16[32,1024]{1,0:T(8,128)(2,1)S(1)} %get-tuple-element.16.att_ref) | copy-start | bytes 196612
  57.3 20.4 %collective-permute-start.7 = (bf16[32,1024]{1,0:T(8,128)(2,1)S(1)}, bf16[32,1024]{1,0:T(8,128)(2,1)S(1)}, u32[]{:S(2)}, u32[]{:S(2)}) collective-permute-start(bf16[32,1024]{1,0:T(8,128)(2,1)S(1)} %get-tuple-element.21), channel_id=1, source_target_pairs={{0,1},{1,0},{2,3},{3,2},{4,5},{5,4},{6,7},{7,6},{8,9},{9,8},{10,11... | collective-permute-start | bytes 196616 | tf_op jit(solution)/shard_map/ppermute | solution.py:486
  60.2 38.3 %collective-permute-start.6 = (bf16[32,1024]{1,0:T(8,128)(2,1)S(1)}, bf16[32,1024]{1,0:T(8,128)(2,1)S(1)}, u32[]{:S(2)}, u32[]{:S(2)}) collective-permute-start(bf16[32,1024]{1,0:T(8,128)(2,1)S(1)} %get-tuple-element.20), channel_id=1, source_target_pairs={{0,1},{1,0},{2,3},{3,2},{4,5},{5,4},{6,7},{7,6},{8,9},{9,8},{10,11... | collective-permute-start | bytes 196616 | tf_op jit(solution)/shard_map/ppermute | solution.py:486
  60.3 24.0 %collective-permute-start.9 = (bf16[32,1024]{1,0:T(8,128)(2,1)S(1)}, bf16[32,1024]{1,0:T(8,128)(2,1)S(1)}, u32[]{:S(2)}, u32[]{:S(2)}) collective-permute-start(bf16[32,1024]{1,0:T(8,128)(2,1)S(1)} %get-tuple-element.23), channel_id=1, source_target_pairs={{0,1},{1,0},{2,3},{3,2},{4,5},{5,4},{6,7},{7,6},{8,9},{9,8},{10,11... | collective-permute-start | bytes 196616 | tf_op jit(solution)/shard_map/ppermute | solution.py:486
  62.2 5.8 %copy-start = (bf16[1024,8192]{1,0:T(8,128)(2,1)S(1)}, bf16[1024,8192]{1,0:T(8,128)(2,1)}, u32[]{:S(2)}) copy-start(bf16[1024,8192]{1,0:T(8,128)(2,1)} %weight_ref.3) | copy-start | bytes 50331652
  72.1 18.4 %collective-permute-start.11 = (bf16[32,1024]{1,0:T(8,128)(2,1)S(1)}, bf16[32,1024]{1,0:T(8,128)(2,1)S(1)}, u32[]{:S(2)}, u32[]{:S(2)}) collective-permute-start(bf16[32,1024]{1,0:T(8,128)(2,1)S(1)} %get-tuple-element.25), channel_id=1, source_target_pairs={{0,1},{1,0},{2,3},{3,2},{4,5},{5,4},{6,7},{7,6},{8,9},{9,8},{10,11... | collective-permute-start | bytes 196616 | tf_op jit(solution)/shard_map/ppermute | solution.py:486
  77.7 4.0 %collective-permute-start.2 = (f32[32,128]{1,0:T(8,128)}, f32[32,128]{1,0:T(8,128)S(1)}, u32[]{:S(2)}, u32[]{:S(2)}) collective-permute-start(f32[32,128]{1,0:T(8,128)} %shrink_part.1), channel_id=1, source_target_pairs={{0,1},{1,0},{2,3},{3,2},{4,5},{5,4},{6,7},{7,6},{8,9},{9,8},{10,11... | collective-permute-start | bytes 49160 | tf_op jit(solution)/shard_map/ppermute | solution.py:486
  81.7 22.4 %collective-permute-start.8 = (bf16[32,1024]{1,0:T(8,128)(2,1)S(1)}, bf16[32,1024]{1,0:T(8,128)(2,1)S(1)}, u32[]{:S(2)}, u32[]{:S(2)}) collective-permute-start(bf16[32,1024]{1,0:T(8,128)(2,1)S(1)} %add_convert_fusion.3), channel_id=1, source_target_pairs={{0,2},{1,3},{2,0},{3,1},{4,6},{5,7},{6,4},{7,5},{8,10},{9,11},{10,... | collective-permute-start | bytes 196616 | tf_op jit(solution)/shard_map/ppermute | solution.py:489
  84.2 3.8 %collective-permute-start.3 = (f32[32,128]{1,0:T(8,128)S(1)}, f32[32,128]{1,0:T(8,128)S(1)}, u32[]{:S(2)}, u32[]{:S(2)}) collective-permute-start(f32[32,128]{1,0:T(8,128)S(1)} %add.27), channel_id=1, source_target_pairs={{0,2},{1,3},{2,0},{3,1},{4,6},{5,7},{6,4},{7,5},{8,10},{9,11},{10,... | collective-permute-start | bytes 49160 | tf_op jit(solution)/shard_map/ppermute | solution.py:489
  88.0 16.1 %collective-permute-start.10 = (bf16[32,1024]{1,0:T(8,128)(2,1)S(1)}, bf16[32,1024]{1,0:T(8,128)(2,1)S(1)}, u32[]{:S(2)}, u32[]{:S(2)}) collective-permute-start(bf16[32,1024]{1,0:T(8,128)(2,1)S(1)} %add_convert_fusion.2), channel_id=1, source_target_pairs={{0,4},{1,5},{2,6},{3,7},{4,0},{5,1},{6,2},{7,3},{8,12},{9,13},{10,... | collective-permute-start | bytes 196616 | tf_op jit(solution)/shard_map/ppermute | solution.py:489
  90.5 5.2 %collective-permute-start.4 = (f32[32,128]{1,0:T(8,128)S(1)}, f32[32,128]{1,0:T(8,128)S(1)}, u32[]{:S(2)}, u32[]{:S(2)}) collective-permute-start(f32[32,128]{1,0:T(8,128)S(1)} %add.28), channel_id=1, source_target_pairs={{0,4},{1,5},{2,6},{3,7},{4,0},{5,1},{6,2},{7,3},{8,12},{9,13},{10,... | collective-permute-start | bytes 49160 | tf_op jit(solution)/shard_map/ppermute | solution.py:489
  95.8 8.3 %collective-permute-start.12 = (bf16[32,1024]{1,0:T(8,128)(2,1)S(1)}, bf16[32,1024]{1,0:T(8,128)(2,1)S(1)}, u32[]{:S(2)}, u32[]{:S(2)}) collective-permute-start(bf16[32,1024]{1,0:T(8,128)(2,1)S(1)} %add_convert_fusion.1), channel_id=1, source_target_pairs={{0,6},{1,7},{2,4},{3,5},{4,2},{5,3},{6,0},{7,1},{8,14},{9,15},{10,... | collective-permute-start | bytes 196616 | tf_op jit(solution)/shard_map/ppermute | solution.py:489
  105.1 12.7 %copy-start.8 = (bf16[32,1024]{1,0:T(8,128)(2,1)}, bf16[32,1024]{1,0:T(8,128)(2,1)S(1)}, u32[]{:S(2)}) copy-start(bf16[32,1024]{1,0:T(8,128)(2,1)S(1)} %add_convert_fusion.refs_0_) | copy-start | bytes 196612
  105.1 6.1 %collective-permute-start.14 = (bf16[32,1024]{1,0:T(8,128)(2,1)S(1)}, bf16[32,1024]{1,0:T(8,128)(2,1)S(1)}, u32[]{:S(2)}, u32[]{:S(2)}) collective-permute-start(bf16[32,1024]{1,0:T(8,128)(2,1)S(1)} %add_convert_fusion.refs_0_), channel_id=1, source_target_pairs={{0,2},{1,3},{2,0},{3,1},{4,6},{5,7},{6,4},{7,5},{8,10},{9,11},{10,... | collective-permute-start | bytes 196616 | tf_op jit(solution)/shard_map/ppermute | solution.py:489
  105.1 6.4 %collective-permute-start.16 = (bf16[32,1024]{1,0:T(8,128)(2,1)S(1)}, bf16[32,1024]{1,0:T(8,128)(2,1)S(1)}, u32[]{:S(2)}, u32[]{:S(2)}) collective-permute-start(bf16[32,1024]{1,0:T(8,128)(2,1)S(1)} %add_convert_fusion.refs_0_), channel_id=1, source_target_pairs={{0,4},{1,5},{2,6},{3,7},{4,0},{5,1},{6,2},{7,3},{8,12},{9,13},{10,... | collective-permute-start | bytes 196616 | tf_op jit(solution)/shard_map/ppermute | solution.py:489
  107.5 6.1 %collective-permute-start.18 = (bf16[32,1024]{1,0:T(8,128)(2,1)S(1)}, bf16[32,1024]{1,0:T(8,128)(2,1)S(1)}, u32[]{:S(2)}, u32[]{:S(2)}) collective-permute-start(bf16[32,1024]{1,0:T(8,128)(2,1)S(1)} %add_convert_fusion.refs_0_), channel_id=1, source_target_pairs={{0,6},{1,7},{2,4},{3,5},{4,2},{5,3},{6,0},{7,1},{8,14},{9,15},{10,... | collective-permute-start | bytes 196616 | tf_op jit(solution)/shard_map/ppermute | solution.py:489
  109.5 5.3 %collective-permute-start.13 = (bf16[32,1024]{1,0:T(8,128)(2,1)S(1)}, bf16[32,1024]{1,0:T(8,128)(2,1)S(1)}, u32[]{:S(2)}, u32[]{:S(2)}) collective-permute-start(bf16[32,1024]{1,0:T(8,128)(2,1)S(1)} %add_convert_fusion.refs_0_), channel_id=1, source_target_pairs={{0,1},{1,0},{2,3},{3,2},{4,5},{5,4},{6,7},{7,6},{8,9},{9,8},{10,11... | collective-permute-start | bytes 196616 | tf_op jit(solution)/shard_map/ppermute | solution.py:486
  111.2 6.6 %copy-start.10 = (bf16[32,1024]{1,0:T(8,128)(2,1)}, bf16[32,1024]{1,0:T(8,128)(2,1)S(1)}, u32[]{:S(2)}) copy-start(bf16[32,1024]{1,0:T(8,128)(2,1)S(1)} %collective-permute-done.14.refs_2_) | copy-start | bytes 196612
  111.2 4.3 %collective-permute-start.15 = (bf16[32,1024]{1,0:T(8,128)(2,1)S(1)}, bf16[32,1024]{1,0:T(8,128)(2,1)S(1)}, u32[]{:S(2)}, u32[]{:S(2)}) collective-permute-start(bf16[32,1024]{1,0:T(8,128)(2,1)S(1)} %collective-permute-done.14.refs_2_), channel_id=1, source_target_pairs={{0,1},{1,0},{2,3},{3,2},{4,5},{5,4},{6,7},{7,6},{8,9},{9,8},{10,11... | collective-permute-start | bytes 196616 | tf_op jit(solution)/shard_map/ppermute | solution.py:486
  111.6 6.2 %copy-start.11 = (bf16[32,1024]{1,0:T(8,128)(2,1)}, bf16[32,1024]{1,0:T(8,128)(2,1)S(1)}, u32[]{:S(2)}) copy-start(bf16[32,1024]{1,0:T(8,128)(2,1)S(1)} %collective-permute-done.16.refs_4_) | copy-start | bytes 196612
  111.6 4.6 %collective-permute-start.17 = (bf16[32,1024]{1,0:T(8,128)(2,1)S(1)}, bf16[32,1024]{1,0:T(8,128)(2,1)S(1)}, u32[]{:S(2)}, u32[]{:S(2)}) collective-permute-start(bf16[32,1024]{1,0:T(8,128)(2,1)S(1)} %collective-permute-done.16.refs_4_), channel_id=1, source_target_pairs={{0,1},{1,0},{2,3},{3,2},{4,5},{5,4},{6,7},{7,6},{8,9},{9,8},{10,11... | collective-permute-start | bytes 196616 | tf_op jit(solution)/shard_map/ppermute | solution.py:486
  113.5 4.3 %copy-start.12 = (bf16[32,1024]{1,0:T(8,128)(2,1)}, bf16[32,1024]{1,0:T(8,128)(2,1)S(1)}, u32[]{:S(2)}) copy-start(bf16[32,1024]{1,0:T(8,128)(2,1)S(1)} %collective-permute-done.18.refs_6_) | copy-start | bytes 196612
  113.5 4.3 %collective-permute-start.19 = (bf16[32,1024]{1,0:T(8,128)(2,1)S(1)}, bf16[32,1024]{1,0:T(8,128)(2,1)S(1)}, u32[]{:S(2)}, u32[]{:S(2)}) collective-permute-start(bf16[32,1024]{1,0:T(8,128)(2,1)S(1)} %collective-permute-done.18.refs_6_), channel_id=1, source_target_pairs={{0,1},{1,0},{2,3},{3,2},{4,5},{5,4},{6,7},{7,6},{8,9},{9,8},{10,11... | collective-permute-start | bytes 196616 | tf_op jit(solution)/shard_map/ppermute | solution.py:486
  114.8 3.0 %copy-start.13 = (bf16[32,1024]{1,0:T(8,128)(2,1)}, bf16[32,1024]{1,0:T(8,128)(2,1)S(1)}, u32[]{:S(2)}) copy-start(bf16[32,1024]{1,0:T(8,128)(2,1)S(1)} %collective-permute-done.13.refs_1_) | copy-start | bytes 196612
  115.4 2.4 %copy-start.14 = (bf16[32,1024]{1,0:T(8,128)(2,1)}, bf16[32,1024]{1,0:T(8,128)(2,1)S(1)}, u32[]{:S(2)}) copy-start(bf16[32,1024]{1,0:T(8,128)(2,1)S(1)} %collective-permute-done.15.refs_3_) | copy-start | bytes 196612
  (7 other events, 6.1 us)

commit v2 on v1

v2 whole, which is shorter than its diff:
```python
import functools

import jax
import jax.numpy as jnp
from jax import lax
from jax.experimental import pallas as pl
from jax.experimental.pallas import tpu as pltpu
from jax.sharding import PartitionSpec as P

F32 = jnp.float32
BF16 = jnp.bfloat16
LOG2E = 1.4426950408889634
ANY = pl.BlockSpec(memory_space=pl.ANY)
VMEM = pl.BlockSpec(memory_space=pltpu.VMEM)
SMEM = pl.BlockSpec(memory_space=pltpu.SMEM)
MIB = 1 << 20
DISTINCT = 8
ROOM = pltpu.CompilerParams(vmem_limit_bytes=54 * MIB)


def nt_dot(a, b):
    return lax.dot_general(a, b, (((1,), (1,)), ((), ())), preferred_element_type=F32)


def nn_dot(a, b):
    return jnp.dot(a, b, preferred_element_type=F32)


def distinct_list(ids_ref, pool_slot_ref, seen, list_id, list_pos):
    rows = ids_ref.shape[0]
    for i in range(pool_slot_ref.shape[0]):
        seen[i] = 0
    for j in range(DISTINCT + 1):
        list_id[j] = -1
        list_pos[j] = 0
    found = jnp.int32(0)
    for r in range(rows):
        one = ids_ref[r]
        fresh = 1 - seen[one]
        seen[one] = 1
        spot = jnp.minimum(found, DISTINCT)
        list_id[spot] = jnp.where(fresh == 1, one, list_id[spot])
        list_pos[spot] = jnp.where(fresh == 1, pool_slot_ref[one], list_pos[spot])
        found = found + fresh


def list_scratch(pool_slot):
    return [
        pltpu.SMEM((pool_slot.shape[0],), jnp.int32),
        pltpu.SMEM((DISTINCT + 1,), jnp.int32),
        pltpu.SMEM((DISTINCT + 1,), jnp.int32),
    ]


def page_copies(pages_ref, outs, list_pos, sem, wait):
    pool = pages_ref.shape[0]
    me = lax.axis_index("req")
    for j in range(DISTINCT):
        pos = list_pos[j]

        @pl.when(pos // pool == me)
        def _():
            for i, out in enumerate(outs):
                copy = pltpu.make_async_copy(pages_ref.at[pos % pool, i], out.at[j], sem.at[i, j])
                if wait:
                    copy.wait()
                else:
                    copy.start()


def attend_kernel(
    n_z,
    len_ref,
    ids_ref,
    slot_ref,
    q_ref,
    prefix_ref,
    suffix_ref,
    weight_ref,
    pages_ref,
    att_ref,
    shrink_ref,
    expand_ref,
    row_slot_ref,
    slot_mine_ref,
    *rest,
):
    piece_refs = rest[:n_z]
    (
        kv,
        suf,
        wbuf,
        scores,
        tail,
        rowbuf,
        peak,
        total,
        acc,
        seen,
        list_id,
        list_pos,
        sem_kv,
        sem_suf,
        sem_w,
        sem_page,
    ) = rest[n_z:]
    rows = q_ref.shape[0]
    head_dim = prefix_ref.shape[3]
    heads = q_ref.shape[1] // head_dim
    n_q = rows * heads
    tokens = prefix_ref.shape[2]
    span = suffix_ref.shape[3]
    width = piece_refs[0].shape[1]
    me = lax.axis_index("tensor")
    z, y = me // 2, me % 2
    scale2 = float(head_dim) ** -0.5 * LOG2E

    n_part = 4
    part = tokens // n_part
    kv_copies = [
        [
            pltpu.make_async_copy(
                prefix_ref.at[0, i, pl.ds(j * part, part)],
                kv.at[i, pl.ds(j * part, part)],
                sem_kv.at[i, j],
            )
            for j in range(n_part)
        ]
        for i in range(2)
    ]
    n_sgrp = 4
    sgrp = rows // n_sgrp
    suf_copies = [
        pltpu.make_async_copy(
            suffix_ref.at[pl.ds(j * sgrp, sgrp), 0], suf.at[pl.ds(j * sgrp, sgrp)], sem_suf.at[j]
        )
        for j in range(n_sgrp)
    ]
    w_copies = []
    for k in range(n_z):
        column = pl.multiple_of(((z ^ k) * 2 + (1 - y)) * width, width)
        w_copies.append(
            pltpu.make_async_copy(weight_ref.at[:, pl.ds(column, width)], wbuf.at[k], sem_w.at[k])
        )
    for c in kv_copies[0] + suf_copies + kv_copies[1]:
        c.start()
    distinct_list(ids_ref, slot_ref, seen, list_id, list_pos)
    page_copies(pages_ref, (shrink_ref, expand_ref), list_pos, sem_page, False)
    row_index = lax.broadcasted_iota(jnp.int32, (rows, 128), 0)
    row_id = jnp.full((rows, 128), -2, jnp.int32)
    for r in range(rows):
        row_id = jnp.where(row_index == r, ids_ref[r], row_id)
    row_slot = jnp.full((rows, 128), -1, jnp.int32)
    slot_index = lax.broadcasted_iota(jnp.int32, (DISTINCT, 128), 0)
    slot_mine = jnp.zeros((DISTINCT, 128), jnp.int32)
    mine = lax.axis_index("req")
    for j in range(DISTINCT):
        row_slot = jnp.where(row_id == list_id[j], j, row_slot)
        owned = (list_pos[j] // pages_ref.shape[0] == mine).astype(jnp.int32)
        slot_mine = jnp.where(slot_index == j, owned, slot_mine)
    row_slot_ref[...] = row_slot
    slot_mine_ref[...] = slot_mine

    for h in range(heads):
        rowbuf[pl.ds(h, rows, stride=heads), :] = q_ref[:, h * head_dim : (h + 1) * head_dim].astype(F32)
    query = rowbuf[...].astype(BF16)
    peak[...] = jnp.full(peak.shape, -3.0e38, F32)

    chunk = 1024
    for j in range(n_part):
        kv_copies[0][j].wait()
        if j == 0:
            for c in w_copies[:1]:
                c.start()

        @pl.loop(0, part // chunk)
        def _(i):
            base = pl.multiple_of(j * part + i * chunk, chunk)
            best = peak[...]
            for b in range(chunk // 256):
                block = nt_dot(query, kv[0, pl.ds(base + b * 256, 256), :])
                scores[:, pl.ds(base + b * 256, 256)] = block
                best = jnp.maximum(best, jnp.maximum(block[:, :128], block[:, 128:]))
            peak[...] = best

    for c in w_copies[1:]:
        c.start()

    lanes = lax.broadcasted_iota(jnp.int32, (heads, span), 1)
    for j in range(n_sgrp):
        suf_copies[j].wait()
        for i in range(j * sgrp // 2, (j + 1) * sgrp // 2):
            keys = suf[2 * i : 2 * i + 2, 0].reshape(2 * span, head_dim)
            both = nt_dot(query[2 * heads * i : 2 * heads * (i + 1)], keys)
            for a in range(2):
                mine = both[a * heads : (a + 1) * heads, a * span : (a + 1) * span]
                row = 2 * i + a
                tail[row * heads : (row + 1) * heads, :] = jnp.where(lanes < len_ref[row], mine, -1.0e30)
    best = peak[...]
    for b in range(span // 128):
        best = jnp.maximum(best, tail[:, b * 128 : (b + 1) * 128])
    top = jnp.max(best, axis=1, keepdims=True)
    peak[...] = jnp.broadcast_to(top, peak.shape)

    for j in range(n_part):
        kv_copies[1][j].wait()
    total[...] = jnp.zeros(total.shape, F32)
    acc[...] = jnp.zeros(acc.shape, F32)

    @pl.loop(0, tokens // chunk)
    def _(i):
        base = pl.multiple_of(i * chunk, chunk)
        high = peak[...]
        summed = total[...]
        parts = []
        for b in range(chunk // 128):
            e = jnp.exp2((scores[:, pl.ds(base + b * 128, 128)] - high) * scale2)
            summed = summed + e
            parts.append(e.astype(BF16))
        total[...] = summed
        acc[...] += nn_dot(jnp.concatenate(parts, axis=1), kv[1, pl.ds(base, chunk), :])

    zeros = jnp.zeros((heads, span), F32)
    for i in range(rows // 2):
        lo = 2 * heads * i
        high = jnp.concatenate([peak[lo : lo + 2 * heads, :]] * (span // 128), axis=1)
        e = jnp.exp2((tail[lo : lo + 2 * heads, :] - high) * scale2)
        part_sum = e[:, :128]
        for b in range(1, span // 128):
            part_sum = part_sum + e[:, b * 128 : (b + 1) * 128]
        total[lo : lo + 2 * heads, :] += part_sum
        diag = jnp.concatenate(
            [
                jnp.concatenate([e[:heads], zeros], axis=1),
                jnp.concatenate([zeros, e[heads:]], axis=1),
            ],
            axis=0,
        ).astype(BF16)
        vals = suf[2 * i : 2 * i + 2, 1].reshape(2 * span, head_dim)
        acc[lo : lo + 2 * heads, :] += nn_dot(diag, vals)

    norm = jnp.sum(total[...], axis=1, keepdims=True)
    rowbuf[...] = acc[...] / norm
    for h in range(heads):
        att_ref[:, h * head_dim : (h + 1) * head_dim] = rowbuf[pl.ds(h, rows, stride=heads), :].astype(BF16)
    attended = att_ref[...]
    for k in range(n_z):
        w_copies[k].wait()
        piece_refs[k][...] = nn_dot(attended, wbuf[k]).astype(BF16)
    page_copies(pages_ref, (shrink_ref, expand_ref), list_pos, sem_page, True)


def attend(suffix_len, ids, pool_slot, queries, prefix_kv, suffix_kv, out_weight, pages, n_tensor):
    rows = queries.shape[0]
    n_z = n_tensor // 2
    width = out_weight.shape[1] // n_tensor
    tokens, head_dim = prefix_kv.shape[2:]
    n_q = rows * queries.shape[1] // head_dim
    span = suffix_kv.shape[3]
    return pl.pallas_call(
        functools.partial(attend_kernel, n_z),
        out_shape=[
            jax.ShapeDtypeStruct(queries.shape, BF16),
            jax.ShapeDtypeStruct((DISTINCT,) + pages.shape[2:], BF16),
            jax.ShapeDtypeStruct((DISTINCT,) + pages.shape[2:], BF16),
            jax.ShapeDtypeStruct((rows, 128), jnp.int32),
            jax.ShapeDtypeStruct((DISTINCT, 128), jnp.int32),
        ]
        + [jax.ShapeDtypeStruct((rows, width), BF16)] * n_z,
        in_specs=[SMEM, SMEM, SMEM, VMEM, ANY, ANY, ANY, ANY],
        out_specs=[VMEM] * (5 + n_z),
        scratch_shapes=[
            pltpu.VMEM((2, tokens, head_dim), BF16),
            pltpu.VMEM((rows, 2, span, head_dim), BF16),
            pltpu.VMEM((n_z, out_weight.shape[0], width), BF16),
            pltpu.VMEM((n_q, tokens), F32),
            pltpu.VMEM((n_q, span), F32),
            pltpu.VMEM((n_q, head_dim), F32),
            pltpu.VMEM((n_q, 128), F32),
            pltpu.VMEM((n_q, 128), F32),
            pltpu.VMEM((n_q, head_dim), F32),
        ]
        + list_scratch(pool_slot)
        + [
            pltpu.SemaphoreType.DMA((2, 4)),
            pltpu.SemaphoreType.DMA((4,)),
            pltpu.SemaphoreType.DMA((n_z,)),
            pltpu.SemaphoreType.DMA((2, DISTINCT)),
        ],
        compiler_params=ROOM,
        cost_estimate=pl.CostEstimate(
            flops=2 * 2 * n_q * tokens * head_dim,
            bytes_accessed=16 * MIB,
            transcendentals=n_q * tokens,
        ),
        name="attend",
    )(suffix_len, ids, pool_slot, queries, prefix_kv, suffix_kv, out_weight, pages)


def own_kernel(n_z, att_ref, weight_ref, after_ref, *rest):
    piece_refs = rest[:n_z]
    wbuf, sem_w = rest[n_z:]
    width = piece_refs[0].shape[1]
    me = lax.axis_index("tensor")
    z, y = me // 2, me % 2
    copies = []
    for k in range(n_z):
        column = pl.multiple_of(((z ^ k) * 2 + y) * width, width)
        copies.append(
            pltpu.make_async_copy(weight_ref.at[:, pl.ds(column, width)], wbuf.at[k], sem_w.at[k])
        )
    order = list(range(1, n_z)) + [0]
    for k in order:
        copies[k].start()
    attended = att_ref[...]
    for k in order:
        copies[k].wait()
        piece_refs[k][...] = nn_dot(attended, wbuf[k])


def own_part(attended, out_weight, after, n_tensor):
    rows = attended.shape[0]
    n_z = n_tensor // 2
    width = out_weight.shape[1] // n_tensor
    return pl.pallas_call(
        functools.partial(own_kernel, n_z),
        out_shape=[jax.ShapeDtypeStruct((rows, width), F32)] * n_z,
        in_specs=[VMEM, ANY, ANY],
        out_specs=[VMEM] * n_z,
        scratch_shapes=[
            pltpu.VMEM((n_z, out_weight.shape[0], width), BF16),
            pltpu.SemaphoreType.DMA((n_z,)),
        ],
        compiler_params=ROOM,
        cost_estimate=pl.CostEstimate(
            flops=2 * rows * out_weight.shape[0] * width * n_z,
            bytes_accessed=8 * MIB,
            transcendentals=0,
        ),
        name="own_part",
    )(attended, out_weight, after)


def collect_kernel(ids_ref, slot_ref, pages_ref, shrink_ref, expand_ref, seen, list_id, list_pos, sem):
    distinct_list(ids_ref, slot_ref, seen, list_id, list_pos)
    for wait in (False, True):
        page_copies(pages_ref, (shrink_ref, expand_ref), list_pos, sem, wait)


def collect_pages(ids, pool_slot, pages):
    shape = jax.ShapeDtypeStruct((DISTINCT,) + pages.shape[2:], BF16)
    return pl.pallas_call(
        collect_kernel,
        out_shape=[shape, shape],
        in_specs=[SMEM, SMEM, ANY],
        out_specs=[VMEM, VMEM],
        scratch_shapes=list_scratch(pool_slot) + [pltpu.SemaphoreType.DMA((2, DISTINCT))],
        compiler_params=ROOM,
        cost_estimate=pl.CostEstimate(flops=0, bytes_accessed=2 * MIB, transcendentals=0),
        name="collect_pages",
    )(ids, pool_slot, pages)


def merged(own_ref, other_ref, slot_mine):
    rank = own_ref.shape[1]
    tiles = []
    for j in range(DISTINCT):
        hit = jnp.broadcast_to(slot_mine[j : j + 1, :1], (rank, 1)) == 1
        tiles.append(jnp.where(hit, own_ref[j].astype(F32), other_ref[j].astype(F32)).astype(BF16))
    return jnp.concatenate(tiles, axis=0)


def lane_place(shape, rank):
    return lax.broadcasted_iota(jnp.int32, shape, 1) // rank


def shrink_kernel(att_ref, row_slot_ref, slot_mine_ref, own_ref, other_ref, out_ref):
    rank = own_ref.shape[1]
    per_tile = 128 // rank
    low = nt_dot(att_ref[...], merged(own_ref, other_ref, slot_mine_ref[...]))
    row_slot = row_slot_ref[...]
    place = lane_place(row_slot.shape, rank)
    picked = jnp.zeros(row_slot.shape, F32)
    for tile in range(DISTINCT // per_tile):
        hit = row_slot == place + tile * per_tile
        picked = jnp.where(hit, low[:, tile * 128 : (tile + 1) * 128], picked)
    out_ref[...] = picked


def shrink_part(attended, row_slot, slot_mine, own, other):
    rows = attended.shape[0]
    return pl.pallas_call(
        shrink_kernel,
        out_shape=jax.ShapeDtypeStruct((rows, 128), F32),
        in_specs=[VMEM] * 5,
        out_specs=VMEM,
        compiler_params=ROOM,
        cost_estimate=pl.CostEstimate(flops=1 << 25, bytes_accessed=2 * MIB, transcendentals=0),
        name="shrink_part",
    )(attended, row_slot, slot_mine, own, other)


def finish_kernel(n_z, *refs):
    row_slot_ref, slot_mine_ref, own_ref, other_ref, rank_ref, rank_y_ref = refs[:6]
    base_ref, base_y_ref, residual_ref = refs[6:9]
    moved = refs[9 : 9 + n_z - 1]
    out_ref = refs[9 + n_z - 1]
    rank = own_ref.shape[1]
    per_tile = 128 // rank
    width = base_ref.shape[1]
    me = lax.axis_index("tensor")
    low = rank_ref[...] + rank_y_ref[...]
    for ref in moved:
        low = low + ref[:, width:].astype(F32)
    row_slot = row_slot_ref[...]
    place = lane_place(row_slot.shape, rank)
    tiles = []
    for tile in range(DISTINCT // per_tile):
        tiles.append(jnp.where(row_slot == place + tile * per_tile, low, 0.0).astype(BF16))
    total = nn_dot(jnp.concatenate(tiles, axis=1), merged(own_ref, other_ref, slot_mine_ref[...]))
    column = pl.ds(pl.multiple_of(me * width, width), width)
    total = total + (residual_ref[:, column].astype(F32) + (base_ref[...] + base_y_ref[...].astype(F32)))
    for ref in moved:
        total = total + ref[:, :width].astype(F32)
    out_ref[...] = total.astype(BF16)


def finish(n_z, *operands):
    rows, width = operands[6].shape
    return pl.pallas_call(
        functools.partial(finish_kernel, n_z),
        out_shape=jax.ShapeDtypeStruct((rows, width), BF16),
        in_specs=[VMEM] * len(operands),
        out_specs=VMEM,
        compiler_params=ROOM,
        cost_estimate=pl.CostEstimate(flops=1 << 25, bytes_accessed=2 * MIB, transcendentals=0),
        name="finish",
    )(*operands)


def place_kernel(n_z, *refs):
    blocks = refs[: 2 * n_z]
    out_ref = refs[2 * n_z]
    width = blocks[0].shape[1]
    me = lax.axis_index("tensor")
    z, y = me // 2, me % 2
    for k in range(n_z):
        for other in range(2):
            where = (z ^ k) * 2 + (y ^ other)
            out_ref[:, pl.ds(pl.multiple_of(where * width, width), width)] = blocks[2 * k + other][...]


def place(blocks, n_tensor):
    rows, width = blocks[0].shape
    return pl.pallas_call(
        functools.partial(place_kernel, n_tensor // 2),
        out_shape=jax.ShapeDtypeStruct((rows, width * n_tensor), BF16),
        in_specs=[VMEM] * n_tensor,
        out_specs=VMEM,
        compiler_params=ROOM,
        cost_estimate=pl.CostEstimate(flops=0, bytes_accessed=1 * MIB, transcendentals=0),
        name="place",
    )(*blocks)


def body(
    n_tensor,
    queries,
    prefix_kv,
    suffix_kv,
    suffix_len,
    residual,
    out_weight,
    adapter_pages,
    adapter_ids,
    pool_slot,
):
    n_z = n_tensor // 2

    def along_y(x):
        return lax.ppermute(x, "tensor", [(t, t ^ 1) for t in range(n_tensor)])

    def along_z(x, k):
        return lax.ppermute(x, "tensor", [(t, t ^ (2 * k)) for t in range(n_tensor)])

    def across(x):
        return lax.ppermute(x, "req", [(0, 1), (1, 0)])

    other_ids = across(adapter_ids)
    found_shrink, found_expand = collect_pages(other_ids, pool_slot, adapter_pages)
    other_shrink = across(found_shrink)
    other_expand = across(found_expand)
    attended, own_shrink, own_expand, row_slot, slot_mine, *pieces = attend(
        suffix_len, adapter_ids, pool_slot, queries, prefix_kv, suffix_kv, out_weight, adapter_pages, n_tensor
    )
    send_order = list(range(1, n_z)) + [0]
    got_y = {k: along_y(pieces[k]) for k in send_order}
    rank_own = shrink_part(attended, row_slot, slot_mine, own_shrink, other_shrink)
    rank_y = along_y(rank_own)
    own = own_part(attended, out_weight, rank_own, n_tensor)
    rank_both = (rank_own + rank_y).astype(BF16)
    moved = []
    for k in range(1, n_z):
        both = (got_y[k].astype(F32) + own[k]).astype(BF16)
        moved.append(along_z(jnp.concatenate([both, rank_both], axis=1), k))
    result = finish(
        n_z, row_slot, slot_mine, own_expand, other_expand, rank_own, rank_y, own[0], got_y[0], residual, *moved
    )
    blocks = []
    held = [result] + [along_z(result, k) for k in range(1, n_z)]
    for k in range(n_z):
        blocks += [held[k], along_y(held[k])]
    return place(blocks, n_tensor)


def solution(mesh):
    return jax.shard_map(
        functools.partial(body, mesh.shape["tensor"]),
        mesh=mesh,
        in_specs=(
            P(("group", "req"), "tensor"),
            P(("group", "tensor"), None, None, None),
            P(("group", "req"), "tensor", None, None, None),
            P(("group", "req")),
            P(("group", "req"), None),
            P("tensor", None),
            P("req", None, None, "tensor"),
            P(("group", "req")),
            P(),
        ),
        out_specs=P(("group", "req"), None),
        check_vma=False,
    )
```

time: 136 us -> 67.7 us (0.50)
  Pallas kernels: 82.3 us -> 29.4 us
  local copies, waits for them, and re-layouts: 11.7 us -> 2.77 us
  waiting for transfers between devices: 14.8 us -> 10.5 us
  starting transfers between devices: 24.3 us -> 21.6 us
    pallas_call x1, Pallas kernels: 42.9 us -> 3.77 us  [collect_pages(): pl.pallas_call(collect_kernel, out_shape=[shape, shape], in_specs=[SMEM,...]
    pallas_call x1, Pallas kernels: 17.1 us -> 1.9 us  [place(): pl.pallas_call(functools.partial(place_kernel, n_tensor // 2), out_shape=...]
    unnamed x38 -> x36, local copies, waits for them, and re-layouts: 10.9 us -> 2.77 us
    ppermute x8 -> x6, waiting for transfers between devices: 8.64 us -> 3.19 us  [along_z(): return lax.ppermute(x, 'tensor', [(t, t ^ 2 * k) for t in range(n_tensor)])]
    pallas_call x1, Pallas kernels: 9.67 us -> 12.7 us  [attend(): pl.pallas_call(functools.partial(attend_kernel, n_z), out_shape=[jax.Shap...]
    convert_element_type x3, other arithmetic: 0.05 us -> 2.76 us  [body(): both = (got_y[k].astype(F32) + own[k]).astype(BF16)]
    ppermute x8 -> x6, starting transfers between devices: 11.5 us -> 9.11 us  [along_z(): return lax.ppermute(x, 'tensor', [(t, t ^ 2 * k) for t in range(n_tensor)])]
    pallas_call x1, Pallas kernels: 3.5 us -> 5.49 us  [own_part(): pl.pallas_call(functools.partial(own_kernel, n_z), out_shape=[jax.ShapeDt...]
  transfers between devices with their start and end apart: 20 -> 18, of which waited for: 8 -> 7; matrix products, arithmetic and copies ran while one was open for 2% -> 4% of each run, Pallas kernels for 16% -> 31%
where the time goes in v2:
time: 67.7 us; the launch traced here: 67.3 us
  Pallas kernels  29.4 us (43%)
  starting transfers between devices  21.6 us (32%)
  waiting for transfers between devices  10.5 us (16%)
  other arithmetic  2.79 us (4%)
  local copies, waits for them, and re-layouts  2.77 us (4%)
    pallas_call x1, Pallas kernels, attend(): pl.pallas_call(functools.partial(attend_kernel, n_z), out_shape=[jax.Shap...  12.7 us
    ppermute x9, starting transfers between devices, along_y(): return lax.ppermute(x, 'tensor', [(t, t ^ 1) for t in range(n_tensor)])  11.7 us
    ppermute x6, starting transfers between devices, along_z(): return lax.ppermute(x, 'tensor', [(t, t ^ 2 * k) for t in range(n_tensor)])  9.11 us
    ppermute x9, waiting for transfers between devices, along_y(): return lax.ppermute(x, 'tensor', [(t, t ^ 1) for t in range(n_tensor)])  6.35 us
    pallas_call x1, Pallas kernels, own_part(): pl.pallas_call(functools.partial(own_kernel, n_z), out_shape=[jax.ShapeDt...  5.49 us
    pallas_call x1, Pallas kernels, collect_pages(): pl.pallas_call(collect_kernel, out_shape=[shape, shape], in_specs=[SMEM,...  3.77 us
    ppermute x6, waiting for transfers between devices, along_z(): return lax.ppermute(x, 'tensor', [(t, t ^ 2 * k) for t in range(n_tensor)])  3.19 us
    pallas_call x1, Pallas kernels, finish(): pl.pallas_call(functools.partial(finish_kernel, n_z), out_shape=jax.Shape...  2.92 us
  transfers between devices with their start and end apart: 18, of which 7 were waited for; matrix products, arithmetic and copies ran while one was open for 4% of the time, Pallas kernels for 31%

profile of v2, /device:TPU:0, one launch (start us, length us, event | category | flops | bytes accessed | tf_op | source)
XLA Modules:
  0.0 67.3 jit_solution(11040516021294132136)
XLA Ops:
  0.0 0.5 collective-permute-start
  0.5 1.0 %collective-permute-done.ids_ref = s32[32]{0:T(128)S(1)} collective-permute-done((s32[32]{0:T(128)}, s32[32]{0:T(128)S(1)}, u32[]{:S(2)}, u32[]{:S(2)}) %collective-permute-start) | collective-permute-done | bytes 160 | tf_op jit(solution)/shard_map/ppermute | solution.py:487
  1.4 0.5 copy-done.15
  1.9 3.8 %collect_pages.1 = (bf16[8,64,1024]{2,1,0:T(8,128)(2,1)}, bf16[8,64,1024]{2,1,0:T(8,128)(2,1)}) custom-call(s32[32]{0:T(128)} %copy-done.15, s32[128]{0:T(128)} %slot_ref.3, bf16[64,2,64,1024]{3,2,1,0:T(8,128)(2,1)} %pages_ref.3), custom_call_target="tpu_custom_call" | custom-call | bytes 2097152 | tf_op jit(solution)/shard_map/collect_pages/pallas_call | solution.py:352
  6.1 12.7 %attend.1 = (bf16[32,1024]{1,0:T(8,128)(2,1)}, bf16[8,64,1024]{2,1,0:T(8,128)(2,1)}, bf16[8,64,1024]{2,1,0:T(8,128)(2,1)}, s32[32,128]{1,0:T(8,128)}, s32[8,128]...) custom-call(s32[32]{0:T(128)} %len_ref.1, ...), custom_call_target="tpu_custom_call" | custom-call | flops 1073741824 | bytes 16777216 | tf_op jit(solution)/shard_map/attend/pallas_call | solution.py:260
  18.8 2.8 %collective-permute-start.9 = (bf16[32,1024]{1,0:T(8,128)(2,1)}, bf16[32,1024]{1,0:T(8,128)(2,1)S(1)}, u32[]{:S(2)}, u32[]{:S(2)}) collective-permute-start(bf16[32,1024]{1,0:T(8,128)(2,1)} %get-tuple-element.33), channel_id=1, source_target_pairs={{0,1},{1,0},{2,3},{3,2},{4,5},{5,4},{6,7},{7,6},{8,9},{9,8},{10,11... | collective-permute-start | bytes 196616 | tf_op jit(solution)/shard_map/ppermute | solution.py:481
  21.7 1.9 %collective-permute-start.7 = (bf16[32,1024]{1,0:T(8,128)(2,1)}, bf16[32,1024]{1,0:T(8,128)(2,1)S(1)}, u32[]{:S(2)}, u32[]{:S(2)}) collective-permute-start(bf16[32,1024]{1,0:T(8,128)(2,1)} %get-tuple-element.31), channel_id=1, source_target_pairs={{0,1},{1,0},{2,3},{3,2},{4,5},{5,4},{6,7},{7,6},{8,9},{9,8},{10,11... | collective-permute-start | bytes 196616 | tf_op jit(solution)/shard_map/ppermute | solution.py:481
  23.6 1.0 %copy-done.1 = bf16[8,64,1024]{2,1,0:T(8,128)(2,1)} copy-done((bf16[8,64,1024]{2,1,0:T(8,128)(2,1)}, bf16[8,64,1024]{2,1,0:T(8,128)(2,1)S(1)}, u32[]{:S(2)}) %copy-start.1) | copy-done | bytes 1048600
  24.6 2.7 %shrink_part.1.after_ref.refs_4_ = f32[32,128]{1,0:T(8,128)} custom-call(bf16[32,1024]{1,0:T(8,128)(2,1)} %get-tuple-element.24.att_ref, s32[32,128]{1,0:T(8,128)} %get-tuple-element.20.row_slot_ref.refs_0_, s32[8,128]{1,0:T(8,128)} %get-tuple-element.21.slot_mine_ref.refs_1_, bf16[8,64,1024]{2,1,0:T(8,128)(2,1)} %get-tuple-element.25.own_ref, ...), custom_call_target="tpu_custom_call" | custom-call | flops 33554432 | bytes 2097152 | tf_op jit(solution)/shard_map/shrink_part/pallas_call | solution.py:392
  27.4 5.5 %own_part.1 = (f32[32,1024]{1,0:T(8,128)}, f32[32,1024]{1,0:T(8,128)}, f32[32,1024]{1,0:T(8,128)}, f32[32,1024]{1,0:T(8,128)}) custom-call(bf16[32,1024]{1,0:T(8,128)(2,1)} %get-tuple-element.24.att_ref, bf16[1024,8192]{1,0:T(8,128)(2,1)} %weight_ref.3, f32[32,128]{1,0:T(8,128)} %shrink_part.1.after_ref.refs_4_), custom_call_target="tpu_custom_call" | custom-call | flops 268435456 | bytes 8388608 | tf_op jit(solution)/shard_map/own_part/pallas_call | solution.py:325
  32.9 0.9 %add_convert_fusion = bf16[32,1024]{1,0:T(8,128)(2,1)S(1)} fusion(f32[32,1024]{1,0:T(8,128)} %get-tuple-element.34, bf16[32,1024]{1,0:T(8,128)(2,1)S(1)} %collective-permute-done.9), kind=kLoop, calls=%fused_computation | loop fusion | flops 98304 | bytes 262144 | tf_op jit(solution)/shard_map/convert_element_type | solution.py:504
  33.8 0.9 %add_convert_fusion.1 = bf16[32,1024]{1,0:T(8,128)(2,1)S(1)} fusion(f32[32,1024]{1,0:T(8,128)} %get-tuple-element.32, bf16[32,1024]{1,0:T(8,128)(2,1)S(1)} %collective-permute-done.7), kind=kLoop, calls=%fused_computation.1 | loop fusion | flops 98304 | bytes 262144 | tf_op jit(solution)/shard_map/convert_element_type | solution.py:504
  34.8 0.9 %add_convert_fusion.2 = bf16[32,1024]{1,0:T(8,128)(2,1)S(1)} fusion(f32[32,1024]{1,0:T(8,128)} %get-tuple-element.30, bf16[32,1024]{1,0:T(8,128)(2,1)S(1)} %collective-permute-done.5), kind=kLoop, calls=%fused_computation.2 | loop fusion | flops 98304 | bytes 262144 | tf_op jit(solution)/shard_map/convert_element_type | solution.py:504
  35.7 4.1 %collective-permute-start.10 = (bf16[32,1152]{1,0:T(8,128)(2,1)S(1)}, bf16[32,1152]{1,0:T(8,128)(2,1)S(1)}, u32[]{:S(2)}, u32[]{:S(2)}) collective-permute-start(bf16[32,1152]{1,0:T(8,128)(2,1)S(1)} %get-tuple-element.35), channel_id=1, source_target_pairs={{0,6},{1,7},{2,4},{3,5},{4,2},{5,3},{6,0},{7,1},{8,14},{9,15},{10,... | collective-permute-start | bytes 221192 | tf_op jit(solution)/shard_map/ppermute | solution.py:484
  39.8 0.6 collective-permute-start.6
  40.5 1.7 %collective-permute-start.4 = (bf16[32,1024]{1,0:T(8,128)(2,1)S(1)}, bf16[32,1024]{1,0:T(8,128)(2,1)S(1)}, u32[]{:S(2)}, u32[]{:S(2)}) collective-permute-start(bf16[32,1024]{1,0:T(8,128)(2,1)S(1)} %copy-done.17), channel_id=1, source_target_pairs={{0,1},{1,0},{2,3},{3,2},{4,5},{5,4},{6,7},{7,6},{8,9},{9,8},{10,11... | collective-permute-start | bytes 196616 | tf_op jit(solution)/shard_map/ppermute | solution.py:481
  42.1 2.6 %collective-permute-done.4.refs_7_ = bf16[32,1024]{1,0:T(8,128)(2,1)S(1)} collective-permute-done((bf16[32,1024]{1,0:T(8,128)(2,1)S(1)}, bf16[32,1024]{1,0:T(8,128)(2,1)S(1)}, u32[]{:S(2)}, u32[]{:S(2)}) %collective-permute-start.4) | collective-permute-done | bytes 65568 | tf_op jit(solution)/shard_map/ppermute | solution.py:481
  44.8 1.6 %collective-permute-done.8.refs_10_ = bf16[32,1152]{1,0:T(8,128)(2,1)S(1)} collective-permute-done((bf16[32,1152]{1,0:T(8,128)(2,1)S(1)}, bf16[32,1152]{1,0:T(8,128)(2,1)S(1)}, u32[]{:S(2)}, u32[]{:S(2)}) %collective-permute-start.8) | collective-permute-done | bytes 73760 | tf_op jit(solution)/shard_map/ppermute | solution.py:484
  46.4 0.6 copy-done.4
  47.0 2.9 %finish.1.refs_0_ = bf16[32,1024]{1,0:T(8,128)(2,1)} custom-call(s32[32,128]{1,0:T(8,128)} %get-tuple-element.20.row_slot_ref.refs_0_, s32[8,128]{1,0:T(8,128)} %get-tuple-element.21.slot_mine_ref.refs_1_, bf16[8,64,1024]{2,1,0:T(8,128)(2,1)} %get-tuple-element.22.refs_2_, bf16[8,64,1024]{2,1,0:T(8,128)(2,1)} %copy-done, ...), custom_call_target="tpu_custom_call" | custom-call | flops 33554432 | bytes 2097152 | tf_op jit(solution)/shard_map/finish/pallas_call | solution.py:430
  50.0 2.5 %collective-permute-start.16 = (bf16[32,1024]{1,0:T(8,128)(2,1)}, bf16[32,1024]{1,0:T(8,128)(2,1)S(1)}, u32[]{:S(2)}, u32[]{:S(2)}) collective-permute-start(bf16[32,1024]{1,0:T(8,128)(2,1)} %finish.1.refs_0_), channel_id=1, source_target_pairs={{0,6},{1,7},{2,4},{3,5},{4,2},{5,3},{6,0},{7,1},{8,14},{9,15},{10,... | collective-permute-start | bytes 196616 | tf_op jit(solution)/shard_map/ppermute | solution.py:484
  52.5 1.9 %collective-permute-start.12 = (bf16[32,1024]{1,0:T(8,128)(2,1)}, bf16[32,1024]{1,0:T(8,128)(2,1)S(1)}, u32[]{:S(2)}, u32[]{:S(2)}) collective-permute-start(bf16[32,1024]{1,0:T(8,128)(2,1)} %finish.1.refs_0_), channel_id=1, source_target_pairs={{0,2},{1,3},{2,0},{3,1},{4,6},{5,7},{6,4},{7,5},{8,10},{9,11},{10,... | collective-permute-start | bytes 196616 | tf_op jit(solution)/shard_map/ppermute | solution.py:484
  54.3 1.5 %collective-permute-start.11 = (bf16[32,1024]{1,0:T(8,128)(2,1)}, bf16[32,1024]{1,0:T(8,128)(2,1)S(1)}, u32[]{:S(2)}, u32[]{:S(2)}) collective-permute-start(bf16[32,1024]{1,0:T(8,128)(2,1)} %finish.1.refs_0_), channel_id=1, source_target_pairs={{0,1},{1,0},{2,3},{3,2},{4,5},{5,4},{6,7},{7,6},{8,9},{9,8},{10,11... | collective-permute-start | bytes 196616 | tf_op jit(solution)/shard_map/ppermute | solution.py:481
  55.9 0.4 collective-permute-done.16.refs_6_
  56.3 1.5 %collective-permute-start.17 = (bf16[32,1024]{1,0:T(8,128)(2,1)S(1)}, bf16[32,1024]{1,0:T(8,128)(2,1)S(1)}, u32[]{:S(2)}, u32[]{:S(2)}) collective-permute-start(bf16[32,1024]{1,0:T(8,128)(2,1)S(1)} %collective-permute-done.16.refs_6_), channel_id=1, source_target_pairs={{0,1},{1,0},{2,3},{3,2},{4,5},{5,4},{6,7},{7,6},{8,9},{9,8},{10,11... | collective-permute-start | bytes 196616 | tf_op jit(solution)/shard_map/ppermute | solution.py:481
  57.8 1.2 %collective-permute-done.14.refs_4_ = bf16[32,1024]{1,0:T(8,128)(2,1)S(1)} collective-permute-done((bf16[32,1024]{1,0:T(8,128)(2,1)}, bf16[32,1024]{1,0:T(8,128)(2,1)S(1)}, u32[]{:S(2)}, u32[]{:S(2)}) %collective-permute-start.14) | collective-permute-done | bytes 65568 | tf_op jit(solution)/shard_map/ppermute | solution.py:484
  59.0 1.5 %collective-permute-start.15 = (bf16[32,1024]{1,0:T(8,128)(2,1)S(1)}, bf16[32,1024]{1,0:T(8,128)(2,1)S(1)}, u32[]{:S(2)}, u32[]{:S(2)}) collective-permute-start(bf16[32,1024]{1,0:T(8,128)(2,1)S(1)} %collective-permute-done.14.refs_4_), channel_id=1, source_target_pairs={{0,1},{1,0},{2,3},{3,2},{4,5},{5,4},{6,7},{7,6},{8,9},{9,8},{10,11... | collective-permute-start | bytes 196616 | tf_op jit(solution)/shard_map/ppermute | solution.py:481
  60.5 0.5 collective-permute-start.13
  61.0 2.7 %collective-permute-done.15.refs_5_ = bf16[32,1024]{1,0:T(8,128)(2,1)S(1)} collective-permute-done((bf16[32,1024]{1,0:T(8,128)(2,1)S(1)}, bf16[32,1024]{1,0:T(8,128)(2,1)S(1)}, u32[]{:S(2)}, u32[]{:S(2)}) %collective-permute-start.15) | collective-permute-done | bytes 65568 | tf_op jit(solution)/shard_map/ppermute | solution.py:481
  63.7 1.0 %collective-permute-done.13.refs_3_ = bf16[32,1024]{1,0:T(8,128)(2,1)S(1)} collective-permute-done((bf16[32,1024]{1,0:T(8,128)(2,1)S(1)}, bf16[32,1024]{1,0:T(8,128)(2,1)S(1)}, u32[]{:S(2)}, u32[]{:S(2)}) %collective-permute-start.13) | collective-permute-done | bytes 65568 | tf_op jit(solution)/shard_map/ppermute | solution.py:481
  64.8 0.6 copy-done.14
  65.4 1.9 %place.1 = bf16[32,8192]{1,0:T(8,128)(2,1)} custom-call(bf16[32,1024]{1,0:T(8,128)(2,1)} %finish.1.refs_0_, bf16[32,1024]{1,0:T(8,128)(2,1)} %copy-done.10, bf16[32,1024]{1,0:T(8,128)(2,1)} %copy-done.9, bf16[32,1024]{1,0:T(8,128)(2,1)} %copy-done.14, bf16[32,1024]{1,0:T(8,128)(2,1)} %copy-done.8, bf16[32,1024]{1,0:T(8,128)(2,1)} %copy-done.13, ...), custom_call_target="tpu_custom_call" | custom-call | bytes 1048576 | tf_op jit(solution)/shard_map/place/pallas_call | solution.py:455
  (51 shorter events, 0.7 us)
Async XLA Ops:
  0.0 1.4 %collective-permute-start = (s32[32]{0:T(128)}, s32[32]{0:T(128)S(1)}, u32[]{:S(2)}, u32[]{:S(2)}) collective-permute-start(s32[32]{0:T(128)} %ids_ref.1), channel_id=1, source_target_pairs={{0,8},{8,0},{1,9},{9,1},{2,10},{10,2},{3,11},{11,3},{4,12},{12,4},... | collective-permute-start | bytes 392 | tf_op jit(solution)/shard_map/ppermute | solution.py:487
  5.7 17.9 %copy-start.16 = (bf16[8,64,1024]{2,1,0:T(8,128)(2,1)S(1)}, bf16[8,64,1024]{2,1,0:T(8,128)(2,1)}, u32[]{:S(2)}) copy-start(bf16[8,64,1024]{2,1,0:T(8,128)(2,1)} %get-tuple-element.23) | copy-start | bytes 3145732
  5.7 17.9 %collective-permute-start.2 = (bf16[8,64,1024]{2,1,0:T(8,128)(2,1)}, bf16[8,64,1024]{2,1,0:T(8,128)(2,1)S(1)}, u32[]{:S(2)}, u32[]{:S(2)}) collective-permute-start(bf16[8,64,1024]{2,1,0:T(8,128)(2,1)} %get-tuple-element.26), channel_id=1, source_target_pairs={{0,8},{8,0},{1,9},{9,1},{2,10},{10,2},{3,11},{11,3},{4,12},{12,4},... | collective-permute-start | bytes 3145736 | tf_op jit(solution)/shard_map/ppermute | solution.py:487
  18.8 21.7 %copy-start.17 = (bf16[32,1024]{1,0:T(8,128)(2,1)S(1)}, bf16[32,1024]{1,0:T(8,128)(2,1)}, u32[]{:S(2)}) copy-start(bf16[32,1024]{1,0:T(8,128)(2,1)} %get-tuple-element.28) | copy-start | bytes 196612
  18.8 14.1 %collective-permute-start.9 = (bf16[32,1024]{1,0:T(8,128)(2,1)}, bf16[32,1024]{1,0:T(8,128)(2,1)S(1)}, u32[]{:S(2)}, u32[]{:S(2)}) collective-permute-start(bf16[32,1024]{1,0:T(8,128)(2,1)} %get-tuple-element.33), channel_id=1, source_target_pairs={{0,1},{1,0},{2,3},{3,2},{4,5},{5,4},{6,7},{7,6},{8,9},{9,8},{10,11... | collective-permute-start | bytes 196616 | tf_op jit(solution)/shard_map/ppermute | solution.py:481
  21.6 13.2 %collective-permute-start.5 = (bf16[32,1024]{1,0:T(8,128)(2,1)}, bf16[32,1024]{1,0:T(8,128)(2,1)S(1)}, u32[]{:S(2)}, u32[]{:S(2)}) collective-permute-start(bf16[32,1024]{1,0:T(8,128)(2,1)} %get-tuple-element.29), channel_id=1, source_target_pairs={{0,1},{1,0},{2,3},{3,2},{4,5},{5,4},{6,7},{7,6},{8,9},{9,8},{10,11... | collective-permute-start | bytes 196616 | tf_op jit(solution)/shard_map/ppermute | solution.py:481
  21.7 12.1 %collective-permute-start.7 = (bf16[32,1024]{1,0:T(8,128)(2,1)}, bf16[32,1024]{1,0:T(8,128)(2,1)S(1)}, u32[]{:S(2)}, u32[]{:S(2)}) collective-permute-start(bf16[32,1024]{1,0:T(8,128)(2,1)} %get-tuple-element.31), channel_id=1, source_target_pairs={{0,1},{1,0},{2,3},{3,2},{4,5},{5,4},{6,7},{7,6},{8,9},{9,8},{10,11... | collective-permute-start | bytes 196616 | tf_op jit(solution)/shard_map/ppermute | solution.py:481
  23.6 21.1 %collective-permute-start.1 = (bf16[8,64,1024]{2,1,0:T(8,128)(2,1)S(1)}, bf16[8,64,1024]{2,1,0:T(8,128)(2,1)S(1)}, u32[]{:S(2)}, u32[]{:S(2)}) collective-permute-start(bf16[8,64,1024]{2,1,0:T(8,128)(2,1)S(1)} %copy-done.16), channel_id=1, source_target_pairs={{0,8},{8,0},{1,9},{9,1},{2,10},{10,2},{3,11},{11,3},{4,12},{12,4},... | collective-permute-start | bytes 3145736 | tf_op jit(solution)/shard_map/ppermute | solution.py:487
  23.6 1.0 %copy-start.1 = (bf16[8,64,1024]{2,1,0:T(8,128)(2,1)}, bf16[8,64,1024]{2,1,0:T(8,128)(2,1)S(1)}, u32[]{:S(2)}) copy-start(bf16[8,64,1024]{2,1,0:T(8,128)(2,1)S(1)} %collective-permute-done.2.other_ref) | copy-start | bytes 3145732
  27.3 8.4 %copy-start.2 = (f32[32,128]{1,0:T(8,128)S(1)}, f32[32,128]{1,0:T(8,128)}, u32[]{:S(2)}) copy-start(f32[32,128]{1,0:T(8,128)} %shrink_part.1.after_ref.refs_4_) | copy-start | bytes 49156
  27.3 8.4 %collective-permute-start.3 = (f32[32,128]{1,0:T(8,128)}, f32[32,128]{1,0:T(8,128)S(1)}, u32[]{:S(2)}, u32[]{:S(2)}) collective-permute-start(f32[32,128]{1,0:T(8,128)} %shrink_part.1.after_ref.refs_4_), channel_id=1, source_target_pairs={{0,1},{1,0},{2,3},{3,2},{4,5},{5,4},{6,7},{7,6},{8,9},{9,8},{10,11... | collective-permute-start | bytes 49160 | tf_op jit(solution)/shard_map/ppermute | solution.py:481
  35.7 10.7 %copy-start.6 = (f32[32,128]{1,0:T(8,128)}, f32[32,128]{1,0:T(8,128)S(1)}, u32[]{:S(2)}) copy-start(f32[32,128]{1,0:T(8,128)S(1)} %collective-permute-done.3.refs_5_) | copy-start | bytes 49156
  35.7 9.0 %collective-permute-start.10 = (bf16[32,1152]{1,0:T(8,128)(2,1)S(1)}, bf16[32,1152]{1,0:T(8,128)(2,1)S(1)}, u32[]{:S(2)}, u32[]{:S(2)}) collective-permute-start(bf16[32,1152]{1,0:T(8,128)(2,1)S(1)} %get-tuple-element.35), channel_id=1, source_target_pairs={{0,6},{1,7},{2,4},{3,5},{4,2},{5,3},{6,0},{7,1},{8,14},{9,15},{10,... | collective-permute-start | bytes 221192 | tf_op jit(solution)/shard_map/ppermute | solution.py:484
  39.8 6.5 %collective-permute-start.8 = (bf16[32,1152]{1,0:T(8,128)(2,1)S(1)}, bf16[32,1152]{1,0:T(8,128)(2,1)S(1)}, u32[]{:S(2)}, u32[]{:S(2)}) collective-permute-start(bf16[32,1152]{1,0:T(8,128)(2,1)S(1)} %get-tuple-element.36), channel_id=1, source_target_pairs={{0,4},{1,5},{2,6},{3,7},{4,0},{5,1},{6,2},{7,3},{8,12},{9,13},{10,... | collective-permute-start | bytes 221192 | tf_op jit(solution)/shard_map/ppermute | solution.py:484
  39.8 6.5 %collective-permute-start.6 = (bf16[32,1152]{1,0:T(8,128)(2,1)S(1)}, bf16[32,1152]{1,0:T(8,128)(2,1)S(1)}, u32[]{:S(2)}, u32[]{:S(2)}) collective-permute-start(bf16[32,1152]{1,0:T(8,128)(2,1)S(1)} %get-tuple-element.37), channel_id=1, source_target_pairs={{0,2},{1,3},{2,0},{3,1},{4,6},{5,7},{6,4},{7,5},{8,10},{9,11},{10,... | collective-permute-start | bytes 221192 | tf_op jit(solution)/shard_map/ppermute | solution.py:484
  40.5 4.3 %collective-permute-start.4 = (bf16[32,1024]{1,0:T(8,128)(2,1)S(1)}, bf16[32,1024]{1,0:T(8,128)(2,1)S(1)}, u32[]{:S(2)}, u32[]{:S(2)}) collective-permute-start(bf16[32,1024]{1,0:T(8,128)(2,1)S(1)} %copy-done.17), channel_id=1, source_target_pairs={{0,1},{1,0},{2,3},{3,2},{4,5},{5,4},{6,7},{7,6},{8,9},{9,8},{10,11... | collective-permute-start | bytes 196616 | tf_op jit(solution)/shard_map/ppermute | solution.py:481
  44.7 1.6 %copy-start.11 = (bf16[32,1024]{1,0:T(8,128)(2,1)}, bf16[32,1024]{1,0:T(8,128)(2,1)S(1)}, u32[]{:S(2)}) copy-start(bf16[32,1024]{1,0:T(8,128)(2,1)S(1)} %collective-permute-done.4.refs_7_) | copy-start | bytes 196612
  44.7 1.7 %copy-start = (bf16[8,64,1024]{2,1,0:T(8,128)(2,1)}, bf16[8,64,1024]{2,1,0:T(8,128)(2,1)S(1)}, u32[]{:S(2)}) copy-start(bf16[8,64,1024]{2,1,0:T(8,128)(2,1)S(1)} %collective-permute-done.1.refs_3_) | copy-start | bytes 3145732
  44.8 1.7 %copy-start.3 = (bf16[32,1152]{1,0:T(8,128)(2,1)}, bf16[32,1152]{1,0:T(8,128)(2,1)S(1)}, u32[]{:S(2)}) copy-start(bf16[32,1152]{1,0:T(8,128)(2,1)S(1)} %collective-permute-done.10.refs_11_) | copy-start | bytes 221188
  50.0 6.3 %collective-permute-start.16 = (bf16[32,1024]{1,0:T(8,128)(2,1)}, bf16[32,1024]{1,0:T(8,128)(2,1)S(1)}, u32[]{:S(2)}, u32[]{:S(2)}) collective-permute-start(bf16[32,1024]{1,0:T(8,128)(2,1)} %finish.1.refs_0_), channel_id=1, source_target_pairs={{0,6},{1,7},{2,4},{3,5},{4,2},{5,3},{6,0},{7,1},{8,14},{9,15},{10,... | collective-permute-start | bytes 196616 | tf_op jit(solution)/shard_map/ppermute | solution.py:484
  52.5 6.5 %collective-permute-start.14 = (bf16[32,1024]{1,0:T(8,128)(2,1)}, bf16[32,1024]{1,0:T(8,128)(2,1)S(1)}, u32[]{:S(2)}, u32[]{:S(2)}) collective-permute-start(bf16[32,1024]{1,0:T(8,128)(2,1)} %finish.1.refs_0_), channel_id=1, source_target_pairs={{0,4},{1,5},{2,6},{3,7},{4,0},{5,1},{6,2},{7,3},{8,12},{9,13},{10,... | collective-permute-start | bytes 196616 | tf_op jit(solution)/shard_map/ppermute | solution.py:484
  52.5 8.0 %collective-permute-start.12 = (bf16[32,1024]{1,0:T(8,128)(2,1)}, bf16[32,1024]{1,0:T(8,128)(2,1)S(1)}, u32[]{:S(2)}, u32[]{:S(2)}) collective-permute-start(bf16[32,1024]{1,0:T(8,128)(2,1)} %finish.1.refs_0_), channel_id=1, source_target_pairs={{0,2},{1,3},{2,0},{3,1},{4,6},{5,7},{6,4},{7,5},{8,10},{9,11},{10,... | collective-permute-start | bytes 196616 | tf_op jit(solution)/shard_map/ppermute | solution.py:484
  54.3 6.7 %collective-permute-start.11 = (bf16[32,1024]{1,0:T(8,128)(2,1)}, bf16[32,1024]{1,0:T(8,128)(2,1)S(1)}, u32[]{:S(2)}, u32[]{:S(2)}) collective-permute-start(bf16[32,1024]{1,0:T(8,128)(2,1)} %finish.1.refs_0_), channel_id=1, source_target_pairs={{0,1},{1,0},{2,3},{3,2},{4,5},{5,4},{6,7},{7,6},{8,9},{9,8},{10,11... | collective-permute-start | bytes 196616 | tf_op jit(solution)/shard_map/ppermute | solution.py:481
  56.3 8.5 %copy-start.7 = (bf16[32,1024]{1,0:T(8,128)(2,1)}, bf16[32,1024]{1,0:T(8,128)(2,1)S(1)}, u32[]{:S(2)}) copy-start(bf16[32,1024]{1,0:T(8,128)(2,1)S(1)} %collective-permute-done.16.refs_6_) | copy-start | bytes 196612
  56.3 4.8 %collective-permute-start.17 = (bf16[32,1024]{1,0:T(8,128)(2,1)S(1)}, bf16[32,1024]{1,0:T(8,128)(2,1)S(1)}, u32[]{:S(2)}, u32[]{:S(2)}) collective-permute-start(bf16[32,1024]{1,0:T(8,128)(2,1)S(1)} %collective-permute-done.16.refs_6_), channel_id=1, source_target_pairs={{0,1},{1,0},{2,3},{3,2},{4,5},{5,4},{6,7},{7,6},{8,9},{9,8},{10,11... | collective-permute-start | bytes 196616 | tf_op jit(solution)/shard_map/ppermute | solution.py:481
  59.0 5.8 %copy-start.8 = (bf16[32,1024]{1,0:T(8,128)(2,1)}, bf16[32,1024]{1,0:T(8,128)(2,1)S(1)}, u32[]{:S(2)}) copy-start(bf16[32,1024]{1,0:T(8,128)(2,1)S(1)} %collective-permute-done.14.refs_4_) | copy-start | bytes 196612
  59.0 4.7 %collective-permute-start.15 = (bf16[32,1024]{1,0:T(8,128)(2,1)S(1)}, bf16[32,1024]{1,0:T(8,128)(2,1)S(1)}, u32[]{:S(2)}, u32[]{:S(2)}) collective-permute-start(bf16[32,1024]{1,0:T(8,128)(2,1)S(1)} %collective-permute-done.14.refs_4_), channel_id=1, source_target_pairs={{0,1},{1,0},{2,3},{3,2},{4,5},{5,4},{6,7},{7,6},{8,9},{9,8},{10,11... | collective-permute-start | bytes 196616 | tf_op jit(solution)/shard_map/ppermute | solution.py:481
  60.5 4.3 %copy-start.9 = (bf16[32,1024]{1,0:T(8,128)(2,1)}, bf16[32,1024]{1,0:T(8,128)(2,1)S(1)}, u32[]{:S(2)}) copy-start(bf16[32,1024]{1,0:T(8,128)(2,1)S(1)} %collective-permute-done.12.refs_2_) | copy-start | bytes 196612
  60.5 4.3 %collective-permute-start.13 = (bf16[32,1024]{1,0:T(8,128)(2,1)S(1)}, bf16[32,1024]{1,0:T(8,128)(2,1)S(1)}, u32[]{:S(2)}, u32[]{:S(2)}) collective-permute-start(bf16[32,1024]{1,0:T(8,128)(2,1)S(1)} %collective-permute-done.12.refs_2_), channel_id=1, source_target_pairs={{0,1},{1,0},{2,3},{3,2},{4,5},{5,4},{6,7},{7,6},{8,9},{9,8},{10,11... | collective-permute-start | bytes 196616 | tf_op jit(solution)/shard_map/ppermute | solution.py:481
  61.0 3.8 %copy-start.10 = (bf16[32,1024]{1,0:T(8,128)(2,1)}, bf16[32,1024]{1,0:T(8,128)(2,1)S(1)}, u32[]{:S(2)}) copy-start(bf16[32,1024]{1,0:T(8,128)(2,1)S(1)} %collective-permute-done.11.refs_1_) | copy-start | bytes 196612
  61.0 3.8 %copy-start.12 = (bf16[32,1024]{1,0:T(8,128)(2,1)}, bf16[32,1024]{1,0:T(8,128)(2,1)S(1)}, u32[]{:S(2)}) copy-start(bf16[32,1024]{1,0:T(8,128)(2,1)S(1)} %collective-permute-done.17.refs_7_) | copy-start | bytes 196612
  63.7 1.1 %copy-start.13 = (bf16[32,1024]{1,0:T(8,128)(2,1)}, bf16[32,1024]{1,0:T(8,128)(2,1)S(1)}, u32[]{:S(2)}) copy-start(bf16[32,1024]{1,0:T(8,128)(2,1)S(1)} %collective-permute-done.15.refs_5_) | copy-start | bytes 196612
  (4 other events, 2.4 us)

commit v3 on v2

v3 whole, which is shorter than its diff:
```python
import functools

import jax
import jax.numpy as jnp
from jax import lax
from jax.experimental import pallas as pl
from jax.experimental.pallas import tpu as pltpu
from jax.sharding import PartitionSpec as P

F32 = jnp.float32
BF16 = jnp.bfloat16
LOG2E = 1.4426950408889634
ANY = pl.BlockSpec(memory_space=pl.ANY)
VMEM = pl.BlockSpec(memory_space=pltpu.VMEM)
SMEM = pl.BlockSpec(memory_space=pltpu.SMEM)
MIB = 1 << 20
DISTINCT = 8


def in_hbm(x):
    return pltpu.with_memory_space_constraint(x, pltpu.HBM)


def params(mib):
    return pltpu.CompilerParams(vmem_limit_bytes=mib * MIB)


def nt_dot(a, b):
    return lax.dot_general(a, b, (((1,), (1,)), ((), ())), preferred_element_type=F32)


def nn_dot(a, b):
    return jnp.dot(a, b, preferred_element_type=F32)


def distinct_list(ids_ref, pool_slot_ref, seen, list_id, list_pos):
    rows = ids_ref.shape[0]
    for i in range(pool_slot_ref.shape[0]):
        seen[i] = 0
    for j in range(DISTINCT + 1):
        list_id[j] = -1
        list_pos[j] = 0
    found = jnp.int32(0)
    for r in range(rows):
        one = ids_ref[r]
        fresh = 1 - seen[one]
        seen[one] = 1
        spot = jnp.minimum(found, DISTINCT)
        list_id[spot] = jnp.where(fresh == 1, one, list_id[spot])
        list_pos[spot] = jnp.where(fresh == 1, pool_slot_ref[one], list_pos[spot])
        found = found + fresh


def list_scratch(pool_slot):
    return [
        pltpu.SMEM((pool_slot.shape[0],), jnp.int32),
        pltpu.SMEM((DISTINCT + 1,), jnp.int32),
        pltpu.SMEM((DISTINCT + 1,), jnp.int32),
    ]


def page_copies(pages_ref, outs, list_pos, sem, wait):
    pool = pages_ref.shape[0]
    me = lax.axis_index("req")
    for j in range(DISTINCT):
        pos = list_pos[j]

        @pl.when(pos // pool == me)
        def _():
            for i, out in enumerate(outs):
                copy = pltpu.make_async_copy(pages_ref.at[pos % pool, i], out.at[j], sem.at[i, j])
                if wait:
                    copy.wait()
                else:
                    copy.start()


def attend_kernel(
    n_z,
    len_ref,
    ids_ref,
    slot_ref,
    q_ref,
    prefix_ref,
    suffix_ref,
    weight_ref,
    pages_ref,
    residual_ref,
    att_ref,
    shrink_ref,
    expand_ref,
    row_slot_ref,
    slot_mine_ref,
    res_ref,
    *rest,
):
    w_refs = rest[: 2 * n_z]
    (
        kv,
        suf,
        scores,
        tail,
        rowbuf,
        peak,
        total,
        acc,
        seen,
        list_id,
        list_pos,
        sem_kv,
        sem_suf,
        sem_w,
        sem_page,
    ) = rest[2 * n_z :]
    rows = q_ref.shape[0]
    head_dim = prefix_ref.shape[3]
    heads = q_ref.shape[1] // head_dim
    tokens = prefix_ref.shape[2]
    span = suffix_ref.shape[3]
    width = res_ref.shape[1]
    me = lax.axis_index("tensor")
    z, y = me // 2, me % 2
    scale2 = float(head_dim) ** -0.5 * LOG2E

    n_part = 4
    part = tokens // n_part
    kv_copies = [
        [
            pltpu.make_async_copy(
                prefix_ref.at[0, i, pl.ds(j * part, part)],
                kv.at[i, pl.ds(j * part, part)],
                sem_kv.at[i, j],
            )
            for j in range(n_part)
        ]
        for i in range(2)
    ]
    n_sgrp = 4
    sgrp = rows // n_sgrp
    suf_copies = [
        [
            pltpu.make_async_copy(
                suffix_ref.at[pl.ds(j * sgrp, sgrp), 0, i],
                suf.at[i, pl.ds(j * sgrp, sgrp)],
                sem_suf.at[i, j],
            )
            for j in range(n_sgrp)
        ]
        for i in range(2)
    ]
    w_copies = []
    for side in (1, 0):
        for k in list(range(1, n_z)) + [0]:
            column = pl.multiple_of(((z ^ k) * 2 + (y ^ side)) * width, width)
            spot = side * n_z + k
            w_copies.append(
                pltpu.make_async_copy(weight_ref.at[:, pl.ds(column, width)], w_refs[spot], sem_w.at[spot])
            )
    w_copies.append(
        pltpu.make_async_copy(
            residual_ref.at[:, pl.ds(pl.multiple_of(me * width, width), width)], res_ref, sem_w.at[2 * n_z]
        )
    )
    for c in kv_copies[0] + suf_copies[0] + kv_copies[1] + suf_copies[1]:
        c.start()
    distinct_list(ids_ref, slot_ref, seen, list_id, list_pos)
    row_index = lax.broadcasted_iota(jnp.int32, (rows, 128), 0)
    row_id = jnp.full((rows, 128), -2, jnp.int32)
    for r in range(rows):
        row_id = jnp.where(row_index == r, ids_ref[r], row_id)
    row_slot = jnp.full((rows, 128), -1, jnp.int32)
    slot_index = lax.broadcasted_iota(jnp.int32, (DISTINCT, 128), 0)
    slot_mine = jnp.zeros((DISTINCT, 128), jnp.int32)
    mine = lax.axis_index("req")
    for j in range(DISTINCT):
        row_slot = jnp.where(row_id == list_id[j], j, row_slot)
        owned = (list_pos[j] // pages_ref.shape[0] == mine).astype(jnp.int32)
        slot_mine = jnp.where(slot_index == j, owned, slot_mine)
    row_slot_ref[...] = row_slot
    slot_mine_ref[...] = slot_mine

    for h in range(heads):
        rowbuf[pl.ds(h, rows, stride=heads), :] = q_ref[:, h * head_dim : (h + 1) * head_dim].astype(F32)
    query = rowbuf[...].astype(BF16)
    best = jnp.full(peak.shape, -3.0e38, F32)
    for j in range(n_part):
        kv_copies[0][j].wait()
        if j == 1:
            page_copies(pages_ref, (shrink_ref, expand_ref), list_pos, sem_page, False)
            for c in w_copies:
                c.start()
        for b in range(part // 256):
            base = j * part + b * 256
            block = nt_dot(query, kv[0, base : base + 256, :])
            scores[:, base : base + 256] = block
            best = jnp.maximum(best, jnp.maximum(block[:, :128], block[:, 128:]))

    lanes = lax.broadcasted_iota(jnp.int32, (heads, span), 1)
    for j in range(n_sgrp):
        suf_copies[0][j].wait()
        for i in range(j * sgrp // 2, (j + 1) * sgrp // 2):
            keys = suf[0, 2 * i : 2 * i + 2].reshape(2 * span, head_dim)
            both = nt_dot(query[2 * heads * i : 2 * heads * (i + 1)], keys)
            for a in range(2):
                mine = both[a * heads : (a + 1) * heads, a * span : (a + 1) * span]
                row = 2 * i + a
                tail[row * heads : (row + 1) * heads, :] = jnp.where(lanes < len_ref[row], mine, -1.0e30)
    for b in range(span // 128):
        best = jnp.maximum(best, tail[:, b * 128 : (b + 1) * 128])
    peak[...] = jnp.broadcast_to(jnp.max(best, axis=1, keepdims=True), peak.shape)

    for j in range(n_part):
        kv_copies[1][j].wait()
    total[...] = jnp.zeros(total.shape, F32)
    acc[...] = jnp.zeros(acc.shape, F32)
    chunk = min(2048, tokens)

    @pl.loop(0, tokens // chunk)
    def _(i):
        base = pl.multiple_of(i * chunk, chunk)
        high = peak[...]
        summed = total[...]
        parts = []
        for b in range(chunk // 128):
            e = jnp.exp2((scores[:, pl.ds(base + b * 128, 128)] - high) * scale2)
            summed = summed + e
            parts.append(e.astype(BF16))
        total[...] = summed
        acc[...] += nn_dot(jnp.concatenate(parts, axis=1), kv[1, pl.ds(base, chunk), :])

    zeros = jnp.zeros((heads, span), F32)
    for i in range(rows // 2):
        if (2 * i) % sgrp == 0:
            suf_copies[1][2 * i // sgrp].wait()
        lo = 2 * heads * i
        high = jnp.concatenate([peak[lo : lo + 2 * heads, :]] * (span // 128), axis=1)
        e = jnp.exp2((tail[lo : lo + 2 * heads, :] - high) * scale2)
        part_sum = e[:, :128]
        for b in range(1, span // 128):
            part_sum = part_sum + e[:, b * 128 : (b + 1) * 128]
        total[lo : lo + 2 * heads, :] += part_sum
        diag = jnp.concatenate(
            [
                jnp.concatenate([e[:heads], zeros], axis=1),
                jnp.concatenate([zeros, e[heads:]], axis=1),
            ],
            axis=0,
        ).astype(BF16)
        vals = suf[1, 2 * i : 2 * i + 2].reshape(2 * span, head_dim)
        acc[lo : lo + 2 * heads, :] += nn_dot(diag, vals)

    norm = jnp.sum(total[...], axis=1, keepdims=True)
    rowbuf[...] = acc[...] / norm
    for h in range(heads):
        att_ref[:, h * head_dim : (h + 1) * head_dim] = rowbuf[pl.ds(h, rows, stride=heads), :].astype(BF16)
    page_copies(pages_ref, (shrink_ref, expand_ref), list_pos, sem_page, True)
    for c in w_copies:
        c.wait()


def attend(
    suffix_len, ids, pool_slot, queries, prefix_kv, suffix_kv, out_weight, pages, residual, n_tensor
):
    rows = queries.shape[0]
    n_z = n_tensor // 2
    width = out_weight.shape[1] // n_tensor
    tokens, head_dim = prefix_kv.shape[2:]
    n_q = rows * queries.shape[1] // head_dim
    span = suffix_kv.shape[3]
    out = pl.pallas_call(
        functools.partial(attend_kernel, n_z),
        out_shape=[
            pltpu.VMEM(queries.shape, BF16),
            pltpu.VMEM((DISTINCT,) + pages.shape[2:], BF16),
            pltpu.VMEM((DISTINCT,) + pages.shape[2:], BF16),
            pltpu.VMEM((rows, 128), jnp.int32),
            pltpu.VMEM((DISTINCT, 128), jnp.int32),
            pltpu.VMEM((rows, width), BF16),
        ]
        + [pltpu.VMEM((out_weight.shape[0], width), BF16)] * n_tensor,
        in_specs=[SMEM, SMEM, SMEM, VMEM, ANY, ANY, ANY, ANY, ANY],
        out_specs=[VMEM] * (6 + n_tensor),
        scratch_shapes=[
            pltpu.VMEM((2, tokens, head_dim), BF16),
            pltpu.VMEM((2, rows, span, head_dim), BF16),
            pltpu.VMEM((n_q, tokens), F32),
            pltpu.VMEM((n_q, span), F32),
            pltpu.VMEM((n_q, head_dim), F32),
            pltpu.VMEM((n_q, 128), F32),
            pltpu.VMEM((n_q, 128), F32),
            pltpu.VMEM((n_q, head_dim), F32),
        ]
        + list_scratch(pool_slot)
        + [
            pltpu.SemaphoreType.DMA((2, 4)),
            pltpu.SemaphoreType.DMA((2, 4)),
            pltpu.SemaphoreType.DMA((n_tensor + 1,)),
            pltpu.SemaphoreType.DMA((2, DISTINCT)),
        ],
        compiler_params=params(24),
        cost_estimate=pl.CostEstimate(
            flops=2 * 2 * n_q * tokens * head_dim,
            bytes_accessed=26 * MIB,
            transcendentals=n_q * tokens,
        ),
        name="attend",
    )(
        suffix_len,
        ids,
        pool_slot,
        queries,
        in_hbm(prefix_kv),
        in_hbm(suffix_kv),
        in_hbm(out_weight),
        in_hbm(pages),
        in_hbm(residual),
    )
    return out[:6], out[6 : 6 + n_z], out[6 + n_z :]


def small_call(kernel, name, out_shape, operands, flops=1 << 27):
    return pl.pallas_call(
        kernel,
        out_shape=out_shape,
        in_specs=[VMEM] * len(operands),
        out_specs=jax.tree.map(lambda _: VMEM, out_shape),
        compiler_params=params(8),
        cost_estimate=pl.CostEstimate(flops=flops, bytes_accessed=2 * MIB, transcendentals=0),
        name=name,
    )(*operands)


def collect_kernel(ids_ref, slot_ref, pages_ref, out_ref, seen, list_id, list_pos, sem):
    distinct_list(ids_ref, slot_ref, seen, list_id, list_pos)
    for wait in (False, True):
        page_copies(pages_ref, (out_ref.at[0], out_ref.at[1]), list_pos, sem, wait)


def collect_pages(ids, pool_slot, pages):
    return pl.pallas_call(
        collect_kernel,
        out_shape=pltpu.VMEM((2, DISTINCT) + pages.shape[2:], BF16),
        in_specs=[SMEM, SMEM, ANY],
        out_specs=VMEM,
        scratch_shapes=list_scratch(pool_slot) + [pltpu.SemaphoreType.DMA((2, DISTINCT))],
        compiler_params=params(4),
        cost_estimate=pl.CostEstimate(flops=0, bytes_accessed=2 * MIB, transcendentals=0),
        name="collect_pages",
    )(ids, pool_slot, in_hbm(pages))


def merged(own_ref, other, half, slot_mine):
    rank = own_ref.shape[1]
    tiles = []
    for j in range(DISTINCT):
        hit = jnp.broadcast_to(slot_mine[j : j + 1, :1], (rank, 1)) == 1
        tiles.append(jnp.where(hit, own_ref[j].astype(F32), other[half, j].astype(F32)).astype(BF16))
    return jnp.concatenate(tiles, axis=0)


def lane_place(shape, rank):
    return lax.broadcasted_iota(jnp.int32, shape, 1) // rank


def first_kernel(n, att_ref, row_slot_ref, slot_mine_ref, own_ref, other_ref, *rest):
    w_refs = rest[:n]
    out_ref, rank_ref = rest[n:]
    width = w_refs[0].shape[1]
    attended = att_ref[...]
    for k in range(n):
        out_ref[:, k * width : (k + 1) * width] = nn_dot(attended, w_refs[k][...]).astype(BF16)
    rank = own_ref.shape[1]
    per_tile = 128 // rank
    low = nt_dot(attended, merged(own_ref, other_ref, 0, slot_mine_ref[...]))
    row_slot = row_slot_ref[...]
    place = lane_place(row_slot.shape, rank)
    picked = jnp.zeros(row_slot.shape, F32)
    for tile in range(DISTINCT // per_tile):
        hit = row_slot == place + tile * per_tile
        picked = jnp.where(hit, low[:, tile * 128 : (tile + 1) * 128], picked)
    rank_ref[...] = picked
    out_ref[:, n * width :] = picked.astype(BF16)


def second_kernel(n, att_ref, *rest):
    w_refs = rest[:n]
    out_ref = rest[-1]
    width = w_refs[0].shape[1]
    attended = att_ref[...]
    for k in range(n):
        out_ref[:, k * width : (k + 1) * width] = nn_dot(attended, w_refs[k][...]).astype(BF16)


def add_kernel(spot, first_spot, att_ref, w_ref, from_ref, first_ref, rank_ref, out_ref):
    width = w_ref.shape[1]
    both = nn_dot(att_ref[...], w_ref[...]) + from_ref[:, spot * width : (spot + 1) * width].astype(F32)
    out_ref[:, :width] = both.astype(BF16)
    rank_both = rank_ref[...] + first_ref[:, first_spot * width :].astype(F32)
    out_ref[:, width:] = rank_both.astype(BF16)


def finish_kernel(n_z, spot, first_spot, *refs):
    att_ref, w_ref, row_slot_ref, slot_mine_ref, own_ref, other_ref = refs[:6]
    rank_ref, first_ref, from_ref, res_ref = refs[6:10]
    moved = refs[10 : 10 + n_z - 1]
    out_ref = refs[10 + n_z - 1]
    rank = own_ref.shape[1]
    per_tile = 128 // rank
    width = w_ref.shape[1]
    low = rank_ref[...] + first_ref[:, first_spot * width :].astype(F32)
    for ref in moved:
        low = low + ref[:, width:].astype(F32)
    row_slot = row_slot_ref[...]
    place = lane_place(row_slot.shape, rank)
    tiles = []
    for tile in range(DISTINCT // per_tile):
        tiles.append(jnp.where(row_slot == place + tile * per_tile, low, 0.0).astype(BF16))
    total = nn_dot(jnp.concatenate(tiles, axis=1), merged(own_ref, other_ref, 1, slot_mine_ref[...]))
    total = total + nn_dot(att_ref[...], w_ref[...])
    total = total + (res_ref[...].astype(F32) + from_ref[:, spot * width : (spot + 1) * width].astype(F32))
    for ref in moved:
        total = total + ref[:, :width].astype(F32)
    out_ref[...] = total.astype(BF16)


def place_kernel(n_z, *refs):
    blocks = refs[: 2 * n_z]
    out_ref = refs[2 * n_z]
    width = blocks[0].shape[1]
    me = lax.axis_index("tensor")
    z, y = me // 2, me % 2
    for k in range(n_z):
        for other in range(2):
            where = (z ^ k) * 2 + (y ^ other)
            out_ref[:, pl.ds(pl.multiple_of(where * width, width), width)] = blocks[2 * k + other][...]


def place(blocks, n_tensor):
    rows, width = blocks[0].shape
    return pl.pallas_call(
        functools.partial(place_kernel, n_tensor // 2),
        out_shape=jax.ShapeDtypeStruct((rows, width * n_tensor), BF16),
        in_specs=[VMEM] * n_tensor,
        out_specs=VMEM,
        compiler_params=params(4),
        cost_estimate=pl.CostEstimate(flops=0, bytes_accessed=1 * MIB, transcendentals=0),
        name="place",
    )(*blocks)


def body(
    n_tensor,
    queries,
    prefix_kv,
    suffix_kv,
    suffix_len,
    residual,
    out_weight,
    adapter_pages,
    adapter_ids,
    pool_slot,
):
    n_z = n_tensor // 2

    def along_y(x):
        return lax.ppermute(x, "tensor", [(t, t ^ 1) for t in range(n_tensor)])

    def along_z(x, k):
        return lax.ppermute(x, "tensor", [(t, t ^ (2 * k)) for t in range(n_tensor)])

    def across(x):
        return lax.ppermute(x, "req", [(0, 1), (1, 0)])

    rows = queries.shape[0]
    width = out_weight.shape[1] // n_tensor
    other_ids = across(adapter_ids)
    other_pages = across(collect_pages(other_ids, pool_slot, adapter_pages))
    (attended, own_shrink, own_expand, row_slot, slot_mine, res), own_w, far_w = attend(
        suffix_len,
        adapter_ids,
        pool_slot,
        queries,
        prefix_kv,
        suffix_kv,
        out_weight,
        adapter_pages,
        residual,
        n_tensor,
    )
    order = list(range(1, n_z)) + [0]
    first, second = order[: n_z // 2], order[n_z // 2 :]
    n_first, n_second = len(first), len(second)
    first_out, rank_own = small_call(
        functools.partial(first_kernel, n_first),
        "first_blocks",
        [pltpu.VMEM((rows, n_first * width + 128), BF16), pltpu.VMEM((rows, 128), F32)],
        [attended, row_slot, slot_mine, own_shrink, other_pages] + [far_w[k] for k in first],
    )
    from_first = along_y(first_out)
    second_out = small_call(
        functools.partial(second_kernel, n_second),
        "second_blocks",
        pltpu.VMEM((rows, n_second * width), BF16),
        [attended] + [far_w[k] for k in second] + [rank_own],
    )
    from_second = along_y(second_out)
    moved = []
    for k in range(1, n_z):
        source, spot = (from_first, first.index(k)) if k in first else (from_second, second.index(k))
        piece = small_call(
            functools.partial(add_kernel, spot, n_first),
            "add_block",
            pltpu.VMEM((rows, width + 128), BF16),
            [attended, own_w[k], source, from_first, rank_own],
        )
        moved.append(along_z(piece, k))
    result = small_call(
        functools.partial(finish_kernel, n_z, second.index(0), n_first),
        "finish",
        pltpu.VMEM((rows, width), BF16),
        [attended, own_w[0], row_slot, slot_mine, own_expand, other_pages, rank_own, from_first, from_second, res]
        + moved,
    )
    blocks = []
    held = [result] + [along_z(result, k) for k in range(1, n_z)]
    for k in range(n_z):
        blocks += [held[k], along_y(held[k])]
    return place(blocks, n_tensor)


def solution(mesh):
    return jax.shard_map(
        functools.partial(body, mesh.shape["tensor"]),
        mesh=mesh,
        in_specs=(
            P(("group", "req"), "tensor"),
            P(("group", "tensor"), None, None, None),
            P(("group", "req"), "tensor", None, None, None),
            P(("group", "req")),
            P(("group", "req"), None),
            P("tensor", None),
            P("req", None, None, "tensor"),
            P(("group", "req")),
            P(),
        ),
        out_specs=P(("group", "req"), None),
        check_vma=False,
    )
```

time: 67.7 us -> 50.2 us (0.74)
  Pallas kernels: 29.4 us -> 17.2 us
  waiting for transfers between devices: 10.5 us -> 13.9 us
  starting transfers between devices: 21.6 us -> 18.3 us
  other arithmetic: 2.79 us -> 0 us
  local copies, waits for them, and re-layouts: 2.77 us -> 0.67 us
    pallas_call x5 -> x8, Pallas kernels: 27.5 us -> 16.4 us  [the longest x1 10 us: attend(): pl.pallas_call(functools.partial(attend_kernel, n_z), out_shape=[pltpu.VM...]
    ppermute x9 -> x6, starting transfers between devices: 11.7 us -> 7.97 us  [along_y(): return lax.ppermute(x, 'tensor', [(t, t ^ 1) for t in range(n_tensor)])]
    convert_element_type x4 -> x0, other arithmetic: 2.77 us -> none  [the longest x3 2.76 us: body(): both = (got_y[k].astype(F32) + own[k]).astype(BF16)]
    ppermute x6, waiting for transfers between devices: 3.19 us -> 5.82 us  [along_z(): return lax.ppermute(x, 'tensor', [(t, t ^ 2 * k) for t in range(n_tensor)])]
    unnamed x36 -> x10, local copies, waits for them, and re-layouts: 2.77 us -> 0.67 us
    pallas_call x1, Pallas kernels: 1.9 us -> 0.84 us  [place(): pl.pallas_call(functools.partial(place_kernel, n_tensor // 2), out_shape=...]
    ppermute x9 -> x6, waiting for transfers between devices: 6.35 us -> 7.15 us  [along_y(): return lax.ppermute(x, 'tensor', [(t, t ^ 1) for t in range(n_tensor)])]
    ppermute x6, starting transfers between devices: 9.11 us -> 9.81 us  [along_z(): return lax.ppermute(x, 'tensor', [(t, t ^ 2 * k) for t in range(n_tensor)])]
  transfers between devices with their start and end apart: 18 -> 14, of which waited for: 7 -> 8; matrix products, arithmetic and copies ran while one was open for 4% -> 0% of each run, Pallas kernels for 31% -> 24%
where the time goes in v3:
time: 50.2 us
  starting transfers between devices  18.3 us (36%)
  Pallas kernels  17.2 us (34%)
  waiting for transfers between devices  13.9 us (28%)
  local copies, waits for them, and re-layouts  0.67 us (1%)
    pallas_call x1, Pallas kernels, attend(): pl.pallas_call(functools.partial(attend_kernel, n_z), out_shape=[pltpu.VM...  10 us
    ppermute x6, starting transfers between devices, along_z(): return lax.ppermute(x, 'tensor', [(t, t ^ 2 * k) for t in range(n_tensor)])  9.81 us
    ppermute x6, starting transfers between devices, along_y(): return lax.ppermute(x, 'tensor', [(t, t ^ 1) for t in range(n_tensor)])  7.97 us
    ppermute x6, waiting for transfers between devices, along_y(): return lax.ppermute(x, 'tensor', [(t, t ^ 1) for t in range(n_tensor)])  7.15 us
    ppermute x6, waiting for transfers between devices, along_z(): return lax.ppermute(x, 'tensor', [(t, t ^ 2 * k) for t in range(n_tensor)])  5.82 us
    pallas_call x6, Pallas kernels, small_call(): pl.pallas_call(kernel, out_shape=out_shape, in_specs=[VMEM] * len(operand...  4.11 us
    pallas_call x1, Pallas kernels, collect_pages(): pl.pallas_call(collect_kernel, out_shape=pltpu.VMEM((2, DISTINCT) + pages...  2.24 us
  transfers between devices with their start and end apart: 14, of which 8 were waited for; matrix products, arithmetic and copies ran while one was open for 0% of the time, Pallas kernels for 24%

profile of v3, /device:TPU:0, one launch (start us, length us, event | category | flops | bytes accessed | tf_op | source)
XLA Modules:
  0.0 50.2 jit_solution(13471819948975204654)
XLA Ops:
  0.0 0.5 collective-permute-start
  0.5 1.0 %collective-permute-done.ids_ref = s32[32]{0:T(128)S(1)} collective-permute-done((s32[32]{0:T(128)}, s32[32]{0:T(128)S(1)}, u32[]{:S(2)}, u32[]{:S(2)}) %collective-permute-start) | collective-permute-done | bytes 160 | tf_op jit(solution)/shard_map/ppermute | solution.py:472
  1.4 0.7 %copy-done.1 = s32[128]{0:T(128)S(1)} copy-done((s32[128]{0:T(128)S(1)}, s32[128]{0:T(128)}, u32[]{:S(2)}) %copy-start.1) | copy-done | bytes 536
  2.1 2.2 %collect_pages.1 = bf16[2,8,64,1024]{3,2,1,0:T(8,128)(2,1)S(1)} custom-call(s32[32]{0:T(128)S(1)} %collective-permute-done.ids_ref, s32[128]{0:T(128)S(1)} %copy-done.1, bf16[64,2,64,1024]{3,2,1,0:T(8,128)(2,1)} %pages_ref.3), custom_call_target="tpu_custom_call" | custom-call | bytes 2097152 | tf_op jit(solution)/shard_map/collect_pages/pallas_call | solution.py:340
  4.3 0.1 collective-permute-start.1
  4.4 10.0 %attend.1 = (bf16[32,1024]{1,0:T(8,128)(2,1)S(1)}, bf16[8,64,1024]{2,1,0:T(8,128)(2,1)S(1)}, bf16[8,64,1024]{2,1,0:T(8,128)(2,1)S(1)}, s32[32,128]{1,0:T(8,128)S...) custom-call(s32[32]{0:T(128)S(1)} %copy-done.3, ...), custom_call_target="tpu_custom_call" | custom-call | flops 1073741824 | bytes 27262976 | tf_op jit(solution)/shard_map/attend/pallas_call | solution.py:270
  14.5 1.1 %first_blocks.1 = (bf16[32,2176]{1,0:T(8,128)(2,1)S(1)}, f32[32,128]{1,0:T(8,128)S(1)}) custom-call(bf16[32,1024]{1,0:T(8,128)(2,1)S(1)} %get-tuple-element.21.att_ref.refs_0_, s32[32,128]{1,0:T(8,128)S(1)} %get-tuple-element.23.row_slot_ref.refs_2_, s32[8,128]{1,0:T(8,128)S(1)} %get-tuple-element.24.slot_mine_ref.refs_3_, ...), custom_call_target="tpu_custom_call" | custom-call | flops 134217728 | bytes 2097152 | tf_op jit(solution)/shard_map/first_blocks/pallas_call | solution.py:322
  15.6 2.9 %collective-permute-start.2 = (bf16[32,2176]{1,0:T(8,128)(2,1)S(1)}, bf16[32,2176]{1,0:T(8,128)(2,1)S(1)}, u32[]{:S(2)}, u32[]{:S(2)}) collective-permute-start(bf16[32,2176]{1,0:T(8,128)(2,1)S(1)} %get-tuple-element.30), channel_id=1, source_target_pairs={{0,1},{1,0},{2,3},{3,2},{4,5},{5,4},{6,7},{7,6},{8,9},{9,8},{10,11... | collective-permute-start | bytes 417800 | tf_op jit(solution)/shard_map/ppermute | solution.py:466
  18.5 0.8 %second_blocks.1 = bf16[32,2048]{1,0:T(8,128)(2,1)S(1)} custom-call(bf16[32,1024]{1,0:T(8,128)(2,1)S(1)} %get-tuple-element.21.att_ref.refs_0_, bf16[1024,1024]{1,0:T(8,128)(2,1)S(1)} %get-tuple-element.31.rest_0_, bf16[1024,1024]{1,0:T(8,128)(2,1)S(1)} %get-tuple-element.32.rest_1_, f32[32,128]{1,0:T(8,128)S(1)} %get-tuple-element.29.rest_2_.rank_ref.refs_6_), custom_call_target="tpu_custom_call" | custom-call | flops 134217728 | bytes 2097152 | tf_op jit(solution)/shard_map/second_blocks/pallas_call | solution.py:322
  19.3 0.0 collective-permute-start.3
  19.3 3.6 %collective-permute-done.2.from_ref.first_ref.refs_7_ = bf16[32,2176]{1,0:T(8,128)(2,1)S(1)} collective-permute-done((bf16[32,2176]{1,0:T(8,128)(2,1)S(1)}, bf16[32,2176]{1,0:T(8,128)(2,1)S(1)}, u32[]{:S(2)}, u32[]{:S(2)}) %collective-permute-start.2) | collective-permute-done | bytes 139296 | tf_op jit(solution)/shard_map/ppermute | solution.py:466
  22.9 0.5 add_block.3
  23.4 2.1 %collective-permute-start.4 = (bf16[32,1152]{1,0:T(8,128)(2,1)S(1)}, bf16[32,1152]{1,0:T(8,128)(2,1)S(1)}, u32[]{:S(2)}, u32[]{:S(2)}) collective-permute-start(bf16[32,1152]{1,0:T(8,128)(2,1)S(1)} %add_block.3), channel_id=1, source_target_pairs={{0,2},{1,3},{2,0},{3,1},{4,6},{5,7},{6,4},{7,5},{8,10},{9,11},{10,... | collective-permute-start | bytes 221192 | tf_op jit(solution)/shard_map/ppermute | solution.py:469
  25.5 0.5 add_block.4
  26.0 2.6 %collective-permute-start.5 = (bf16[32,1152]{1,0:T(8,128)(2,1)S(1)}, bf16[32,1152]{1,0:T(8,128)(2,1)S(1)}, u32[]{:S(2)}, u32[]{:S(2)}) collective-permute-start(bf16[32,1152]{1,0:T(8,128)(2,1)S(1)} %add_block.4), channel_id=1, source_target_pairs={{0,4},{1,5},{2,6},{3,7},{4,0},{5,1},{6,2},{7,3},{8,12},{9,13},{10,... | collective-permute-start | bytes 221192 | tf_op jit(solution)/shard_map/ppermute | solution.py:469
  28.6 0.5 add_block.5
  29.0 0.6 %collective-permute-start.6 = (bf16[32,1152]{1,0:T(8,128)(2,1)S(1)}, bf16[32,1152]{1,0:T(8,128)(2,1)S(1)}, u32[]{:S(2)}, u32[]{:S(2)}) collective-permute-start(bf16[32,1152]{1,0:T(8,128)(2,1)S(1)} %add_block.5), channel_id=1, source_target_pairs={{0,6},{1,7},{2,4},{3,5},{4,2},{5,3},{6,0},{7,1},{8,14},{9,15},{10,... | collective-permute-start | bytes 221192 | tf_op jit(solution)/shard_map/ppermute | solution.py:469
  29.7 3.2 %collective-permute-done.5.refs_11_ = bf16[32,1152]{1,0:T(8,128)(2,1)S(1)} collective-permute-done((bf16[32,1152]{1,0:T(8,128)(2,1)S(1)}, bf16[32,1152]{1,0:T(8,128)(2,1)S(1)}, u32[]{:S(2)}, u32[]{:S(2)}) %collective-permute-start.5) | collective-permute-done | bytes 73760 | tf_op jit(solution)/shard_map/ppermute | solution.py:469
  32.9 2.4 %collective-permute-done.6.refs_12_ = bf16[32,1152]{1,0:T(8,128)(2,1)S(1)} collective-permute-done((bf16[32,1152]{1,0:T(8,128)(2,1)S(1)}, bf16[32,1152]{1,0:T(8,128)(2,1)S(1)}, u32[]{:S(2)}, u32[]{:S(2)}) %collective-permute-start.6) | collective-permute-done | bytes 73760 | tf_op jit(solution)/shard_map/ppermute | solution.py:469
  35.2 0.8 %finish.1.refs_0_ = bf16[32,1024]{1,0:T(8,128)(2,1)S(1)} custom-call(bf16[32,1024]{1,0:T(8,128)(2,1)S(1)} %get-tuple-element.21.att_ref.refs_0_, bf16[1024,1024]{1,0:T(8,128)(2,1)S(1)} %get-tuple-element.22.refs_1_, s32[32,128]{1,0:T(8,128)S(1)} %get-tuple-element.23.row_slot_ref.refs_2_, s32[8,128]{1,0:T(8,128)S(1)} %get-tuple-element.24.slot_mine_ref.refs_3_, ...), custom_call_target="tpu_custom_call" | custom-call | flops 134217728 | bytes 2097152 | tf_op jit(solution)/shard_map/finish/pallas_call | solution.py:322
  36.0 1.0 %collective-permute-start.12 = (bf16[32,1024]{1,0:T(8,128)(2,1)S(1)}, bf16[32,1024]{1,0:T(8,128)(2,1)S(1)}, u32[]{:S(2)}, u32[]{:S(2)}) collective-permute-start(bf16[32,1024]{1,0:T(8,128)(2,1)S(1)} %finish.1.refs_0_), channel_id=1, source_target_pairs={{0,6},{1,7},{2,4},{3,5},{4,2},{5,3},{6,0},{7,1},{8,14},{9,15},{10,... | collective-permute-start | bytes 196616 | tf_op jit(solution)/shard_map/ppermute | solution.py:469
  37.1 0.5 %collective-permute-start.10 = (bf16[32,1024]{1,0:T(8,128)(2,1)S(1)}, bf16[32,1024]{1,0:T(8,128)(2,1)S(1)}, u32[]{:S(2)}, u32[]{:S(2)}) collective-permute-start(bf16[32,1024]{1,0:T(8,128)(2,1)S(1)} %finish.1.refs_0_), channel_id=1, source_target_pairs={{0,4},{1,5},{2,6},{3,7},{4,0},{5,1},{6,2},{7,3},{8,12},{9,13},{10,... | collective-permute-start | bytes 196616 | tf_op jit(solution)/shard_map/ppermute | solution.py:469
  37.6 2.9 %collective-permute-start.8 = (bf16[32,1024]{1,0:T(8,128)(2,1)S(1)}, bf16[32,1024]{1,0:T(8,128)(2,1)S(1)}, u32[]{:S(2)}, u32[]{:S(2)}) collective-permute-start(bf16[32,1024]{1,0:T(8,128)(2,1)S(1)} %finish.1.refs_0_), channel_id=1, source_target_pairs={{0,2},{1,3},{2,0},{3,1},{4,6},{5,7},{6,4},{7,5},{8,10},{9,11},{10,... | collective-permute-start | bytes 196616 | tf_op jit(solution)/shard_map/ppermute | solution.py:469
  40.5 1.5 %collective-permute-start.7 = (bf16[32,1024]{1,0:T(8,128)(2,1)S(1)}, bf16[32,1024]{1,0:T(8,128)(2,1)S(1)}, u32[]{:S(2)}, u32[]{:S(2)}) collective-permute-start(bf16[32,1024]{1,0:T(8,128)(2,1)S(1)} %finish.1.refs_0_), channel_id=1, source_target_pairs={{0,1},{1,0},{2,3},{3,2},{4,5},{5,4},{6,7},{7,6},{8,9},{9,8},{10,11... | collective-permute-start | bytes 196616 | tf_op jit(solution)/shard_map/ppermute | solution.py:466
  42.0 0.2 collective-permute-done.12.refs_6_
  42.2 1.5 %collective-permute-start.13 = (bf16[32,1024]{1,0:T(8,128)(2,1)S(1)}, bf16[32,1024]{1,0:T(8,128)(2,1)S(1)}, u32[]{:S(2)}, u32[]{:S(2)}) collective-permute-start(bf16[32,1024]{1,0:T(8,128)(2,1)S(1)} %collective-permute-done.12.refs_6_), channel_id=1, source_target_pairs={{0,1},{1,0},{2,3},{3,2},{4,5},{5,4},{6,7},{7,6},{8,9},{9,8},{10,11... | collective-permute-start | bytes 196616 | tf_op jit(solution)/shard_map/ppermute | solution.py:466
  43.8 1.3 %collective-permute-start.11 = (bf16[32,1024]{1,0:T(8,128)(2,1)S(1)}, bf16[32,1024]{1,0:T(8,128)(2,1)S(1)}, u32[]{:S(2)}, u32[]{:S(2)}) collective-permute-start(bf16[32,1024]{1,0:T(8,128)(2,1)S(1)} %collective-permute-done.10.refs_4_), channel_id=1, source_target_pairs={{0,1},{1,0},{2,3},{3,2},{4,5},{5,4},{6,7},{7,6},{8,9},{9,8},{10,11... | collective-permute-start | bytes 196616 | tf_op jit(solution)/shard_map/ppermute | solution.py:466
  45.1 0.7 %collective-permute-start.9 = (bf16[32,1024]{1,0:T(8,128)(2,1)S(1)}, bf16[32,1024]{1,0:T(8,128)(2,1)S(1)}, u32[]{:S(2)}, u32[]{:S(2)}) collective-permute-start(bf16[32,1024]{1,0:T(8,128)(2,1)S(1)} %collective-permute-done.8.refs_2_), channel_id=1, source_target_pairs={{0,1},{1,0},{2,3},{3,2},{4,5},{5,4},{6,7},{7,6},{8,9},{9,8},{10,11... | collective-permute-start | bytes 196616 | tf_op jit(solution)/shard_map/ppermute | solution.py:466
  45.8 0.7 %collective-permute-done.13.refs_7_ = bf16[32,1024]{1,0:T(8,128)(2,1)S(1)} collective-permute-done((bf16[32,1024]{1,0:T(8,128)(2,1)S(1)}, bf16[32,1024]{1,0:T(8,128)(2,1)S(1)}, u32[]{:S(2)}, u32[]{:S(2)}) %collective-permute-start.13) | collective-permute-done | bytes 65568 | tf_op jit(solution)/shard_map/ppermute | solution.py:466
  46.5 1.5 %collective-permute-done.11.refs_5_ = bf16[32,1024]{1,0:T(8,128)(2,1)S(1)} collective-permute-done((bf16[32,1024]{1,0:T(8,128)(2,1)S(1)}, bf16[32,1024]{1,0:T(8,128)(2,1)S(1)}, u32[]{:S(2)}, u32[]{:S(2)}) %collective-permute-start.11) | collective-permute-done | bytes 65568 | tf_op jit(solution)/shard_map/ppermute | solution.py:466
  48.0 1.3 %collective-permute-done.9.refs_3_ = bf16[32,1024]{1,0:T(8,128)(2,1)S(1)} collective-permute-done((bf16[32,1024]{1,0:T(8,128)(2,1)S(1)}, bf16[32,1024]{1,0:T(8,128)(2,1)S(1)}, u32[]{:S(2)}, u32[]{:S(2)}) %collective-permute-start.9) | collective-permute-done | bytes 65568 | tf_op jit(solution)/shard_map/ppermute | solution.py:466
  49.3 0.8 %place.1 = bf16[32,8192]{1,0:T(8,128)(2,1)} custom-call(bf16[32,1024]{1,0:T(8,128)(2,1)S(1)} %finish.1.refs_0_, bf16[32,1024]{1,0:T(8,128)(2,1)S(1)} %collective-permute-done.7.refs_1_, bf16[32,1024]{1,0:T(8,128)(2,1)S(1)} %collective-permute-done.8.refs_2_, bf16[32,1024]{1,0:T(8,128)(2,1)S(1)} %collective-permute-done.9.refs_3_, ...), custom_call_target="tpu_custom_call" | custom-call | bytes 1048576 | tf_op jit(solution)/shard_map/place/pallas_call | solution.py:440
  (15 shorter events, 0.0 us)
Async XLA Ops:
  0.0 4.4 %copy-start = (bf16[32,1024]{1,0:T(8,128)(2,1)S(1)}, bf16[32,1024]{1,0:T(8,128)(2,1)}, u32[]{:S(2)}) copy-start(bf16[32,1024]{1,0:T(8,128)(2,1)} %q_ref.1) | copy-start | bytes 196612
  0.0 1.4 %collective-permute-start = (s32[32]{0:T(128)}, s32[32]{0:T(128)S(1)}, u32[]{:S(2)}, u32[]{:S(2)}) collective-permute-start(s32[32]{0:T(128)} %ids_ref.1), channel_id=1, source_target_pairs={{0,8},{8,0},{1,9},{9,1},{2,10},{10,2},{3,11},{11,3},{4,12},{12,4},... | collective-permute-start | bytes 392 | tf_op jit(solution)/shard_map/ppermute | solution.py:472
  1.4 0.7 %copy-start.1 = (s32[128]{0:T(128)S(1)}, s32[128]{0:T(128)}, u32[]{:S(2)}) copy-start(s32[128]{0:T(128)} %slot_ref.3) | copy-start | bytes 1540
  2.1 2.4 %copy-start.2 = (s32[128]{0:T(128)S(1)}, s32[128]{0:T(128)}, u32[]{:S(2)}) copy-start(s32[128]{0:T(128)} %slot_ref.3) | copy-start | bytes 1540
  2.1 2.4 %copy-start.3 = (s32[32]{0:T(128)S(1)}, s32[32]{0:T(128)}, u32[]{:S(2)}) copy-start(s32[32]{0:T(128)} %len_ref.1) | copy-start | bytes 388
  2.1 2.4 %copy-start.4 = (s32[32]{0:T(128)S(1)}, s32[32]{0:T(128)}, u32[]{:S(2)}) copy-start(s32[32]{0:T(128)} %ids_ref.1) | copy-start | bytes 388
  4.3 10.1 %collective-permute-start.1 = (bf16[2,8,64,1024]{3,2,1,0:T(8,128)(2,1)S(1)}, bf16[2,8,64,1024]{3,2,1,0:T(8,128)(2,1)S(1)}, u32[]{:S(2)}, u32[]{:S(2)}) collective-permute-start(bf16[2,8,64,1024]{3,2,1,0:T(8,128)(2,1)S(1)} %collect_pages.1), channel_id=1, source_target_pairs={{0,8},{8,0},{1,9},{9,1},{2,10},{10,2},{3,11},{11,3},{4,12},{12,4},... | collective-permute-start | bytes 6291464 | tf_op jit(solution)/shard_map/ppermute | solution.py:472
  15.6 7.3 %collective-permute-start.2 = (bf16[32,2176]{1,0:T(8,128)(2,1)S(1)}, bf16[32,2176]{1,0:T(8,128)(2,1)S(1)}, u32[]{:S(2)}, u32[]{:S(2)}) collective-permute-start(bf16[32,2176]{1,0:T(8,128)(2,1)S(1)} %get-tuple-element.30), channel_id=1, source_target_pairs={{0,1},{1,0},{2,3},{3,2},{4,5},{5,4},{6,7},{7,6},{8,9},{9,8},{10,11... | collective-permute-start | bytes 417800 | tf_op jit(solution)/shard_map/ppermute | solution.py:466
  19.3 9.3 %collective-permute-start.3 = (bf16[32,2048]{1,0:T(8,128)(2,1)S(1)}, bf16[32,2048]{1,0:T(8,128)(2,1)S(1)}, u32[]{:S(2)}, u32[]{:S(2)}) collective-permute-start(bf16[32,2048]{1,0:T(8,128)(2,1)S(1)} %second_blocks.1), channel_id=1, source_target_pairs={{0,1},{1,0},{2,3},{3,2},{4,5},{5,4},{6,7},{7,6},{8,9},{9,8},{10,11... | collective-permute-start | bytes 393224 | tf_op jit(solution)/shard_map/ppermute | solution.py:466
  23.4 6.3 %collective-permute-start.4 = (bf16[32,1152]{1,0:T(8,128)(2,1)S(1)}, bf16[32,1152]{1,0:T(8,128)(2,1)S(1)}, u32[]{:S(2)}, u32[]{:S(2)}) collective-permute-start(bf16[32,1152]{1,0:T(8,128)(2,1)S(1)} %add_block.3), channel_id=1, source_target_pairs={{0,2},{1,3},{2,0},{3,1},{4,6},{5,7},{6,4},{7,5},{8,10},{9,11},{10,... | collective-permute-start | bytes 221192 | tf_op jit(solution)/shard_map/ppermute | solution.py:469
  26.0 6.9 %collective-permute-start.5 = (bf16[32,1152]{1,0:T(8,128)(2,1)S(1)}, bf16[32,1152]{1,0:T(8,128)(2,1)S(1)}, u32[]{:S(2)}, u32[]{:S(2)}) collective-permute-start(bf16[32,1152]{1,0:T(8,128)(2,1)S(1)} %add_block.4), channel_id=1, source_target_pairs={{0,4},{1,5},{2,6},{3,7},{4,0},{5,1},{6,2},{7,3},{8,12},{9,13},{10,... | collective-permute-start | bytes 221192 | tf_op jit(solution)/shard_map/ppermute | solution.py:469
  29.0 6.2 %collective-permute-start.6 = (bf16[32,1152]{1,0:T(8,128)(2,1)S(1)}, bf16[32,1152]{1,0:T(8,128)(2,1)S(1)}, u32[]{:S(2)}, u32[]{:S(2)}) collective-permute-start(bf16[32,1152]{1,0:T(8,128)(2,1)S(1)} %add_block.5), channel_id=1, source_target_pairs={{0,6},{1,7},{2,4},{3,5},{4,2},{5,3},{6,0},{7,1},{8,14},{9,15},{10,... | collective-permute-start | bytes 221192 | tf_op jit(solution)/shard_map/ppermute | solution.py:469
  36.0 6.2 %collective-permute-start.12 = (bf16[32,1024]{1,0:T(8,128)(2,1)S(1)}, bf16[32,1024]{1,0:T(8,128)(2,1)S(1)}, u32[]{:S(2)}, u32[]{:S(2)}) collective-permute-start(bf16[32,1024]{1,0:T(8,128)(2,1)S(1)} %finish.1.refs_0_), channel_id=1, source_target_pairs={{0,6},{1,7},{2,4},{3,5},{4,2},{5,3},{6,0},{7,1},{8,14},{9,15},{10,... | collective-permute-start | bytes 196616 | tf_op jit(solution)/shard_map/ppermute | solution.py:469
  37.1 6.7 %collective-permute-start.10 = (bf16[32,1024]{1,0:T(8,128)(2,1)S(1)}, bf16[32,1024]{1,0:T(8,128)(2,1)S(1)}, u32[]{:S(2)}, u32[]{:S(2)}) collective-permute-start(bf16[32,1024]{1,0:T(8,128)(2,1)S(1)} %finish.1.refs_0_), channel_id=1, source_target_pairs={{0,4},{1,5},{2,6},{3,7},{4,0},{5,1},{6,2},{7,3},{8,12},{9,13},{10,... | collective-permute-start | bytes 196616 | tf_op jit(solution)/shard_map/ppermute | solution.py:469
  37.6 7.5 %collective-permute-start.8 = (bf16[32,1024]{1,0:T(8,128)(2,1)S(1)}, bf16[32,1024]{1,0:T(8,128)(2,1)S(1)}, u32[]{:S(2)}, u32[]{:S(2)}) collective-permute-start(bf16[32,1024]{1,0:T(8,128)(2,1)S(1)} %finish.1.refs_0_), channel_id=1, source_target_pairs={{0,2},{1,3},{2,0},{3,1},{4,6},{5,7},{6,4},{7,5},{8,10},{9,11},{10,... | collective-permute-start | bytes 196616 | tf_op jit(solution)/shard_map/ppermute | solution.py:469
  40.5 5.3 %collective-permute-start.7 = (bf16[32,1024]{1,0:T(8,128)(2,1)S(1)}, bf16[32,1024]{1,0:T(8,128)(2,1)S(1)}, u32[]{:S(2)}, u32[]{:S(2)}) collective-permute-start(bf16[32,1024]{1,0:T(8,128)(2,1)S(1)} %finish.1.refs_0_), channel_id=1, source_target_pairs={{0,1},{1,0},{2,3},{3,2},{4,5},{5,4},{6,7},{7,6},{8,9},{9,8},{10,11... | collective-permute-start | bytes 196616 | tf_op jit(solution)/shard_map/ppermute | solution.py:466
  42.2 4.3 %collective-permute-start.13 = (bf16[32,1024]{1,0:T(8,128)(2,1)S(1)}, bf16[32,1024]{1,0:T(8,128)(2,1)S(1)}, u32[]{:S(2)}, u32[]{:S(2)}) collective-permute-start(bf16[32,1024]{1,0:T(8,128)(2,1)S(1)} %collective-permute-done.12.refs_6_), channel_id=1, source_target_pairs={{0,1},{1,0},{2,3},{3,2},{4,5},{5,4},{6,7},{7,6},{8,9},{9,8},{10,11... | collective-permute-start | bytes 196616 | tf_op jit(solution)/shard_map/ppermute | solution.py:466
  43.8 4.3 %collective-permute-start.11 = (bf16[32,1024]{1,0:T(8,128)(2,1)S(1)}, bf16[32,1024]{1,0:T(8,128)(2,1)S(1)}, u32[]{:S(2)}, u32[]{:S(2)}) collective-permute-start(bf16[32,1024]{1,0:T(8,128)(2,1)S(1)} %collective-permute-done.10.refs_4_), channel_id=1, source_target_pairs={{0,1},{1,0},{2,3},{3,2},{4,5},{5,4},{6,7},{7,6},{8,9},{9,8},{10,11... | collective-permute-start | bytes 196616 | tf_op jit(solution)/shard_map/ppermute | solution.py:466
  45.1 4.3 %collective-permute-start.9 = (bf16[32,1024]{1,0:T(8,128)(2,1)S(1)}, bf16[32,1024]{1,0:T(8,128)(2,1)S(1)}, u32[]{:S(2)}, u32[]{:S(2)}) collective-permute-start(bf16[32,1024]{1,0:T(8,128)(2,1)S(1)} %collective-permute-done.8.refs_2_), channel_id=1, source_target_pairs={{0,1},{1,0},{2,3},{3,2},{4,5},{5,4},{6,7},{7,6},{8,9},{9,8},{10,11... | collective-permute-start | bytes 196616 | tf_op jit(solution)/shard_map/ppermute | solution.py:466

commit v4 on v3

v4 whole, which is shorter than its diff:
```python
import functools

import jax
import jax.numpy as jnp
from jax import lax
from jax.experimental import pallas as pl
from jax.experimental.pallas import tpu as pltpu
from jax.sharding import PartitionSpec as P

F32 = jnp.float32
BF16 = jnp.bfloat16
LOG2E = 1.4426950408889634
ANY = pl.BlockSpec(memory_space=pl.ANY)
VMEM = pl.BlockSpec(memory_space=pltpu.VMEM)
SMEM = pl.BlockSpec(memory_space=pltpu.SMEM)
MIB = 1 << 20
DISTINCT = 8


def in_hbm(x):
    return pltpu.with_memory_space_constraint(x, pltpu.HBM)


def params(mib):
    return pltpu.CompilerParams(vmem_limit_bytes=mib * MIB)


def nt_dot(a, b):
    return lax.dot_general(a, b, (((1,), (1,)), ((), ())), preferred_element_type=F32)


def nn_dot(a, b):
    return jnp.dot(a, b, preferred_element_type=F32)


def distinct_list(ids_ref, pool_slot_ref, seen, list_id, list_pos):
    rows = ids_ref.shape[0]
    for i in range(pool_slot_ref.shape[0]):
        seen[i] = 0
    for j in range(DISTINCT + 1):
        list_id[j] = -1
        list_pos[j] = 0
    found = jnp.int32(0)
    for r in range(rows):
        one = ids_ref[r]
        fresh = 1 - seen[one]
        seen[one] = 1
        spot = jnp.minimum(found, DISTINCT)
        list_id[spot] = jnp.where(fresh == 1, one, list_id[spot])
        list_pos[spot] = jnp.where(fresh == 1, pool_slot_ref[one], list_pos[spot])
        found = found + fresh


def list_scratch(pool_slot):
    return [
        pltpu.SMEM((pool_slot.shape[0],), jnp.int32),
        pltpu.SMEM((DISTINCT + 1,), jnp.int32),
        pltpu.SMEM((DISTINCT + 1,), jnp.int32),
    ]


def page_copies(pages_ref, outs, list_pos, sem, wait):
    pool = pages_ref.shape[0]
    me = lax.axis_index("req")
    for j in range(DISTINCT):
        pos = list_pos[j]

        @pl.when(pos // pool == me)
        def _():
            for i, out in enumerate(outs):
                copy = pltpu.make_async_copy(pages_ref.at[pos % pool, i], out.at[j], sem.at[i, j])
                if wait:
                    copy.wait()
                else:
                    copy.start()


def suffix_scores_kernel(
    len_ref, q_ref, prefix_ref, suffix_ref, query_ref, tail_ref, keys_ref, suf, rowbuf, sem, sem_suf
):
    rows = q_ref.shape[0]
    head_dim = prefix_ref.shape[3]
    heads = q_ref.shape[1] // head_dim
    span = suffix_ref.shape[3]
    groups = sem_suf.shape[0]
    size = rows // groups
    copies = [
        pltpu.make_async_copy(
            suffix_ref.at[pl.ds(j * size, size), 0, 0], suf.at[pl.ds(j * size, size)], sem_suf.at[j]
        )
        for j in range(groups)
    ]
    fetch = pltpu.make_async_copy(prefix_ref.at[0, 0], keys_ref, sem.at[0])
    for c in copies + [fetch]:
        c.start()
    for h in range(heads):
        rowbuf[pl.ds(h, rows, stride=heads), :] = q_ref[:, h * head_dim : (h + 1) * head_dim].astype(F32)
    query = rowbuf[...].astype(BF16)
    query_ref[...] = query
    lanes = lax.broadcasted_iota(jnp.int32, (heads, span), 1)
    for j in range(groups):
        copies[j].wait()
        for i in range(j * size // 2, (j + 1) * size // 2):
            keys = suf[2 * i : 2 * i + 2].reshape(2 * span, head_dim)
            both = nt_dot(query[2 * heads * i : 2 * heads * (i + 1)], keys)
            for a in range(2):
                mine = both[a * heads : (a + 1) * heads, a * span : (a + 1) * span]
                row = 2 * i + a
                tail_ref[row * heads : (row + 1) * heads, :] = jnp.where(lanes < len_ref[row], mine, -1.0e30)
    fetch.wait()


def weight_copies(weight_ref, outs, spots, sem):
    me = lax.axis_index("tensor")
    z, y = me // 2, me % 2
    copies = []
    for i, (side, k) in enumerate(spots):
        width = outs[i].shape[1]
        column = pl.multiple_of(((z ^ k) * 2 + (y ^ side)) * width, width)
        copies.append(pltpu.make_async_copy(weight_ref.at[:, pl.ds(column, width)], outs[i], sem.at[i]))
    return copies


def prefix_scores_kernel(spots, ids_ref, slot_ref, query_ref, tail_ref, keys_ref, prefix_ref, suffix_ref, *rest):
    pages_ref, weight_ref = rest[:2]
    scores_ref, peak_ref, out_pages_ref, vals_ref, suf_vals_ref = rest[2:7]
    w_refs = rest[7 : 7 + len(spots)]
    seen, list_id, list_pos, sem, sem_page, sem_w = rest[7 + len(spots) :]
    tokens = keys_ref.shape[0]
    fetch = [
        pltpu.make_async_copy(prefix_ref.at[0, 1], vals_ref, sem.at[0]),
        pltpu.make_async_copy(suffix_ref.at[:, 0, 1], suf_vals_ref, sem.at[1]),
    ] + weight_copies(weight_ref, w_refs, spots, sem_w)
    distinct_list(ids_ref, slot_ref, seen, list_id, list_pos)
    outs = (out_pages_ref.at[0], out_pages_ref.at[1])
    page_copies(pages_ref, outs, list_pos, sem_page, False)
    for c in fetch:
        c.start()
    query = query_ref[...]
    best = jnp.maximum(tail_ref[:, :128], tail_ref[:, 128:256])
    for b in range(2, tail_ref.shape[1] // 128):
        best = jnp.maximum(best, tail_ref[:, b * 128 : (b + 1) * 128])
    for base in range(0, tokens, 256):
        block = nt_dot(query, keys_ref[base : base + 256, :])
        scores_ref[:, base : base + 256] = block
        best = jnp.maximum(best, jnp.maximum(block[:, :128], block[:, 128:]))
    peak_ref[...] = jnp.broadcast_to(jnp.max(best, axis=1, keepdims=True), peak_ref.shape)
    page_copies(pages_ref, outs, list_pos, sem_page, True)
    for c in fetch:
        c.wait()


def values_kernel(spots, ids_ref, slot_ref, scores, tail, peak, vals_ref, suf_vals_ref, *rest):
    pages_ref, weight_ref, residual_ref = rest[:3]
    att_ref, shrink_ref, expand_ref, row_slot_ref, slot_mine_ref, res_ref = rest[3:9]
    w_refs = rest[9 : 9 + len(spots)]
    rowbuf, total, acc, seen, list_id, list_pos, sem, sem_page, sem_w = rest[9 + len(spots) :]
    rows, head_dim, span = suf_vals_ref.shape[0], vals_ref.shape[1], suf_vals_ref.shape[1]
    tokens = vals_ref.shape[0]
    heads = att_ref.shape[1] // head_dim
    width = res_ref.shape[1]
    me = lax.axis_index("tensor")
    scale2 = float(head_dim) ** -0.5 * LOG2E
    fetch = weight_copies(weight_ref, w_refs, spots, sem_w)
    fetch.append(
        pltpu.make_async_copy(
            residual_ref.at[:, pl.ds(pl.multiple_of(me * width, width), width)], res_ref, sem.at[0]
        )
    )
    for c in fetch:
        c.start()
    distinct_list(ids_ref, slot_ref, seen, list_id, list_pos)
    page_copies(pages_ref, (shrink_ref, expand_ref), list_pos, sem_page, False)
    row_index = lax.broadcasted_iota(jnp.int32, (rows, 128), 0)
    row_id = jnp.full((rows, 128), -2, jnp.int32)
    for r in range(rows):
        row_id = jnp.where(row_index == r, ids_ref[r], row_id)
    row_slot = jnp.full((rows, 128), -1, jnp.int32)
    slot_index = lax.broadcasted_iota(jnp.int32, (DISTINCT, 128), 0)
    slot_mine = jnp.zeros((DISTINCT, 128), jnp.int32)
    mine = lax.axis_index("req")
    for j in range(DISTINCT):
        row_slot = jnp.where(row_id == list_id[j], j, row_slot)
        owned = (list_pos[j] // pages_ref.shape[0] == mine).astype(jnp.int32)
        slot_mine = jnp.where(slot_index == j, owned, slot_mine)
    row_slot_ref[...] = row_slot
    slot_mine_ref[...] = slot_mine

    total[...] = jnp.zeros(total.shape, F32)
    acc[...] = jnp.zeros(acc.shape, F32)
    chunk = min(2048, tokens)

    @pl.loop(0, tokens // chunk)
    def _(i):
        base = pl.multiple_of(i * chunk, chunk)
        high = peak[...]
        summed = total[...]
        parts = []
        for b in range(chunk // 128):
            e = jnp.exp2((scores[:, pl.ds(base + b * 128, 128)] - high) * scale2)
            summed = summed + e
            parts.append(e.astype(BF16))
        total[...] = summed
        acc[...] += nn_dot(jnp.concatenate(parts, axis=1), vals_ref[pl.ds(base, chunk), :])

    zeros = jnp.zeros((heads, span), F32)
    for i in range(rows // 2):
        lo = 2 * heads * i
        high = jnp.concatenate([peak[lo : lo + 2 * heads, :]] * (span // 128), axis=1)
        e = jnp.exp2((tail[lo : lo + 2 * heads, :] - high) * scale2)
        part_sum = e[:, :128]
        for b in range(1, span // 128):
            part_sum = part_sum + e[:, b * 128 : (b + 1) * 128]
        total[lo : lo + 2 * heads, :] += part_sum
        diag = jnp.concatenate(
            [
                jnp.concatenate([e[:heads], zeros], axis=1),
                jnp.concatenate([zeros, e[heads:]], axis=1),
            ],
            axis=0,
        ).astype(BF16)
        vals = suf_vals_ref[2 * i : 2 * i + 2].reshape(2 * span, head_dim)
        acc[lo : lo + 2 * heads, :] += nn_dot(diag, vals)

    norm = jnp.sum(total[...], axis=1, keepdims=True)
    rowbuf[...] = acc[...] / norm
    for h in range(heads):
        att_ref[:, h * head_dim : (h + 1) * head_dim] = rowbuf[pl.ds(h, rows, stride=heads), :].astype(BF16)
    page_copies(pages_ref, (shrink_ref, expand_ref), list_pos, sem_page, True)
    for c in fetch:
        c.wait()


def kernel_call(kernel, name, out_shape, specs, scratch, operands, mib, flops, bytes_accessed):
    return pl.pallas_call(
        kernel,
        out_shape=out_shape,
        in_specs=specs,
        out_specs=[VMEM] * len(out_shape),
        scratch_shapes=scratch,
        compiler_params=params(mib),
        cost_estimate=pl.CostEstimate(flops=flops, bytes_accessed=bytes_accessed, transcendentals=0),
        name=name,
    )(*operands)


def attend(
    suffix_len, ids, other_ids, pool_slot, queries, prefix_kv, suffix_kv, out_weight, pages, residual, n_tensor, across
):
    rows = queries.shape[0]
    n_z = n_tensor // 2
    in_rows = out_weight.shape[0]
    width = out_weight.shape[1] // n_tensor
    tokens, head_dim = prefix_kv.shape[2:]
    n_q = rows * queries.shape[1] // head_dim
    span = suffix_kv.shape[3]
    prefix_kv, suffix_kv, out_weight = in_hbm(prefix_kv), in_hbm(suffix_kv), in_hbm(out_weight)
    pages, residual = in_hbm(pages), in_hbm(residual)
    query, tail, keys = kernel_call(
        suffix_scores_kernel,
        "suffix_scores",
        [pltpu.VMEM((n_q, head_dim), BF16), pltpu.VMEM((n_q, span), F32), pltpu.VMEM((tokens, head_dim), BF16)],
        [SMEM, VMEM, ANY, ANY],
        [
            pltpu.VMEM((rows, span, head_dim), BF16),
            pltpu.VMEM((n_q, head_dim), F32),
            pltpu.SemaphoreType.DMA((1,)),
            pltpu.SemaphoreType.DMA((4,)),
        ],
        [suffix_len, queries, prefix_kv, suffix_kv],
        6,
        1 << 30,
        6 * MIB,
    )
    far = list(range(n_z - 1, -1, -1))
    early = [(0, k) for k in far[: n_z // 2]]
    late = [(1, k) for k in far] + [(0, k) for k in far[n_z // 2 :]]
    scores, peak, out_pages, vals, suf_vals, *early_w = kernel_call(
        functools.partial(prefix_scores_kernel, early),
        "prefix_scores",
        [
            pltpu.VMEM((n_q, tokens), F32),
            pltpu.VMEM((n_q, 128), F32),
            pltpu.VMEM((2, DISTINCT) + pages.shape[2:], BF16),
            pltpu.VMEM((tokens, head_dim), BF16),
            pltpu.VMEM((rows, span, head_dim), BF16),
        ]
        + [pltpu.VMEM((in_rows, width), BF16)] * len(early),
        [SMEM, SMEM, VMEM, VMEM, VMEM, ANY, ANY, ANY, ANY],
        list_scratch(pool_slot)
        + [
            pltpu.SemaphoreType.DMA((2,)),
            pltpu.SemaphoreType.DMA((2, DISTINCT)),
            pltpu.SemaphoreType.DMA((len(early),)),
        ],
        [other_ids, pool_slot, query, tail, keys, prefix_kv, suffix_kv, pages, out_weight],
        4,
        2 * n_q * tokens * head_dim,
        9 * MIB,
    )
    other_pages = across(out_pages)
    attended, own_shrink, own_expand, row_slot, slot_mine, res, *late_w = kernel_call(
        functools.partial(values_kernel, late),
        "values",
        [
            pltpu.VMEM(queries.shape, BF16),
            pltpu.VMEM((DISTINCT,) + pages.shape[2:], BF16),
            pltpu.VMEM((DISTINCT,) + pages.shape[2:], BF16),
            pltpu.VMEM((rows, 128), jnp.int32),
            pltpu.VMEM((DISTINCT, 128), jnp.int32),
            pltpu.VMEM((rows, width), BF16),
        ]
        + [pltpu.VMEM((in_rows, width), BF16)] * len(late),
        [SMEM, SMEM, VMEM, VMEM, VMEM, VMEM, VMEM, ANY, ANY, ANY],
        [
            pltpu.VMEM((n_q, head_dim), F32),
            pltpu.VMEM((n_q, 128), F32),
            pltpu.VMEM((n_q, head_dim), F32),
        ]
        + list_scratch(pool_slot)
        + [
            pltpu.SemaphoreType.DMA((1,)),
            pltpu.SemaphoreType.DMA((2, DISTINCT)),
            pltpu.SemaphoreType.DMA((len(late),)),
        ],
        [ids, pool_slot, scores, tail, peak, vals, suf_vals, pages, out_weight, residual],
        6,
        2 * n_q * tokens * head_dim,
        14 * MIB,
    )
    weights = dict(zip(early + late, list(early_w) + list(late_w)))
    return attended, own_shrink, own_expand, other_pages, row_slot, slot_mine, res, weights


def small_call(kernel, name, out_shape, operands, flops=1 << 27):
    return pl.pallas_call(
        kernel,
        out_shape=out_shape,
        in_specs=[VMEM] * len(operands),
        out_specs=jax.tree.map(lambda _: VMEM, out_shape),
        compiler_params=params(8),
        cost_estimate=pl.CostEstimate(flops=flops, bytes_accessed=2 * MIB, transcendentals=0),
        name=name,
    )(*operands)


def merged(own_ref, other, half, slot_mine):
    rank = own_ref.shape[1]
    tiles = []
    for j in range(DISTINCT):
        hit = jnp.broadcast_to(slot_mine[j : j + 1, :1], (rank, 1)) == 1
        tiles.append(jnp.where(hit, own_ref[j].astype(F32), other[half, j].astype(F32)).astype(BF16))
    return jnp.concatenate(tiles, axis=0)


def lane_place(shape, rank):
    return lax.broadcasted_iota(jnp.int32, shape, 1) // rank


def far_kernel(n, att_ref, row_slot_ref, slot_mine_ref, own_ref, other_ref, *rest):
    w_refs = rest[:n]
    out_ref, rank_ref = rest[n:]
    width = w_refs[0].shape[1]
    attended = att_ref[...]
    for k in range(n):
        out_ref[:, k * width : (k + 1) * width] = nn_dot(attended, w_refs[k][...]).astype(BF16)
    rank = own_ref.shape[1]
    per_tile = 128 // rank
    low = nt_dot(attended, merged(own_ref, other_ref, 0, slot_mine_ref[...]))
    row_slot = row_slot_ref[...]
    place = lane_place(row_slot.shape, rank)
    picked = jnp.zeros(row_slot.shape, F32)
    for tile in range(DISTINCT // per_tile):
        hit = row_slot == place + tile * per_tile
        picked = jnp.where(hit, low[:, tile * 128 : (tile + 1) * 128], picked)
    rank_ref[...] = picked
    out_ref[:, n * width :] = picked.astype(BF16)


def near_kernel(att_ref, w_ref, cross_w_ref, rank_ref, out_ref, cross_ref):
    width = w_ref.shape[1]
    attended = att_ref[...]
    rank = rank_ref[...].astype(BF16)
    for w, out in ((w_ref, out_ref), (cross_w_ref, cross_ref)):
        out[:, :width] = nn_dot(attended, w[...]).astype(BF16)
        out[:, width:] = rank


def block_kernel(att_ref, w_ref, after_ref, out_ref):
    out_ref[...] = nn_dot(att_ref[...], w_ref[...]).astype(BF16)


def add_kernel(spot, att_ref, w_ref, from_ref, rank_ref, out_ref):
    width = w_ref.shape[1]
    both = nn_dot(att_ref[...], w_ref[...]) + from_ref[:, spot * width : (spot + 1) * width].astype(F32)
    out_ref[:, :width] = both.astype(BF16)
    rank_both = rank_ref[...] + from_ref[:, from_ref.shape[1] - 128 :].astype(F32)
    out_ref[:, width:] = rank_both.astype(BF16)


def finish_kernel(*refs):
    att_ref, w_ref, row_slot_ref, slot_mine_ref, own_ref, other_ref = refs[:6]
    rank_ref, far_ref, from_ref, res_ref = refs[6:10]
    moved, out_ref = refs[10:-1], refs[-1]
    rank = own_ref.shape[1]
    per_tile = 128 // rank
    width = w_ref.shape[1]
    low = rank_ref[...] + far_ref[:, far_ref.shape[1] - 128 :].astype(F32)
    for ref in moved:
        low = low + ref[:, width:].astype(F32)
    row_slot = row_slot_ref[...]
    place = lane_place(row_slot.shape, rank)
    tiles = []
    for tile in range(DISTINCT // per_tile):
        tiles.append(jnp.where(row_slot == place + tile * per_tile, low, 0.0).astype(BF16))
    total = nn_dot(jnp.concatenate(tiles, axis=1), merged(own_ref, other_ref, 1, slot_mine_ref[...]))
    total = total + nn_dot(att_ref[...], w_ref[...])
    total = total + (res_ref[...].astype(F32) + from_ref[...].astype(F32))
    for ref in moved:
        total = total + ref[:, :width].astype(F32)
    out_ref[...] = total.astype(BF16)


def place_kernel(n_z, *refs):
    blocks = refs[: 2 * n_z]
    out_ref = refs[2 * n_z]
    width = blocks[0].shape[1]
    me = lax.axis_index("tensor")
    z, y = me // 2, me % 2
    for k in range(n_z):
        for other in range(2):
            where = (z ^ k) * 2 + (y ^ other)
            out_ref[:, pl.ds(pl.multiple_of(where * width, width), width)] = blocks[2 * k + other][...]


def place(blocks, n_tensor):
    rows, width = blocks[0].shape
    return pl.pallas_call(
        functools.partial(place_kernel, n_tensor // 2),
        out_shape=jax.ShapeDtypeStruct((rows, width * n_tensor), BF16),
        in_specs=[VMEM] * n_tensor,
        out_specs=VMEM,
        compiler_params=params(4),
        cost_estimate=pl.CostEstimate(flops=0, bytes_accessed=1 * MIB, transcendentals=0),
        name="place",
    )(*blocks)


def body(
    n_tensor,
    queries,
    prefix_kv,
    suffix_kv,
    suffix_len,
    residual,
    out_weight,
    adapter_pages,
    adapter_ids,
    pool_slot,
):
    n_z = n_tensor // 2

    def along_y(x):
        return lax.ppermute(x, "tensor", [(t, t ^ 1) for t in range(n_tensor)])

    def along_z(x, k):
        return lax.ppermute(x, "tensor", [(t, t ^ (2 * k)) for t in range(n_tensor)])

    def along_both(x, k):
        return lax.ppermute(x, "tensor", [(t, t ^ (2 * k) ^ 1) for t in range(n_tensor)])

    def across(x):
        return lax.ppermute(x, "req", [(0, 1), (1, 0)])

    rows = queries.shape[0]
    width = out_weight.shape[1] // n_tensor
    attended, own_shrink, own_expand, other_pages, row_slot, slot_mine, res, weights = attend(
        suffix_len,
        adapter_ids,
        across(adapter_ids),
        pool_slot,
        queries,
        prefix_kv,
        suffix_kv,
        out_weight,
        adapter_pages,
        residual,
        n_tensor,
        across,
    )
    far = list(range(n_z - 1, 1, -1))
    piece_shape = pltpu.VMEM((rows, width + 128), BF16)
    far_out, rank_own = small_call(
        functools.partial(far_kernel, len(far)),
        "far_blocks",
        [pltpu.VMEM((rows, len(far) * width + 128), BF16), pltpu.VMEM((rows, 128), F32)],
        [attended, row_slot, slot_mine, own_shrink, other_pages] + [weights[1, k] for k in far],
    )
    from_far = along_y(far_out)
    straight, cross = small_call(
        near_kernel,
        "near_blocks",
        [piece_shape, piece_shape],
        [attended, weights[0, 1], weights[1, 1], rank_own],
    )
    moved = [along_z(straight, 1), along_both(cross, 1)]
    for spot, k in enumerate(far):
        piece = small_call(
            functools.partial(add_kernel, spot),
            "add_block",
            piece_shape,
            [attended, weights[0, k], from_far, rank_own],
        )
        moved.append(along_z(piece, k))
    own_far = small_call(
        block_kernel, "own_far_block", pltpu.VMEM((rows, width), BF16), [attended, weights[1, 0], piece]
    )
    from_own = along_y(own_far)
    result = small_call(
        finish_kernel,
        "finish",
        pltpu.VMEM((rows, width), BF16),
        [attended, weights[0, 0], row_slot, slot_mine, own_expand, other_pages, rank_own, from_far, from_own, res]
        + moved,
    )
    held = [result] + [along_z(result, k) for k in range(1, n_z)]
    blocks = []
    for k in range(n_z):
        blocks += [held[k], along_both(result, k) if k < 2 else along_y(held[k])]
    return place(blocks, n_tensor)


def solution(mesh):
    return jax.shard_map(
        functools.partial(body, mesh.shape["tensor"]),
        mesh=mesh,
        in_specs=(
            P(("group", "req"), "tensor"),
            P(("group", "tensor"), None, None, None),
            P(("group", "req"), "tensor", None, None, None),
            P(("group", "req")),
            P(("group", "req"), None),
            P("tensor", None),
            P("req", None, None, "tensor"),
            P(("group", "req")),
            P(),
        ),
        out_specs=P(("group", "req"), None),
        check_vma=False,
    )
```

time: 50.2 us -> 50.4 us (level)
  waiting for transfers between devices: 13.9 us -> 7.86 us
  Pallas kernels: 17.2 us -> 20.1 us
  starting transfers between devices: 18.3 us -> 20.6 us
  local copies, waits for them, and re-layouts: 0.67 us -> 1.5 us
    ppermute x6, waiting for transfers between devices: 5.82 us -> 1.23 us  [along_z(): return lax.ppermute(x, 'tensor', [(t, t ^ 2 * k) for t in range(n_tensor)])]
    ppermute x0 -> x3, starting transfers between devices: none -> 3.35 us  [along_both(): lax.ppermute(x, 'tensor', [(t, t ^ 2 * k ^ 1) for t in range(n_tensor)])]
    pallas_call x2 -> x3, Pallas kernels: 12.2 us -> 15.1 us  [kernel_call(): pl.pallas_call(kernel, out_shape=out_shape, in_specs=specs, out_specs=[VM...]
    ppermute x6, starting transfers between devices: 9.81 us -> 8.29 us  [along_z(): return lax.ppermute(x, 'tensor', [(t, t ^ 2 * k) for t in range(n_tensor)])]
    ppermute x2, waiting for transfers between devices: 0.96 us -> 0.01 us  [across(): return lax.ppermute(x, 'req', [(0, 1), (1, 0)])]
    unnamed x10 -> x8, local copies, waits for them, and re-layouts: 0.67 us -> 1.5 us
    ppermute x6 -> x4, waiting for transfers between devices: 7.15 us -> 6.48 us  [along_y(): return lax.ppermute(x, 'tensor', [(t, t ^ 1) for t in range(n_tensor)])]
    ppermute x6 -> x4, starting transfers between devices: 7.97 us -> 8.48 us  [along_y(): return lax.ppermute(x, 'tensor', [(t, t ^ 1) for t in range(n_tensor)])]
  transfers between devices with their start and end apart: 14 -> 15, of which waited for: 8 -> 7; matrix products, arithmetic and copies ran while one was open for 0% -> 0% of each run, Pallas kernels for 24% -> 22%
where the time goes in v4:
time: 50.4 us; the launch traced here: 50.2 us
  starting transfers between devices  20.6 us (41%)
  Pallas kernels  20.1 us (40%)
  waiting for transfers between devices  7.86 us (16%)
  local copies, waits for them, and re-layouts  1.5 us (3%)
    pallas_call x3, Pallas kernels, kernel_call(): pl.pallas_call(kernel, out_shape=out_shape, in_specs=specs, out_specs=[VM...  15.1 us
    ppermute x4, starting transfers between devices, along_y(): return lax.ppermute(x, 'tensor', [(t, t ^ 1) for t in range(n_tensor)])  8.48 us
    ppermute x6, starting transfers between devices, along_z(): return lax.ppermute(x, 'tensor', [(t, t ^ 2 * k) for t in range(n_tensor)])  8.29 us
    ppermute x4, waiting for transfers between devices, along_y(): return lax.ppermute(x, 'tensor', [(t, t ^ 1) for t in range(n_tensor)])  6.48 us
    pallas_call x6, Pallas kernels, small_call(): pl.pallas_call(kernel, out_shape=out_shape, in_specs=[VMEM] * len(operand...  4.13 us
    ppermute x3, starting transfers between devices, along_both(): lax.ppermute(x, 'tensor', [(t, t ^ 2 * k ^ 1) for t in range(n_tensor)])  3.35 us
    unnamed x8, local copies, waits for them, and re-layouts  1.5 us
    ppermute x6, waiting for transfers between devices, along_z(): return lax.ppermute(x, 'tensor', [(t, t ^ 2 * k) for t in range(n_tensor)])  1.23 us
  transfers between devices with their start and end apart: 15, of which 7 were waited for; matrix products, arithmetic and copies ran while one was open for 0% of the time, Pallas kernels for 22%

profile of v4, /device:TPU:0, one launch (start us, length us, event | category | flops | bytes accessed | tf_op | source)
XLA Modules:
  0.0 50.2 jit_solution(6834290473900848138)
XLA Ops:
  0.0 0.5 collective-permute-start
  0.5 0.8 %copy-done = bf16[32,1024]{1,0:T(8,128)(2,1)S(1)} copy-done((bf16[32,1024]{1,0:T(8,128)(2,1)S(1)}, bf16[32,1024]{1,0:T(8,128)(2,1)}, u32[]{:S(2)}) %copy-start) | copy-done | bytes 65560
  1.3 0.7 %copy-done.2 = s32[32]{0:T(128)S(1)} copy-done((s32[32]{0:T(128)S(1)}, s32[32]{0:T(128)}, u32[]{:S(2)}) %copy-start.2) | copy-done | bytes 152
  2.0 2.8 %suffix_scores.1 = (bf16[256,128]{1,0:T(8,128)(2,1)S(1)}, f32[256,256]{1,0:T(8,128)S(1)}, bf16[8192,128]{1,0:T(8,128)(2,1)S(1)}) custom-call(s32[32]{0:T(128)S(1)} %copy-done.2, bf16[32,1024]{1,0:T(8,128)(2,1)S(1)} %copy-done, bf16[1,2,8192,128]{3,2,1,0:T(8,128)(2,1)} %prefix_ref.3, bf16[32,1,2,256,128]{4,3,2,1,0:T(8,128)(2,1)} %suffix_ref.3), custom_call_target="tpu_custom_call" | custom-call | flops 1073741824 | bytes 6291456 | tf_op jit(solution)/shard_map/suffix_scores/pallas_call | solution.py:235
  4.8 6.2 %prefix_scores.1 = (f32[256,8192]{1,0:T(8,128)S(1)}, f32[256,128]{1,0:T(8,128)S(1)}, bf16[2,8,64,1024]{3,2,1,0:T(8,128)(2,1)S(1)}, bf16[8192,128]{1,0:T(8,128)(2...) custom-call(s32[32]{0:T(128)S(1)} %collective-permute-done.ids_ref, ...), custom_call_target="tpu_custom_call" | custom-call | flops 536870912 | bytes 9437184 | tf_op jit(solution)/shard_map/prefix_scores/pallas_call | solution.py:235
  11.0 0.1 collective-permute-start.1
  11.1 6.1 %values.1 = (bf16[32,1024]{1,0:T(8,128)(2,1)S(1)}, bf16[8,64,1024]{2,1,0:T(8,128)(2,1)S(1)}, bf16[8,64,1024]{2,1,0:T(8,128)(2,1)S(1)}, s32[32,128]{1,0:T(8,128)S...) custom-call(s32[32]{0:T(128)S(1)} %copy-done.3, ...), custom_call_target="tpu_custom_call" | custom-call | flops 536870912 | bytes 14680064 | tf_op jit(solution)/shard_map/values/pallas_call | solution.py:235
  17.2 1.1 %far_blocks.1 = (bf16[32,2176]{1,0:T(8,128)(2,1)S(1)}, f32[32,128]{1,0:T(8,128)S(1)}) custom-call(bf16[32,1024]{1,0:T(8,128)(2,1)S(1)} %get-tuple-element.38.att_ref.refs_0_, s32[32,128]{1,0:T(8,128)S(1)} %get-tuple-element.40.row_slot_ref.refs_2_, s32[8,128]{1,0:T(8,128)S(1)} %get-tuple-element.41.slot_mine_ref.refs_3_, ...), custom_call_target="tpu_custom_call" | custom-call | flops 134217728 | bytes 2097152 | tf_op jit(solution)/shard_map/far_blocks/pallas_call | solution.py:336
  18.3 2.9 %collective-permute-start.2 = (bf16[32,2176]{1,0:T(8,128)(2,1)S(1)}, bf16[32,2176]{1,0:T(8,128)(2,1)S(1)}, u32[]{:S(2)}, u32[]{:S(2)}) collective-permute-start(bf16[32,2176]{1,0:T(8,128)(2,1)S(1)} %get-tuple-element.48), channel_id=1, source_target_pairs={{0,1},{1,0},{2,3},{3,2},{4,5},{5,4},{6,7},{7,6},{8,9},{9,8},{10,11... | collective-permute-start | bytes 417800 | tf_op jit(solution)/shard_map/ppermute | solution.py:464
  21.2 0.8 %near_blocks.1 = (bf16[32,1152]{1,0:T(8,128)(2,1)S(1)}, bf16[32,1152]{1,0:T(8,128)(2,1)S(1)}) custom-call(bf16[32,1024]{1,0:T(8,128)(2,1)S(1)} %get-tuple-element.38.att_ref.refs_0_, bf16[1024,1024]{1,0:T(8,128)(2,1)S(1)} %get-tuple-element.52.w_ref, bf16[1024,1024]{1,0:T(8,128)(2,1)S(1)} %get-tuple-element.53.cross_w_ref, ...), custom_call_target="tpu_custom_call" | custom-call | flops 134217728 | bytes 2097152 | tf_op jit(solution)/shard_map/near_blocks/pallas_call | solution.py:336
  22.0 1.6 %collective-permute-start.4 = (bf16[32,1152]{1,0:T(8,128)(2,1)S(1)}, bf16[32,1152]{1,0:T(8,128)(2,1)S(1)}, u32[]{:S(2)}, u32[]{:S(2)}) collective-permute-start(bf16[32,1152]{1,0:T(8,128)(2,1)S(1)} %get-tuple-element.54), channel_id=1, source_target_pairs={{0,2},{1,3},{2,0},{3,1},{4,6},{5,7},{6,4},{7,5},{8,10},{9,11},{10,... | collective-permute-start | bytes 221192 | tf_op jit(solution)/shard_map/ppermute | solution.py:467
  23.6 1.5 %collective-permute-done.2.from_ref.refs_7_ = bf16[32,2176]{1,0:T(8,128)(2,1)S(1)} collective-permute-done((bf16[32,2176]{1,0:T(8,128)(2,1)S(1)}, bf16[32,2176]{1,0:T(8,128)(2,1)S(1)}, u32[]{:S(2)}, u32[]{:S(2)}) %collective-permute-start.2) | collective-permute-done | bytes 139296 | tf_op jit(solution)/shard_map/ppermute | solution.py:464
  25.1 0.5 add_block.3
  25.6 3.8 %collective-permute-start.6 = (bf16[32,1152]{1,0:T(8,128)(2,1)S(1)}, bf16[32,1152]{1,0:T(8,128)(2,1)S(1)}, u32[]{:S(2)}, u32[]{:S(2)}) collective-permute-start(bf16[32,1152]{1,0:T(8,128)(2,1)S(1)} %add_block.3), channel_id=1, source_target_pairs={{0,6},{1,7},{2,4},{3,5},{4,2},{5,3},{6,0},{7,1},{8,14},{9,15},{10,... | collective-permute-start | bytes 221192 | tf_op jit(solution)/shard_map/ppermute | solution.py:467
  29.4 0.5 add_block.2.after_ref
  29.9 0.0 collective-permute-start.7
  29.9 0.5 own_far_block.1
  30.4 2.1 %collective-permute-start.3 = (bf16[32,1024]{1,0:T(8,128)(2,1)S(1)}, bf16[32,1024]{1,0:T(8,128)(2,1)S(1)}, u32[]{:S(2)}, u32[]{:S(2)}) collective-permute-start(bf16[32,1024]{1,0:T(8,128)(2,1)S(1)} %own_far_block.1), channel_id=1, source_target_pairs={{0,1},{1,0},{2,3},{3,2},{4,5},{5,4},{6,7},{7,6},{8,9},{9,8},{10,11... | collective-permute-start | bytes 196616 | tf_op jit(solution)/shard_map/ppermute | solution.py:464
  32.5 2.2 %collective-permute-done.3.refs_8_ = bf16[32,1024]{1,0:T(8,128)(2,1)S(1)} collective-permute-done((bf16[32,1024]{1,0:T(8,128)(2,1)S(1)}, bf16[32,1024]{1,0:T(8,128)(2,1)S(1)}, u32[]{:S(2)}, u32[]{:S(2)}) %collective-permute-start.3) | collective-permute-done | bytes 65568 | tf_op jit(solution)/shard_map/ppermute | solution.py:464
  34.7 0.8 %collective-permute-done.7.refs_13_ = bf16[32,1152]{1,0:T(8,128)(2,1)S(1)} collective-permute-done((bf16[32,1152]{1,0:T(8,128)(2,1)S(1)}, bf16[32,1152]{1,0:T(8,128)(2,1)S(1)}, u32[]{:S(2)}, u32[]{:S(2)}) %collective-permute-start.7) | collective-permute-done | bytes 73760 | tf_op jit(solution)/shard_map/ppermute | solution.py:467
  35.5 0.8 %finish.1.refs_0_ = bf16[32,1024]{1,0:T(8,128)(2,1)S(1)} custom-call(bf16[32,1024]{1,0:T(8,128)(2,1)S(1)} %get-tuple-element.38.att_ref.refs_0_, bf16[1024,1024]{1,0:T(8,128)(2,1)S(1)} %get-tuple-element.39.refs_1_, s32[32,128]{1,0:T(8,128)S(1)} %get-tuple-element.40.row_slot_ref.refs_2_, s32[8,128]{1,0:T(8,128)S(1)} %get-tuple-element.41.slot_mine_ref.refs_3_, ...), custom_call_target="tpu_custom_call" | custom-call | flops 134217728 | bytes 2097152 | tf_op jit(solution)/shard_map/finish/pallas_call | solution.py:336
  36.3 2.7 %collective-permute-start.13 = (bf16[32,1024]{1,0:T(8,128)(2,1)S(1)}, bf16[32,1024]{1,0:T(8,128)(2,1)S(1)}, u32[]{:S(2)}, u32[]{:S(2)}) collective-permute-start(bf16[32,1024]{1,0:T(8,128)(2,1)S(1)} %finish.1.refs_0_), channel_id=1, source_target_pairs={{0,6},{1,7},{2,4},{3,5},{4,2},{5,3},{6,0},{7,1},{8,14},{9,15},{10,... | collective-permute-start | bytes 196616 | tf_op jit(solution)/shard_map/ppermute | solution.py:467
  39.0 2.9 %collective-permute-start.10 = (bf16[32,1024]{1,0:T(8,128)(2,1)S(1)}, bf16[32,1024]{1,0:T(8,128)(2,1)S(1)}, u32[]{:S(2)}, u32[]{:S(2)}) collective-permute-start(bf16[32,1024]{1,0:T(8,128)(2,1)S(1)} %finish.1.refs_0_), channel_id=1, source_target_pairs={{0,3},{1,2},{2,1},{3,0},{4,7},{5,6},{6,5},{7,4},{8,11},{9,10},{10,... | collective-permute-start | bytes 196616 | tf_op jit(solution)/shard_map/ppermute | solution.py:470
  41.9 0.1 collective-permute-start.9
  42.1 0.5 collective-permute-start.8
  42.5 2.1 %collective-permute-start.14 = (bf16[32,1024]{1,0:T(8,128)(2,1)S(1)}, bf16[32,1024]{1,0:T(8,128)(2,1)S(1)}, u32[]{:S(2)}, u32[]{:S(2)}) collective-permute-start(bf16[32,1024]{1,0:T(8,128)(2,1)S(1)} %collective-permute-done.13.refs_6_), channel_id=1, source_target_pairs={{0,1},{1,0},{2,3},{3,2},{4,5},{5,4},{6,7},{7,6},{8,9},{9,8},{10,11... | collective-permute-start | bytes 196616 | tf_op jit(solution)/shard_map/ppermute | solution.py:464
  44.6 0.4 collective-permute-done.11.refs_4_
  45.1 1.4 %collective-permute-start.12 = (bf16[32,1024]{1,0:T(8,128)(2,1)S(1)}, bf16[32,1024]{1,0:T(8,128)(2,1)S(1)}, u32[]{:S(2)}, u32[]{:S(2)}) collective-permute-start(bf16[32,1024]{1,0:T(8,128)(2,1)S(1)} %collective-permute-done.11.refs_4_), channel_id=1, source_target_pairs={{0,1},{1,0},{2,3},{3,2},{4,5},{5,4},{6,7},{7,6},{8,9},{9,8},{10,11... | collective-permute-start | bytes 196616 | tf_op jit(solution)/shard_map/ppermute | solution.py:464
  46.4 0.1 collective-permute-done.8.refs_1_
  46.6 0.7 %collective-permute-done.14.refs_7_ = bf16[32,1024]{1,0:T(8,128)(2,1)S(1)} collective-permute-done((bf16[32,1024]{1,0:T(8,128)(2,1)S(1)}, bf16[32,1024]{1,0:T(8,128)(2,1)S(1)}, u32[]{:S(2)}, u32[]{:S(2)}) %collective-permute-start.14) | collective-permute-done | bytes 65568 | tf_op jit(solution)/shard_map/ppermute | solution.py:464
  47.3 2.1 %collective-permute-done.12.refs_5_ = bf16[32,1024]{1,0:T(8,128)(2,1)S(1)} collective-permute-done((bf16[32,1024]{1,0:T(8,128)(2,1)S(1)}, bf16[32,1024]{1,0:T(8,128)(2,1)S(1)}, u32[]{:S(2)}, u32[]{:S(2)}) %collective-permute-start.12) | collective-permute-done | bytes 65568 | tf_op jit(solution)/shard_map/ppermute | solution.py:464
  49.3 0.8 %place.1 = bf16[32,8192]{1,0:T(8,128)(2,1)} custom-call(bf16[32,1024]{1,0:T(8,128)(2,1)S(1)} %finish.1.refs_0_, bf16[32,1024]{1,0:T(8,128)(2,1)S(1)} %collective-permute-done.8.refs_1_, bf16[32,1024]{1,0:T(8,128)(2,1)S(1)} %collective-permute-done.9.refs_2_, bf16[32,1024]{1,0:T(8,128)(2,1)S(1)} %collective-permute-done.10.refs_3_, ...), custom_call_target="tpu_custom_call" | custom-call | bytes 1048576 | tf_op jit(solution)/shard_map/place/pallas_call | solution.py:438
  (16 shorter events, 0.0 us)
Async XLA Ops:
  0.0 4.8 %collective-permute-start = (s32[32]{0:T(128)}, s32[32]{0:T(128)S(1)}, u32[]{:S(2)}, u32[]{:S(2)}) collective-permute-start(s32[32]{0:T(128)} %ids_ref.1), channel_id=1, source_target_pairs={{0,8},{8,0},{1,9},{9,1},{2,10},{10,2},{3,11},{11,3},{4,12},{12,4},... | collective-permute-start | bytes 392 | tf_op jit(solution)/shard_map/ppermute | solution.py:473
  0.5 0.8 %copy-start = (bf16[32,1024]{1,0:T(8,128)(2,1)S(1)}, bf16[32,1024]{1,0:T(8,128)(2,1)}, u32[]{:S(2)}) copy-start(bf16[32,1024]{1,0:T(8,128)(2,1)} %q_ref.1) | copy-start | bytes 196612
  1.3 0.7 %copy-start.2 = (s32[32]{0:T(128)S(1)}, s32[32]{0:T(128)}, u32[]{:S(2)}) copy-start(s32[32]{0:T(128)} %len_ref.1) | copy-start | bytes 388
  1.9 2.9 %copy-start.1 = (s32[128]{0:T(128)S(1)}, s32[128]{0:T(128)}, u32[]{:S(2)}) copy-start(s32[128]{0:T(128)} %slot_ref.3) | copy-start | bytes 1540
  4.8 6.3 %copy-start.3 = (s32[32]{0:T(128)S(1)}, s32[32]{0:T(128)}, u32[]{:S(2)}) copy-start(s32[32]{0:T(128)} %ids_ref.1) | copy-start | bytes 388
  11.0 6.2 %collective-permute-start.1 = (bf16[2,8,64,1024]{3,2,1,0:T(8,128)(2,1)S(1)}, bf16[2,8,64,1024]{3,2,1,0:T(8,128)(2,1)S(1)}, u32[]{:S(2)}, u32[]{:S(2)}) collective-permute-start(bf16[2,8,64,1024]{3,2,1,0:T(8,128)(2,1)S(1)} %get-tuple-element.43), channel_id=1, source_target_pairs={{0,8},{8,0},{1,9},{9,1},{2,10},{10,2},{3,11},{11,3},{4,12},{12,4},... | collective-permute-start | bytes 6291464 | tf_op jit(solution)/shard_map/ppermute | solution.py:473
  18.3 6.8 %collective-permute-start.2 = (bf16[32,2176]{1,0:T(8,128)(2,1)S(1)}, bf16[32,2176]{1,0:T(8,128)(2,1)S(1)}, u32[]{:S(2)}, u32[]{:S(2)}) collective-permute-start(bf16[32,2176]{1,0:T(8,128)(2,1)S(1)} %get-tuple-element.48), channel_id=1, source_target_pairs={{0,1},{1,0},{2,3},{3,2},{4,5},{5,4},{6,7},{7,6},{8,9},{9,8},{10,11... | collective-permute-start | bytes 417800 | tf_op jit(solution)/shard_map/ppermute | solution.py:464
  22.0 10.5 %collective-permute-start.4 = (bf16[32,1152]{1,0:T(8,128)(2,1)S(1)}, bf16[32,1152]{1,0:T(8,128)(2,1)S(1)}, u32[]{:S(2)}, u32[]{:S(2)}) collective-permute-start(bf16[32,1152]{1,0:T(8,128)(2,1)S(1)} %get-tuple-element.54), channel_id=1, source_target_pairs={{0,2},{1,3},{2,0},{3,1},{4,6},{5,7},{6,4},{7,5},{8,10},{9,11},{10,... | collective-permute-start | bytes 221192 | tf_op jit(solution)/shard_map/ppermute | solution.py:467
  23.6 8.9 %collective-permute-start.5 = (bf16[32,1152]{1,0:T(8,128)(2,1)S(1)}, bf16[32,1152]{1,0:T(8,128)(2,1)S(1)}, u32[]{:S(2)}, u32[]{:S(2)}) collective-permute-start(bf16[32,1152]{1,0:T(8,128)(2,1)S(1)} %get-tuple-element.55), channel_id=1, source_target_pairs={{0,3},{1,2},{2,1},{3,0},{4,7},{5,6},{6,5},{7,4},{8,11},{9,10},{10,... | collective-permute-start | bytes 221192 | tf_op jit(solution)/shard_map/ppermute | solution.py:470
  25.6 9.1 %collective-permute-start.6 = (bf16[32,1152]{1,0:T(8,128)(2,1)S(1)}, bf16[32,1152]{1,0:T(8,128)(2,1)S(1)}, u32[]{:S(2)}, u32[]{:S(2)}) collective-permute-start(bf16[32,1152]{1,0:T(8,128)(2,1)S(1)} %add_block.3), channel_id=1, source_target_pairs={{0,6},{1,7},{2,4},{3,5},{4,2},{5,3},{6,0},{7,1},{8,14},{9,15},{10,... | collective-permute-start | bytes 221192 | tf_op jit(solution)/shard_map/ppermute | solution.py:467
  29.9 5.6 %collective-permute-start.7 = (bf16[32,1152]{1,0:T(8,128)(2,1)S(1)}, bf16[32,1152]{1,0:T(8,128)(2,1)S(1)}, u32[]{:S(2)}, u32[]{:S(2)}) collective-permute-start(bf16[32,1152]{1,0:T(8,128)(2,1)S(1)} %add_block.2.after_ref), channel_id=1, source_target_pairs={{0,4},{1,5},{2,6},{3,7},{4,0},{5,1},{6,2},{7,3},{8,12},{9,13},{10,... | collective-permute-start | bytes 221192 | tf_op jit(solution)/shard_map/ppermute | solution.py:467
  30.4 4.4 %collective-permute-start.3 = (bf16[32,1024]{1,0:T(8,128)(2,1)S(1)}, bf16[32,1024]{1,0:T(8,128)(2,1)S(1)}, u32[]{:S(2)}, u32[]{:S(2)}) collective-permute-start(bf16[32,1024]{1,0:T(8,128)(2,1)S(1)} %own_far_block.1), channel_id=1, source_target_pairs={{0,1},{1,0},{2,3},{3,2},{4,5},{5,4},{6,7},{7,6},{8,9},{9,8},{10,11... | collective-permute-start | bytes 196616 | tf_op jit(solution)/shard_map/ppermute | solution.py:464
  36.3 6.2 %collective-permute-start.13 = (bf16[32,1024]{1,0:T(8,128)(2,1)S(1)}, bf16[32,1024]{1,0:T(8,128)(2,1)S(1)}, u32[]{:S(2)}, u32[]{:S(2)}) collective-permute-start(bf16[32,1024]{1,0:T(8,128)(2,1)S(1)} %finish.1.refs_0_), channel_id=1, source_target_pairs={{0,6},{1,7},{2,4},{3,5},{4,2},{5,3},{6,0},{7,1},{8,14},{9,15},{10,... | collective-permute-start | bytes 196616 | tf_op jit(solution)/shard_map/ppermute | solution.py:467
  39.0 6.0 %collective-permute-start.11 = (bf16[32,1024]{1,0:T(8,128)(2,1)S(1)}, bf16[32,1024]{1,0:T(8,128)(2,1)S(1)}, u32[]{:S(2)}, u32[]{:S(2)}) collective-permute-start(bf16[32,1024]{1,0:T(8,128)(2,1)S(1)} %finish.1.refs_0_), channel_id=1, source_target_pairs={{0,4},{1,5},{2,6},{3,7},{4,0},{5,1},{6,2},{7,3},{8,12},{9,13},{10,... | collective-permute-start | bytes 196616 | tf_op jit(solution)/shard_map/ppermute | solution.py:467
  39.0 7.4 %collective-permute-start.10 = (bf16[32,1024]{1,0:T(8,128)(2,1)S(1)}, bf16[32,1024]{1,0:T(8,128)(2,1)S(1)}, u32[]{:S(2)}, u32[]{:S(2)}) collective-permute-start(bf16[32,1024]{1,0:T(8,128)(2,1)S(1)} %finish.1.refs_0_), channel_id=1, source_target_pairs={{0,3},{1,2},{2,1},{3,0},{4,7},{5,6},{6,5},{7,4},{8,11},{9,10},{10,... | collective-permute-start | bytes 196616 | tf_op jit(solution)/shard_map/ppermute | solution.py:470
  41.9 4.5 %collective-permute-start.9 = (bf16[32,1024]{1,0:T(8,128)(2,1)S(1)}, bf16[32,1024]{1,0:T(8,128)(2,1)S(1)}, u32[]{:S(2)}, u32[]{:S(2)}) collective-permute-start(bf16[32,1024]{1,0:T(8,128)(2,1)S(1)} %finish.1.refs_0_), channel_id=1, source_target_pairs={{0,2},{1,3},{2,0},{3,1},{4,6},{5,7},{6,4},{7,5},{8,10},{9,11},{10,... | collective-permute-start | bytes 196616 | tf_op jit(solution)/shard_map/ppermute | solution.py:467
  42.1 4.5 %collective-permute-start.8 = (bf16[32,1024]{1,0:T(8,128)(2,1)S(1)}, bf16[32,1024]{1,0:T(8,128)(2,1)S(1)}, u32[]{:S(2)}, u32[]{:S(2)}) collective-permute-start(bf16[32,1024]{1,0:T(8,128)(2,1)S(1)} %finish.1.refs_0_), channel_id=1, source_target_pairs={{0,1},{1,0},{2,3},{3,2},{4,5},{5,4},{6,7},{7,6},{8,9},{9,8},{10,11... | collective-permute-start | bytes 196616 | tf_op jit(solution)/shard_map/ppermute | solution.py:470
  42.5 4.7 %collective-permute-start.14 = (bf16[32,1024]{1,0:T(8,128)(2,1)S(1)}, bf16[32,1024]{1,0:T(8,128)(2,1)S(1)}, u32[]{:S(2)}, u32[]{:S(2)}) collective-permute-start(bf16[32,1024]{1,0:T(8,128)(2,1)S(1)} %collective-permute-done.13.refs_6_), channel_id=1, source_target_pairs={{0,1},{1,0},{2,3},{3,2},{4,5},{5,4},{6,7},{7,6},{8,9},{9,8},{10,11... | collective-permute-start | bytes 196616 | tf_op jit(solution)/shard_map/ppermute | solution.py:464
  45.1 4.3 %collective-permute-start.12 = (bf16[32,1024]{1,0:T(8,128)(2,1)S(1)}, bf16[32,1024]{1,0:T(8,128)(2,1)S(1)}, u32[]{:S(2)}, u32[]{:S(2)}) collective-permute-start(bf16[32,1024]{1,0:T(8,128)(2,1)S(1)} %collective-permute-done.11.refs_4_), channel_id=1, source_target_pairs={{0,1},{1,0},{2,3},{3,2},{4,5},{5,4},{6,7},{7,6},{8,9},{9,8},{10,11... | collective-permute-start | bytes 196616 | tf_op jit(solution)/shard_map/ppermute | solution.py:464

commit v5 on v4

--- a/solution.py
+++ b/solution.py
@@ -75,39 +75,43 @@
                     copy.start()
 
 
-def suffix_scores_kernel(
-    len_ref, q_ref, prefix_ref, suffix_ref, query_ref, tail_ref, keys_ref, suf, rowbuf, sem, sem_suf
+def prefix_scores_kernel(
+    q_ref, prefix_ref, suffix_ref, query_ref, scores_ref, peak_ref, vals_ref, suf_keys_ref, qbuf, keys, rowbuf, sem, sem_keys
 ):
     rows = q_ref.shape[0]
-    head_dim = prefix_ref.shape[3]
+    tokens, head_dim = keys.shape
     heads = q_ref.shape[1] // head_dim
-    span = suffix_ref.shape[3]
-    groups = sem_suf.shape[0]
-    size = rows // groups
-    copies = [
+    parts = sem_keys.shape[0]
+    size = tokens // parts
+    key_copies = [
         pltpu.make_async_copy(
-            suffix_ref.at[pl.ds(j * size, size), 0, 0], suf.at[pl.ds(j * size, size)], sem_suf.at[j]
+            prefix_ref.at[0, 0, pl.ds(j * size, size)], keys.at[pl.ds(j * size, size)], sem_keys.at[j]
         )
-        for j in range(groups)
+        for j in range(parts)
     ]
-    fetch = pltpu.make_async_copy(prefix_ref.at[0, 0], keys_ref, sem.at[0])
-    for c in copies + [fetch]:
+    fetch_q = pltpu.make_async_copy(q_ref, qbuf, sem.at[0])
+    fetch = [
+        pltpu.make_async_copy(suffix_ref.at[:, 0, 0], suf_keys_ref, sem.at[1]),
+        pltpu.make_async_copy(prefix_ref.at[0, 1], vals_ref, sem.at[2]),
+    ]
+    for c in [fetch_q] + key_copies + fetch:
         c.start()
+    fetch_q.wait()
     for h in range(heads):
-        rowbuf[pl.ds(h, rows, stride=heads), :] = q_ref[:, h * head_dim : (h + 1) * head_dim].astype(F32)
+        rowbuf[pl.ds(h, rows, stride=heads), :] = qbuf[:, h * head_dim : (h + 1) * head_dim].astype(F32)
     query = rowbuf[...].astype(BF16)
     query_ref[...] = query
-    lanes = lax.broadcasted_iota(jnp.int32, (heads, span), 1)
-    for j in range(groups):
-        copies[j].wait()
-        for i in range(j * size // 2, (j + 1) * size // 2):
-            keys = suf[2 * i : 2 * i + 2].reshape(2 * span, head_dim)
-            both = nt_dot(query[2 * heads * i : 2 * heads * (i + 1)], keys)
-            for a in range(2):
-                mine = both[a * heads : (a + 1) * heads, a * span : (a + 1) * span]
-                row = 2 * i + a
-                tail_ref[row * heads : (row + 1) * heads, :] = jnp.where(lanes < len_ref[row], mine, -1.0e30)
-    fetch.wait()
+    best = jnp.full(peak_ref.shape, -3.0e38, F32)
+    step = min(512, size)
+    for j in range(parts):
+        key_copies[j].wait()
+        for base in range(j * size, (j + 1) * size, step):
+            block = nt_dot(keys[base : base + step, :], query)
+            scores_ref[base : base + step, :] = block
+            best = jnp.maximum(best, jnp.max(block.reshape(step // 8, 8, block.shape[1]), axis=0))
+    peak_ref[...] = best
+    for c in fetch:
+        c.wait()
 
 
 def weight_copies(weight_ref, outs, spots, sem):
@@ -121,42 +125,55 @@
     return copies
 
 
-def prefix_scores_kernel(spots, ids_ref, slot_ref, query_ref, tail_ref, keys_ref, prefix_ref, suffix_ref, *rest):
-    pages_ref, weight_ref = rest[:2]
-    scores_ref, peak_ref, out_pages_ref, vals_ref, suf_vals_ref = rest[2:7]
-    w_refs = rest[7 : 7 + len(spots)]
-    seen, list_id, list_pos, sem, sem_page, sem_w = rest[7 + len(spots) :]
-    tokens = keys_ref.shape[0]
-    fetch = [
-        pltpu.make_async_copy(prefix_ref.at[0, 1], vals_ref, sem.at[0]),
-        pltpu.make_async_copy(suffix_ref.at[:, 0, 1], suf_vals_ref, sem.at[1]),
-    ] + weight_copies(weight_ref, w_refs, spots, sem_w)
+def suffix_scores_kernel(spots, ids_ref, slot_ref, query_ref, suf_keys_ref, vals_ref, peak_ref, *rest):
+    len_ref, suffix_ref, pages_ref, weight_ref = rest[:4]
+    tail_ref, high_ref, high_row_ref, vals_t_ref, out_pages_ref, suf_vals_ref = rest[4:10]
+    w_refs = rest[10 : 10 + len(spots)]
+    lens, seen, list_id, list_pos, sem, sem_page, sem_w = rest[10 + len(spots) :]
+    rows, span, head_dim = suf_keys_ref.shape
+    tokens = vals_ref.shape[0]
+    heads = query_ref.shape[0] // rows
+    fetch_len = pltpu.make_async_copy(len_ref, lens, sem.at[1])
+    fetch_len.start()
+    fetch = [pltpu.make_async_copy(suffix_ref.at[:, 0, 1], suf_vals_ref, sem.at[0])]
+    fetch += weight_copies(weight_ref, w_refs, spots, sem_w)
     distinct_list(ids_ref, slot_ref, seen, list_id, list_pos)
     outs = (out_pages_ref.at[0], out_pages_ref.at[1])
     page_copies(pages_ref, outs, list_pos, sem_page, False)
     for c in fetch:
         c.start()
     query = query_ref[...]
+    lanes = lax.broadcasted_iota(jnp.int32, (heads, span), 1)
+    fetch_len.wait()
+    for i in range(rows // 2):
+        keys = suf_keys_ref[2 * i : 2 * i + 2].reshape(2 * span, head_dim)
+        both = nt_dot(query[2 * heads * i : 2 * heads * (i + 1)], keys)
+        for a in range(2):
+            mine = both[a * heads : (a + 1) * heads, a * span : (a + 1) * span]
+            row = 2 * i + a
+            tail_ref[row * heads : (row + 1) * heads, :] = jnp.where(lanes < lens[row], mine, -1.0e30)
+    step = min(1024, tokens)
+    for base in range(0, tokens, step):
+        vals_t_ref[:, base : base + step] = vals_ref[base : base + step, :].astype(F32).T.astype(BF16)
     best = jnp.maximum(tail_ref[:, :128], tail_ref[:, 128:256])
-    for b in range(2, tail_ref.shape[1] // 128):
+    for b in range(2, span // 128):
         best = jnp.maximum(best, tail_ref[:, b * 128 : (b + 1) * 128])
-    for base in range(0, tokens, 256):
-        block = nt_dot(query, keys_ref[base : base + 256, :])
-        scores_ref[:, base : base + 256] = block
-        best = jnp.maximum(best, jnp.maximum(block[:, :128], block[:, 128:]))
-    peak_ref[...] = jnp.broadcast_to(jnp.max(best, axis=1, keepdims=True), peak_ref.shape)
+    across_rows = jnp.broadcast_to(jnp.max(peak_ref[...], axis=0, keepdims=True), (128, peak_ref.shape[1]))
+    high = jnp.maximum(across_rows.T, jnp.max(best, axis=1, keepdims=True))
+    high_ref[...] = high
+    high_row_ref[...] = high.T[:8]
     page_copies(pages_ref, outs, list_pos, sem_page, True)
     for c in fetch:
         c.wait()
 
 
-def values_kernel(spots, ids_ref, slot_ref, scores, tail, peak, vals_ref, suf_vals_ref, *rest):
+def values_kernel(spots, ids_ref, slot_ref, scores, tail, peak, peak_row, vals_t_ref, suf_vals_ref, *rest):
     pages_ref, weight_ref, residual_ref = rest[:3]
     att_ref, shrink_ref, expand_ref, row_slot_ref, slot_mine_ref, res_ref = rest[3:9]
     w_refs = rest[9 : 9 + len(spots)]
-    rowbuf, total, acc, seen, list_id, list_pos, sem, sem_page, sem_w = rest[9 + len(spots) :]
-    rows, head_dim, span = suf_vals_ref.shape[0], vals_ref.shape[1], suf_vals_ref.shape[1]
-    tokens = vals_ref.shape[0]
+    rowbuf, total, acc, total_row, acc_t, seen, list_id, list_pos, sem, sem_page, sem_w = rest[9 + len(spots) :]
+    rows, span, head_dim = suf_vals_ref.shape
+    tokens = vals_t_ref.shape[1]
     heads = att_ref.shape[1] // head_dim
     width = res_ref.shape[1]
     me = lax.axis_index("tensor")
@@ -186,23 +203,23 @@
     row_slot_ref[...] = row_slot
     slot_mine_ref[...] = slot_mine
 
-    total[...] = jnp.zeros(total.shape, F32)
-    acc[...] = jnp.zeros(acc.shape, F32)
+    total_row[...] = jnp.zeros(total_row.shape, F32)
+    acc_t[...] = jnp.zeros(acc_t.shape, F32)
+    n_q = acc_t.shape[1]
     chunk = min(2048, tokens)
 
     @pl.loop(0, tokens // chunk)
     def _(i):
         base = pl.multiple_of(i * chunk, chunk)
-        high = peak[...]
-        summed = total[...]
-        parts = []
-        for b in range(chunk // 128):
-            e = jnp.exp2((scores[:, pl.ds(base + b * 128, 128)] - high) * scale2)
-            summed = summed + e
-            parts.append(e.astype(BF16))
-        total[...] = summed
-        acc[...] += nn_dot(jnp.concatenate(parts, axis=1), vals_ref[pl.ds(base, chunk), :])
-
+        high_row = peak_row[...]
+        block = scores[pl.ds(base, chunk), :].reshape(chunk // 8, 8, n_q)
+        e = jnp.exp2((block - high_row[None]) * scale2)
+        total_row[...] += jnp.sum(e, axis=0)
+        weights = e.reshape(chunk, n_q).astype(BF16)
+        acc_t[...] += nn_dot(vals_t_ref[:, pl.ds(base, chunk)], weights)
+
+    across_rows = jnp.broadcast_to(jnp.sum(total_row[...], axis=0, keepdims=True), (128, n_q))
+    acc[...] = acc_t[...].T
     zeros = jnp.zeros((heads, span), F32)
     for i in range(rows // 2):
         lo = 2 * heads * i
@@ -211,7 +228,7 @@
         part_sum = e[:, :128]
         for b in range(1, span // 128):
             part_sum = part_sum + e[:, b * 128 : (b + 1) * 128]
-        total[lo : lo + 2 * heads, :] += part_sum
+        total[lo : lo + 2 * heads, :] = part_sum
         diag = jnp.concatenate(
             [
                 jnp.concatenate([e[:heads], zeros], axis=1),
@@ -222,7 +239,7 @@
         vals = suf_vals_ref[2 * i : 2 * i + 2].reshape(2 * span, head_dim)
         acc[lo : lo + 2 * heads, :] += nn_dot(diag, vals)
 
-    norm = jnp.sum(total[...], axis=1, keepdims=True)
+    norm = across_rows.T + jnp.sum(total[...], axis=1, keepdims=True)
     rowbuf[...] = acc[...] / norm
     for h in range(heads):
         att_ref[:, h * head_dim : (h + 1) * head_dim] = rowbuf[pl.ds(h, rows, stride=heads), :].astype(BF16)
@@ -256,47 +273,56 @@
     span = suffix_kv.shape[3]
     prefix_kv, suffix_kv, out_weight = in_hbm(prefix_kv), in_hbm(suffix_kv), in_hbm(out_weight)
     pages, residual = in_hbm(pages), in_hbm(residual)
-    query, tail, keys = kernel_call(
-        suffix_scores_kernel,
-        "suffix_scores",
-        [pltpu.VMEM((n_q, head_dim), BF16), pltpu.VMEM((n_q, span), F32), pltpu.VMEM((tokens, head_dim), BF16)],
-        [SMEM, VMEM, ANY, ANY],
+    query, scores, peak, vals, suf_keys = kernel_call(
+        prefix_scores_kernel,
+        "prefix_scores",
         [
+            pltpu.VMEM((n_q, head_dim), BF16),
+            pltpu.VMEM((tokens, n_q), F32),
+            pltpu.VMEM((8, n_q), F32),
+            pltpu.VMEM((tokens, head_dim), BF16),
             pltpu.VMEM((rows, span, head_dim), BF16),
+        ],
+        [ANY, ANY, ANY],
+        [
+            pltpu.VMEM(queries.shape, BF16),
+            pltpu.VMEM((tokens, head_dim), BF16),
             pltpu.VMEM((n_q, head_dim), F32),
-            pltpu.SemaphoreType.DMA((1,)),
+            pltpu.SemaphoreType.DMA((3,)),
             pltpu.SemaphoreType.DMA((4,)),
         ],
-        [suffix_len, queries, prefix_kv, suffix_kv],
-        6,
-        1 << 30,
+        [in_hbm(queries), prefix_kv, suffix_kv],
+        8,
+        2 * n_q * tokens * head_dim,
         6 * MIB,
     )
     far = list(range(n_z - 1, -1, -1))
     early = [(0, k) for k in far[: n_z // 2]]
     late = [(1, k) for k in far] + [(0, k) for k in far[n_z // 2 :]]
-    scores, peak, out_pages, vals, suf_vals, *early_w = kernel_call(
-        functools.partial(prefix_scores_kernel, early),
-        "prefix_scores",
+    tail, high, high_row, vals_t, out_pages, suf_vals, *early_w = kernel_call(
+        functools.partial(suffix_scores_kernel, early),
+        "suffix_scores",
         [
-            pltpu.VMEM((n_q, tokens), F32),
+            pltpu.VMEM((n_q, span), F32),
             pltpu.VMEM((n_q, 128), F32),
+            pltpu.VMEM((8, n_q), F32),
+            pltpu.VMEM((head_dim, tokens), BF16),
             pltpu.VMEM((2, DISTINCT) + pages.shape[2:], BF16),
-            pltpu.VMEM((tokens, head_dim), BF16),
             pltpu.VMEM((rows, span, head_dim), BF16),
         ]
         + [pltpu.VMEM((in_rows, width), BF16)] * len(early),
-        [SMEM, SMEM, VMEM, VMEM, VMEM, ANY, ANY, ANY, ANY],
-        list_scratch(pool_slot)
+        [SMEM, SMEM, VMEM, VMEM, VMEM, VMEM, ANY, ANY, ANY, ANY],
+        [pltpu.SMEM((rows,), jnp.int32)]
+        + list_scratch(pool_slot)
         + [
             pltpu.SemaphoreType.DMA((2,)),
             pltpu.SemaphoreType.DMA((2, DISTINCT)),
             pltpu.SemaphoreType.DMA((len(early),)),
         ],
-        [other_ids, pool_slot, query, tail, keys, prefix_kv, suffix_kv, pages, out_weight],
-        4,
-        2 * n_q * tokens * head_dim,
-        9 * MIB,
+        [other_ids, pool_slot, query, suf_keys, vals, peak, in_hbm(suffix_len), suffix_kv, pages, out_weight],
+        8,
+        1 << 29,
+        7 * MIB,
     )
     other_pages = across(out_pages)
     attended, own_shrink, own_expand, row_slot, slot_mine, res, *late_w = kernel_call(
@@ -311,11 +337,13 @@
             pltpu.VMEM((rows, width), BF16),
         ]
         + [pltpu.VMEM((in_rows, width), BF16)] * len(late),
-        [SMEM, SMEM, VMEM, VMEM, VMEM, VMEM, VMEM, ANY, ANY, ANY],
+        [SMEM, SMEM, VMEM, VMEM, VMEM, VMEM, VMEM, VMEM, ANY, ANY, ANY],
         [
             pltpu.VMEM((n_q, head_dim), F32),
             pltpu.VMEM((n_q, 128), F32),
             pltpu.VMEM((n_q, head_dim), F32),
+            pltpu.VMEM((8, n_q), F32),
+            pltpu.VMEM((head_dim, n_q), F32),
         ]
         + list_scratch(pool_slot)
         + [
@@ -323,8 +351,8 @@
             pltpu.SemaphoreType.DMA((2, DISTINCT)),
             pltpu.SemaphoreType.DMA((len(late),)),
         ],
-        [ids, pool_slot, scores, tail, peak, vals, suf_vals, pages, out_weight, residual],
-        6,
+        [ids, pool_slot, scores, tail, high, high_row, vals_t, suf_vals, pages, out_weight, residual],
+        8,
         2 * n_q * tokens * head_dim,
         14 * MIB,
     )

time: 50.4 us -> 47.3 us (0.938)
  Pallas kernels: 20.1 us -> 18.4 us
  local copies, waits for them, and re-layouts: 1.5 us -> 0.01 us
    pallas_call x3, Pallas kernels: 15.1 us -> 13.4 us  [kernel_call(): pl.pallas_call(kernel, out_shape=out_shape, in_specs=specs, out_specs=[VM...]
    unnamed x8 -> x4, local copies, waits for them, and re-layouts: 1.5 us -> 0.01 us
  transfers between devices with their start and end apart: 15 -> 15, of which waited for: 7 -> 8; matrix products, arithmetic and copies ran while one was open for 0% -> 0% of each run, Pallas kernels for 22% -> 24%
where the time goes in v5:
time: 47.3 us; the launch traced here: 47.1 us
  starting transfers between devices  20.5 us (43%)
  Pallas kernels  18.4 us (39%)
  waiting for transfers between devices  8.13 us (17%)
    pallas_call x3, Pallas kernels, kernel_call(): pl.pallas_call(kernel, out_shape=out_shape, in_specs=specs, out_specs=[VM...  13.4 us
    ppermute x6, starting transfers between devices, along_z(): return lax.ppermute(x, 'tensor', [(t, t ^ 2 * k) for t in range(n_tensor)])  8.24 us
    ppermute x4, starting transfers between devices, along_y(): return lax.ppermute(x, 'tensor', [(t, t ^ 1) for t in range(n_tensor)])  8.13 us
    ppermute x4, waiting for transfers between devices, along_y(): return lax.ppermute(x, 'tensor', [(t, t ^ 1) for t in range(n_tensor)])  6.5 us
    pallas_call x6, Pallas kernels, small_call(): pl.pallas_call(kernel, out_shape=out_shape, in_specs=[VMEM] * len(operand...  4.1 us
    ppermute x3, starting transfers between devices, along_both(): lax.ppermute(x, 'tensor', [(t, t ^ 2 * k ^ 1) for t in range(n_tensor)])  3.55 us
    ppermute x6, waiting for transfers between devices, along_z(): return lax.ppermute(x, 'tensor', [(t, t ^ 2 * k) for t in range(n_tensor)])  1.45 us
  transfers between devices with their start and end apart: 15, of which 8 were waited for; matrix products, arithmetic and copies ran while one was open for 0% of the time, Pallas kernels for 24%

profile of v5, /device:TPU:0, one launch (start us, length us, event | category | flops | bytes accessed | tf_op | source)
XLA Modules:
  0.0 47.1 jit_solution(2308628627118043157)
XLA Ops:
  0.0 0.5 collective-permute-start
  0.5 3.0 %prefix_scores.1 = (bf16[256,128]{1,0:T(8,128)(2,1)S(1)}, f32[8192,256]{1,0:T(8,128)S(1)}, f32[8,256]{1,0:T(8,128)S(1)}, bf16[8192,128]{1,0:T(8,128)(2,1)S(1)}, bf16[32,256,128]{2,1,0:T(8,128)(2,1)S(1)}) custom-call(bf16[32,1024]{1,0:T(8,128)(2,1)} %q_ref.1, bf16[1,2,8192,128]{3,2,1,0:T(8,128)(2,1)} %prefix_ref.1, bf16[32,1,2,256,128]{4,3,2,1,0:T(8,128)(2,1)} %rest_1_.2), custom_call_target="tpu_custom_call" | custom-call | flops 536870912 | bytes 6291456 | tf_op jit(solution)/shard_map/prefix_scores/pallas_call | solution.py:252
  3.4 0.0 copy-start.1
  3.5 4.3 %suffix_scores.1 = (f32[256,256]{1,0:T(8,128)S(1)}, f32[256,128]{1,0:T(8,128)S(1)}, f32[8,256]{1,0:T(8,128)S(1)}, bf16[128,8192]{1,0:T(8,128)(2,1)S(1)}, bf16[2,...) custom-call(s32[32]{0:T(128)S(1)} %collective-permute-done.ids_ref, ...), custom_call_target="tpu_custom_call" | custom-call | flops 536870912 | bytes 7340032 | tf_op jit(solution)/shard_map/suffix_scores/pallas_call | solution.py:252
  7.8 0.1 collective-permute-start.1
  7.9 6.1 %values.1 = (bf16[32,1024]{1,0:T(8,128)(2,1)S(1)}, bf16[8,64,1024]{2,1,0:T(8,128)(2,1)S(1)}, bf16[8,64,1024]{2,1,0:T(8,128)(2,1)S(1)}, s32[32,128]{1,0:T(8,128)S...) custom-call(s32[32]{0:T(128)S(1)} %copy-done.1, ...), custom_call_target="tpu_custom_call" | custom-call | flops 536870912 | bytes 14680064 | tf_op jit(solution)/shard_map/values/pallas_call | solution.py:252
  14.1 1.1 %far_blocks.1 = (bf16[32,2176]{1,0:T(8,128)(2,1)S(1)}, f32[32,128]{1,0:T(8,128)S(1)}) custom-call(bf16[32,1024]{1,0:T(8,128)(2,1)S(1)} %get-tuple-element.44.att_ref.refs_0_, s32[32,128]{1,0:T(8,128)S(1)} %get-tuple-element.46.row_slot_ref.refs_2_, s32[8,128]{1,0:T(8,128)S(1)} %get-tuple-element.47.slot_mine_ref.refs_3_, ...), custom_call_target="tpu_custom_call" | custom-call | flops 134217728 | bytes 2097152 | tf_op jit(solution)/shard_map/far_blocks/pallas_call | solution.py:364
  15.2 3.0 %collective-permute-start.2 = (bf16[32,2176]{1,0:T(8,128)(2,1)S(1)}, bf16[32,2176]{1,0:T(8,128)(2,1)S(1)}, u32[]{:S(2)}, u32[]{:S(2)}) collective-permute-start(bf16[32,2176]{1,0:T(8,128)(2,1)S(1)} %get-tuple-element.54), channel_id=1, source_target_pairs={{0,1},{1,0},{2,3},{3,2},{4,5},{5,4},{6,7},{7,6},{8,9},{9,8},{10,11... | collective-permute-start | bytes 417800 | tf_op jit(solution)/shard_map/ppermute | solution.py:492
  18.2 0.8 %near_blocks.1 = (bf16[32,1152]{1,0:T(8,128)(2,1)S(1)}, bf16[32,1152]{1,0:T(8,128)(2,1)S(1)}) custom-call(bf16[32,1024]{1,0:T(8,128)(2,1)S(1)} %get-tuple-element.44.att_ref.refs_0_, bf16[1024,1024]{1,0:T(8,128)(2,1)S(1)} %get-tuple-element.58.w_ref, bf16[1024,1024]{1,0:T(8,128)(2,1)S(1)} %get-tuple-element.59.cross_w_ref, ...), custom_call_target="tpu_custom_call" | custom-call | flops 134217728 | bytes 2097152 | tf_op jit(solution)/shard_map/near_blocks/pallas_call | solution.py:364
  19.1 1.6 %collective-permute-start.4 = (bf16[32,1152]{1,0:T(8,128)(2,1)S(1)}, bf16[32,1152]{1,0:T(8,128)(2,1)S(1)}, u32[]{:S(2)}, u32[]{:S(2)}) collective-permute-start(bf16[32,1152]{1,0:T(8,128)(2,1)S(1)} %get-tuple-element.60), channel_id=1, source_target_pairs={{0,2},{1,3},{2,0},{3,1},{4,6},{5,7},{6,4},{7,5},{8,10},{9,11},{10,... | collective-permute-start | bytes 221192 | tf_op jit(solution)/shard_map/ppermute | solution.py:495
  20.7 1.4 %collective-permute-done.2.from_ref.refs_7_ = bf16[32,2176]{1,0:T(8,128)(2,1)S(1)} collective-permute-done((bf16[32,2176]{1,0:T(8,128)(2,1)S(1)}, bf16[32,2176]{1,0:T(8,128)(2,1)S(1)}, u32[]{:S(2)}, u32[]{:S(2)}) %collective-permute-start.2) | collective-permute-done | bytes 139296 | tf_op jit(solution)/shard_map/ppermute | solution.py:492
  22.0 0.5 add_block.3
  22.5 3.8 %collective-permute-start.6 = (bf16[32,1152]{1,0:T(8,128)(2,1)S(1)}, bf16[32,1152]{1,0:T(8,128)(2,1)S(1)}, u32[]{:S(2)}, u32[]{:S(2)}) collective-permute-start(bf16[32,1152]{1,0:T(8,128)(2,1)S(1)} %add_block.3), channel_id=1, source_target_pairs={{0,6},{1,7},{2,4},{3,5},{4,2},{5,3},{6,0},{7,1},{8,14},{9,15},{10,... | collective-permute-start | bytes 221192 | tf_op jit(solution)/shard_map/ppermute | solution.py:495
  26.3 0.5 add_block.2.after_ref
  26.8 0.0 collective-permute-start.7
  26.8 0.5 own_far_block.1
  27.3 2.2 %collective-permute-start.3 = (bf16[32,1024]{1,0:T(8,128)(2,1)S(1)}, bf16[32,1024]{1,0:T(8,128)(2,1)S(1)}, u32[]{:S(2)}, u32[]{:S(2)}) collective-permute-start(bf16[32,1024]{1,0:T(8,128)(2,1)S(1)} %own_far_block.1), channel_id=1, source_target_pairs={{0,1},{1,0},{2,3},{3,2},{4,5},{5,4},{6,7},{7,6},{8,9},{9,8},{10,11... | collective-permute-start | bytes 196616 | tf_op jit(solution)/shard_map/ppermute | solution.py:492
  29.5 2.2 %collective-permute-done.3.refs_8_ = bf16[32,1024]{1,0:T(8,128)(2,1)S(1)} collective-permute-done((bf16[32,1024]{1,0:T(8,128)(2,1)S(1)}, bf16[32,1024]{1,0:T(8,128)(2,1)S(1)}, u32[]{:S(2)}, u32[]{:S(2)}) %collective-permute-start.3) | collective-permute-done | bytes 65568 | tf_op jit(solution)/shard_map/ppermute | solution.py:492
  31.8 0.6 %collective-permute-done.7.refs_13_ = bf16[32,1152]{1,0:T(8,128)(2,1)S(1)} collective-permute-done((bf16[32,1152]{1,0:T(8,128)(2,1)S(1)}, bf16[32,1152]{1,0:T(8,128)(2,1)S(1)}, u32[]{:S(2)}, u32[]{:S(2)}) %collective-permute-start.7) | collective-permute-done | bytes 73760 | tf_op jit(solution)/shard_map/ppermute | solution.py:495
  32.4 0.8 %finish.1.refs_0_ = bf16[32,1024]{1,0:T(8,128)(2,1)S(1)} custom-call(bf16[32,1024]{1,0:T(8,128)(2,1)S(1)} %get-tuple-element.44.att_ref.refs_0_, bf16[1024,1024]{1,0:T(8,128)(2,1)S(1)} %get-tuple-element.45.refs_1_, s32[32,128]{1,0:T(8,128)S(1)} %get-tuple-element.46.row_slot_ref.refs_2_, s32[8,128]{1,0:T(8,128)S(1)} %get-tuple-element.47.slot_mine_ref.refs_3_, ...), custom_call_target="tpu_custom_call" | custom-call | flops 134217728 | bytes 2097152 | tf_op jit(solution)/shard_map/finish/pallas_call | solution.py:364
  33.2 2.7 %collective-permute-start.13 = (bf16[32,1024]{1,0:T(8,128)(2,1)S(1)}, bf16[32,1024]{1,0:T(8,128)(2,1)S(1)}, u32[]{:S(2)}, u32[]{:S(2)}) collective-permute-start(bf16[32,1024]{1,0:T(8,128)(2,1)S(1)} %finish.1.refs_0_), channel_id=1, source_target_pairs={{0,6},{1,7},{2,4},{3,5},{4,2},{5,3},{6,0},{7,1},{8,14},{9,15},{10,... | collective-permute-start | bytes 196616 | tf_op jit(solution)/shard_map/ppermute | solution.py:495
  35.8 3.1 %collective-permute-start.10 = (bf16[32,1024]{1,0:T(8,128)(2,1)S(1)}, bf16[32,1024]{1,0:T(8,128)(2,1)S(1)}, u32[]{:S(2)}, u32[]{:S(2)}) collective-permute-start(bf16[32,1024]{1,0:T(8,128)(2,1)S(1)} %finish.1.refs_0_), channel_id=1, source_target_pairs={{0,3},{1,2},{2,1},{3,0},{4,7},{5,6},{6,5},{7,4},{8,11},{9,10},{10,... | collective-permute-start | bytes 196616 | tf_op jit(solution)/shard_map/ppermute | solution.py:498
  38.9 0.1 collective-permute-start.9
  39.1 0.4 collective-permute-start.8
  39.5 0.6 %collective-permute-done.13.refs_6_ = bf16[32,1024]{1,0:T(8,128)(2,1)S(1)} collective-permute-done((bf16[32,1024]{1,0:T(8,128)(2,1)S(1)}, bf16[32,1024]{1,0:T(8,128)(2,1)S(1)}, u32[]{:S(2)}, u32[]{:S(2)}) %collective-permute-start.13) | collective-permute-done | bytes 65568 | tf_op jit(solution)/shard_map/ppermute | solution.py:495
  40.1 1.9 %collective-permute-start.14 = (bf16[32,1024]{1,0:T(8,128)(2,1)S(1)}, bf16[32,1024]{1,0:T(8,128)(2,1)S(1)}, u32[]{:S(2)}, u32[]{:S(2)}) collective-permute-start(bf16[32,1024]{1,0:T(8,128)(2,1)S(1)} %collective-permute-done.13.refs_6_), channel_id=1, source_target_pairs={{0,1},{1,0},{2,3},{3,2},{4,5},{5,4},{6,7},{7,6},{8,9},{9,8},{10,11... | collective-permute-start | bytes 196616 | tf_op jit(solution)/shard_map/ppermute | solution.py:492
  42.0 1.0 %collective-permute-start.12 = (bf16[32,1024]{1,0:T(8,128)(2,1)S(1)}, bf16[32,1024]{1,0:T(8,128)(2,1)S(1)}, u32[]{:S(2)}, u32[]{:S(2)}) collective-permute-start(bf16[32,1024]{1,0:T(8,128)(2,1)S(1)} %collective-permute-done.11.refs_4_), channel_id=1, source_target_pairs={{0,1},{1,0},{2,3},{3,2},{4,5},{5,4},{6,7},{7,6},{8,9},{9,8},{10,11... | collective-permute-start | bytes 196616 | tf_op jit(solution)/shard_map/ppermute | solution.py:492
  43.0 0.2 collective-permute-done.9.refs_2_
  43.2 0.2 collective-permute-done.8.refs_1_
  43.4 1.1 %collective-permute-done.14.refs_7_ = bf16[32,1024]{1,0:T(8,128)(2,1)S(1)} collective-permute-done((bf16[32,1024]{1,0:T(8,128)(2,1)S(1)}, bf16[32,1024]{1,0:T(8,128)(2,1)S(1)}, u32[]{:S(2)}, u32[]{:S(2)}) %collective-permute-start.14) | collective-permute-done | bytes 65568 | tf_op jit(solution)/shard_map/ppermute | solution.py:492
  44.5 1.8 %collective-permute-done.12.refs_5_ = bf16[32,1024]{1,0:T(8,128)(2,1)S(1)} collective-permute-done((bf16[32,1024]{1,0:T(8,128)(2,1)S(1)}, bf16[32,1024]{1,0:T(8,128)(2,1)S(1)}, u32[]{:S(2)}, u32[]{:S(2)}) %collective-permute-start.12) | collective-permute-done | bytes 65568 | tf_op jit(solution)/shard_map/ppermute | solution.py:492
  46.3 0.8 %place.1 = bf16[32,8192]{1,0:T(8,128)(2,1)} custom-call(bf16[32,1024]{1,0:T(8,128)(2,1)S(1)} %finish.1.refs_0_, bf16[32,1024]{1,0:T(8,128)(2,1)S(1)} %collective-permute-done.8.refs_1_, bf16[32,1024]{1,0:T(8,128)(2,1)S(1)} %collective-permute-done.9.refs_2_, bf16[32,1024]{1,0:T(8,128)(2,1)S(1)} %collective-permute-done.10.refs_3_, ...), custom_call_target="tpu_custom_call" | custom-call | bytes 1048576 | tf_op jit(solution)/shard_map/place/pallas_call | solution.py:466
  (12 shorter events, 0.0 us)
Async XLA Ops:
  0.0 3.4 %copy-start = (s32[128]{0:T(128)S(1)}, s32[128]{0:T(128)}, u32[]{:S(2)}) copy-start(s32[128]{0:T(128)} %slot_ref.3) | copy-start | bytes 1540
  0.0 3.4 %collective-permute-start = (s32[32]{0:T(128)}, s32[32]{0:T(128)S(1)}, u32[]{:S(2)}, u32[]{:S(2)}) collective-permute-start(s32[32]{0:T(128)} %ids_ref.1), channel_id=1, source_target_pairs={{0,8},{8,0},{1,9},{9,1},{2,10},{10,2},{3,11},{11,3},{4,12},{12,4},... | collective-permute-start | bytes 392 | tf_op jit(solution)/shard_map/ppermute | solution.py:501
  3.4 4.5 %copy-start.1 = (s32[32]{0:T(128)S(1)}, s32[32]{0:T(128)}, u32[]{:S(2)}) copy-start(s32[32]{0:T(128)} %ids_ref.1) | copy-start | bytes 388
  7.8 6.3 %collective-permute-start.1 = (bf16[2,8,64,1024]{3,2,1,0:T(8,128)(2,1)S(1)}, bf16[2,8,64,1024]{3,2,1,0:T(8,128)(2,1)S(1)}, u32[]{:S(2)}, u32[]{:S(2)}) collective-permute-start(bf16[2,8,64,1024]{3,2,1,0:T(8,128)(2,1)S(1)} %get-tuple-element.49), channel_id=1, source_target_pairs={{0,8},{8,0},{1,9},{9,1},{2,10},{10,2},{3,11},{11,3},{4,12},{12,4},... | collective-permute-start | bytes 6291464 | tf_op jit(solution)/shard_map/ppermute | solution.py:501
  15.2 6.8 %collective-permute-start.2 = (bf16[32,2176]{1,0:T(8,128)(2,1)S(1)}, bf16[32,2176]{1,0:T(8,128)(2,1)S(1)}, u32[]{:S(2)}, u32[]{:S(2)}) collective-permute-start(bf16[32,2176]{1,0:T(8,128)(2,1)S(1)} %get-tuple-element.54), channel_id=1, source_target_pairs={{0,1},{1,0},{2,3},{3,2},{4,5},{5,4},{6,7},{7,6},{8,9},{9,8},{10,11... | collective-permute-start | bytes 417800 | tf_op jit(solution)/shard_map/ppermute | solution.py:492
  19.1 10.5 %collective-permute-start.4 = (bf16[32,1152]{1,0:T(8,128)(2,1)S(1)}, bf16[32,1152]{1,0:T(8,128)(2,1)S(1)}, u32[]{:S(2)}, u32[]{:S(2)}) collective-permute-start(bf16[32,1152]{1,0:T(8,128)(2,1)S(1)} %get-tuple-element.60), channel_id=1, source_target_pairs={{0,2},{1,3},{2,0},{3,1},{4,6},{5,7},{6,4},{7,5},{8,10},{9,11},{10,... | collective-permute-start | bytes 221192 | tf_op jit(solution)/shard_map/ppermute | solution.py:495
  20.7 8.9 %collective-permute-start.5 = (bf16[32,1152]{1,0:T(8,128)(2,1)S(1)}, bf16[32,1152]{1,0:T(8,128)(2,1)S(1)}, u32[]{:S(2)}, u32[]{:S(2)}) collective-permute-start(bf16[32,1152]{1,0:T(8,128)(2,1)S(1)} %get-tuple-element.61), channel_id=1, source_target_pairs={{0,3},{1,2},{2,1},{3,0},{4,7},{5,6},{6,5},{7,4},{8,11},{9,10},{10,... | collective-permute-start | bytes 221192 | tf_op jit(solution)/shard_map/ppermute | solution.py:498
  22.5 9.2 %collective-permute-start.6 = (bf16[32,1152]{1,0:T(8,128)(2,1)S(1)}, bf16[32,1152]{1,0:T(8,128)(2,1)S(1)}, u32[]{:S(2)}, u32[]{:S(2)}) collective-permute-start(bf16[32,1152]{1,0:T(8,128)(2,1)S(1)} %add_block.3), channel_id=1, source_target_pairs={{0,6},{1,7},{2,4},{3,5},{4,2},{5,3},{6,0},{7,1},{8,14},{9,15},{10,... | collective-permute-start | bytes 221192 | tf_op jit(solution)/shard_map/ppermute | solution.py:495
  26.8 5.6 %collective-permute-start.7 = (bf16[32,1152]{1,0:T(8,128)(2,1)S(1)}, bf16[32,1152]{1,0:T(8,128)(2,1)S(1)}, u32[]{:S(2)}, u32[]{:S(2)}) collective-permute-start(bf16[32,1152]{1,0:T(8,128)(2,1)S(1)} %add_block.2.after_ref), channel_id=1, source_target_pairs={{0,4},{1,5},{2,6},{3,7},{4,0},{5,1},{6,2},{7,3},{8,12},{9,13},{10,... | collective-permute-start | bytes 221192 | tf_op jit(solution)/shard_map/ppermute | solution.py:495
  27.3 4.5 %collective-permute-start.3 = (bf16[32,1024]{1,0:T(8,128)(2,1)S(1)}, bf16[32,1024]{1,0:T(8,128)(2,1)S(1)}, u32[]{:S(2)}, u32[]{:S(2)}) collective-permute-start(bf16[32,1024]{1,0:T(8,128)(2,1)S(1)} %own_far_block.1), channel_id=1, source_target_pairs={{0,1},{1,0},{2,3},{3,2},{4,5},{5,4},{6,7},{7,6},{8,9},{9,8},{10,11... | collective-permute-start | bytes 196616 | tf_op jit(solution)/shard_map/ppermute | solution.py:492
  33.2 6.9 %collective-permute-start.13 = (bf16[32,1024]{1,0:T(8,128)(2,1)S(1)}, bf16[32,1024]{1,0:T(8,128)(2,1)S(1)}, u32[]{:S(2)}, u32[]{:S(2)}) collective-permute-start(bf16[32,1024]{1,0:T(8,128)(2,1)S(1)} %finish.1.refs_0_), channel_id=1, source_target_pairs={{0,6},{1,7},{2,4},{3,5},{4,2},{5,3},{6,0},{7,1},{8,14},{9,15},{10,... | collective-permute-start | bytes 196616 | tf_op jit(solution)/shard_map/ppermute | solution.py:495
  35.8 6.2 %collective-permute-start.11 = (bf16[32,1024]{1,0:T(8,128)(2,1)S(1)}, bf16[32,1024]{1,0:T(8,128)(2,1)S(1)}, u32[]{:S(2)}, u32[]{:S(2)}) collective-permute-start(bf16[32,1024]{1,0:T(8,128)(2,1)S(1)} %finish.1.refs_0_), channel_id=1, source_target_pairs={{0,4},{1,5},{2,6},{3,7},{4,0},{5,1},{6,2},{7,3},{8,12},{9,13},{10,... | collective-permute-start | bytes 196616 | tf_op jit(solution)/shard_map/ppermute | solution.py:495
  35.8 7.1 %collective-permute-start.10 = (bf16[32,1024]{1,0:T(8,128)(2,1)S(1)}, bf16[32,1024]{1,0:T(8,128)(2,1)S(1)}, u32[]{:S(2)}, u32[]{:S(2)}) collective-permute-start(bf16[32,1024]{1,0:T(8,128)(2,1)S(1)} %finish.1.refs_0_), channel_id=1, source_target_pairs={{0,3},{1,2},{2,1},{3,0},{4,7},{5,6},{6,5},{7,4},{8,11},{9,10},{10,... | collective-permute-start | bytes 196616 | tf_op jit(solution)/shard_map/ppermute | solution.py:498
  38.9 4.3 %collective-permute-start.9 = (bf16[32,1024]{1,0:T(8,128)(2,1)S(1)}, bf16[32,1024]{1,0:T(8,128)(2,1)S(1)}, u32[]{:S(2)}, u32[]{:S(2)}) collective-permute-start(bf16[32,1024]{1,0:T(8,128)(2,1)S(1)} %finish.1.refs_0_), channel_id=1, source_target_pairs={{0,2},{1,3},{2,0},{3,1},{4,6},{5,7},{6,4},{7,5},{8,10},{9,11},{10,... | collective-permute-start | bytes 196616 | tf_op jit(solution)/shard_map/ppermute | solution.py:495
  39.1 4.3 %collective-permute-start.8 = (bf16[32,1024]{1,0:T(8,128)(2,1)S(1)}, bf16[32,1024]{1,0:T(8,128)(2,1)S(1)}, u32[]{:S(2)}, u32[]{:S(2)}) collective-permute-start(bf16[32,1024]{1,0:T(8,128)(2,1)S(1)} %finish.1.refs_0_), channel_id=1, source_target_pairs={{0,1},{1,0},{2,3},{3,2},{4,5},{5,4},{6,7},{7,6},{8,9},{9,8},{10,11... | collective-permute-start | bytes 196616 | tf_op jit(solution)/shard_map/ppermute | solution.py:498
  40.1 4.4 %collective-permute-start.14 = (bf16[32,1024]{1,0:T(8,128)(2,1)S(1)}, bf16[32,1024]{1,0:T(8,128)(2,1)S(1)}, u32[]{:S(2)}, u32[]{:S(2)}) collective-permute-start(bf16[32,1024]{1,0:T(8,128)(2,1)S(1)} %collective-permute-done.13.refs_6_), channel_id=1, source_target_pairs={{0,1},{1,0},{2,3},{3,2},{4,5},{5,4},{6,7},{7,6},{8,9},{9,8},{10,11... | collective-permute-start | bytes 196616 | tf_op jit(solution)/shard_map/ppermute | solution.py:492
  42.0 4.3 %collective-permute-start.12 = (bf16[32,1024]{1,0:T(8,128)(2,1)S(1)}, bf16[32,1024]{1,0:T(8,128)(2,1)S(1)}, u32[]{:S(2)}, u32[]{:S(2)}) collective-permute-start(bf16[32,1024]{1,0:T(8,128)(2,1)S(1)} %collective-permute-done.11.refs_4_), channel_id=1, source_target_pairs={{0,1},{1,0},{2,3},{3,2},{4,5},{5,4},{6,7},{7,6},{8,9},{9,8},{10,11... | collective-permute-start | bytes 196616 | tf_op jit(solution)/shard_map/ppermute | solution.py:492

commit v6 on v5

--- a/solution.py
+++ b/solution.py
@@ -125,23 +125,22 @@
     return copies
 
 
-def suffix_scores_kernel(spots, ids_ref, slot_ref, query_ref, suf_keys_ref, vals_ref, peak_ref, *rest):
+def suffix_scores_kernel(spots, ids_ref, slot_ref, query_ref, suf_keys_ref, peak_ref, *rest):
     len_ref, suffix_ref, pages_ref, weight_ref = rest[:4]
-    tail_ref, high_ref, high_row_ref, vals_t_ref, out_pages_ref, suf_vals_ref = rest[4:10]
-    w_refs = rest[10 : 10 + len(spots)]
-    lens, seen, list_id, list_pos, sem, sem_page, sem_w = rest[10 + len(spots) :]
+    tail_ref, high_ref, high_row_ref, out_pages_ref, suf_vals_ref = rest[4:9]
+    w_refs = rest[9 : 9 + len(spots)]
+    lens, seen, list_id, list_pos, sem, sem_page, sem_w = rest[9 + len(spots) :]
     rows, span, head_dim = suf_keys_ref.shape
-    tokens = vals_ref.shape[0]
     heads = query_ref.shape[0] // rows
     fetch_len = pltpu.make_async_copy(len_ref, lens, sem.at[1])
     fetch_len.start()
     fetch = [pltpu.make_async_copy(suffix_ref.at[:, 0, 1], suf_vals_ref, sem.at[0])]
     fetch += weight_copies(weight_ref, w_refs, spots, sem_w)
+    for c in fetch:
+        c.start()
     distinct_list(ids_ref, slot_ref, seen, list_id, list_pos)
     outs = (out_pages_ref.at[0], out_pages_ref.at[1])
     page_copies(pages_ref, outs, list_pos, sem_page, False)
-    for c in fetch:
-        c.start()
     query = query_ref[...]
     lanes = lax.broadcasted_iota(jnp.int32, (heads, span), 1)
     fetch_len.wait()
@@ -152,9 +151,6 @@
             mine = both[a * heads : (a + 1) * heads, a * span : (a + 1) * span]
             row = 2 * i + a
             tail_ref[row * heads : (row + 1) * heads, :] = jnp.where(lanes < lens[row], mine, -1.0e30)
-    step = min(1024, tokens)
-    for base in range(0, tokens, step):
-        vals_t_ref[:, base : base + step] = vals_ref[base : base + step, :].astype(F32).T.astype(BF16)
     best = jnp.maximum(tail_ref[:, :128], tail_ref[:, 128:256])
     for b in range(2, span // 128):
         best = jnp.maximum(best, tail_ref[:, b * 128 : (b + 1) * 128])
@@ -167,13 +163,13 @@
         c.wait()
 
 
-def values_kernel(spots, ids_ref, slot_ref, scores, tail, peak, peak_row, vals_t_ref, suf_vals_ref, *rest):
+def values_kernel(spots, ids_ref, slot_ref, scores, tail, peak, peak_row, vals_ref, suf_vals_ref, *rest):
     pages_ref, weight_ref, residual_ref = rest[:3]
     att_ref, shrink_ref, expand_ref, row_slot_ref, slot_mine_ref, res_ref = rest[3:9]
     w_refs = rest[9 : 9 + len(spots)]
-    rowbuf, total, acc, total_row, acc_t, seen, list_id, list_pos, sem, sem_page, sem_w = rest[9 + len(spots) :]
+    rowbuf, total, acc, seen, list_id, list_pos, sem, sem_page, sem_w = rest[9 + len(spots) :]
     rows, span, head_dim = suf_vals_ref.shape
-    tokens = vals_t_ref.shape[1]
+    tokens = vals_ref.shape[0]
     heads = att_ref.shape[1] // head_dim
     width = res_ref.shape[1]
     me = lax.axis_index("tensor")
@@ -203,23 +199,19 @@
     row_slot_ref[...] = row_slot
     slot_mine_ref[...] = slot_mine
 
-    total_row[...] = jnp.zeros(total_row.shape, F32)
-    acc_t[...] = jnp.zeros(acc_t.shape, F32)
-    n_q = acc_t.shape[1]
-    chunk = min(2048, tokens)
-
-    @pl.loop(0, tokens // chunk)
-    def _(i):
-        base = pl.multiple_of(i * chunk, chunk)
-        high_row = peak_row[...]
-        block = scores[pl.ds(base, chunk), :].reshape(chunk // 8, 8, n_q)
+    n_q = acc.shape[0]
+    chunk = min(1024, tokens)
+    high_row = peak_row[...]
+    total_row = jnp.zeros((8, n_q), F32)
+    acc_t = jnp.zeros((head_dim, n_q), F32)
+    for base in range(0, tokens, chunk):
+        block = scores[base : base + chunk, :].reshape(chunk // 8, 8, n_q)
         e = jnp.exp2((block - high_row[None]) * scale2)
-        total_row[...] += jnp.sum(e, axis=0)
+        total_row = total_row + jnp.sum(e, axis=0)
         weights = e.reshape(chunk, n_q).astype(BF16)
-        acc_t[...] += nn_dot(vals_t_ref[:, pl.ds(base, chunk)], weights)
-
-    across_rows = jnp.broadcast_to(jnp.sum(total_row[...], axis=0, keepdims=True), (128, n_q))
-    acc[...] = acc_t[...].T
+        acc_t = acc_t + nn_dot(vals_ref[base : base + chunk, :].T, weights)
+    across_rows = jnp.broadcast_to(jnp.sum(total_row, axis=0, keepdims=True), (128, n_q))
+    acc[...] = acc_t.T
     zeros = jnp.zeros((heads, span), F32)
     for i in range(rows // 2):
         lo = 2 * heads * i
@@ -299,19 +291,18 @@
     far = list(range(n_z - 1, -1, -1))
     early = [(0, k) for k in far[: n_z // 2]]
     late = [(1, k) for k in far] + [(0, k) for k in far[n_z // 2 :]]
-    tail, high, high_row, vals_t, out_pages, suf_vals, *early_w = kernel_call(
+    tail, high, high_row, out_pages, suf_vals, *early_w = kernel_call(
         functools.partial(suffix_scores_kernel, early),
         "suffix_scores",
         [
             pltpu.VMEM((n_q, span), F32),
             pltpu.VMEM((n_q, 128), F32),
             pltpu.VMEM((8, n_q), F32),
-            pltpu.VMEM((head_dim, tokens), BF16),
             pltpu.VMEM((2, DISTINCT) + pages.shape[2:], BF16),
             pltpu.VMEM((rows, span, head_dim), BF16),
         ]
         + [pltpu.VMEM((in_rows, width), BF16)] * len(early),
-        [SMEM, SMEM, VMEM, VMEM, VMEM, VMEM, ANY, ANY, ANY, ANY],
+        [SMEM, SMEM, VMEM, VMEM, VMEM, ANY, ANY, ANY, ANY],
         [pltpu.SMEM((rows,), jnp.int32)]
         + list_scratch(pool_slot)
         + [
@@ -319,7 +310,7 @@
             pltpu.SemaphoreType.DMA((2, DISTINCT)),
             pltpu.SemaphoreType.DMA((len(early),)),
         ],
-        [other_ids, pool_slot, query, suf_keys, vals, peak, in_hbm(suffix_len), suffix_kv, pages, out_weight],
+        [other_ids, pool_slot, query, suf_keys, peak, in_hbm(suffix_len), suffix_kv, pages, out_weight],
         8,
         1 << 29,
         7 * MIB,
@@ -342,8 +333,6 @@
             pltpu.VMEM((n_q, head_dim), F32),
             pltpu.VMEM((n_q, 128), F32),
             pltpu.VMEM((n_q, head_dim), F32),
-            pltpu.VMEM((8, n_q), F32),
-            pltpu.VMEM((head_dim, n_q), F32),
         ]
         + list_scratch(pool_slot)
         + [
@@ -351,7 +340,7 @@
             pltpu.SemaphoreType.DMA((2, DISTINCT)),
             pltpu.SemaphoreType.DMA((len(late),)),
         ],
-        [ids, pool_slot, scores, tail, high, high_row, vals_t, suf_vals, pages, out_weight, residual],
+        [ids, pool_slot, scores, tail, high, high_row, vals, suf_vals, pages, out_weight, residual],
         8,
         2 * n_q * tokens * head_dim,
         14 * MIB,
@@ -418,12 +407,16 @@
     out_ref[...] = nn_dot(att_ref[...], w_ref[...]).astype(BF16)
 
 
-def add_kernel(spot, att_ref, w_ref, from_ref, rank_ref, out_ref):
+def add_kernel(spot, n_near, att_ref, w_ref, from_ref, rank_ref, *rest):
+    near_refs, out_ref = rest[:n_near], rest[-1]
     width = w_ref.shape[1]
     both = nn_dot(att_ref[...], w_ref[...]) + from_ref[:, spot * width : (spot + 1) * width].astype(F32)
     out_ref[:, :width] = both.astype(BF16)
-    rank_both = rank_ref[...] + from_ref[:, from_ref.shape[1] - 128 :].astype(F32)
-    out_ref[:, width:] = rank_both.astype(BF16)
+    if near_refs:
+        low = rank_ref[...] + from_ref[:, from_ref.shape[1] - 128 :].astype(F32)
+        for ref in near_refs:
+            low = low + ref[:, width:].astype(F32)
+        out_ref[:, width:] = low.astype(BF16)
 
 
 def finish_kernel(*refs):
@@ -435,7 +428,8 @@
     width = w_ref.shape[1]
     low = rank_ref[...] + far_ref[:, far_ref.shape[1] - 128 :].astype(F32)
     for ref in moved:
-        low = low + ref[:, width:].astype(F32)
+        if ref.shape[1] > width:
+            low = low + ref[:, width:].astype(F32)
     row_slot = row_slot_ref[...]
     place = lane_place(row_slot.shape, rank)
     tiles = []
@@ -449,22 +443,20 @@
     out_ref[...] = total.astype(BF16)
 
 
-def place_kernel(n_z, *refs):
-    blocks = refs[: 2 * n_z]
-    out_ref = refs[2 * n_z]
+def place_kernel(spots, *refs):
+    blocks, out_ref = refs[:-1], refs[-1]
     width = blocks[0].shape[1]
     me = lax.axis_index("tensor")
     z, y = me // 2, me % 2
-    for k in range(n_z):
-        for other in range(2):
-            where = (z ^ k) * 2 + (y ^ other)
-            out_ref[:, pl.ds(pl.multiple_of(where * width, width), width)] = blocks[2 * k + other][...]
-
-
-def place(blocks, n_tensor):
+    for block, (k, side) in zip(blocks, spots):
+        where = (z ^ k) * 2 + (y ^ side)
+        out_ref[:, pl.ds(pl.multiple_of(where * width, width), width)] = block[...]
+
+
+def place(blocks, spots, n_tensor):
     rows, width = blocks[0].shape
     return pl.pallas_call(
-        functools.partial(place_kernel, n_tensor // 2),
+        functools.partial(place_kernel, spots),
         out_shape=jax.ShapeDtypeStruct((rows, width * n_tensor), BF16),
         in_specs=[VMEM] * n_tensor,
         out_specs=VMEM,
@@ -532,14 +524,18 @@
         [attended, weights[0, 1], weights[1, 1], rank_own],
     )
     moved = [along_z(straight, 1), along_both(cross, 1)]
+    near = list(moved)
+    after = []
     for spot, k in enumerate(far):
+        beside = near if k % 2 else []
         piece = small_call(
-            functools.partial(add_kernel, spot),
+            functools.partial(add_kernel, spot, len(beside)),
             "add_block",
-            piece_shape,
-            [attended, weights[0, k], from_far, rank_own],
+            piece_shape if k % 2 else pltpu.VMEM((rows, width), BF16),
+            [attended, weights[0, k], from_far, rank_own] + beside + after,
         )
         moved.append(along_z(piece, k))
+        after = [piece]
     own_far = small_call(
         block_kernel, "own_far_block", pltpu.VMEM((rows, width), BF16), [attended, weights[1, 0], piece]
     )
@@ -552,10 +548,10 @@
         + moved,
     )
     held = [result] + [along_z(result, k) for k in range(1, n_z)]
-    blocks = []
-    for k in range(n_z):
-        blocks += [held[k], along_both(result, k) if k < 2 else along_y(held[k])]
-    return place(blocks, n_tensor)
+    crossed = [along_both(result, k) if k < 3 else along_y(held[k]) for k in range(n_z)]
+    spots = [(0, 0)] + [(k, side) for k in range(1, n_z) for side in (0, 1)]
+    spots.insert(len(spots) - 2, (0, 1))
+    return place([(crossed if side else held)[k] for k, side in spots], spots, n_tensor)
 
 
 def solution(mesh):

time: 47.3 us -> 52.3 us (1.11)
  waiting for transfers between devices: 8.13 us -> 13.6 us
  starting transfers between devices: 20.5 us -> 18.5 us
  Pallas kernels: 18.4 us -> 19.9 us
    ppermute x6, waiting for transfers between devices: 1.45 us -> 6.42 us  [along_z(): return lax.ppermute(x, 'tensor', [(t, t ^ 2 * k) for t in range(n_tensor)])]
    ppermute x3 -> x4, waiting for transfers between devices: 0.17 us -> 3.25 us  [along_both(): lax.ppermute(x, 'tensor', [(t, t ^ 2 * k ^ 1) for t in range(n_tensor)])]
    ppermute x4 -> x3, starting transfers between devices: 8.13 us -> 5.33 us  [along_y(): return lax.ppermute(x, 'tensor', [(t, t ^ 1) for t in range(n_tensor)])]
    ppermute x4 -> x3, waiting for transfers between devices: 6.5 us -> 3.96 us  [along_y(): return lax.ppermute(x, 'tensor', [(t, t ^ 1) for t in range(n_tensor)])]
    pallas_call x3, Pallas kernels: 13.4 us -> 14.9 us  [kernel_call(): pl.pallas_call(kernel, out_shape=out_shape, in_specs=specs, out_specs=[VM...]
    ppermute x6, starting transfers between devices: 8.24 us -> 9.7 us  [along_z(): return lax.ppermute(x, 'tensor', [(t, t ^ 2 * k) for t in range(n_tensor)])]
    ppermute x3 -> x4, starting transfers between devices: 3.55 us -> 2.82 us  [along_both(): lax.ppermute(x, 'tensor', [(t, t ^ 2 * k ^ 1) for t in range(n_tensor)])]
where the time goes in v6:
time: 52.3 us; the launch traced here: 52.1 us
  Pallas kernels  19.9 us (38%)
  starting transfers between devices  18.5 us (35%)
  waiting for transfers between devices  13.6 us (26%)
    pallas_call x3, Pallas kernels, kernel_call(): pl.pallas_call(kernel, out_shape=out_shape, in_specs=specs, out_specs=[VM...  14.9 us
    ppermute x6, starting transfers between devices, along_z(): return lax.ppermute(x, 'tensor', [(t, t ^ 2 * k) for t in range(n_tensor)])  9.7 us
    ppermute x6, waiting for transfers between devices, along_z(): return lax.ppermute(x, 'tensor', [(t, t ^ 2 * k) for t in range(n_tensor)])  6.42 us
    ppermute x3, starting transfers between devices, along_y(): return lax.ppermute(x, 'tensor', [(t, t ^ 1) for t in range(n_tensor)])  5.33 us
    pallas_call x6, Pallas kernels, small_call(): pl.pallas_call(kernel, out_shape=out_shape, in_specs=[VMEM] * len(operand...  4.12 us
    ppermute x3, waiting for transfers between devices, along_y(): return lax.ppermute(x, 'tensor', [(t, t ^ 1) for t in range(n_tensor)])  3.96 us
    ppermute x4, waiting for transfers between devices, along_both(): lax.ppermute(x, 'tensor', [(t, t ^ 2 * k ^ 1) for t in range(n_tensor)])  3.25 us
    ppermute x4, starting transfers between devices, along_both(): lax.ppermute(x, 'tensor', [(t, t ^ 2 * k ^ 1) for t in range(n_tensor)])  2.82 us
  transfers between devices with their start and end apart: 15, of which 8 were waited for; matrix products, arithmetic and copies ran while one was open for 0% of the time, Pallas kernels for 24%

profile of v6, /device:TPU:0, one launch (start us, length us, event | category | flops | bytes accessed | tf_op | source)
XLA Modules:
  0.0 52.1 jit_solution(9397770484269492909)
XLA Ops:
  0.0 0.5 collective-permute-start
  0.5 3.0 %prefix_scores.1 = (bf16[256,128]{1,0:T(8,128)(2,1)S(1)}, f32[8192,256]{1,0:T(8,128)S(1)}, f32[8,256]{1,0:T(8,128)S(1)}, bf16[8192,128]{1,0:T(8,128)(2,1)S(1)}, bf16[32,256,128]{2,1,0:T(8,128)(2,1)S(1)}) custom-call(bf16[32,1024]{1,0:T(8,128)(2,1)} %q_ref.1, bf16[1,2,8192,128]{3,2,1,0:T(8,128)(2,1)} %prefix_ref.1, bf16[32,1,2,256,128]{4,3,2,1,0:T(8,128)(2,1)} %rest_1_.2), custom_call_target="tpu_custom_call" | custom-call | flops 536870912 | bytes 6291456 | tf_op jit(solution)/shard_map/prefix_scores/pallas_call | solution.py:244
  3.4 0.0 copy-start.1
  3.5 4.1 %suffix_scores.1 = (f32[256,256]{1,0:T(8,128)S(1)}, f32[256,128]{1,0:T(8,128)S(1)}, f32[8,256]{1,0:T(8,128)S(1)}, bf16[2,8,64,1024]{3,2,1,0:T(8,128)(2,1)S(1)}, ...) custom-call(s32[32]{0:T(128)S(1)} %collective-permute-done.ids_ref, ...), custom_call_target="tpu_custom_call" | custom-call | flops 536870912 | bytes 7340032 | tf_op jit(solution)/shard_map/suffix_scores/pallas_call | solution.py:244
  7.6 0.2 collective-permute-start.1
  7.8 7.9 %values.1 = (bf16[32,1024]{1,0:T(8,128)(2,1)S(1)}, bf16[8,64,1024]{2,1,0:T(8,128)(2,1)S(1)}, bf16[8,64,1024]{2,1,0:T(8,128)(2,1)S(1)}, s32[32,128]{1,0:T(8,128)S...) custom-call(s32[32]{0:T(128)S(1)} %copy-done.1, ...), custom_call_target="tpu_custom_call" | custom-call | flops 536870912 | bytes 14680064 | tf_op jit(solution)/shard_map/values/pallas_call | solution.py:244
  15.7 1.1 %far_blocks.1 = (bf16[32,2176]{1,0:T(8,128)(2,1)S(1)}, f32[32,128]{1,0:T(8,128)S(1)}) custom-call(bf16[32,1024]{1,0:T(8,128)(2,1)S(1)} %get-tuple-element.42.att_ref.refs_0_, s32[32,128]{1,0:T(8,128)S(1)} %get-tuple-element.44.row_slot_ref.refs_2_, s32[8,128]{1,0:T(8,128)S(1)} %get-tuple-element.45.slot_mine_ref.refs_3_, ...), custom_call_target="tpu_custom_call" | custom-call | flops 134217728 | bytes 2097152 | tf_op jit(solution)/shard_map/far_blocks/pallas_call | solution.py:353
  16.8 3.0 %collective-permute-start.2 = (bf16[32,2176]{1,0:T(8,128)(2,1)S(1)}, bf16[32,2176]{1,0:T(8,128)(2,1)S(1)}, u32[]{:S(2)}, u32[]{:S(2)}) collective-permute-start(bf16[32,2176]{1,0:T(8,128)(2,1)S(1)} %get-tuple-element.52), channel_id=1, source_target_pairs={{0,1},{1,0},{2,3},{3,2},{4,5},{5,4},{6,7},{7,6},{8,9},{9,8},{10,11... | collective-permute-start | bytes 417800 | tf_op jit(solution)/shard_map/ppermute | solution.py:484
  19.8 0.8 %near_blocks.1 = (bf16[32,1152]{1,0:T(8,128)(2,1)S(1)}, bf16[32,1152]{1,0:T(8,128)(2,1)S(1)}) custom-call(bf16[32,1024]{1,0:T(8,128)(2,1)S(1)} %get-tuple-element.42.att_ref.refs_0_, bf16[1024,1024]{1,0:T(8,128)(2,1)S(1)} %get-tuple-element.56.w_ref, bf16[1024,1024]{1,0:T(8,128)(2,1)S(1)} %get-tuple-element.57.cross_w_ref, ...), custom_call_target="tpu_custom_call" | custom-call | flops 134217728 | bytes 2097152 | tf_op jit(solution)/shard_map/near_blocks/pallas_call | solution.py:353
  20.6 1.6 %collective-permute-start.3 = (bf16[32,1152]{1,0:T(8,128)(2,1)S(1)}, bf16[32,1152]{1,0:T(8,128)(2,1)S(1)}, u32[]{:S(2)}, u32[]{:S(2)}) collective-permute-start(bf16[32,1152]{1,0:T(8,128)(2,1)S(1)} %get-tuple-element.58), channel_id=1, source_target_pairs={{0,2},{1,3},{2,0},{3,1},{4,6},{5,7},{6,4},{7,5},{8,10},{9,11},{10,... | collective-permute-start | bytes 221192 | tf_op jit(solution)/shard_map/ppermute | solution.py:487
  22.2 3.5 %collective-permute-done.3.rest_0_.refs_10_ = bf16[32,1152]{1,0:T(8,128)(2,1)S(1)} collective-permute-done((bf16[32,1152]{1,0:T(8,128)(2,1)S(1)}, bf16[32,1152]{1,0:T(8,128)(2,1)S(1)}, u32[]{:S(2)}, u32[]{:S(2)}) %collective-permute-start.3) | collective-permute-done | bytes 73760 | tf_op jit(solution)/shard_map/ppermute | solution.py:487
  25.7 1.8 %collective-permute-done.4.rest_1_.refs_11_ = bf16[32,1152]{1,0:T(8,128)(2,1)S(1)} collective-permute-done((bf16[32,1152]{1,0:T(8,128)(2,1)S(1)}, bf16[32,1152]{1,0:T(8,128)(2,1)S(1)}, u32[]{:S(2)}, u32[]{:S(2)}) %collective-permute-start.4) | collective-permute-done | bytes 73760 | tf_op jit(solution)/shard_map/ppermute | solution.py:490
  27.5 0.5 add_block.2.rest_0_
  27.9 2.6 %collective-permute-start.6 = (bf16[32,1152]{1,0:T(8,128)(2,1)S(1)}, bf16[32,1152]{1,0:T(8,128)(2,1)S(1)}, u32[]{:S(2)}, u32[]{:S(2)}) collective-permute-start(bf16[32,1152]{1,0:T(8,128)(2,1)S(1)} %add_block.2.rest_0_), channel_id=1, source_target_pairs={{0,6},{1,7},{2,4},{3,5},{4,2},{5,3},{6,0},{7,1},{8,14},{9,15},{10,... | collective-permute-start | bytes 221192 | tf_op jit(solution)/shard_map/ppermute | solution.py:487
  30.6 0.5 add_block.3.after_ref
  31.0 0.5 own_far_block.1
  31.5 1.2 %collective-permute-start.5 = (bf16[32,1024]{1,0:T(8,128)(2,1)S(1)}, bf16[32,1024]{1,0:T(8,128)(2,1)S(1)}, u32[]{:S(2)}, u32[]{:S(2)}) collective-permute-start(bf16[32,1024]{1,0:T(8,128)(2,1)S(1)} %own_far_block.1), channel_id=1, source_target_pairs={{0,1},{1,0},{2,3},{3,2},{4,5},{5,4},{6,7},{7,6},{8,9},{9,8},{10,11... | collective-permute-start | bytes 196616 | tf_op jit(solution)/shard_map/ppermute | solution.py:484
  32.7 3.1 %collective-permute-done.5.refs_8_ = bf16[32,1024]{1,0:T(8,128)(2,1)S(1)} collective-permute-done((bf16[32,1024]{1,0:T(8,128)(2,1)S(1)}, bf16[32,1024]{1,0:T(8,128)(2,1)S(1)}, u32[]{:S(2)}, u32[]{:S(2)}) %collective-permute-start.5) | collective-permute-done | bytes 65568 | tf_op jit(solution)/shard_map/ppermute | solution.py:484
  35.8 2.2 %collective-permute-done.7.refs_13_ = bf16[32,1024]{1,0:T(8,128)(2,1)S(1)} collective-permute-done((bf16[32,1024]{1,0:T(8,128)(2,1)S(1)}, bf16[32,1024]{1,0:T(8,128)(2,1)S(1)}, u32[]{:S(2)}, u32[]{:S(2)}) %collective-permute-start.7) | collective-permute-done | bytes 65568 | tf_op jit(solution)/shard_map/ppermute | solution.py:487
  37.9 0.8 %finish.1.refs_0_ = bf16[32,1024]{1,0:T(8,128)(2,1)S(1)} custom-call(bf16[32,1024]{1,0:T(8,128)(2,1)S(1)} %get-tuple-element.42.att_ref.refs_0_, bf16[1024,1024]{1,0:T(8,128)(2,1)S(1)} %get-tuple-element.43.refs_1_, s32[32,128]{1,0:T(8,128)S(1)} %get-tuple-element.44.row_slot_ref.refs_2_, s32[8,128]{1,0:T(8,128)S(1)} %get-tuple-element.45.slot_mine_ref.refs_3_, ...), custom_call_target="tpu_custom_call" | custom-call | flops 134217728 | bytes 2097152 | tf_op jit(solution)/shard_map/finish/pallas_call | solution.py:353
  38.7 1.5 %collective-permute-start.13 = (bf16[32,1024]{1,0:T(8,128)(2,1)S(1)}, bf16[32,1024]{1,0:T(8,128)(2,1)S(1)}, u32[]{:S(2)}, u32[]{:S(2)}) collective-permute-start(bf16[32,1024]{1,0:T(8,128)(2,1)S(1)} %finish.1.refs_0_), channel_id=1, source_target_pairs={{0,6},{1,7},{2,4},{3,5},{4,2},{5,3},{6,0},{7,1},{8,14},{9,15},{10,... | collective-permute-start | bytes 196616 | tf_op jit(solution)/shard_map/ppermute | solution.py:487
  40.2 0.9 %collective-permute-start.12 = (bf16[32,1024]{1,0:T(8,128)(2,1)S(1)}, bf16[32,1024]{1,0:T(8,128)(2,1)S(1)}, u32[]{:S(2)}, u32[]{:S(2)}) collective-permute-start(bf16[32,1024]{1,0:T(8,128)(2,1)S(1)} %finish.1.refs_0_), channel_id=1, source_target_pairs={{0,1},{1,0},{2,3},{3,2},{4,5},{5,4},{6,7},{7,6},{8,9},{9,8},{10,11... | collective-permute-start | bytes 196616 | tf_op jit(solution)/shard_map/ppermute | solution.py:490
  41.2 0.4 collective-permute-start.11
  41.6 3.1 %collective-permute-start.10 = (bf16[32,1024]{1,0:T(8,128)(2,1)S(1)}, bf16[32,1024]{1,0:T(8,128)(2,1)S(1)}, u32[]{:S(2)}, u32[]{:S(2)}) collective-permute-start(bf16[32,1024]{1,0:T(8,128)(2,1)S(1)} %finish.1.refs_0_), channel_id=1, source_target_pairs={{0,4},{1,5},{2,6},{3,7},{4,0},{5,1},{6,2},{7,3},{8,12},{9,13},{10,... | collective-permute-start | bytes 196616 | tf_op jit(solution)/shard_map/ppermute | solution.py:487
  44.6 1.5 %collective-permute-start.9 = (bf16[32,1024]{1,0:T(8,128)(2,1)S(1)}, bf16[32,1024]{1,0:T(8,128)(2,1)S(1)}, u32[]{:S(2)}, u32[]{:S(2)}) collective-permute-start(bf16[32,1024]{1,0:T(8,128)(2,1)S(1)} %finish.1.refs_0_), channel_id=1, source_target_pairs={{0,3},{1,2},{2,1},{3,0},{4,7},{5,6},{6,5},{7,4},{8,11},{9,10},{10,... | collective-permute-start | bytes 196616 | tf_op jit(solution)/shard_map/ppermute | solution.py:490
  46.1 0.9 %collective-permute-start.8 = (bf16[32,1024]{1,0:T(8,128)(2,1)S(1)}, bf16[32,1024]{1,0:T(8,128)(2,1)S(1)}, u32[]{:S(2)}, u32[]{:S(2)}) collective-permute-start(bf16[32,1024]{1,0:T(8,128)(2,1)S(1)} %finish.1.refs_0_), channel_id=1, source_target_pairs={{0,2},{1,3},{2,0},{3,1},{4,6},{5,7},{6,4},{7,5},{8,10},{9,11},{10,... | collective-permute-start | bytes 196616 | tf_op jit(solution)/shard_map/ppermute | solution.py:487
  47.0 1.1 %collective-permute-start.14 = (bf16[32,1024]{1,0:T(8,128)(2,1)S(1)}, bf16[32,1024]{1,0:T(8,128)(2,1)S(1)}, u32[]{:S(2)}, u32[]{:S(2)}) collective-permute-start(bf16[32,1024]{1,0:T(8,128)(2,1)S(1)} %collective-permute-done.13.refs_6_), channel_id=1, source_target_pairs={{0,1},{1,0},{2,3},{3,2},{4,5},{5,4},{6,7},{7,6},{8,9},{9,8},{10,11... | collective-permute-start | bytes 196616 | tf_op jit(solution)/shard_map/ppermute | solution.py:484
  48.1 0.4 collective-permute-done.10.refs_3_
  48.5 1.5 %collective-permute-done.9.refs_2_ = bf16[32,1024]{1,0:T(8,128)(2,1)S(1)} collective-permute-done((bf16[32,1024]{1,0:T(8,128)(2,1)S(1)}, bf16[32,1024]{1,0:T(8,128)(2,1)S(1)}, u32[]{:S(2)}, u32[]{:S(2)}) %collective-permute-start.9) | collective-permute-done | bytes 65568 | tf_op jit(solution)/shard_map/ppermute | solution.py:490
  50.0 0.4 collective-permute-done.8.refs_1_
  50.4 0.9 %collective-permute-done.14.refs_7_ = bf16[32,1024]{1,0:T(8,128)(2,1)S(1)} collective-permute-done((bf16[32,1024]{1,0:T(8,128)(2,1)S(1)}, bf16[32,1024]{1,0:T(8,128)(2,1)S(1)}, u32[]{:S(2)}, u32[]{:S(2)}) %collective-permute-start.14) | collective-permute-done | bytes 65568 | tf_op jit(solution)/shard_map/ppermute | solution.py:484
  51.3 0.8 %place.1 = bf16[32,8192]{1,0:T(8,128)(2,1)} custom-call(bf16[32,1024]{1,0:T(8,128)(2,1)S(1)} %finish.1.refs_0_, bf16[32,1024]{1,0:T(8,128)(2,1)S(1)} %collective-permute-done.8.refs_1_, bf16[32,1024]{1,0:T(8,128)(2,1)S(1)} %collective-permute-done.9.refs_2_, bf16[32,1024]{1,0:T(8,128)(2,1)S(1)} %collective-permute-done.10.refs_3_, ...), custom_call_target="tpu_custom_call" | custom-call | bytes 1048576 | tf_op jit(solution)/shard_map/place/pallas_call | solution.py:458
  (12 shorter events, 0.0 us)
Async XLA Ops:
  0.0 3.4 %copy-start = (s32[128]{0:T(128)S(1)}, s32[128]{0:T(128)}, u32[]{:S(2)}) copy-start(s32[128]{0:T(128)} %slot_ref.3) | copy-start | bytes 1540
  0.0 3.4 %collective-permute-start = (s32[32]{0:T(128)}, s32[32]{0:T(128)S(1)}, u32[]{:S(2)}, u32[]{:S(2)}) collective-permute-start(s32[32]{0:T(128)} %ids_ref.1), channel_id=1, source_target_pairs={{0,8},{8,0},{1,9},{9,1},{2,10},{10,2},{3,11},{11,3},{4,12},{12,4},... | collective-permute-start | bytes 392 | tf_op jit(solution)/shard_map/ppermute | solution.py:493
  3.4 4.3 %copy-start.1 = (s32[32]{0:T(128)S(1)}, s32[32]{0:T(128)}, u32[]{:S(2)}) copy-start(s32[32]{0:T(128)} %ids_ref.1) | copy-start | bytes 388
  7.6 8.1 %collective-permute-start.1 = (bf16[2,8,64,1024]{3,2,1,0:T(8,128)(2,1)S(1)}, bf16[2,8,64,1024]{3,2,1,0:T(8,128)(2,1)S(1)}, u32[]{:S(2)}, u32[]{:S(2)}) collective-permute-start(bf16[2,8,64,1024]{3,2,1,0:T(8,128)(2,1)S(1)} %get-tuple-element.47), channel_id=1, source_target_pairs={{0,8},{8,0},{1,9},{9,1},{2,10},{10,2},{3,11},{11,3},{4,12},{12,4},... | collective-permute-start | bytes 6291464 | tf_op jit(solution)/shard_map/ppermute | solution.py:493
  16.8 10.7 %collective-permute-start.2 = (bf16[32,2176]{1,0:T(8,128)(2,1)S(1)}, bf16[32,2176]{1,0:T(8,128)(2,1)S(1)}, u32[]{:S(2)}, u32[]{:S(2)}) collective-permute-start(bf16[32,2176]{1,0:T(8,128)(2,1)S(1)} %get-tuple-element.52), channel_id=1, source_target_pairs={{0,1},{1,0},{2,3},{3,2},{4,5},{5,4},{6,7},{7,6},{8,9},{9,8},{10,11... | collective-permute-start | bytes 417800 | tf_op jit(solution)/shard_map/ppermute | solution.py:484
  20.6 5.1 %collective-permute-start.3 = (bf16[32,1152]{1,0:T(8,128)(2,1)S(1)}, bf16[32,1152]{1,0:T(8,128)(2,1)S(1)}, u32[]{:S(2)}, u32[]{:S(2)}) collective-permute-start(bf16[32,1152]{1,0:T(8,128)(2,1)S(1)} %get-tuple-element.58), channel_id=1, source_target_pairs={{0,2},{1,3},{2,0},{3,1},{4,6},{5,7},{6,4},{7,5},{8,10},{9,11},{10,... | collective-permute-start | bytes 221192 | tf_op jit(solution)/shard_map/ppermute | solution.py:487
  22.2 5.3 %collective-permute-start.4 = (bf16[32,1152]{1,0:T(8,128)(2,1)S(1)}, bf16[32,1152]{1,0:T(8,128)(2,1)S(1)}, u32[]{:S(2)}, u32[]{:S(2)}) collective-permute-start(bf16[32,1152]{1,0:T(8,128)(2,1)S(1)} %get-tuple-element.59), channel_id=1, source_target_pairs={{0,3},{1,2},{2,1},{3,0},{4,7},{5,6},{6,5},{7,4},{8,11},{9,10},{10,... | collective-permute-start | bytes 221192 | tf_op jit(solution)/shard_map/ppermute | solution.py:490
  27.9 10.0 %collective-permute-start.6 = (bf16[32,1152]{1,0:T(8,128)(2,1)S(1)}, bf16[32,1152]{1,0:T(8,128)(2,1)S(1)}, u32[]{:S(2)}, u32[]{:S(2)}) collective-permute-start(bf16[32,1152]{1,0:T(8,128)(2,1)S(1)} %add_block.2.rest_0_), channel_id=1, source_target_pairs={{0,6},{1,7},{2,4},{3,5},{4,2},{5,3},{6,0},{7,1},{8,14},{9,15},{10,... | collective-permute-start | bytes 221192 | tf_op jit(solution)/shard_map/ppermute | solution.py:487
  31.5 4.3 %collective-permute-start.5 = (bf16[32,1024]{1,0:T(8,128)(2,1)S(1)}, bf16[32,1024]{1,0:T(8,128)(2,1)S(1)}, u32[]{:S(2)}, u32[]{:S(2)}) collective-permute-start(bf16[32,1024]{1,0:T(8,128)(2,1)S(1)} %own_far_block.1), channel_id=1, source_target_pairs={{0,1},{1,0},{2,3},{3,2},{4,5},{5,4},{6,7},{7,6},{8,9},{9,8},{10,11... | collective-permute-start | bytes 196616 | tf_op jit(solution)/shard_map/ppermute | solution.py:484
  32.7 5.2 %collective-permute-start.7 = (bf16[32,1024]{1,0:T(8,128)(2,1)S(1)}, bf16[32,1024]{1,0:T(8,128)(2,1)S(1)}, u32[]{:S(2)}, u32[]{:S(2)}) collective-permute-start(bf16[32,1024]{1,0:T(8,128)(2,1)S(1)} %add_block.3.after_ref), channel_id=1, source_target_pairs={{0,4},{1,5},{2,6},{3,7},{4,0},{5,1},{6,2},{7,3},{8,12},{9,13},{10,... | collective-permute-start | bytes 196616 | tf_op jit(solution)/shard_map/ppermute | solution.py:487
  38.7 7.4 %collective-permute-start.13 = (bf16[32,1024]{1,0:T(8,128)(2,1)S(1)}, bf16[32,1024]{1,0:T(8,128)(2,1)S(1)}, u32[]{:S(2)}, u32[]{:S(2)}) collective-permute-start(bf16[32,1024]{1,0:T(8,128)(2,1)S(1)} %finish.1.refs_0_), channel_id=1, source_target_pairs={{0,6},{1,7},{2,4},{3,5},{4,2},{5,3},{6,0},{7,1},{8,14},{9,15},{10,... | collective-permute-start | bytes 196616 | tf_op jit(solution)/shard_map/ppermute | solution.py:487
  40.2 6.8 %collective-permute-start.12 = (bf16[32,1024]{1,0:T(8,128)(2,1)S(1)}, bf16[32,1024]{1,0:T(8,128)(2,1)S(1)}, u32[]{:S(2)}, u32[]{:S(2)}) collective-permute-start(bf16[32,1024]{1,0:T(8,128)(2,1)S(1)} %finish.1.refs_0_), channel_id=1, source_target_pairs={{0,1},{1,0},{2,3},{3,2},{4,5},{5,4},{6,7},{7,6},{8,9},{9,8},{10,11... | collective-permute-start | bytes 196616 | tf_op jit(solution)/shard_map/ppermute | solution.py:490
  41.2 7.0 %collective-permute-start.11 = (bf16[32,1024]{1,0:T(8,128)(2,1)S(1)}, bf16[32,1024]{1,0:T(8,128)(2,1)S(1)}, u32[]{:S(2)}, u32[]{:S(2)}) collective-permute-start(bf16[32,1024]{1,0:T(8,128)(2,1)S(1)} %finish.1.refs_0_), channel_id=1, source_target_pairs={{0,5},{1,4},{2,7},{3,6},{4,1},{5,0},{6,3},{7,2},{8,13},{9,12},{10,... | collective-permute-start | bytes 196616 | tf_op jit(solution)/shard_map/ppermute | solution.py:490
  41.6 6.9 %collective-permute-start.10 = (bf16[32,1024]{1,0:T(8,128)(2,1)S(1)}, bf16[32,1024]{1,0:T(8,128)(2,1)S(1)}, u32[]{:S(2)}, u32[]{:S(2)}) collective-permute-start(bf16[32,1024]{1,0:T(8,128)(2,1)S(1)} %finish.1.refs_0_), channel_id=1, source_target_pairs={{0,4},{1,5},{2,6},{3,7},{4,0},{5,1},{6,2},{7,3},{8,12},{9,13},{10,... | collective-permute-start | bytes 196616 | tf_op jit(solution)/shard_map/ppermute | solution.py:487
  44.6 5.3 %collective-permute-start.9 = (bf16[32,1024]{1,0:T(8,128)(2,1)S(1)}, bf16[32,1024]{1,0:T(8,128)(2,1)S(1)}, u32[]{:S(2)}, u32[]{:S(2)}) collective-permute-start(bf16[32,1024]{1,0:T(8,128)(2,1)S(1)} %finish.1.refs_0_), channel_id=1, source_target_pairs={{0,3},{1,2},{2,1},{3,0},{4,7},{5,6},{6,5},{7,4},{8,11},{9,10},{10,... | collective-permute-start | bytes 196616 | tf_op jit(solution)/shard_map/ppermute | solution.py:490
  46.1 4.3 %collective-permute-start.8 = (bf16[32,1024]{1,0:T(8,128)(2,1)S(1)}, bf16[32,1024]{1,0:T(8,128)(2,1)S(1)}, u32[]{:S(2)}, u32[]{:S(2)}) collective-permute-start(bf16[32,1024]{1,0:T(8,128)(2,1)S(1)} %finish.1.refs_0_), channel_id=1, source_target_pairs={{0,2},{1,3},{2,0},{3,1},{4,6},{5,7},{6,4},{7,5},{8,10},{9,11},{10,... | collective-permute-start | bytes 196616 | tf_op jit(solution)/shard_map/ppermute | solution.py:487
  47.0 4.3 %collective-permute-start.14 = (bf16[32,1024]{1,0:T(8,128)(2,1)S(1)}, bf16[32,1024]{1,0:T(8,128)(2,1)S(1)}, u32[]{:S(2)}, u32[]{:S(2)}) collective-permute-start(bf16[32,1024]{1,0:T(8,128)(2,1)S(1)} %collective-permute-done.13.refs_6_), channel_id=1, source_target_pairs={{0,1},{1,0},{2,3},{3,2},{4,5},{5,4},{6,7},{7,6},{8,9},{9,8},{10,11... | collective-permute-start | bytes 196616 | tf_op jit(solution)/shard_map/ppermute | solution.py:484

commit v7 on v5

--- a/solution.py
+++ b/solution.py
@@ -298,7 +298,7 @@
     )
     far = list(range(n_z - 1, -1, -1))
     early = [(0, k) for k in far[: n_z // 2]]
-    late = [(1, k) for k in far] + [(0, k) for k in far[n_z // 2 :]]
+    late = [(1, k) for k in far if k] + [(0, k) for k in far[n_z // 2 :] if k]
     tail, high, high_row, vals_t, out_pages, suf_vals, *early_w = kernel_call(
         functools.partial(suffix_scores_kernel, early),
         "suffix_scores",
@@ -405,20 +405,39 @@
     out_ref[:, n * width :] = picked.astype(BF16)
 
 
-def near_kernel(att_ref, w_ref, cross_w_ref, rank_ref, out_ref, cross_ref):
+def near_kernel(att_ref, w_ref, rank_ref, *rest):
+    out_ref = rest[-1]
     width = w_ref.shape[1]
-    attended = att_ref[...]
-    rank = rank_ref[...].astype(BF16)
-    for w, out in ((w_ref, out_ref), (cross_w_ref, cross_ref)):
-        out[:, :width] = nn_dot(attended, w[...]).astype(BF16)
-        out[:, width:] = rank
+    out_ref[:, :width] = nn_dot(att_ref[...], w_ref[...]).astype(BF16)
+    out_ref[:, width:] = rank_ref[...].astype(BF16)
+
+
+def load_kernel(spots, weight_ref, after_ref, out_ref, sem):
+    (copy,) = weight_copies(weight_ref, [out_ref], spots, sem)
+    copy.start()
+    copy.wait()
+
+
+def load_block(weight, spot, after, n_tensor):
+    return kernel_call(
+        functools.partial(load_kernel, [spot]),
+        "load_block",
+        [pltpu.VMEM((weight.shape[0], weight.shape[1] // n_tensor), BF16)],
+        [ANY, VMEM],
+        [pltpu.SemaphoreType.DMA((1,))],
+        [in_hbm(weight), after],
+        2,
+        0,
+        2 * MIB,
+    )[0]
 
 
 def block_kernel(att_ref, w_ref, after_ref, out_ref):
     out_ref[...] = nn_dot(att_ref[...], w_ref[...]).astype(BF16)
 
 
-def add_kernel(spot, att_ref, w_ref, from_ref, rank_ref, out_ref):
+def add_kernel(spot, att_ref, w_ref, from_ref, rank_ref, *rest):
+    out_ref = rest[-1]
     width = w_ref.shape[1]
     both = nn_dot(att_ref[...], w_ref[...]) + from_ref[:, spot * width : (spot + 1) * width].astype(F32)
     out_ref[:, :width] = both.astype(BF16)
@@ -449,22 +468,20 @@
     out_ref[...] = total.astype(BF16)
 
 
-def place_kernel(n_z, *refs):
-    blocks = refs[: 2 * n_z]
-    out_ref = refs[2 * n_z]
+def place_kernel(spots, *refs):
+    blocks, out_ref = refs[:-1], refs[-1]
     width = blocks[0].shape[1]
     me = lax.axis_index("tensor")
     z, y = me // 2, me % 2
-    for k in range(n_z):
-        for other in range(2):
-            where = (z ^ k) * 2 + (y ^ other)
-            out_ref[:, pl.ds(pl.multiple_of(where * width, width), width)] = blocks[2 * k + other][...]
-
-
-def place(blocks, n_tensor):
+    for block, (k, side) in zip(blocks, spots):
+        where = (z ^ k) * 2 + (y ^ side)
+        out_ref[:, pl.ds(pl.multiple_of(where * width, width), width)] = block[...]
+
+
+def place(blocks, spots, n_tensor):
     rows, width = blocks[0].shape
     return pl.pallas_call(
-        functools.partial(place_kernel, n_tensor // 2),
+        functools.partial(place_kernel, spots),
         out_shape=jax.ShapeDtypeStruct((rows, width * n_tensor), BF16),
         in_specs=[VMEM] * n_tensor,
         out_specs=VMEM,
@@ -525,25 +542,26 @@
         [attended, row_slot, slot_mine, own_shrink, other_pages] + [weights[1, k] for k in far],
     )
     from_far = along_y(far_out)
-    straight, cross = small_call(
-        near_kernel,
-        "near_blocks",
-        [piece_shape, piece_shape],
-        [attended, weights[0, 1], weights[1, 1], rank_own],
-    )
-    moved = [along_z(straight, 1), along_both(cross, 1)]
+    straight = small_call(near_kernel, "near_block", piece_shape, [attended, weights[0, 1], rank_own])
+    weights[1, 0] = load_block(out_weight, (1, 0), straight, n_tensor)
+    moved = [along_z(straight, 1)]
+    after = []
     for spot, k in enumerate(far):
         piece = small_call(
             functools.partial(add_kernel, spot),
             "add_block",
             piece_shape,
-            [attended, weights[0, k], from_far, rank_own],
+            [attended, weights[0, k], from_far, rank_own] + after,
         )
         moved.append(along_z(piece, k))
+        after = [piece]
+    cross = small_call(near_kernel, "cross_block", piece_shape, [attended, weights[1, 1], rank_own, piece])
+    moved.append(along_both(cross, 1))
     own_far = small_call(
-        block_kernel, "own_far_block", pltpu.VMEM((rows, width), BF16), [attended, weights[1, 0], piece]
+        block_kernel, "own_far_block", pltpu.VMEM((rows, width), BF16), [attended, weights[1, 0], cross]
     )
     from_own = along_y(own_far)
+    weights[0, 0] = load_block(out_weight, (0, 0), own_far, n_tensor)
     result = small_call(
         finish_kernel,
         "finish",
@@ -552,10 +570,10 @@
         + moved,
     )
     held = [result] + [along_z(result, k) for k in range(1, n_z)]
-    blocks = []
-    for k in range(n_z):
-        blocks += [held[k], along_both(result, k) if k < 2 else along_y(held[k])]
-    return place(blocks, n_tensor)
+    crossed = [along_both(result, k) if k < 2 else along_y(held[k]) for k in range(n_z)]
+    spots = [(0, 0), (1, 1), (1, 0)] + [(k, side) for k in range(2, n_z) for side in (0, 1)]
+    spots.insert(len(spots) - 2, (0, 1))
+    return place([(crossed if side else held)[k] for k, side in spots], spots, n_tensor)
 
 
 def solution(mesh):

time: 47.3 us -> 47.8 us (1.011)
  Pallas kernels: 18.4 us -> 20.5 us
  starting transfers between devices: 20.5 us -> 19.2 us
    ppermute x4, starting transfers between devices: 8.13 us -> 4.58 us  [along_y(): return lax.ppermute(x, 'tensor', [(t, t ^ 1) for t in range(n_tensor)])]
    pallas_call x3 -> x5, Pallas kernels: 13.4 us -> 15.4 us  [kernel_call(): pl.pallas_call(kernel, out_shape=out_shape, in_specs=specs, out_specs=[VM...]
    ppermute x6, starting transfers between devices: 8.24 us -> 10.2 us  [along_z(): return lax.ppermute(x, 'tensor', [(t, t ^ 2 * k) for t in range(n_tensor)])]
    ppermute x4, waiting for transfers between devices: 6.5 us -> 5.43 us  [along_y(): return lax.ppermute(x, 'tensor', [(t, t ^ 1) for t in range(n_tensor)])]
    ppermute x3, waiting for transfers between devices: 0.17 us -> 0.85 us  [along_both(): lax.ppermute(x, 'tensor', [(t, t ^ 2 * k ^ 1) for t in range(n_tensor)])]
    pallas_call x6 -> x7, Pallas kernels: 4.1 us -> 4.21 us  [small_call(): pl.pallas_call(kernel, out_shape=out_shape, in_specs=[VMEM] * len(operand...]
  transfers between devices with their start and end apart: 15 -> 15, of which waited for: 8 -> 6; matrix products, arithmetic and copies ran while one was open for 0% -> 0% of each run, Pallas kernels for 24% -> 28%
where the time goes in v7:
time: 47.8 us; the launch traced here: 47.5 us
  Pallas kernels  20.5 us (43%)
  starting transfers between devices  19.2 us (40%)
  waiting for transfers between devices  7.67 us (16%)
    pallas_call x5, Pallas kernels, kernel_call(): pl.pallas_call(kernel, out_shape=out_shape, in_specs=specs, out_specs=[VM...  15.4 us
    ppermute x6, starting transfers between devices, along_z(): return lax.ppermute(x, 'tensor', [(t, t ^ 2 * k) for t in range(n_tensor)])  10.2 us
    ppermute x4, waiting for transfers between devices, along_y(): return lax.ppermute(x, 'tensor', [(t, t ^ 1) for t in range(n_tensor)])  5.43 us
    ppermute x4, starting transfers between devices, along_y(): return lax.ppermute(x, 'tensor', [(t, t ^ 1) for t in range(n_tensor)])  4.58 us
    pallas_call x7, Pallas kernels, small_call(): pl.pallas_call(kernel, out_shape=out_shape, in_specs=[VMEM] * len(operand...  4.21 us
    ppermute x3, starting transfers between devices, along_both(): lax.ppermute(x, 'tensor', [(t, t ^ 2 * k ^ 1) for t in range(n_tensor)])  3.89 us
    ppermute x6, waiting for transfers between devices, along_z(): return lax.ppermute(x, 'tensor', [(t, t ^ 2 * k) for t in range(n_tensor)])  1.38 us
  transfers between devices with their start and end apart: 15, of which 6 were waited for; matrix products, arithmetic and copies ran while one was open for 0% of the time, Pallas kernels for 28%

profile of v7, /device:TPU:0, one launch (start us, length us, event | category | flops | bytes accessed | tf_op | source)
XLA Modules:
  0.0 47.5 jit_solution(2639804122802442552)
XLA Ops:
  0.0 0.5 collective-permute-start
  0.5 3.0 %prefix_scores.1 = (bf16[256,128]{1,0:T(8,128)(2,1)S(1)}, f32[8192,256]{1,0:T(8,128)S(1)}, f32[8,256]{1,0:T(8,128)S(1)}, bf16[8192,128]{1,0:T(8,128)(2,1)S(1)}, bf16[32,256,128]{2,1,0:T(8,128)(2,1)S(1)}) custom-call(bf16[32,1024]{1,0:T(8,128)(2,1)} %q_ref.1, bf16[1,2,8192,128]{3,2,1,0:T(8,128)(2,1)} %prefix_ref.1, bf16[32,1,2,256,128]{4,3,2,1,0:T(8,128)(2,1)} %rest_1_.2), custom_call_target="tpu_custom_call" | custom-call | flops 536870912 | bytes 6291456 | tf_op jit(solution)/shard_map/prefix_scores/pallas_call | solution.py:252
  3.5 4.3 %suffix_scores.1 = (f32[256,256]{1,0:T(8,128)S(1)}, f32[256,128]{1,0:T(8,128)S(1)}, f32[8,256]{1,0:T(8,128)S(1)}, bf16[128,8192]{1,0:T(8,128)(2,1)S(1)}, bf16[2,...) custom-call(s32[32]{0:T(128)S(1)} %collective-permute-done.ids_ref, ...), custom_call_target="tpu_custom_call" | custom-call | flops 536870912 | bytes 7340032 | tf_op jit(solution)/shard_map/suffix_scores/pallas_call | solution.py:252
  7.8 0.1 collective-permute-start.1
  7.9 4.9 %values.1 = (bf16[32,1024]{1,0:T(8,128)(2,1)S(1)}, bf16[8,64,1024]{2,1,0:T(8,128)(2,1)S(1)}, bf16[8,64,1024]{2,1,0:T(8,128)(2,1)S(1)}, s32[32,128]{1,0:T(8,128)S...) custom-call(s32[32]{0:T(128)S(1)} %copy-done.1, ...), custom_call_target="tpu_custom_call" | custom-call | flops 536870912 | bytes 14680064 | tf_op jit(solution)/shard_map/values/pallas_call | solution.py:252
  12.8 1.1 %far_blocks.1 = (bf16[32,2176]{1,0:T(8,128)(2,1)S(1)}, f32[32,128]{1,0:T(8,128)S(1)}) custom-call(bf16[32,1024]{1,0:T(8,128)(2,1)S(1)} %get-tuple-element.40.att_ref.refs_0_, s32[32,128]{1,0:T(8,128)S(1)} %get-tuple-element.42.row_slot_ref.refs_2_, s32[8,128]{1,0:T(8,128)S(1)} %get-tuple-element.43.slot_mine_ref.refs_3_, ...), custom_call_target="tpu_custom_call" | custom-call | flops 134217728 | bytes 2097152 | tf_op jit(solution)/shard_map/far_blocks/pallas_call | solution.py:364
  14.0 3.0 %collective-permute-start.2 = (bf16[32,2176]{1,0:T(8,128)(2,1)S(1)}, bf16[32,2176]{1,0:T(8,128)(2,1)S(1)}, u32[]{:S(2)}, u32[]{:S(2)}) collective-permute-start(bf16[32,2176]{1,0:T(8,128)(2,1)S(1)} %get-tuple-element.51), channel_id=1, source_target_pairs={{0,1},{1,0},{2,3},{3,2},{4,5},{5,4},{6,7},{7,6},{8,9},{9,8},{10,11... | collective-permute-start | bytes 417800 | tf_op jit(solution)/shard_map/ppermute | solution.py:509
  16.9 0.5 near_block.1.after_ref
  17.4 1.6 %collective-permute-start.4 = (bf16[32,1152]{1,0:T(8,128)(2,1)S(1)}, bf16[32,1152]{1,0:T(8,128)(2,1)S(1)}, u32[]{:S(2)}, u32[]{:S(2)}) collective-permute-start(bf16[32,1152]{1,0:T(8,128)(2,1)S(1)} %near_block.1.after_ref), channel_id=1, source_target_pairs={{0,2},{1,3},{2,0},{3,1},{4,6},{5,7},{6,4},{7,5},{8,10},{9,11},{10,... | collective-permute-start | bytes 221192 | tf_op jit(solution)/shard_map/ppermute | solution.py:512
  19.0 1.6 %load_block.2.w_ref = bf16[1024,1024]{1,0:T(8,128)(2,1)S(1)} custom-call(bf16[1024,8192]{1,0:T(8,128)(2,1)} %weight_ref.3, bf16[32,1152]{1,0:T(8,128)(2,1)S(1)} %near_block.1.after_ref), custom_call_target="tpu_custom_call" | custom-call | bytes 2097152 | tf_op jit(solution)/shard_map/load_block/pallas_call | solution.py:252
  20.6 0.2 collective-permute-done.2.from_ref.refs_7_
  20.8 0.5 add_block.2.rest_0_
  21.3 3.8 %collective-permute-start.5 = (bf16[32,1152]{1,0:T(8,128)(2,1)S(1)}, bf16[32,1152]{1,0:T(8,128)(2,1)S(1)}, u32[]{:S(2)}, u32[]{:S(2)}) collective-permute-start(bf16[32,1152]{1,0:T(8,128)(2,1)S(1)} %add_block.2.rest_0_), channel_id=1, source_target_pairs={{0,6},{1,7},{2,4},{3,5},{4,2},{5,3},{6,0},{7,1},{8,14},{9,15},{10,... | collective-permute-start | bytes 221192 | tf_op jit(solution)/shard_map/ppermute | solution.py:512
  25.1 0.5 add_block.3.rest_0_
  25.6 0.5 cross_block.1.after_ref
  26.0 1.8 %collective-permute-start.7 = (bf16[32,1152]{1,0:T(8,128)(2,1)S(1)}, bf16[32,1152]{1,0:T(8,128)(2,1)S(1)}, u32[]{:S(2)}, u32[]{:S(2)}) collective-permute-start(bf16[32,1152]{1,0:T(8,128)(2,1)S(1)} %cross_block.1.after_ref), channel_id=1, source_target_pairs={{0,3},{1,2},{2,1},{3,0},{4,7},{5,6},{6,5},{7,4},{8,11},{9,10},{10,... | collective-permute-start | bytes 221192 | tf_op jit(solution)/shard_map/ppermute | solution.py:515
  27.8 0.5 own_far_block.1.after_ref
  28.2 0.3 collective-permute-start.3
  28.5 1.6 %load_block.3.refs_1_ = bf16[1024,1024]{1,0:T(8,128)(2,1)S(1)} custom-call(bf16[1024,8192]{1,0:T(8,128)(2,1)} %weight_ref.3, bf16[32,1024]{1,0:T(8,128)(2,1)S(1)} %own_far_block.1.after_ref), custom_call_target="tpu_custom_call" | custom-call | bytes 2097152 | tf_op jit(solution)/shard_map/load_block/pallas_call | solution.py:252
  30.2 2.6 %collective-permute-done.3.refs_8_ = bf16[32,1024]{1,0:T(8,128)(2,1)S(1)} collective-permute-done((bf16[32,1024]{1,0:T(8,128)(2,1)S(1)}, bf16[32,1024]{1,0:T(8,128)(2,1)S(1)}, u32[]{:S(2)}, u32[]{:S(2)}) %collective-permute-start.3) | collective-permute-done | bytes 65568 | tf_op jit(solution)/shard_map/ppermute | solution.py:509
  32.8 0.8 %finish.1.refs_0_ = bf16[32,1024]{1,0:T(8,128)(2,1)S(1)} custom-call(bf16[32,1024]{1,0:T(8,128)(2,1)S(1)} %get-tuple-element.40.att_ref.refs_0_, bf16[1024,1024]{1,0:T(8,128)(2,1)S(1)} %load_block.3.refs_1_, s32[32,128]{1,0:T(8,128)S(1)} %get-tuple-element.42.row_slot_ref.refs_2_, s32[8,128]{1,0:T(8,128)S(1)} %get-tuple-element.43.slot_mine_ref.refs_3_, ...), custom_call_target="tpu_custom_call" | custom-call | flops 134217728 | bytes 2097152 | tf_op jit(solution)/shard_map/finish/pallas_call | solution.py:364
  33.6 3.4 %collective-permute-start.13 = (bf16[32,1024]{1,0:T(8,128)(2,1)S(1)}, bf16[32,1024]{1,0:T(8,128)(2,1)S(1)}, u32[]{:S(2)}, u32[]{:S(2)}) collective-permute-start(bf16[32,1024]{1,0:T(8,128)(2,1)S(1)} %finish.1.refs_0_), channel_id=1, source_target_pairs={{0,6},{1,7},{2,4},{3,5},{4,2},{5,3},{6,0},{7,1},{8,14},{9,15},{10,... | collective-permute-start | bytes 196616 | tf_op jit(solution)/shard_map/ppermute | solution.py:512
  37.0 0.5 %collective-permute-start.12 = (bf16[32,1024]{1,0:T(8,128)(2,1)S(1)}, bf16[32,1024]{1,0:T(8,128)(2,1)S(1)}, u32[]{:S(2)}, u32[]{:S(2)}) collective-permute-start(bf16[32,1024]{1,0:T(8,128)(2,1)S(1)} %finish.1.refs_0_), channel_id=1, source_target_pairs={{0,1},{1,0},{2,3},{3,2},{4,5},{5,4},{6,7},{7,6},{8,9},{9,8},{10,11... | collective-permute-start | bytes 196616 | tf_op jit(solution)/shard_map/ppermute | solution.py:515
  37.5 1.3 %collective-permute-start.9 = (bf16[32,1024]{1,0:T(8,128)(2,1)S(1)}, bf16[32,1024]{1,0:T(8,128)(2,1)S(1)}, u32[]{:S(2)}, u32[]{:S(2)}) collective-permute-start(bf16[32,1024]{1,0:T(8,128)(2,1)S(1)} %finish.1.refs_0_), channel_id=1, source_target_pairs={{0,2},{1,3},{2,0},{3,1},{4,6},{5,7},{6,4},{7,5},{8,10},{9,11},{10,... | collective-permute-start | bytes 196616 | tf_op jit(solution)/shard_map/ppermute | solution.py:512
  38.8 1.6 %collective-permute-start.8 = (bf16[32,1024]{1,0:T(8,128)(2,1)S(1)}, bf16[32,1024]{1,0:T(8,128)(2,1)S(1)}, u32[]{:S(2)}, u32[]{:S(2)}) collective-permute-start(bf16[32,1024]{1,0:T(8,128)(2,1)S(1)} %finish.1.refs_0_), channel_id=1, source_target_pairs={{0,3},{1,2},{2,1},{3,0},{4,7},{5,6},{6,5},{7,4},{8,11},{9,10},{10,... | collective-permute-start | bytes 196616 | tf_op jit(solution)/shard_map/ppermute | solution.py:515
  40.5 0.5 %collective-permute-start.14 = (bf16[32,1024]{1,0:T(8,128)(2,1)S(1)}, bf16[32,1024]{1,0:T(8,128)(2,1)S(1)}, u32[]{:S(2)}, u32[]{:S(2)}) collective-permute-start(bf16[32,1024]{1,0:T(8,128)(2,1)S(1)} %collective-permute-done.13.refs_6_), channel_id=1, source_target_pairs={{0,1},{1,0},{2,3},{3,2},{4,5},{5,4},{6,7},{7,6},{8,9},{9,8},{10,11... | collective-permute-start | bytes 196616 | tf_op jit(solution)/shard_map/ppermute | solution.py:509
  41.0 1.4 %collective-permute-done.10.refs_3_ = bf16[32,1024]{1,0:T(8,128)(2,1)S(1)} collective-permute-done((bf16[32,1024]{1,0:T(8,128)(2,1)S(1)}, bf16[32,1024]{1,0:T(8,128)(2,1)S(1)}, u32[]{:S(2)}, u32[]{:S(2)}) %collective-permute-start.10) | collective-permute-done | bytes 65568 | tf_op jit(solution)/shard_map/ppermute | solution.py:512
  42.4 0.8 %collective-permute-start.11 = (bf16[32,1024]{1,0:T(8,128)(2,1)S(1)}, bf16[32,1024]{1,0:T(8,128)(2,1)S(1)}, u32[]{:S(2)}, u32[]{:S(2)}) collective-permute-start(bf16[32,1024]{1,0:T(8,128)(2,1)S(1)} %collective-permute-done.10.refs_3_), channel_id=1, source_target_pairs={{0,1},{1,0},{2,3},{3,2},{4,5},{5,4},{6,7},{7,6},{8,9},{9,8},{10,11... | collective-permute-start | bytes 196616 | tf_op jit(solution)/shard_map/ppermute | solution.py:509
  43.2 0.8 %collective-permute-done.8.refs_1_ = bf16[32,1024]{1,0:T(8,128)(2,1)S(1)} collective-permute-done((bf16[32,1024]{1,0:T(8,128)(2,1)S(1)}, bf16[32,1024]{1,0:T(8,128)(2,1)S(1)}, u32[]{:S(2)}, u32[]{:S(2)}) %collective-permute-start.8) | collective-permute-done | bytes 65568 | tf_op jit(solution)/shard_map/ppermute | solution.py:515
  44.0 0.7 %collective-permute-done.14.refs_7_ = bf16[32,1024]{1,0:T(8,128)(2,1)S(1)} collective-permute-done((bf16[32,1024]{1,0:T(8,128)(2,1)S(1)}, bf16[32,1024]{1,0:T(8,128)(2,1)S(1)}, u32[]{:S(2)}, u32[]{:S(2)}) %collective-permute-start.14) | collective-permute-done | bytes 65568 | tf_op jit(solution)/shard_map/ppermute | solution.py:509
  44.7 1.9 %collective-permute-done.11.refs_4_ = bf16[32,1024]{1,0:T(8,128)(2,1)S(1)} collective-permute-done((bf16[32,1024]{1,0:T(8,128)(2,1)S(1)}, bf16[32,1024]{1,0:T(8,128)(2,1)S(1)}, u32[]{:S(2)}, u32[]{:S(2)}) %collective-permute-start.11) | collective-permute-done | bytes 65568 | tf_op jit(solution)/shard_map/ppermute | solution.py:509
  46.6 0.8 %place.1 = bf16[32,8192]{1,0:T(8,128)(2,1)} custom-call(bf16[32,1024]{1,0:T(8,128)(2,1)S(1)} %finish.1.refs_0_, bf16[32,1024]{1,0:T(8,128)(2,1)S(1)} %collective-permute-done.8.refs_1_, bf16[32,1024]{1,0:T(8,128)(2,1)S(1)} %collective-permute-done.9.refs_2_, bf16[32,1024]{1,0:T(8,128)(2,1)S(1)} %collective-permute-done.10.refs_3_, ...), custom_call_target="tpu_custom_call" | custom-call | bytes 1048576 | tf_op jit(solution)/shard_map/place/pallas_call | solution.py:483
  (15 shorter events, 0.0 us)
Async XLA Ops:
  0.0 3.4 %copy-start = (s32[128]{0:T(128)S(1)}, s32[128]{0:T(128)}, u32[]{:S(2)}) copy-start(s32[128]{0:T(128)} %slot_ref.3) | copy-start | bytes 1540
  0.0 3.4 %collective-permute-start = (s32[32]{0:T(128)}, s32[32]{0:T(128)S(1)}, u32[]{:S(2)}, u32[]{:S(2)}) collective-permute-start(s32[32]{0:T(128)} %ids_ref.1), channel_id=1, source_target_pairs={{0,8},{8,0},{1,9},{9,1},{2,10},{10,2},{3,11},{11,3},{4,12},{12,4},... | collective-permute-start | bytes 392 | tf_op jit(solution)/shard_map/ppermute | solution.py:518
  3.4 4.4 %copy-start.1 = (s32[32]{0:T(128)S(1)}, s32[32]{0:T(128)}, u32[]{:S(2)}) copy-start(s32[32]{0:T(128)} %ids_ref.1) | copy-start | bytes 388
  7.8 5.0 %collective-permute-start.1 = (bf16[2,8,64,1024]{3,2,1,0:T(8,128)(2,1)S(1)}, bf16[2,8,64,1024]{3,2,1,0:T(8,128)(2,1)S(1)}, u32[]{:S(2)}, u32[]{:S(2)}) collective-permute-start(bf16[2,8,64,1024]{3,2,1,0:T(8,128)(2,1)S(1)} %get-tuple-element.45), channel_id=1, source_target_pairs={{0,8},{8,0},{1,9},{9,1},{2,10},{10,2},{3,11},{11,3},{4,12},{12,4},... | collective-permute-start | bytes 6291464 | tf_op jit(solution)/shard_map/ppermute | solution.py:518
  14.0 6.8 %collective-permute-start.2 = (bf16[32,2176]{1,0:T(8,128)(2,1)S(1)}, bf16[32,2176]{1,0:T(8,128)(2,1)S(1)}, u32[]{:S(2)}, u32[]{:S(2)}) collective-permute-start(bf16[32,2176]{1,0:T(8,128)(2,1)S(1)} %get-tuple-element.51), channel_id=1, source_target_pairs={{0,1},{1,0},{2,3},{3,2},{4,5},{5,4},{6,7},{7,6},{8,9},{9,8},{10,11... | collective-permute-start | bytes 417800 | tf_op jit(solution)/shard_map/ppermute | solution.py:509
  17.4 12.8 %collective-permute-start.4 = (bf16[32,1152]{1,0:T(8,128)(2,1)S(1)}, bf16[32,1152]{1,0:T(8,128)(2,1)S(1)}, u32[]{:S(2)}, u32[]{:S(2)}) collective-permute-start(bf16[32,1152]{1,0:T(8,128)(2,1)S(1)} %near_block.1.after_ref), channel_id=1, source_target_pairs={{0,2},{1,3},{2,0},{3,1},{4,6},{5,7},{6,4},{7,5},{8,10},{9,11},{10,... | collective-permute-start | bytes 221192 | tf_op jit(solution)/shard_map/ppermute | solution.py:512
  21.3 11.5 %collective-permute-start.5 = (bf16[32,1152]{1,0:T(8,128)(2,1)S(1)}, bf16[32,1152]{1,0:T(8,128)(2,1)S(1)}, u32[]{:S(2)}, u32[]{:S(2)}) collective-permute-start(bf16[32,1152]{1,0:T(8,128)(2,1)S(1)} %add_block.2.rest_0_), channel_id=1, source_target_pairs={{0,6},{1,7},{2,4},{3,5},{4,2},{5,3},{6,0},{7,1},{8,14},{9,15},{10,... | collective-permute-start | bytes 221192 | tf_op jit(solution)/shard_map/ppermute | solution.py:512
  25.6 7.2 %collective-permute-start.6 = (bf16[32,1152]{1,0:T(8,128)(2,1)S(1)}, bf16[32,1152]{1,0:T(8,128)(2,1)S(1)}, u32[]{:S(2)}, u32[]{:S(2)}) collective-permute-start(bf16[32,1152]{1,0:T(8,128)(2,1)S(1)} %add_block.3.rest_0_), channel_id=1, source_target_pairs={{0,4},{1,5},{2,6},{3,7},{4,0},{5,1},{6,2},{7,3},{8,12},{9,13},{10,... | collective-permute-start | bytes 221192 | tf_op jit(solution)/shard_map/ppermute | solution.py:512
  26.0 6.8 %collective-permute-start.7 = (bf16[32,1152]{1,0:T(8,128)(2,1)S(1)}, bf16[32,1152]{1,0:T(8,128)(2,1)S(1)}, u32[]{:S(2)}, u32[]{:S(2)}) collective-permute-start(bf16[32,1152]{1,0:T(8,128)(2,1)S(1)} %cross_block.1.after_ref), channel_id=1, source_target_pairs={{0,3},{1,2},{2,1},{3,0},{4,7},{5,6},{6,5},{7,4},{8,11},{9,10},{10,... | collective-permute-start | bytes 221192 | tf_op jit(solution)/shard_map/ppermute | solution.py:515
  28.2 4.5 %collective-permute-start.3 = (bf16[32,1024]{1,0:T(8,128)(2,1)S(1)}, bf16[32,1024]{1,0:T(8,128)(2,1)S(1)}, u32[]{:S(2)}, u32[]{:S(2)}) collective-permute-start(bf16[32,1024]{1,0:T(8,128)(2,1)S(1)} %own_far_block.1.after_ref), channel_id=1, source_target_pairs={{0,1},{1,0},{2,3},{3,2},{4,5},{5,4},{6,7},{7,6},{8,9},{9,8},{10,11... | collective-permute-start | bytes 196616 | tf_op jit(solution)/shard_map/ppermute | solution.py:509
  33.6 6.9 %collective-permute-start.13 = (bf16[32,1024]{1,0:T(8,128)(2,1)S(1)}, bf16[32,1024]{1,0:T(8,128)(2,1)S(1)}, u32[]{:S(2)}, u32[]{:S(2)}) collective-permute-start(bf16[32,1024]{1,0:T(8,128)(2,1)S(1)} %finish.1.refs_0_), channel_id=1, source_target_pairs={{0,6},{1,7},{2,4},{3,5},{4,2},{5,3},{6,0},{7,1},{8,14},{9,15},{10,... | collective-permute-start | bytes 196616 | tf_op jit(solution)/shard_map/ppermute | solution.py:512
  37.0 5.4 %collective-permute-start.10 = (bf16[32,1024]{1,0:T(8,128)(2,1)S(1)}, bf16[32,1024]{1,0:T(8,128)(2,1)S(1)}, u32[]{:S(2)}, u32[]{:S(2)}) collective-permute-start(bf16[32,1024]{1,0:T(8,128)(2,1)S(1)} %finish.1.refs_0_), channel_id=1, source_target_pairs={{0,4},{1,5},{2,6},{3,7},{4,0},{5,1},{6,2},{7,3},{8,12},{9,13},{10,... | collective-permute-start | bytes 196616 | tf_op jit(solution)/shard_map/ppermute | solution.py:512
  37.0 6.2 %collective-permute-start.12 = (bf16[32,1024]{1,0:T(8,128)(2,1)S(1)}, bf16[32,1024]{1,0:T(8,128)(2,1)S(1)}, u32[]{:S(2)}, u32[]{:S(2)}) collective-permute-start(bf16[32,1024]{1,0:T(8,128)(2,1)S(1)} %finish.1.refs_0_), channel_id=1, source_target_pairs={{0,1},{1,0},{2,3},{3,2},{4,5},{5,4},{6,7},{7,6},{8,9},{9,8},{10,11... | collective-permute-start | bytes 196616 | tf_op jit(solution)/shard_map/ppermute | solution.py:515
  37.5 5.7 %collective-permute-start.9 = (bf16[32,1024]{1,0:T(8,128)(2,1)S(1)}, bf16[32,1024]{1,0:T(8,128)(2,1)S(1)}, u32[]{:S(2)}, u32[]{:S(2)}) collective-permute-start(bf16[32,1024]{1,0:T(8,128)(2,1)S(1)} %finish.1.refs_0_), channel_id=1, source_target_pairs={{0,2},{1,3},{2,0},{3,1},{4,6},{5,7},{6,4},{7,5},{8,10},{9,11},{10,... | collective-permute-start | bytes 196616 | tf_op jit(solution)/shard_map/ppermute | solution.py:512
  38.8 5.2 %collective-permute-start.8 = (bf16[32,1024]{1,0:T(8,128)(2,1)S(1)}, bf16[32,1024]{1,0:T(8,128)(2,1)S(1)}, u32[]{:S(2)}, u32[]{:S(2)}) collective-permute-start(bf16[32,1024]{1,0:T(8,128)(2,1)S(1)} %finish.1.refs_0_), channel_id=1, source_target_pairs={{0,3},{1,2},{2,1},{3,0},{4,7},{5,6},{6,5},{7,4},{8,11},{9,10},{10,... | collective-permute-start | bytes 196616 | tf_op jit(solution)/shard_map/ppermute | solution.py:515
  40.5 4.3 %collective-permute-start.14 = (bf16[32,1024]{1,0:T(8,128)(2,1)S(1)}, bf16[32,1024]{1,0:T(8,128)(2,1)S(1)}, u32[]{:S(2)}, u32[]{:S(2)}) collective-permute-start(bf16[32,1024]{1,0:T(8,128)(2,1)S(1)} %collective-permute-done.13.refs_6_), channel_id=1, source_target_pairs={{0,1},{1,0},{2,3},{3,2},{4,5},{5,4},{6,7},{7,6},{8,9},{9,8},{10,11... | collective-permute-start | bytes 196616 | tf_op jit(solution)/shard_map/ppermute | solution.py:509
  42.4 4.3 %collective-permute-start.11 = (bf16[32,1024]{1,0:T(8,128)(2,1)S(1)}, bf16[32,1024]{1,0:T(8,128)(2,1)S(1)}, u32[]{:S(2)}, u32[]{:S(2)}) collective-permute-start(bf16[32,1024]{1,0:T(8,128)(2,1)S(1)} %collective-permute-done.10.refs_3_), channel_id=1, source_target_pairs={{0,1},{1,0},{2,3},{3,2},{4,5},{5,4},{6,7},{7,6},{8,9},{9,8},{10,11... | collective-permute-start | bytes 196616 | tf_op jit(solution)/shard_map/ppermute | solution.py:509

commit v8 on v7

--- a/solution.py
+++ b/solution.py
@@ -298,7 +298,7 @@
     )
     far = list(range(n_z - 1, -1, -1))
     early = [(0, k) for k in far[: n_z // 2]]
-    late = [(1, k) for k in far if k] + [(0, k) for k in far[n_z // 2 :] if k]
+    late = [(1, k) for k in far] + [(0, k) for k in far[n_z // 2 :] if k]
     tail, high, high_row, vals_t, out_pages, suf_vals, *early_w = kernel_call(
         functools.partial(suffix_scores_kernel, early),
         "suffix_scores",
@@ -412,6 +412,11 @@
     out_ref[:, width:] = rank_ref[...].astype(BF16)
 
 
+def pair_kernel(att_ref, w_ref, cross_w_ref, rank_ref, out_ref, cross_ref):
+    near_kernel(att_ref, w_ref, rank_ref, out_ref)
+    near_kernel(att_ref, cross_w_ref, rank_ref, cross_ref)
+
+
 def load_kernel(spots, weight_ref, after_ref, out_ref, sem):
     (copy,) = weight_copies(weight_ref, [out_ref], spots, sem)
     copy.start()
@@ -533,20 +538,29 @@
         n_tensor,
         across,
     )
-    far = list(range(n_z - 1, 1, -1))
+    via_y = list(range(n_z - 2, 0, -2))
+    direct = list(range(n_z - 1, 1, -2))
     piece_shape = pltpu.VMEM((rows, width + 128), BF16)
     far_out, rank_own = small_call(
-        functools.partial(far_kernel, len(far)),
+        functools.partial(far_kernel, len(via_y)),
         "far_blocks",
-        [pltpu.VMEM((rows, len(far) * width + 128), BF16), pltpu.VMEM((rows, 128), F32)],
-        [attended, row_slot, slot_mine, own_shrink, other_pages] + [weights[1, k] for k in far],
+        [pltpu.VMEM((rows, len(via_y) * width + 128), BF16), pltpu.VMEM((rows, 128), F32)],
+        [attended, row_slot, slot_mine, own_shrink, other_pages] + [weights[1, k] for k in via_y],
     )
     from_far = along_y(far_out)
-    straight = small_call(near_kernel, "near_block", piece_shape, [attended, weights[0, 1], rank_own])
-    weights[1, 0] = load_block(out_weight, (1, 0), straight, n_tensor)
-    moved = [along_z(straight, 1)]
-    after = []
-    for spot, k in enumerate(far):
+    moved = []
+    for k in direct:
+        straight, cross = small_call(
+            pair_kernel,
+            "pair_blocks",
+            [piece_shape, piece_shape],
+            [attended, weights[0, k], weights[1, k], rank_own],
+        )
+        moved += [along_z(straight, k), along_both(cross, k)]
+    near = small_call(near_kernel, "near_block", piece_shape, [attended, weights[0, 1], rank_own, cross])
+    moved.append(along_z(near, 1))
+    after = [near]
+    for spot, k in enumerate(via_y):
         piece = small_call(
             functools.partial(add_kernel, spot),
             "add_block",

time: 47.8 us -> 47.4 us (level)
  starting transfers between devices: 19.2 us -> 22.1 us
  waiting for transfers between devices: 7.67 us -> 5.6 us
  Pallas kernels: 20.5 us -> 19.4 us
    ppermute x6, starting transfers between devices: 10.2 us -> 13.1 us  [along_z(): return lax.ppermute(x, 'tensor', [(t, t ^ 2 * k) for t in range(n_tensor)])]
    ppermute x4, waiting for transfers between devices: 5.43 us -> 3.64 us  [along_y(): return lax.ppermute(x, 'tensor', [(t, t ^ 1) for t in range(n_tensor)])]
    ppermute x6, waiting for transfers between devices: 1.38 us -> 0.02 us  [along_z(): return lax.ppermute(x, 'tensor', [(t, t ^ 2 * k) for t in range(n_tensor)])]
    ppermute x3 -> x4, starting transfers between devices: 3.89 us -> 2.72 us  [along_both(): lax.ppermute(x, 'tensor', [(t, t ^ 2 * k ^ 1) for t in range(n_tensor)])]
    ppermute x4, starting transfers between devices: 4.58 us -> 5.67 us  [along_y(): return lax.ppermute(x, 'tensor', [(t, t ^ 1) for t in range(n_tensor)])]
    ppermute x3 -> x4, waiting for transfers between devices: 0.85 us -> 1.94 us  [along_both(): lax.ppermute(x, 'tensor', [(t, t ^ 2 * k ^ 1) for t in range(n_tensor)])]
    pallas_call x5 -> x4, Pallas kernels: 15.4 us -> 14.4 us  [kernel_call(): pl.pallas_call(kernel, out_shape=out_shape, in_specs=specs, out_specs=[VM...]
  transfers between devices with their start and end apart: 15 -> 16, of which waited for: 6 -> 4; matrix products, arithmetic and copies ran while one was open for 0% -> 0% of each run, Pallas kernels for 28% -> 27%
where the time goes in v8:
time: 47.4 us; the launch traced here: 47.2 us
  starting transfers between devices  22.1 us (47%)
  Pallas kernels  19.4 us (41%)
  waiting for transfers between devices  5.6 us (12%)
    pallas_call x4, Pallas kernels, kernel_call(): pl.pallas_call(kernel, out_shape=out_shape, in_specs=specs, out_specs=[VM...  14.4 us
    ppermute x6, starting transfers between devices, along_z(): return lax.ppermute(x, 'tensor', [(t, t ^ 2 * k) for t in range(n_tensor)])  13.1 us
    ppermute x4, starting transfers between devices, along_y(): return lax.ppermute(x, 'tensor', [(t, t ^ 1) for t in range(n_tensor)])  5.67 us
    pallas_call x7, Pallas kernels, small_call(): pl.pallas_call(kernel, out_shape=out_shape, in_specs=[VMEM] * len(operand...  4.22 us
    ppermute x4, waiting for transfers between devices, along_y(): return lax.ppermute(x, 'tensor', [(t, t ^ 1) for t in range(n_tensor)])  3.64 us
    ppermute x4, starting transfers between devices, along_both(): lax.ppermute(x, 'tensor', [(t, t ^ 2 * k ^ 1) for t in range(n_tensor)])  2.72 us
    ppermute x4, waiting for transfers between devices, along_both(): lax.ppermute(x, 'tensor', [(t, t ^ 2 * k ^ 1) for t in range(n_tensor)])  1.94 us
  transfers between devices with their start and end apart: 16, of which 4 were waited for; matrix products, arithmetic and copies ran while one was open for 0% of the time, Pallas kernels for 27%

profile of v8, /device:TPU:0, one launch (start us, length us, event | category | flops | bytes accessed | tf_op | source)
XLA Modules:
  0.0 47.2 jit_solution(8788294063316246555)
XLA Ops:
  0.0 0.5 collective-permute-start
  0.5 3.0 %prefix_scores.1 = (bf16[256,128]{1,0:T(8,128)(2,1)S(1)}, f32[8192,256]{1,0:T(8,128)S(1)}, f32[8,256]{1,0:T(8,128)S(1)}, bf16[8192,128]{1,0:T(8,128)(2,1)S(1)}, bf16[32,256,128]{2,1,0:T(8,128)(2,1)S(1)}) custom-call(bf16[32,1024]{1,0:T(8,128)(2,1)} %q_ref.1, bf16[1,2,8192,128]{3,2,1,0:T(8,128)(2,1)} %prefix_ref.1, bf16[32,1,2,256,128]{4,3,2,1,0:T(8,128)(2,1)} %rest_1_.2), custom_call_target="tpu_custom_call" | custom-call | flops 536870912 | bytes 6291456 | tf_op jit(solution)/shard_map/prefix_scores/pallas_call | solution.py:252
  3.4 0.0 copy-start.1
  3.5 4.3 %suffix_scores.1 = (f32[256,256]{1,0:T(8,128)S(1)}, f32[256,128]{1,0:T(8,128)S(1)}, f32[8,256]{1,0:T(8,128)S(1)}, bf16[128,8192]{1,0:T(8,128)(2,1)S(1)}, bf16[2,...) custom-call(s32[32]{0:T(128)S(1)} %collective-permute-done.ids_ref, ...), custom_call_target="tpu_custom_call" | custom-call | flops 536870912 | bytes 7340032 | tf_op jit(solution)/shard_map/suffix_scores/pallas_call | solution.py:252
  7.7 0.2 collective-permute-start.1
  7.9 5.5 %values.1 = (bf16[32,1024]{1,0:T(8,128)(2,1)S(1)}, bf16[8,64,1024]{2,1,0:T(8,128)(2,1)S(1)}, bf16[8,64,1024]{2,1,0:T(8,128)(2,1)S(1)}, s32[32,128]{1,0:T(8,128)S...) custom-call(s32[32]{0:T(128)S(1)} %copy-done.1, ...), custom_call_target="tpu_custom_call" | custom-call | flops 536870912 | bytes 14680064 | tf_op jit(solution)/shard_map/values/pallas_call | solution.py:252
  13.5 0.8 %far_blocks.1 = (bf16[32,1152]{1,0:T(8,128)(2,1)S(1)}, f32[32,128]{1,0:T(8,128)S(1)}) custom-call(bf16[32,1024]{1,0:T(8,128)(2,1)S(1)} %get-tuple-element.43.att_ref.refs_0_, s32[32,128]{1,0:T(8,128)S(1)} %get-tuple-element.46.row_slot_ref.refs_2_, s32[8,128]{1,0:T(8,128)S(1)} %get-tuple-element.47.slot_mine_ref.refs_3_, ...), custom_call_target="tpu_custom_call" | custom-call | flops 134217728 | bytes 2097152 | tf_op jit(solution)/shard_map/far_blocks/pallas_call | solution.py:364
  14.3 3.0 %collective-permute-start.2 = (bf16[32,1152]{1,0:T(8,128)(2,1)S(1)}, bf16[32,1152]{1,0:T(8,128)(2,1)S(1)}, u32[]{:S(2)}, u32[]{:S(2)}) collective-permute-start(bf16[32,1152]{1,0:T(8,128)(2,1)S(1)} %get-tuple-element.53), channel_id=1, source_target_pairs={{0,1},{1,0},{2,3},{3,2},{4,5},{5,4},{6,7},{7,6},{8,9},{9,8},{10,11... | collective-permute-start | bytes 221192 | tf_op jit(solution)/shard_map/ppermute | solution.py:514
  17.3 0.8 %pair_blocks.1 = (bf16[32,1152]{1,0:T(8,128)(2,1)S(1)}, bf16[32,1152]{1,0:T(8,128)(2,1)S(1)}) custom-call(bf16[32,1024]{1,0:T(8,128)(2,1)S(1)} %get-tuple-element.43.att_ref.refs_0_, bf16[1024,1024]{1,0:T(8,128)(2,1)S(1)} %get-tuple-element.55.w_ref, bf16[1024,1024]{1,0:T(8,128)(2,1)S(1)} %get-tuple-element.56.cross_w_ref, ...), custom_call_target="tpu_custom_call" | custom-call | flops 134217728 | bytes 2097152 | tf_op jit(solution)/shard_map/pair_blocks/pallas_call | solution.py:364
  18.1 3.6 %collective-permute-start.4 = (bf16[32,1152]{1,0:T(8,128)(2,1)S(1)}, bf16[32,1152]{1,0:T(8,128)(2,1)S(1)}, u32[]{:S(2)}, u32[]{:S(2)}) collective-permute-start(bf16[32,1152]{1,0:T(8,128)(2,1)S(1)} %get-tuple-element.60), channel_id=1, source_target_pairs={{0,6},{1,7},{2,4},{3,5},{4,2},{5,3},{6,0},{7,1},{8,14},{9,15},{10,... | collective-permute-start | bytes 221192 | tf_op jit(solution)/shard_map/ppermute | solution.py:517
  21.7 0.5 near_block.1.rest_0_
  22.2 0.0 collective-permute-done.2.from_ref.refs_7_
  22.2 0.5 add_block.1.rest_0_
  22.7 4.3 %collective-permute-start.7 = (bf16[32,1152]{1,0:T(8,128)(2,1)S(1)}, bf16[32,1152]{1,0:T(8,128)(2,1)S(1)}, u32[]{:S(2)}, u32[]{:S(2)}) collective-permute-start(bf16[32,1152]{1,0:T(8,128)(2,1)S(1)} %add_block.1.rest_0_), channel_id=1, source_target_pairs={{0,4},{1,5},{2,6},{3,7},{4,0},{5,1},{6,2},{7,3},{8,12},{9,13},{10,... | collective-permute-start | bytes 221192 | tf_op jit(solution)/shard_map/ppermute | solution.py:517
  27.0 0.5 cross_block.1.after_ref
  27.4 1.0 %collective-permute-start.8 = (bf16[32,1152]{1,0:T(8,128)(2,1)S(1)}, bf16[32,1152]{1,0:T(8,128)(2,1)S(1)}, u32[]{:S(2)}, u32[]{:S(2)}) collective-permute-start(bf16[32,1152]{1,0:T(8,128)(2,1)S(1)} %cross_block.1.after_ref), channel_id=1, source_target_pairs={{0,3},{1,2},{2,1},{3,0},{4,7},{5,6},{6,5},{7,4},{8,11},{9,10},{10,... | collective-permute-start | bytes 221192 | tf_op jit(solution)/shard_map/ppermute | solution.py:520
  28.4 0.5 own_far_block.1.after_ref
  28.9 0.6 %collective-permute-start.3 = (bf16[32,1024]{1,0:T(8,128)(2,1)S(1)}, bf16[32,1024]{1,0:T(8,128)(2,1)S(1)}, u32[]{:S(2)}, u32[]{:S(2)}) collective-permute-start(bf16[32,1024]{1,0:T(8,128)(2,1)S(1)} %own_far_block.1.after_ref), channel_id=1, source_target_pairs={{0,1},{1,0},{2,3},{3,2},{4,5},{5,4},{6,7},{7,6},{8,9},{9,8},{10,11... | collective-permute-start | bytes 196616 | tf_op jit(solution)/shard_map/ppermute | solution.py:514
  29.5 1.6 %load_block.1.refs_1_ = bf16[1024,1024]{1,0:T(8,128)(2,1)S(1)} custom-call(bf16[1024,8192]{1,0:T(8,128)(2,1)} %weight_ref.1, bf16[32,1024]{1,0:T(8,128)(2,1)S(1)} %own_far_block.1.after_ref), custom_call_target="tpu_custom_call" | custom-call | bytes 2097152 | tf_op jit(solution)/shard_map/load_block/pallas_call | solution.py:252
  31.2 2.3 %collective-permute-done.3.refs_8_ = bf16[32,1024]{1,0:T(8,128)(2,1)S(1)} collective-permute-done((bf16[32,1024]{1,0:T(8,128)(2,1)S(1)}, bf16[32,1024]{1,0:T(8,128)(2,1)S(1)}, u32[]{:S(2)}, u32[]{:S(2)}) %collective-permute-start.3) | collective-permute-done | bytes 65568 | tf_op jit(solution)/shard_map/ppermute | solution.py:514
  33.4 0.8 %finish.1.refs_0_ = bf16[32,1024]{1,0:T(8,128)(2,1)S(1)} custom-call(bf16[32,1024]{1,0:T(8,128)(2,1)S(1)} %get-tuple-element.43.att_ref.refs_0_, bf16[1024,1024]{1,0:T(8,128)(2,1)S(1)} %load_block.1.refs_1_, s32[32,128]{1,0:T(8,128)S(1)} %get-tuple-element.46.row_slot_ref.refs_2_, s32[8,128]{1,0:T(8,128)S(1)} %get-tuple-element.47.slot_mine_ref.refs_3_, ...), custom_call_target="tpu_custom_call" | custom-call | flops 134217728 | bytes 2097152 | tf_op jit(solution)/shard_map/finish/pallas_call | solution.py:364
  34.2 1.6 %collective-permute-start.14 = (bf16[32,1024]{1,0:T(8,128)(2,1)S(1)}, bf16[32,1024]{1,0:T(8,128)(2,1)S(1)}, u32[]{:S(2)}, u32[]{:S(2)}) collective-permute-start(bf16[32,1024]{1,0:T(8,128)(2,1)S(1)} %finish.1.refs_0_), channel_id=1, source_target_pairs={{0,6},{1,7},{2,4},{3,5},{4,2},{5,3},{6,0},{7,1},{8,14},{9,15},{10,... | collective-permute-start | bytes 196616 | tf_op jit(solution)/shard_map/ppermute | solution.py:517
  35.8 1.8 %collective-permute-start.11 = (bf16[32,1024]{1,0:T(8,128)(2,1)S(1)}, bf16[32,1024]{1,0:T(8,128)(2,1)S(1)}, u32[]{:S(2)}, u32[]{:S(2)}) collective-permute-start(bf16[32,1024]{1,0:T(8,128)(2,1)S(1)} %finish.1.refs_0_), channel_id=1, source_target_pairs={{0,4},{1,5},{2,6},{3,7},{4,0},{5,1},{6,2},{7,3},{8,12},{9,13},{10,... | collective-permute-start | bytes 196616 | tf_op jit(solution)/shard_map/ppermute | solution.py:517
  37.6 0.5 %collective-permute-start.13 = (bf16[32,1024]{1,0:T(8,128)(2,1)S(1)}, bf16[32,1024]{1,0:T(8,128)(2,1)S(1)}, u32[]{:S(2)}, u32[]{:S(2)}) collective-permute-start(bf16[32,1024]{1,0:T(8,128)(2,1)S(1)} %finish.1.refs_0_), channel_id=1, source_target_pairs={{0,1},{1,0},{2,3},{3,2},{4,5},{5,4},{6,7},{7,6},{8,9},{9,8},{10,11... | collective-permute-start | bytes 196616 | tf_op jit(solution)/shard_map/ppermute | solution.py:520
  38.1 1.7 %collective-permute-start.10 = (bf16[32,1024]{1,0:T(8,128)(2,1)S(1)}, bf16[32,1024]{1,0:T(8,128)(2,1)S(1)}, u32[]{:S(2)}, u32[]{:S(2)}) collective-permute-start(bf16[32,1024]{1,0:T(8,128)(2,1)S(1)} %finish.1.refs_0_), channel_id=1, source_target_pairs={{0,2},{1,3},{2,0},{3,1},{4,6},{5,7},{6,4},{7,5},{8,10},{9,11},{10,... | collective-permute-start | bytes 196616 | tf_op jit(solution)/shard_map/ppermute | solution.py:517
  39.8 1.2 %collective-permute-start.9 = (bf16[32,1024]{1,0:T(8,128)(2,1)S(1)}, bf16[32,1024]{1,0:T(8,128)(2,1)S(1)}, u32[]{:S(2)}, u32[]{:S(2)}) collective-permute-start(bf16[32,1024]{1,0:T(8,128)(2,1)S(1)} %finish.1.refs_0_), channel_id=1, source_target_pairs={{0,3},{1,2},{2,1},{3,0},{4,7},{5,6},{6,5},{7,4},{8,11},{9,10},{10,... | collective-permute-start | bytes 196616 | tf_op jit(solution)/shard_map/ppermute | solution.py:520
  41.1 1.1 %collective-permute-start.15 = (bf16[32,1024]{1,0:T(8,128)(2,1)S(1)}, bf16[32,1024]{1,0:T(8,128)(2,1)S(1)}, u32[]{:S(2)}, u32[]{:S(2)}) collective-permute-start(bf16[32,1024]{1,0:T(8,128)(2,1)S(1)} %collective-permute-done.14.refs_6_), channel_id=1, source_target_pairs={{0,1},{1,0},{2,3},{3,2},{4,5},{5,4},{6,7},{7,6},{8,9},{9,8},{10,11... | collective-permute-start | bytes 196616 | tf_op jit(solution)/shard_map/ppermute | solution.py:514
  42.1 1.0 %collective-permute-start.12 = (bf16[32,1024]{1,0:T(8,128)(2,1)S(1)}, bf16[32,1024]{1,0:T(8,128)(2,1)S(1)}, u32[]{:S(2)}, u32[]{:S(2)}) collective-permute-start(bf16[32,1024]{1,0:T(8,128)(2,1)S(1)} %collective-permute-done.11.refs_3_), channel_id=1, source_target_pairs={{0,1},{1,0},{2,3},{3,2},{4,5},{5,4},{6,7},{7,6},{8,9},{9,8},{10,11... | collective-permute-start | bytes 196616 | tf_op jit(solution)/shard_map/ppermute | solution.py:514
  43.1 1.9 %collective-permute-done.9.refs_1_ = bf16[32,1024]{1,0:T(8,128)(2,1)S(1)} collective-permute-done((bf16[32,1024]{1,0:T(8,128)(2,1)S(1)}, bf16[32,1024]{1,0:T(8,128)(2,1)S(1)}, u32[]{:S(2)}, u32[]{:S(2)}) %collective-permute-start.9) | collective-permute-done | bytes 65568 | tf_op jit(solution)/shard_map/ppermute | solution.py:520
  45.0 0.7 %collective-permute-done.15.refs_7_ = bf16[32,1024]{1,0:T(8,128)(2,1)S(1)} collective-permute-done((bf16[32,1024]{1,0:T(8,128)(2,1)S(1)}, bf16[32,1024]{1,0:T(8,128)(2,1)S(1)}, u32[]{:S(2)}, u32[]{:S(2)}) %collective-permute-start.15) | collective-permute-done | bytes 65568 | tf_op jit(solution)/shard_map/ppermute | solution.py:514
  45.7 0.7 %collective-permute-done.12.refs_4_ = bf16[32,1024]{1,0:T(8,128)(2,1)S(1)} collective-permute-done((bf16[32,1024]{1,0:T(8,128)(2,1)S(1)}, bf16[32,1024]{1,0:T(8,128)(2,1)S(1)}, u32[]{:S(2)}, u32[]{:S(2)}) %collective-permute-start.12) | collective-permute-done | bytes 65568 | tf_op jit(solution)/shard_map/ppermute | solution.py:514
  46.4 0.8 %place.1 = bf16[32,8192]{1,0:T(8,128)(2,1)} custom-call(bf16[32,1024]{1,0:T(8,128)(2,1)S(1)} %finish.1.refs_0_, bf16[32,1024]{1,0:T(8,128)(2,1)S(1)} %collective-permute-done.9.refs_1_, bf16[32,1024]{1,0:T(8,128)(2,1)S(1)} %collective-permute-done.10.refs_2_, bf16[32,1024]{1,0:T(8,128)(2,1)S(1)} %collective-permute-done.11.refs_3_, ...), custom_call_target="tpu_custom_call" | custom-call | bytes 1048576 | tf_op jit(solution)/shard_map/place/pallas_call | solution.py:488
  (16 shorter events, 0.0 us)
Async XLA Ops:
  0.0 3.4 %copy-start = (s32[128]{0:T(128)S(1)}, s32[128]{0:T(128)}, u32[]{:S(2)}) copy-start(s32[128]{0:T(128)} %slot_ref.3) | copy-start | bytes 1540
  0.0 3.4 %collective-permute-start = (s32[32]{0:T(128)}, s32[32]{0:T(128)S(1)}, u32[]{:S(2)}, u32[]{:S(2)}) collective-permute-start(s32[32]{0:T(128)} %ids_ref.1), channel_id=1, source_target_pairs={{0,8},{8,0},{1,9},{9,1},{2,10},{10,2},{3,11},{11,3},{4,12},{12,4},... | collective-permute-start | bytes 392 | tf_op jit(solution)/shard_map/ppermute | solution.py:523
  3.4 4.5 %copy-start.1 = (s32[32]{0:T(128)S(1)}, s32[32]{0:T(128)}, u32[]{:S(2)}) copy-start(s32[32]{0:T(128)} %ids_ref.1) | copy-start | bytes 388
  7.7 5.7 %collective-permute-start.1 = (bf16[2,8,64,1024]{3,2,1,0:T(8,128)(2,1)S(1)}, bf16[2,8,64,1024]{3,2,1,0:T(8,128)(2,1)S(1)}, u32[]{:S(2)}, u32[]{:S(2)}) collective-permute-start(bf16[2,8,64,1024]{3,2,1,0:T(8,128)(2,1)S(1)} %get-tuple-element.49), channel_id=1, source_target_pairs={{0,8},{8,0},{1,9},{9,1},{2,10},{10,2},{3,11},{11,3},{4,12},{12,4},... | collective-permute-start | bytes 6291464 | tf_op jit(solution)/shard_map/ppermute | solution.py:523
  14.3 7.9 %collective-permute-start.2 = (bf16[32,1152]{1,0:T(8,128)(2,1)S(1)}, bf16[32,1152]{1,0:T(8,128)(2,1)S(1)}, u32[]{:S(2)}, u32[]{:S(2)}) collective-permute-start(bf16[32,1152]{1,0:T(8,128)(2,1)S(1)} %get-tuple-element.53), channel_id=1, source_target_pairs={{0,1},{1,0},{2,3},{3,2},{4,5},{5,4},{6,7},{7,6},{8,9},{9,8},{10,11... | collective-permute-start | bytes 221192 | tf_op jit(solution)/shard_map/ppermute | solution.py:514
  18.1 10.8 %collective-permute-start.4 = (bf16[32,1152]{1,0:T(8,128)(2,1)S(1)}, bf16[32,1152]{1,0:T(8,128)(2,1)S(1)}, u32[]{:S(2)}, u32[]{:S(2)}) collective-permute-start(bf16[32,1152]{1,0:T(8,128)(2,1)S(1)} %get-tuple-element.60), channel_id=1, source_target_pairs={{0,6},{1,7},{2,4},{3,5},{4,2},{5,3},{6,0},{7,1},{8,14},{9,15},{10,... | collective-permute-start | bytes 221192 | tf_op jit(solution)/shard_map/ppermute | solution.py:517
  21.7 9.4 %collective-permute-start.5 = (bf16[32,1152]{1,0:T(8,128)(2,1)S(1)}, bf16[32,1152]{1,0:T(8,128)(2,1)S(1)}, u32[]{:S(2)}, u32[]{:S(2)}) collective-permute-start(bf16[32,1152]{1,0:T(8,128)(2,1)S(1)} %get-tuple-element.57.rest_0_), channel_id=1, source_target_pairs={{0,7},{1,6},{2,5},{3,4},{4,3},{5,2},{6,1},{7,0},{8,15},{9,14},{10,... | collective-permute-start | bytes 221192 | tf_op jit(solution)/shard_map/ppermute | solution.py:520
  22.2 9.0 %collective-permute-start.6 = (bf16[32,1152]{1,0:T(8,128)(2,1)S(1)}, bf16[32,1152]{1,0:T(8,128)(2,1)S(1)}, u32[]{:S(2)}, u32[]{:S(2)}) collective-permute-start(bf16[32,1152]{1,0:T(8,128)(2,1)S(1)} %near_block.1.rest_0_), channel_id=1, source_target_pairs={{0,2},{1,3},{2,0},{3,1},{4,6},{5,7},{6,4},{7,5},{8,10},{9,11},{10,... | collective-permute-start | bytes 221192 | tf_op jit(solution)/shard_map/ppermute | solution.py:517
  22.7 10.8 %collective-permute-start.7 = (bf16[32,1152]{1,0:T(8,128)(2,1)S(1)}, bf16[32,1152]{1,0:T(8,128)(2,1)S(1)}, u32[]{:S(2)}, u32[]{:S(2)}) collective-permute-start(bf16[32,1152]{1,0:T(8,128)(2,1)S(1)} %add_block.1.rest_0_), channel_id=1, source_target_pairs={{0,4},{1,5},{2,6},{3,7},{4,0},{5,1},{6,2},{7,3},{8,12},{9,13},{10,... | collective-permute-start | bytes 221192 | tf_op jit(solution)/shard_map/ppermute | solution.py:517
  27.4 6.0 %collective-permute-start.8 = (bf16[32,1152]{1,0:T(8,128)(2,1)S(1)}, bf16[32,1152]{1,0:T(8,128)(2,1)S(1)}, u32[]{:S(2)}, u32[]{:S(2)}) collective-permute-start(bf16[32,1152]{1,0:T(8,128)(2,1)S(1)} %cross_block.1.after_ref), channel_id=1, source_target_pairs={{0,3},{1,2},{2,1},{3,0},{4,7},{5,6},{6,5},{7,4},{8,11},{9,10},{10,... | collective-permute-start | bytes 221192 | tf_op jit(solution)/shard_map/ppermute | solution.py:520
  28.9 4.5 %collective-permute-start.3 = (bf16[32,1024]{1,0:T(8,128)(2,1)S(1)}, bf16[32,1024]{1,0:T(8,128)(2,1)S(1)}, u32[]{:S(2)}, u32[]{:S(2)}) collective-permute-start(bf16[32,1024]{1,0:T(8,128)(2,1)S(1)} %own_far_block.1.after_ref), channel_id=1, source_target_pairs={{0,1},{1,0},{2,3},{3,2},{4,5},{5,4},{6,7},{7,6},{8,9},{9,8},{10,11... | collective-permute-start | bytes 196616 | tf_op jit(solution)/shard_map/ppermute | solution.py:514
  34.2 6.8 %collective-permute-start.14 = (bf16[32,1024]{1,0:T(8,128)(2,1)S(1)}, bf16[32,1024]{1,0:T(8,128)(2,1)S(1)}, u32[]{:S(2)}, u32[]{:S(2)}) collective-permute-start(bf16[32,1024]{1,0:T(8,128)(2,1)S(1)} %finish.1.refs_0_), channel_id=1, source_target_pairs={{0,6},{1,7},{2,4},{3,5},{4,2},{5,3},{6,0},{7,1},{8,14},{9,15},{10,... | collective-permute-start | bytes 196616 | tf_op jit(solution)/shard_map/ppermute | solution.py:517
  35.8 6.4 %collective-permute-start.11 = (bf16[32,1024]{1,0:T(8,128)(2,1)S(1)}, bf16[32,1024]{1,0:T(8,128)(2,1)S(1)}, u32[]{:S(2)}, u32[]{:S(2)}) collective-permute-start(bf16[32,1024]{1,0:T(8,128)(2,1)S(1)} %finish.1.refs_0_), channel_id=1, source_target_pairs={{0,4},{1,5},{2,6},{3,7},{4,0},{5,1},{6,2},{7,3},{8,12},{9,13},{10,... | collective-permute-start | bytes 196616 | tf_op jit(solution)/shard_map/ppermute | solution.py:517
  37.6 5.5 %collective-permute-start.13 = (bf16[32,1024]{1,0:T(8,128)(2,1)S(1)}, bf16[32,1024]{1,0:T(8,128)(2,1)S(1)}, u32[]{:S(2)}, u32[]{:S(2)}) collective-permute-start(bf16[32,1024]{1,0:T(8,128)(2,1)S(1)} %finish.1.refs_0_), channel_id=1, source_target_pairs={{0,1},{1,0},{2,3},{3,2},{4,5},{5,4},{6,7},{7,6},{8,9},{9,8},{10,11... | collective-permute-start | bytes 196616 | tf_op jit(solution)/shard_map/ppermute | solution.py:520
  38.1 5.0 %collective-permute-start.10 = (bf16[32,1024]{1,0:T(8,128)(2,1)S(1)}, bf16[32,1024]{1,0:T(8,128)(2,1)S(1)}, u32[]{:S(2)}, u32[]{:S(2)}) collective-permute-start(bf16[32,1024]{1,0:T(8,128)(2,1)S(1)} %finish.1.refs_0_), channel_id=1, source_target_pairs={{0,2},{1,3},{2,0},{3,1},{4,6},{5,7},{6,4},{7,5},{8,10},{9,11},{10,... | collective-permute-start | bytes 196616 | tf_op jit(solution)/shard_map/ppermute | solution.py:517
  39.8 5.2 %collective-permute-start.9 = (bf16[32,1024]{1,0:T(8,128)(2,1)S(1)}, bf16[32,1024]{1,0:T(8,128)(2,1)S(1)}, u32[]{:S(2)}, u32[]{:S(2)}) collective-permute-start(bf16[32,1024]{1,0:T(8,128)(2,1)S(1)} %finish.1.refs_0_), channel_id=1, source_target_pairs={{0,3},{1,2},{2,1},{3,0},{4,7},{5,6},{6,5},{7,4},{8,11},{9,10},{10,... | collective-permute-start | bytes 196616 | tf_op jit(solution)/shard_map/ppermute | solution.py:520
  41.1 4.6 %collective-permute-start.15 = (bf16[32,1024]{1,0:T(8,128)(2,1)S(1)}, bf16[32,1024]{1,0:T(8,128)(2,1)S(1)}, u32[]{:S(2)}, u32[]{:S(2)}) collective-permute-start(bf16[32,1024]{1,0:T(8,128)(2,1)S(1)} %collective-permute-done.14.refs_6_), channel_id=1, source_target_pairs={{0,1},{1,0},{2,3},{3,2},{4,5},{5,4},{6,7},{7,6},{8,9},{9,8},{10,11... | collective-permute-start | bytes 196616 | tf_op jit(solution)/shard_map/ppermute | solution.py:514
  42.1 4.3 %collective-permute-start.12 = (bf16[32,1024]{1,0:T(8,128)(2,1)S(1)}, bf16[32,1024]{1,0:T(8,128)(2,1)S(1)}, u32[]{:S(2)}, u32[]{:S(2)}) collective-permute-start(bf16[32,1024]{1,0:T(8,128)(2,1)S(1)} %collective-permute-done.11.refs_3_), channel_id=1, source_target_pairs={{0,1},{1,0},{2,3},{3,2},{4,5},{5,4},{6,7},{7,6},{8,9},{9,8},{10,11... | collective-permute-start | bytes 196616 | tf_op jit(solution)/shard_map/ppermute | solution.py:514

commit v9 on v7

--- a/solution.py
+++ b/solution.py
@@ -297,8 +297,8 @@
         6 * MIB,
     )
     far = list(range(n_z - 1, -1, -1))
-    early = [(0, k) for k in far[: n_z // 2]]
-    late = [(1, k) for k in far if k] + [(0, k) for k in far[n_z // 2 :] if k]
+    early = [(0, k) for k in far[: n_z // 4]]
+    late = [(1, k) for k in far if k > 1] + [(0, k) for k in far[n_z // 4 :] if k > 1]
     tail, high, high_row, vals_t, out_pages, suf_vals, *early_w = kernel_call(
         functools.partial(suffix_scores_kernel, early),
         "suffix_scores",
@@ -405,11 +405,39 @@
     out_ref[:, n * width :] = picked.astype(BF16)
 
 
-def near_kernel(att_ref, w_ref, rank_ref, *rest):
-    out_ref = rest[-1]
-    width = w_ref.shape[1]
-    out_ref[:, :width] = nn_dot(att_ref[...], w_ref[...]).astype(BF16)
-    out_ref[:, width:] = rank_ref[...].astype(BF16)
+def near_kernel(spots, att_ref, rank_ref, weight_ref, *rest):
+    outs, (wbuf, sem) = rest[: len(spots)], rest[len(spots) :]
+    width = wbuf.shape[2]
+    copies = weight_copies(weight_ref, [wbuf.at[i] for i in range(len(spots))], spots, sem)
+    for c in copies:
+        c.start()
+    attended = att_ref[...]
+    rank = rank_ref[...].astype(BF16)
+    for i, out in enumerate(outs):
+        copies[i].wait()
+        out[:, :width] = nn_dot(attended, wbuf[i]).astype(BF16)
+        if out.shape[1] > width:
+            out[:, width:] = rank
+
+
+def near_blocks(spots, columns, attended, rank_own, weight, after, n_tensor):
+    rows = attended.shape[0]
+    width = weight.shape[1] // n_tensor
+
+    def kernel(att_ref, rank_ref, weight_ref, *rest):
+        near_kernel(spots, att_ref, rank_ref, weight_ref, *rest[len(after) :])
+
+    return kernel_call(
+        kernel,
+        "near_blocks",
+        [pltpu.VMEM((rows, columns), BF16)] * len(spots),
+        [VMEM, VMEM, ANY] + [VMEM] * len(after),
+        [pltpu.VMEM((len(spots), weight.shape[0], width), BF16), pltpu.SemaphoreType.DMA((len(spots),))],
+        [attended, rank_own, in_hbm(weight)] + after,
+        8,
+        1 << 27,
+        2 * len(spots) * MIB,
+    )
 
 
 def load_kernel(spots, weight_ref, after_ref, out_ref, sem):
@@ -430,10 +458,6 @@
         0,
         2 * MIB,
     )[0]
-
-
-def block_kernel(att_ref, w_ref, after_ref, out_ref):
-    out_ref[...] = nn_dot(att_ref[...], w_ref[...]).astype(BF16)
 
 
 def add_kernel(spot, att_ref, w_ref, from_ref, rank_ref, *rest):
@@ -542,9 +566,10 @@
         [attended, row_slot, slot_mine, own_shrink, other_pages] + [weights[1, k] for k in far],
     )
     from_far = along_y(far_out)
-    straight = small_call(near_kernel, "near_block", piece_shape, [attended, weights[0, 1], rank_own])
-    weights[1, 0] = load_block(out_weight, (1, 0), straight, n_tensor)
-    moved = [along_z(straight, 1)]
+    straight, cross = near_blocks(
+        [(0, 1), (1, 1)], width + 128, attended, rank_own, out_weight, [], n_tensor
+    )
+    moved = [along_z(straight, 1), along_both(cross, 1)]
     after = []
     for spot, k in enumerate(far):
         piece = small_call(
@@ -555,11 +580,7 @@
         )
         moved.append(along_z(piece, k))
         after = [piece]
-    cross = small_call(near_kernel, "cross_block", piece_shape, [attended, weights[1, 1], rank_own, piece])
-    moved.append(along_both(cross, 1))
-    own_far = small_call(
-        block_kernel, "own_far_block", pltpu.VMEM((rows, width), BF16), [attended, weights[1, 0], cross]
-    )
+    (own_far,) = near_blocks([(1, 0)], width, attended, rank_own, out_weight, [piece], n_tensor)
     from_own = along_y(own_far)
     weights[0, 0] = load_block(out_weight, (0, 0), own_far, n_tensor)
     result = small_call(

time: 47.8 us -> 46.3 us (0.969)
  waiting for transfers between devices: 7.67 us -> 5.76 us
  Pallas kernels: 20.5 us -> 21 us
    ppermute x4, waiting for transfers between devices: 5.43 us -> 2.92 us  [along_y(): return lax.ppermute(x, 'tensor', [(t, t ^ 1) for t in range(n_tensor)])]
    pallas_call x5 -> x6, Pallas kernels: 15.4 us -> 17.3 us  [kernel_call(): pl.pallas_call(kernel, out_shape=out_shape, in_specs=specs, out_specs=[VM...]
    ppermute x4, starting transfers between devices: 4.58 us -> 6.47 us  [along_y(): return lax.ppermute(x, 'tensor', [(t, t ^ 1) for t in range(n_tensor)])]
    ppermute x3, starting transfers between devices: 3.89 us -> 2.11 us  [along_both(): lax.ppermute(x, 'tensor', [(t, t ^ 2 * k ^ 1) for t in range(n_tensor)])]
    pallas_call x7 -> x4, Pallas kernels: 4.21 us -> 2.83 us  [small_call(): pl.pallas_call(kernel, out_shape=out_shape, in_specs=[VMEM] * len(operand...]
    ppermute x3, waiting for transfers between devices: 0.85 us -> 2 us  [along_both(): lax.ppermute(x, 'tensor', [(t, t ^ 2 * k ^ 1) for t in range(n_tensor)])]
    ppermute x6, waiting for transfers between devices: 1.38 us -> 0.83 us  [along_z(): return lax.ppermute(x, 'tensor', [(t, t ^ 2 * k) for t in range(n_tensor)])]
  transfers between devices with their start and end apart: 15 -> 15, of which waited for: 6 -> 6; matrix products, arithmetic and copies ran while one was open for 0% -> 0% of each run, Pallas kernels for 28% -> 32%
where the time goes in v9:
time: 46.3 us; the launch traced here: 46.2 us
  Pallas kernels  21 us (45%)
  starting transfers between devices  19.3 us (42%)
  waiting for transfers between devices  5.76 us (12%)
    pallas_call x6, Pallas kernels, kernel_call(): pl.pallas_call(kernel, out_shape=out_shape, in_specs=specs, out_specs=[VM...  17.3 us
    ppermute x6, starting transfers between devices, along_z(): return lax.ppermute(x, 'tensor', [(t, t ^ 2 * k) for t in range(n_tensor)])  10.1 us
    ppermute x4, starting transfers between devices, along_y(): return lax.ppermute(x, 'tensor', [(t, t ^ 1) for t in range(n_tensor)])  6.47 us
    ppermute x4, waiting for transfers between devices, along_y(): return lax.ppermute(x, 'tensor', [(t, t ^ 1) for t in range(n_tensor)])  2.92 us
    pallas_call x4, Pallas kernels, small_call(): pl.pallas_call(kernel, out_shape=out_shape, in_specs=[VMEM] * len(operand...  2.83 us
    ppermute x3, starting transfers between devices, along_both(): lax.ppermute(x, 'tensor', [(t, t ^ 2 * k ^ 1) for t in range(n_tensor)])  2.11 us
    ppermute x3, waiting for transfers between devices, along_both(): lax.ppermute(x, 'tensor', [(t, t ^ 2 * k ^ 1) for t in range(n_tensor)])  2 us
  transfers between devices with their start and end apart: 15, of which 6 were waited for; matrix products, arithmetic and copies ran while one was open for 0% of the time, Pallas kernels for 32%

profile of v9, /device:TPU:0, one launch (start us, length us, event | category | flops | bytes accessed | tf_op | source)
XLA Modules:
  0.0 46.2 jit_solution(7857481347711212610)
XLA Ops:
  0.0 0.5 collective-permute-start
  0.5 3.0 %prefix_scores.1 = (bf16[256,128]{1,0:T(8,128)(2,1)S(1)}, f32[8192,256]{1,0:T(8,128)S(1)}, f32[8,256]{1,0:T(8,128)S(1)}, bf16[8192,128]{1,0:T(8,128)(2,1)S(1)}, bf16[32,256,128]{2,1,0:T(8,128)(2,1)S(1)}) custom-call(bf16[32,1024]{1,0:T(8,128)(2,1)} %q_ref.1, bf16[1,2,8192,128]{3,2,1,0:T(8,128)(2,1)} %prefix_ref.1, bf16[32,1,2,256,128]{4,3,2,1,0:T(8,128)(2,1)} %rest_1_.2), custom_call_target="tpu_custom_call" | custom-call | flops 536870912 | bytes 6291456 | tf_op jit(solution)/shard_map/prefix_scores/pallas_call | solution.py:252
  3.5 3.7 %suffix_scores.1 = (f32[256,256]{1,0:T(8,128)S(1)}, f32[256,128]{1,0:T(8,128)S(1)}, f32[8,256]{1,0:T(8,128)S(1)}, bf16[128,8192]{1,0:T(8,128)(2,1)S(1)}, bf16[2,...) custom-call(s32[32]{0:T(128)S(1)} %collective-permute-done.ids_ref, ...), custom_call_target="tpu_custom_call" | custom-call | flops 536870912 | bytes 7340032 | tf_op jit(solution)/shard_map/suffix_scores/pallas_call | solution.py:252
  7.1 0.1 collective-permute-start.1
  7.3 4.3 %values.1 = (bf16[32,1024]{1,0:T(8,128)(2,1)S(1)}, bf16[8,64,1024]{2,1,0:T(8,128)(2,1)S(1)}, bf16[8,64,1024]{2,1,0:T(8,128)(2,1)S(1)}, s32[32,128]{1,0:T(8,128)S...) custom-call(s32[32]{0:T(128)S(1)} %copy-done.1, ...), custom_call_target="tpu_custom_call" | custom-call | flops 536870912 | bytes 14680064 | tf_op jit(solution)/shard_map/values/pallas_call | solution.py:252
  11.6 1.1 %far_blocks.1 = (bf16[32,2176]{1,0:T(8,128)(2,1)S(1)}, f32[32,128]{1,0:T(8,128)S(1)}) custom-call(bf16[32,1024]{1,0:T(8,128)(2,1)S(1)} %get-tuple-element.40.att_ref.refs_0_, s32[32,128]{1,0:T(8,128)S(1)} %get-tuple-element.41.row_slot_ref.refs_2_, s32[8,128]{1,0:T(8,128)S(1)} %get-tuple-element.42.slot_mine_ref.refs_3_, ...), custom_call_target="tpu_custom_call" | custom-call | flops 134217728 | bytes 2097152 | tf_op jit(solution)/shard_map/far_blocks/pallas_call | solution.py:364
  12.7 3.0 %collective-permute-start.2 = (bf16[32,2176]{1,0:T(8,128)(2,1)S(1)}, bf16[32,2176]{1,0:T(8,128)(2,1)S(1)}, u32[]{:S(2)}, u32[]{:S(2)}) collective-permute-start(bf16[32,2176]{1,0:T(8,128)(2,1)S(1)} %get-tuple-element.49), channel_id=1, source_target_pairs={{0,1},{1,0},{2,3},{3,2},{4,5},{5,4},{6,7},{7,6},{8,9},{9,8},{10,11... | collective-permute-start | bytes 417800 | tf_op jit(solution)/shard_map/ppermute | solution.py:533
  15.7 2.7 %near_blocks.3 = (bf16[32,1152]{1,0:T(8,128)(2,1)S(1)}, bf16[32,1152]{1,0:T(8,128)(2,1)S(1)}) custom-call(bf16[32,1024]{1,0:T(8,128)(2,1)S(1)} %get-tuple-element.40.att_ref.refs_0_, f32[32,128]{1,0:T(8,128)S(1)} %get-tuple-element.47.rank_ref.refs_6_, bf16[1024,8192]{1,0:T(8,128)(2,1)} %weight_ref.5), custom_call_target="tpu_custom_call" | custom-call | flops 134217728 | bytes 4194304 | tf_op jit(solution)/shard_map/near_blocks/pallas_call | solution.py:252
  18.5 1.6 %collective-permute-start.4 = (bf16[32,1152]{1,0:T(8,128)(2,1)S(1)}, bf16[32,1152]{1,0:T(8,128)(2,1)S(1)}, u32[]{:S(2)}, u32[]{:S(2)}) collective-permute-start(bf16[32,1152]{1,0:T(8,128)(2,1)S(1)} %get-tuple-element.53), channel_id=1, source_target_pairs={{0,2},{1,3},{2,0},{3,1},{4,6},{5,7},{6,4},{7,5},{8,10},{9,11},{10,... | collective-permute-start | bytes 221192 | tf_op jit(solution)/shard_map/ppermute | solution.py:536
  20.1 0.0 collective-permute-start.5
  20.1 0.5 %add_block.2.rest_0_ = bf16[32,1152]{1,0:T(8,128)(2,1)S(1)} custom-call(bf16[32,1024]{1,0:T(8,128)(2,1)S(1)} %get-tuple-element.40.att_ref.refs_0_, bf16[1024,1024]{1,0:T(8,128)(2,1)S(1)} %get-tuple-element.50.w_ref, bf16[32,2176]{1,0:T(8,128)(2,1)S(1)} %collective-permute-done.2.from_ref.refs_7_, f32[32,128]{1,0:T(8,128)S(1)} %get-tuple-element.47.rank_ref.refs_6_), custom_call_target="tpu_custom_call" | custom-call | flops 134217728 | bytes 2097152 | tf_op jit(solution)/shard_map/add_block/pallas_call | solution.py:364
  20.6 4.0 %collective-permute-start.6 = (bf16[32,1152]{1,0:T(8,128)(2,1)S(1)}, bf16[32,1152]{1,0:T(8,128)(2,1)S(1)}, u32[]{:S(2)}, u32[]{:S(2)}) collective-permute-start(bf16[32,1152]{1,0:T(8,128)(2,1)S(1)} %add_block.2.rest_0_), channel_id=1, source_target_pairs={{0,6},{1,7},{2,4},{3,5},{4,2},{5,3},{6,0},{7,1},{8,14},{9,15},{10,... | collective-permute-start | bytes 221192 | tf_op jit(solution)/shard_map/ppermute | solution.py:536
  24.6 0.5 %add_block.3.rest_0_ = bf16[32,1152]{1,0:T(8,128)(2,1)S(1)} custom-call(bf16[32,1024]{1,0:T(8,128)(2,1)S(1)} %get-tuple-element.40.att_ref.refs_0_, bf16[1024,1024]{1,0:T(8,128)(2,1)S(1)} %get-tuple-element.48.w_ref, bf16[32,2176]{1,0:T(8,128)(2,1)S(1)} %collective-permute-done.2.from_ref.refs_7_, f32[32,128]{1,0:T(8,128)S(1)} %get-tuple-element.47.rank_ref.refs_6_, ...), custom_call_target="tpu_custom_call" | custom-call | flops 134217728 | bytes 2097152 | tf_op jit(solution)/shard_map/add_block/pallas_call | solution.py:364
  25.0 0.0 collective-permute-start.7
  25.1 2.1 %near_blocks.2.after_ref = bf16[32,1024]{1,0:T(8,128)(2,1)S(1)} custom-call(bf16[32,1024]{1,0:T(8,128)(2,1)S(1)} %get-tuple-element.40.att_ref.refs_0_, f32[32,128]{1,0:T(8,128)S(1)} %get-tuple-element.47.rank_ref.refs_6_, bf16[1024,8192]{1,0:T(8,128)(2,1)} %weight_ref.5, bf16[32,1152]{1,0:T(8,128)(2,1)S(1)} %add_block.3.rest_0_), custom_call_target="tpu_custom_call" | custom-call | flops 134217728 | bytes 2097152 | tf_op jit(solution)/shard_map/near_blocks/pallas_call | solution.py:252
  27.2 1.6 %collective-permute-start.3 = (bf16[32,1024]{1,0:T(8,128)(2,1)S(1)}, bf16[32,1024]{1,0:T(8,128)(2,1)S(1)}, u32[]{:S(2)}, u32[]{:S(2)}) collective-permute-start(bf16[32,1024]{1,0:T(8,128)(2,1)S(1)} %near_blocks.2.after_ref), channel_id=1, source_target_pairs={{0,1},{1,0},{2,3},{3,2},{4,5},{5,4},{6,7},{7,6},{8,9},{9,8},{10,11... | collective-permute-start | bytes 196616 | tf_op jit(solution)/shard_map/ppermute | solution.py:533
  28.7 1.6 %load_block.1.refs_1_ = bf16[1024,1024]{1,0:T(8,128)(2,1)S(1)} custom-call(bf16[1024,8192]{1,0:T(8,128)(2,1)} %weight_ref.5, bf16[32,1024]{1,0:T(8,128)(2,1)S(1)} %near_blocks.2.after_ref), custom_call_target="tpu_custom_call" | custom-call | bytes 2097152 | tf_op jit(solution)/shard_map/load_block/pallas_call | solution.py:252
  30.4 1.1 %collective-permute-done.3.refs_8_ = bf16[32,1024]{1,0:T(8,128)(2,1)S(1)} collective-permute-done((bf16[32,1024]{1,0:T(8,128)(2,1)S(1)}, bf16[32,1024]{1,0:T(8,128)(2,1)S(1)}, u32[]{:S(2)}, u32[]{:S(2)}) %collective-permute-start.3) | collective-permute-done | bytes 65568 | tf_op jit(solution)/shard_map/ppermute | solution.py:533
  31.5 0.8 %finish.1.refs_0_ = bf16[32,1024]{1,0:T(8,128)(2,1)S(1)} custom-call(bf16[32,1024]{1,0:T(8,128)(2,1)S(1)} %get-tuple-element.40.att_ref.refs_0_, bf16[1024,1024]{1,0:T(8,128)(2,1)S(1)} %load_block.1.refs_1_, s32[32,128]{1,0:T(8,128)S(1)} %get-tuple-element.41.row_slot_ref.refs_2_, s32[8,128]{1,0:T(8,128)S(1)} %get-tuple-element.42.slot_mine_ref.refs_3_, ...), custom_call_target="tpu_custom_call" | custom-call | flops 134217728 | bytes 2097152 | tf_op jit(solution)/shard_map/finish/pallas_call | solution.py:364
  32.3 2.0 %collective-permute-start.13 = (bf16[32,1024]{1,0:T(8,128)(2,1)S(1)}, bf16[32,1024]{1,0:T(8,128)(2,1)S(1)}, u32[]{:S(2)}, u32[]{:S(2)}) collective-permute-start(bf16[32,1024]{1,0:T(8,128)(2,1)S(1)} %finish.1.refs_0_), channel_id=1, source_target_pairs={{0,6},{1,7},{2,4},{3,5},{4,2},{5,3},{6,0},{7,1},{8,14},{9,15},{10,... | collective-permute-start | bytes 196616 | tf_op jit(solution)/shard_map/ppermute | solution.py:536
  34.2 1.1 %collective-permute-start.10 = (bf16[32,1024]{1,0:T(8,128)(2,1)S(1)}, bf16[32,1024]{1,0:T(8,128)(2,1)S(1)}, u32[]{:S(2)}, u32[]{:S(2)}) collective-permute-start(bf16[32,1024]{1,0:T(8,128)(2,1)S(1)} %finish.1.refs_0_), channel_id=1, source_target_pairs={{0,4},{1,5},{2,6},{3,7},{4,0},{5,1},{6,2},{7,3},{8,12},{9,13},{10,... | collective-permute-start | bytes 196616 | tf_op jit(solution)/shard_map/ppermute | solution.py:536
  35.3 1.5 %collective-permute-start.12 = (bf16[32,1024]{1,0:T(8,128)(2,1)S(1)}, bf16[32,1024]{1,0:T(8,128)(2,1)S(1)}, u32[]{:S(2)}, u32[]{:S(2)}) collective-permute-start(bf16[32,1024]{1,0:T(8,128)(2,1)S(1)} %finish.1.refs_0_), channel_id=1, source_target_pairs={{0,1},{1,0},{2,3},{3,2},{4,5},{5,4},{6,7},{7,6},{8,9},{9,8},{10,11... | collective-permute-start | bytes 196616 | tf_op jit(solution)/shard_map/ppermute | solution.py:539
  36.8 1.4 %collective-permute-start.9 = (bf16[32,1024]{1,0:T(8,128)(2,1)S(1)}, bf16[32,1024]{1,0:T(8,128)(2,1)S(1)}, u32[]{:S(2)}, u32[]{:S(2)}) collective-permute-start(bf16[32,1024]{1,0:T(8,128)(2,1)S(1)} %finish.1.refs_0_), channel_id=1, source_target_pairs={{0,2},{1,3},{2,0},{3,1},{4,6},{5,7},{6,4},{7,5},{8,10},{9,11},{10,... | collective-permute-start | bytes 196616 | tf_op jit(solution)/shard_map/ppermute | solution.py:536
  38.2 0.6 %collective-permute-start.8 = (bf16[32,1024]{1,0:T(8,128)(2,1)S(1)}, bf16[32,1024]{1,0:T(8,128)(2,1)S(1)}, u32[]{:S(2)}, u32[]{:S(2)}) collective-permute-start(bf16[32,1024]{1,0:T(8,128)(2,1)S(1)} %finish.1.refs_0_), channel_id=1, source_target_pairs={{0,3},{1,2},{2,1},{3,0},{4,7},{5,6},{6,5},{7,4},{8,11},{9,10},{10,... | collective-permute-start | bytes 196616 | tf_op jit(solution)/shard_map/ppermute | solution.py:539
  38.8 1.8 %collective-permute-start.14 = (bf16[32,1024]{1,0:T(8,128)(2,1)S(1)}, bf16[32,1024]{1,0:T(8,128)(2,1)S(1)}, u32[]{:S(2)}, u32[]{:S(2)}) collective-permute-start(bf16[32,1024]{1,0:T(8,128)(2,1)S(1)} %collective-permute-done.13.refs_6_), channel_id=1, source_target_pairs={{0,1},{1,0},{2,3},{3,2},{4,5},{5,4},{6,7},{7,6},{8,9},{9,8},{10,11... | collective-permute-start | bytes 196616 | tf_op jit(solution)/shard_map/ppermute | solution.py:533
  40.6 0.4 collective-permute-done.10.refs_3_
  41.1 0.1 collective-permute-start.11
  41.1 0.4 collective-permute-done.9.refs_2_
  41.5 2.0 %collective-permute-done.8.refs_1_ = bf16[32,1024]{1,0:T(8,128)(2,1)S(1)} collective-permute-done((bf16[32,1024]{1,0:T(8,128)(2,1)S(1)}, bf16[32,1024]{1,0:T(8,128)(2,1)S(1)}, u32[]{:S(2)}, u32[]{:S(2)}) %collective-permute-start.8) | collective-permute-done | bytes 65568 | tf_op jit(solution)/shard_map/ppermute | solution.py:539
  43.5 0.3 collective-permute-done.14.refs_7_
  43.8 1.5 %collective-permute-done.11.refs_4_ = bf16[32,1024]{1,0:T(8,128)(2,1)S(1)} collective-permute-done((bf16[32,1024]{1,0:T(8,128)(2,1)S(1)}, bf16[32,1024]{1,0:T(8,128)(2,1)S(1)}, u32[]{:S(2)}, u32[]{:S(2)}) %collective-permute-start.11) | collective-permute-done | bytes 65568 | tf_op jit(solution)/shard_map/ppermute | solution.py:533
  45.3 0.8 %place.1 = bf16[32,8192]{1,0:T(8,128)(2,1)} custom-call(bf16[32,1024]{1,0:T(8,128)(2,1)S(1)} %finish.1.refs_0_, bf16[32,1024]{1,0:T(8,128)(2,1)S(1)} %collective-permute-done.8.refs_1_, bf16[32,1024]{1,0:T(8,128)(2,1)S(1)} %collective-permute-done.9.refs_2_, bf16[32,1024]{1,0:T(8,128)(2,1)S(1)} %collective-permute-done.10.refs_3_, ...), custom_call_target="tpu_custom_call" | custom-call | bytes 1048576 | tf_op jit(solution)/shard_map/place/pallas_call | solution.py:507
  (13 shorter events, 0.0 us)
Async XLA Ops:
  0.0 3.4 %copy-start = (s32[128]{0:T(128)S(1)}, s32[128]{0:T(128)}, u32[]{:S(2)}) copy-start(s32[128]{0:T(128)} %slot_ref.3) | copy-start | bytes 1540
  0.0 3.4 %collective-permute-start = (s32[32]{0:T(128)}, s32[32]{0:T(128)S(1)}, u32[]{:S(2)}, u32[]{:S(2)}) collective-permute-start(s32[32]{0:T(128)} %ids_ref.1), channel_id=1, source_target_pairs={{0,8},{8,0},{1,9},{9,1},{2,10},{10,2},{3,11},{11,3},{4,12},{12,4},... | collective-permute-start | bytes 392 | tf_op jit(solution)/shard_map/ppermute | solution.py:542
  3.4 3.8 %copy-start.1 = (s32[32]{0:T(128)S(1)}, s32[32]{0:T(128)}, u32[]{:S(2)}) copy-start(s32[32]{0:T(128)} %ids_ref.1) | copy-start | bytes 388
  7.1 4.4 %collective-permute-start.1 = (bf16[2,8,64,1024]{3,2,1,0:T(8,128)(2,1)S(1)}, bf16[2,8,64,1024]{3,2,1,0:T(8,128)(2,1)S(1)}, u32[]{:S(2)}, u32[]{:S(2)}) collective-permute-start(bf16[2,8,64,1024]{3,2,1,0:T(8,128)(2,1)S(1)} %get-tuple-element.44), channel_id=1, source_target_pairs={{0,8},{8,0},{1,9},{9,1},{2,10},{10,2},{3,11},{11,3},{4,12},{12,4},... | collective-permute-start | bytes 6291464 | tf_op jit(solution)/shard_map/ppermute | solution.py:542
  12.7 7.4 %collective-permute-start.2 = (bf16[32,2176]{1,0:T(8,128)(2,1)S(1)}, bf16[32,2176]{1,0:T(8,128)(2,1)S(1)}, u32[]{:S(2)}, u32[]{:S(2)}) collective-permute-start(bf16[32,2176]{1,0:T(8,128)(2,1)S(1)} %get-tuple-element.49), channel_id=1, source_target_pairs={{0,1},{1,0},{2,3},{3,2},{4,5},{5,4},{6,7},{7,6},{8,9},{9,8},{10,11... | collective-permute-start | bytes 417800 | tf_op jit(solution)/shard_map/ppermute | solution.py:533
  18.5 11.9 %collective-permute-start.4 = (bf16[32,1152]{1,0:T(8,128)(2,1)S(1)}, bf16[32,1152]{1,0:T(8,128)(2,1)S(1)}, u32[]{:S(2)}, u32[]{:S(2)}) collective-permute-start(bf16[32,1152]{1,0:T(8,128)(2,1)S(1)} %get-tuple-element.53), channel_id=1, source_target_pairs={{0,2},{1,3},{2,0},{3,1},{4,6},{5,7},{6,4},{7,5},{8,10},{9,11},{10,... | collective-permute-start | bytes 221192 | tf_op jit(solution)/shard_map/ppermute | solution.py:536
  20.1 10.3 %collective-permute-start.5 = (bf16[32,1152]{1,0:T(8,128)(2,1)S(1)}, bf16[32,1152]{1,0:T(8,128)(2,1)S(1)}, u32[]{:S(2)}, u32[]{:S(2)}) collective-permute-start(bf16[32,1152]{1,0:T(8,128)(2,1)S(1)} %get-tuple-element.54), channel_id=1, source_target_pairs={{0,3},{1,2},{2,1},{3,0},{4,7},{5,6},{6,5},{7,4},{8,11},{9,10},{10,... | collective-permute-start | bytes 221192 | tf_op jit(solution)/shard_map/ppermute | solution.py:539
  20.6 10.9 %collective-permute-start.6 = (bf16[32,1152]{1,0:T(8,128)(2,1)S(1)}, bf16[32,1152]{1,0:T(8,128)(2,1)S(1)}, u32[]{:S(2)}, u32[]{:S(2)}) collective-permute-start(bf16[32,1152]{1,0:T(8,128)(2,1)S(1)} %add_block.2.rest_0_), channel_id=1, source_target_pairs={{0,6},{1,7},{2,4},{3,5},{4,2},{5,3},{6,0},{7,1},{8,14},{9,15},{10,... | collective-permute-start | bytes 221192 | tf_op jit(solution)/shard_map/ppermute | solution.py:536
  25.0 6.4 %collective-permute-start.7 = (bf16[32,1152]{1,0:T(8,128)(2,1)S(1)}, bf16[32,1152]{1,0:T(8,128)(2,1)S(1)}, u32[]{:S(2)}, u32[]{:S(2)}) collective-permute-start(bf16[32,1152]{1,0:T(8,128)(2,1)S(1)} %add_block.3.rest_0_), channel_id=1, source_target_pairs={{0,4},{1,5},{2,6},{3,7},{4,0},{5,1},{6,2},{7,3},{8,12},{9,13},{10,... | collective-permute-start | bytes 221192 | tf_op jit(solution)/shard_map/ppermute | solution.py:536
  27.2 4.3 %collective-permute-start.3 = (bf16[32,1024]{1,0:T(8,128)(2,1)S(1)}, bf16[32,1024]{1,0:T(8,128)(2,1)S(1)}, u32[]{:S(2)}, u32[]{:S(2)}) collective-permute-start(bf16[32,1024]{1,0:T(8,128)(2,1)S(1)} %near_blocks.2.after_ref), channel_id=1, source_target_pairs={{0,1},{1,0},{2,3},{3,2},{4,5},{5,4},{6,7},{7,6},{8,9},{9,8},{10,11... | collective-permute-start | bytes 196616 | tf_op jit(solution)/shard_map/ppermute | solution.py:533
  32.3 6.5 %collective-permute-start.13 = (bf16[32,1024]{1,0:T(8,128)(2,1)S(1)}, bf16[32,1024]{1,0:T(8,128)(2,1)S(1)}, u32[]{:S(2)}, u32[]{:S(2)}) collective-permute-start(bf16[32,1024]{1,0:T(8,128)(2,1)S(1)} %finish.1.refs_0_), channel_id=1, source_target_pairs={{0,6},{1,7},{2,4},{3,5},{4,2},{5,3},{6,0},{7,1},{8,14},{9,15},{10,... | collective-permute-start | bytes 196616 | tf_op jit(solution)/shard_map/ppermute | solution.py:536
  34.2 6.8 %collective-permute-start.10 = (bf16[32,1024]{1,0:T(8,128)(2,1)S(1)}, bf16[32,1024]{1,0:T(8,128)(2,1)S(1)}, u32[]{:S(2)}, u32[]{:S(2)}) collective-permute-start(bf16[32,1024]{1,0:T(8,128)(2,1)S(1)} %finish.1.refs_0_), channel_id=1, source_target_pairs={{0,4},{1,5},{2,6},{3,7},{4,0},{5,1},{6,2},{7,3},{8,12},{9,13},{10,... | collective-permute-start | bytes 196616 | tf_op jit(solution)/shard_map/ppermute | solution.py:536
  35.3 5.8 %collective-permute-start.12 = (bf16[32,1024]{1,0:T(8,128)(2,1)S(1)}, bf16[32,1024]{1,0:T(8,128)(2,1)S(1)}, u32[]{:S(2)}, u32[]{:S(2)}) collective-permute-start(bf16[32,1024]{1,0:T(8,128)(2,1)S(1)} %finish.1.refs_0_), channel_id=1, source_target_pairs={{0,1},{1,0},{2,3},{3,2},{4,5},{5,4},{6,7},{7,6},{8,9},{9,8},{10,11... | collective-permute-start | bytes 196616 | tf_op jit(solution)/shard_map/ppermute | solution.py:539
  36.8 4.7 %collective-permute-start.9 = (bf16[32,1024]{1,0:T(8,128)(2,1)S(1)}, bf16[32,1024]{1,0:T(8,128)(2,1)S(1)}, u32[]{:S(2)}, u32[]{:S(2)}) collective-permute-start(bf16[32,1024]{1,0:T(8,128)(2,1)S(1)} %finish.1.refs_0_), channel_id=1, source_target_pairs={{0,2},{1,3},{2,0},{3,1},{4,6},{5,7},{6,4},{7,5},{8,10},{9,11},{10,... | collective-permute-start | bytes 196616 | tf_op jit(solution)/shard_map/ppermute | solution.py:536
  38.2 5.3 %collective-permute-start.8 = (bf16[32,1024]{1,0:T(8,128)(2,1)S(1)}, bf16[32,1024]{1,0:T(8,128)(2,1)S(1)}, u32[]{:S(2)}, u32[]{:S(2)}) collective-permute-start(bf16[32,1024]{1,0:T(8,128)(2,1)S(1)} %finish.1.refs_0_), channel_id=1, source_target_pairs={{0,3},{1,2},{2,1},{3,0},{4,7},{5,6},{6,5},{7,4},{8,11},{9,10},{10,... | collective-permute-start | bytes 196616 | tf_op jit(solution)/shard_map/ppermute | solution.py:539
  38.8 5.0 %collective-permute-start.14 = (bf16[32,1024]{1,0:T(8,128)(2,1)S(1)}, bf16[32,1024]{1,0:T(8,128)(2,1)S(1)}, u32[]{:S(2)}, u32[]{:S(2)}) collective-permute-start(bf16[32,1024]{1,0:T(8,128)(2,1)S(1)} %collective-permute-done.13.refs_6_), channel_id=1, source_target_pairs={{0,1},{1,0},{2,3},{3,2},{4,5},{5,4},{6,7},{7,6},{8,9},{9,8},{10,11... | collective-permute-start | bytes 196616 | tf_op jit(solution)/shard_map/ppermute | solution.py:533
  41.1 4.3 %collective-permute-start.11 = (bf16[32,1024]{1,0:T(8,128)(2,1)S(1)}, bf16[32,1024]{1,0:T(8,128)(2,1)S(1)}, u32[]{:S(2)}, u32[]{:S(2)}) collective-permute-start(bf16[32,1024]{1,0:T(8,128)(2,1)S(1)} %collective-permute-done.10.refs_3_), channel_id=1, source_target_pairs={{0,1},{1,0},{2,3},{3,2},{4,5},{5,4},{6,7},{7,6},{8,9},{9,8},{10,11... | collective-permute-start | bytes 196616 | tf_op jit(solution)/shard_map/ppermute | solution.py:533

commit v10 on v9

--- a/solution.py
+++ b/solution.py
@@ -76,7 +76,7 @@
 
 
 def prefix_scores_kernel(
-    q_ref, prefix_ref, suffix_ref, query_ref, scores_ref, peak_ref, vals_ref, suf_keys_ref, qbuf, keys, rowbuf, sem, sem_keys
+    q_ref, prefix_ref, suffix_ref, query_ref, scores_ref, peak_ref, suf_keys_ref, qbuf, keys, rowbuf, sem, sem_keys
 ):
     rows = q_ref.shape[0]
     tokens, head_dim = keys.shape
@@ -90,10 +90,7 @@
         for j in range(parts)
     ]
     fetch_q = pltpu.make_async_copy(q_ref, qbuf, sem.at[0])
-    fetch = [
-        pltpu.make_async_copy(suffix_ref.at[:, 0, 0], suf_keys_ref, sem.at[1]),
-        pltpu.make_async_copy(prefix_ref.at[0, 1], vals_ref, sem.at[2]),
-    ]
+    fetch = [pltpu.make_async_copy(suffix_ref.at[:, 0, 0], suf_keys_ref, sem.at[1])]
     for c in [fetch_q] + key_copies + fetch:
         c.start()
     fetch_q.wait()
@@ -125,18 +122,27 @@
     return copies
 
 
-def suffix_scores_kernel(spots, ids_ref, slot_ref, query_ref, suf_keys_ref, vals_ref, peak_ref, *rest):
-    len_ref, suffix_ref, pages_ref, weight_ref = rest[:4]
-    tail_ref, high_ref, high_row_ref, vals_t_ref, out_pages_ref, suf_vals_ref = rest[4:10]
-    w_refs = rest[10 : 10 + len(spots)]
-    lens, seen, list_id, list_pos, sem, sem_page, sem_w = rest[10 + len(spots) :]
+def suffix_scores_kernel(spots, ids_ref, slot_ref, query_ref, suf_keys_ref, peak_ref, *rest):
+    len_ref, prefix_ref, pages_ref, weight_ref = rest[:4]
+    tail_ref, high_ref, high_row_ref, vals_t_ref, out_pages_ref = rest[4:9]
+    w_refs = rest[9 : 9 + len(spots)]
+    lens, vals_ref, seen, list_id, list_pos, sem, sem_page, sem_w = rest[9 + len(spots) :]
     rows, span, head_dim = suf_keys_ref.shape
     tokens = vals_ref.shape[0]
+    parts = sem.shape[0] - 1
+    size = tokens // parts
     heads = query_ref.shape[0] // rows
-    fetch_len = pltpu.make_async_copy(len_ref, lens, sem.at[1])
+    fetch_len = pltpu.make_async_copy(len_ref, lens, sem.at[parts])
     fetch_len.start()
-    fetch = [pltpu.make_async_copy(suffix_ref.at[:, 0, 1], suf_vals_ref, sem.at[0])]
-    fetch += weight_copies(weight_ref, w_refs, spots, sem_w)
+    val_copies = [
+        pltpu.make_async_copy(
+            prefix_ref.at[0, 1, pl.ds(j * size, size)], vals_ref.at[pl.ds(j * size, size)], sem.at[j]
+        )
+        for j in range(parts)
+    ]
+    for c in val_copies:
+        c.start()
+    fetch = weight_copies(weight_ref, w_refs, spots, sem_w)
     distinct_list(ids_ref, slot_ref, seen, list_id, list_pos)
     outs = (out_pages_ref.at[0], out_pages_ref.at[1])
     page_copies(pages_ref, outs, list_pos, sem_page, False)
@@ -152,9 +158,12 @@
             mine = both[a * heads : (a + 1) * heads, a * span : (a + 1) * span]
             row = 2 * i + a
             tail_ref[row * heads : (row + 1) * heads, :] = jnp.where(lanes < lens[row], mine, -1.0e30)
-    step = min(1024, tokens)
-    for base in range(0, tokens, step):
-        vals_t_ref[:, base : base + step] = vals_ref[base : base + step, :].astype(F32).T.astype(BF16)
+    vals_t_ref[head_dim:, :] = jnp.ones((vals_t_ref.shape[0] - head_dim, tokens), BF16)
+    step = min(1024, size)
+    for j in range(parts):
+        val_copies[j].wait()
+        for base in range(j * size, (j + 1) * size, step):
+            vals_t_ref[:head_dim, base : base + step] = vals_ref[base : base + step, :].astype(F32).T.astype(BF16)
     best = jnp.maximum(tail_ref[:, :128], tail_ref[:, 128:256])
     for b in range(2, span // 128):
         best = jnp.maximum(best, tail_ref[:, b * 128 : (b + 1) * 128])
@@ -167,12 +176,14 @@
         c.wait()
 
 
-def values_kernel(spots, ids_ref, slot_ref, scores, tail, peak, peak_row, vals_t_ref, suf_vals_ref, *rest):
+def values_kernel(spots, ids_ref, slot_ref, scores, tail, peak, peak_row, vals_t_ref, suffix_ref, *rest):
     pages_ref, weight_ref, residual_ref = rest[:3]
     att_ref, shrink_ref, expand_ref, row_slot_ref, slot_mine_ref, res_ref = rest[3:9]
     w_refs = rest[9 : 9 + len(spots)]
-    rowbuf, total, acc, total_row, acc_t, seen, list_id, list_pos, sem, sem_page, sem_w = rest[9 + len(spots) :]
+    suf_vals_ref, rowbuf, total, acc, acc_t, seen, list_id, list_pos, sem, sem_page, sem_w = rest[9 + len(spots) :]
     rows, span, head_dim = suf_vals_ref.shape
+    fetch_vals = pltpu.make_async_copy(suffix_ref.at[:, 0, 1], suf_vals_ref, sem.at[1])
+    fetch_vals.start()
     tokens = vals_t_ref.shape[1]
     heads = att_ref.shape[1] // head_dim
     width = res_ref.shape[1]
@@ -203,7 +214,6 @@
     row_slot_ref[...] = row_slot
     slot_mine_ref[...] = slot_mine
 
-    total_row[...] = jnp.zeros(total_row.shape, F32)
     acc_t[...] = jnp.zeros(acc_t.shape, F32)
     n_q = acc_t.shape[1]
     chunk = min(2048, tokens)
@@ -214,12 +224,12 @@
         high_row = peak_row[...]
         block = scores[pl.ds(base, chunk), :].reshape(chunk // 8, 8, n_q)
         e = jnp.exp2((block - high_row[None]) * scale2)
-        total_row[...] += jnp.sum(e, axis=0)
         weights = e.reshape(chunk, n_q).astype(BF16)
         acc_t[...] += nn_dot(vals_t_ref[:, pl.ds(base, chunk)], weights)
 
-    across_rows = jnp.broadcast_to(jnp.sum(total_row[...], axis=0, keepdims=True), (128, n_q))
-    acc[...] = acc_t[...].T
+    across_rows = jnp.broadcast_to(acc_t[head_dim : head_dim + 1, :], (128, n_q))
+    acc[...] = acc_t[:head_dim, :].T
+    fetch_vals.wait()
     zeros = jnp.zeros((heads, span), F32)
     for i in range(rows // 2):
         lo = 2 * heads * i
@@ -273,14 +283,13 @@
     span = suffix_kv.shape[3]
     prefix_kv, suffix_kv, out_weight = in_hbm(prefix_kv), in_hbm(suffix_kv), in_hbm(out_weight)
     pages, residual = in_hbm(pages), in_hbm(residual)
-    query, scores, peak, vals, suf_keys = kernel_call(
+    query, scores, peak, suf_keys = kernel_call(
         prefix_scores_kernel,
         "prefix_scores",
         [
             pltpu.VMEM((n_q, head_dim), BF16),
             pltpu.VMEM((tokens, n_q), F32),
             pltpu.VMEM((8, n_q), F32),
-            pltpu.VMEM((tokens, head_dim), BF16),
             pltpu.VMEM((rows, span, head_dim), BF16),
         ],
         [ANY, ANY, ANY],
@@ -288,7 +297,7 @@
             pltpu.VMEM(queries.shape, BF16),
             pltpu.VMEM((tokens, head_dim), BF16),
             pltpu.VMEM((n_q, head_dim), F32),
-            pltpu.SemaphoreType.DMA((3,)),
+            pltpu.SemaphoreType.DMA((2,)),
             pltpu.SemaphoreType.DMA((4,)),
         ],
         [in_hbm(queries), prefix_kv, suffix_kv],
@@ -299,27 +308,26 @@
     far = list(range(n_z - 1, -1, -1))
     early = [(0, k) for k in far[: n_z // 4]]
     late = [(1, k) for k in far if k > 1] + [(0, k) for k in far[n_z // 4 :] if k > 1]
-    tail, high, high_row, vals_t, out_pages, suf_vals, *early_w = kernel_call(
+    tail, high, high_row, vals_t, out_pages, *early_w = kernel_call(
         functools.partial(suffix_scores_kernel, early),
         "suffix_scores",
         [
             pltpu.VMEM((n_q, span), F32),
             pltpu.VMEM((n_q, 128), F32),
             pltpu.VMEM((8, n_q), F32),
-            pltpu.VMEM((head_dim, tokens), BF16),
+            pltpu.VMEM((head_dim + 16, tokens), BF16),
             pltpu.VMEM((2, DISTINCT) + pages.shape[2:], BF16),
-            pltpu.VMEM((rows, span, head_dim), BF16),
         ]
         + [pltpu.VMEM((in_rows, width), BF16)] * len(early),
-        [SMEM, SMEM, VMEM, VMEM, VMEM, VMEM, ANY, ANY, ANY, ANY],
-        [pltpu.SMEM((rows,), jnp.int32)]
+        [SMEM, SMEM, VMEM, VMEM, VMEM, ANY, ANY, ANY, ANY],
+        [pltpu.SMEM((rows,), jnp.int32), pltpu.VMEM((tokens, head_dim), BF16)]
         + list_scratch(pool_slot)
         + [
-            pltpu.SemaphoreType.DMA((2,)),
+            pltpu.SemaphoreType.DMA((5,)),
             pltpu.SemaphoreType.DMA((2, DISTINCT)),
             pltpu.SemaphoreType.DMA((len(early),)),
         ],
-        [other_ids, pool_slot, query, suf_keys, vals, peak, in_hbm(suffix_len), suffix_kv, pages, out_weight],
+        [other_ids, pool_slot, query, suf_keys, peak, in_hbm(suffix_len), prefix_kv, pages, out_weight],
         8,
         1 << 29,
         7 * MIB,
@@ -337,21 +345,21 @@
             pltpu.VMEM((rows, width), BF16),
         ]
         + [pltpu.VMEM((in_rows, width), BF16)] * len(late),
-        [SMEM, SMEM, VMEM, VMEM, VMEM, VMEM, VMEM, VMEM, ANY, ANY, ANY],
+        [SMEM, SMEM, VMEM, VMEM, VMEM, VMEM, VMEM, ANY, ANY, ANY, ANY],
         [
+            pltpu.VMEM((rows, span, head_dim), BF16),
             pltpu.VMEM((n_q, head_dim), F32),
             pltpu.VMEM((n_q, 128), F32),
             pltpu.VMEM((n_q, head_dim), F32),
-            pltpu.VMEM((8, n_q), F32),
-            pltpu.VMEM((head_dim, n_q), F32),
+            pltpu.VMEM((head_dim + 16, n_q), F32),
         ]
         + list_scratch(pool_slot)
         + [
-            pltpu.SemaphoreType.DMA((1,)),
+            pltpu.SemaphoreType.DMA((2,)),
             pltpu.SemaphoreType.DMA((2, DISTINCT)),
             pltpu.SemaphoreType.DMA((len(late),)),
         ],
-        [ids, pool_slot, scores, tail, high, high_row, vals_t, suf_vals, pages, out_weight, residual],
+        [ids, pool_slot, scores, tail, high, high_row, vals_t, suffix_kv, pages, out_weight, residual],
         8,
         2 * n_q * tokens * head_dim,
         14 * MIB,
@@ -440,24 +448,29 @@
     )
 
 
-def load_kernel(spots, weight_ref, after_ref, out_ref, sem):
-    (copy,) = weight_copies(weight_ref, [out_ref], spots, sem)
+def own_kernel(
+    att_ref, res_ref, slot_mine_ref, own_ref, other_ref, weight_ref, after_ref, out_ref, pages_ref, wbuf, sem
+):
+    (copy,) = weight_copies(weight_ref, [wbuf], [(0, 0)], sem)
     copy.start()
+    pages_ref[...] = merged(own_ref, other_ref, 1, slot_mine_ref[...])
     copy.wait()
-
-
-def load_block(weight, spot, after, n_tensor):
+    out_ref[...] = nn_dot(att_ref[...], wbuf[...]) + res_ref[...].astype(F32)
+
+
+def own_block(attended, res, slot_mine, own_pages, other_pages, weight, after):
+    rows, width = res.shape
     return kernel_call(
-        functools.partial(load_kernel, [spot]),
-        "load_block",
-        [pltpu.VMEM((weight.shape[0], weight.shape[1] // n_tensor), BF16)],
-        [ANY, VMEM],
-        [pltpu.SemaphoreType.DMA((1,))],
-        [in_hbm(weight), after],
-        2,
+        own_kernel,
+        "own_block",
+        [pltpu.VMEM((rows, width), F32), pltpu.VMEM((DISTINCT * own_pages.shape[1], width), BF16)],
+        [VMEM, VMEM, VMEM, VMEM, VMEM, ANY, VMEM],
+        [pltpu.VMEM((weight.shape[0], width), BF16), pltpu.SemaphoreType.DMA((1,))],
+        [attended, res, slot_mine, own_pages, other_pages, in_hbm(weight), after],
+        8,
         0,
         2 * MIB,
-    )[0]
+    )
 
 
 def add_kernel(spot, att_ref, w_ref, from_ref, rank_ref, *rest):
@@ -470,12 +483,11 @@
 
 
 def finish_kernel(*refs):
-    att_ref, w_ref, row_slot_ref, slot_mine_ref, own_ref, other_ref = refs[:6]
-    rank_ref, far_ref, from_ref, res_ref = refs[6:10]
-    moved, out_ref = refs[10:-1], refs[-1]
-    rank = own_ref.shape[1]
+    own_ref, pages_ref, row_slot_ref, rank_ref, far_ref, from_ref = refs[:6]
+    moved, out_ref = refs[6:-1], refs[-1]
+    rank = pages_ref.shape[0] // DISTINCT
     per_tile = 128 // rank
-    width = w_ref.shape[1]
+    width = own_ref.shape[1]
     low = rank_ref[...] + far_ref[:, far_ref.shape[1] - 128 :].astype(F32)
     for ref in moved:
         low = low + ref[:, width:].astype(F32)
@@ -484,35 +496,43 @@
     tiles = []
     for tile in range(DISTINCT // per_tile):
         tiles.append(jnp.where(row_slot == place + tile * per_tile, low, 0.0).astype(BF16))
-    total = nn_dot(jnp.concatenate(tiles, axis=1), merged(own_ref, other_ref, 1, slot_mine_ref[...]))
-    total = total + nn_dot(att_ref[...], w_ref[...])
-    total = total + (res_ref[...].astype(F32) + from_ref[...].astype(F32))
+    total = nn_dot(jnp.concatenate(tiles, axis=1), pages_ref[...])
+    total = total + (own_ref[...] + from_ref[...].astype(F32))
     for ref in moved:
         total = total + ref[:, :width].astype(F32)
     out_ref[...] = total.astype(BF16)
 
 
 def place_kernel(spots, *refs):
-    blocks, out_ref = refs[:-1], refs[-1]
+    blocks = refs[: len(spots)]
+    out_ref, sem = refs[-2:]
     width = blocks[0].shape[1]
     me = lax.axis_index("tensor")
     z, y = me // 2, me % 2
-    for block, (k, side) in zip(blocks, spots):
-        where = (z ^ k) * 2 + (y ^ side)
-        out_ref[:, pl.ds(pl.multiple_of(where * width, width), width)] = block[...]
-
-
-def place(blocks, spots, n_tensor):
+    copies = []
+    for i, (k, side) in enumerate(spots):
+        column = pl.multiple_of(((z ^ k) * 2 + (y ^ side)) * width, width)
+        copies.append(pltpu.make_async_copy(blocks[i], out_ref.at[:, pl.ds(column, width)], sem.at[i]))
+    for c in copies:
+        c.start()
+    for c in copies:
+        c.wait()
+
+
+def place(blocks, spots, n_tensor, held=None):
     rows, width = blocks[0].shape
+    extra = [] if held is None else [held]
     return pl.pallas_call(
         functools.partial(place_kernel, spots),
-        out_shape=jax.ShapeDtypeStruct((rows, width * n_tensor), BF16),
-        in_specs=[VMEM] * n_tensor,
-        out_specs=VMEM,
+        out_shape=pltpu.HBM((rows, width * n_tensor), BF16),
+        in_specs=[VMEM] * len(blocks) + [ANY] * len(extra),
+        out_specs=ANY,
+        scratch_shapes=[pltpu.SemaphoreType.DMA((len(blocks),))],
+        input_output_aliases={len(blocks): 0} if extra else {},
         compiler_params=params(4),
         cost_estimate=pl.CostEstimate(flops=0, bytes_accessed=1 * MIB, transcendentals=0),
         name="place",
-    )(*blocks)
+    )(*blocks, *extra)
 
 
 def body(
@@ -582,19 +602,22 @@
         after = [piece]
     (own_far,) = near_blocks([(1, 0)], width, attended, rank_own, out_weight, [piece], n_tensor)
     from_own = along_y(own_far)
-    weights[0, 0] = load_block(out_weight, (0, 0), own_far, n_tensor)
+    own, expand_pages = own_block(attended, res, slot_mine, own_expand, other_pages, out_weight, own_far)
     result = small_call(
         finish_kernel,
         "finish",
         pltpu.VMEM((rows, width), BF16),
-        [attended, weights[0, 0], row_slot, slot_mine, own_expand, other_pages, rank_own, from_far, from_own, res]
-        + moved,
+        [own, expand_pages, row_slot, rank_own, from_far, from_own] + moved,
     )
     held = [result] + [along_z(result, k) for k in range(1, n_z)]
     crossed = [along_both(result, k) if k < 2 else along_y(held[k]) for k in range(n_z)]
     spots = [(0, 0), (1, 1), (1, 0)] + [(k, side) for k in range(2, n_z) for side in (0, 1)]
     spots.insert(len(spots) - 2, (0, 1))
-    return place([(crossed if side else held)[k] for k, side in spots], spots, n_tensor)
+    forwarded = [(k, side) for k, side in spots if k > 1 and side]
+    placed = None
+    for group in ([p for p in spots if p not in forwarded], forwarded):
+        placed = place([(crossed if side else held)[k] for k, side in group], group, n_tensor, placed)
+    return placed
 
 
 def solution(mesh):

time: 46.3 us -> 46.5 us (level)
  Pallas kernels: 21 us -> 22.2 us
  waiting for transfers between devices: 5.76 us -> 4.64 us
    ppermute x4, waiting for transfers between devices: 2.92 us -> 1.76 us  [along_y(): return lax.ppermute(x, 'tensor', [(t, t ^ 1) for t in range(n_tensor)])]
    pallas_call x6, Pallas kernels: 17.3 us -> 18.3 us  [kernel_call(): pl.pallas_call(kernel, out_shape=out_shape, in_specs=specs, out_specs=[VM...]
    pallas_call x1 -> x2, Pallas kernels: 0.84 us -> 1.45 us  [place(): pl.pallas_call(functools.partial(place_kernel, spots), out_shape=pltpu.HB...]
  transfers between devices with their start and end apart: 15 -> 15, of which waited for: 6 -> 5; matrix products, arithmetic and copies ran while one was open for 0% -> 0% of each run, Pallas kernels for 32% -> 36%
where the time goes in v10:
time: 46.5 us; the launch traced here: 46.3 us
  Pallas kernels  22.2 us (48%)
  starting transfers between devices  19.3 us (42%)
  waiting for transfers between devices  4.64 us (10%)
    pallas_call x6, Pallas kernels, kernel_call(): pl.pallas_call(kernel, out_shape=out_shape, in_specs=specs, out_specs=[VM...  18.3 us
    ppermute x6, starting transfers between devices, along_z(): return lax.ppermute(x, 'tensor', [(t, t ^ 2 * k) for t in range(n_tensor)])  10.1 us
    ppermute x4, starting transfers between devices, along_y(): return lax.ppermute(x, 'tensor', [(t, t ^ 1) for t in range(n_tensor)])  6.43 us
    pallas_call x4, Pallas kernels, small_call(): pl.pallas_call(kernel, out_shape=out_shape, in_specs=[VMEM] * len(operand...  2.39 us
    ppermute x3, starting transfers between devices, along_both(): lax.ppermute(x, 'tensor', [(t, t ^ 2 * k ^ 1) for t in range(n_tensor)])  2.1 us
    ppermute x3, waiting for transfers between devices, along_both(): lax.ppermute(x, 'tensor', [(t, t ^ 2 * k ^ 1) for t in range(n_tensor)])  2.01 us
    ppermute x4, waiting for transfers between devices, along_y(): return lax.ppermute(x, 'tensor', [(t, t ^ 1) for t in range(n_tensor)])  1.76 us
    pallas_call x2, Pallas kernels, place(): pl.pallas_call(functools.partial(place_kernel, spots), out_shape=pltpu.HB...  1.45 us
  transfers between devices with their start and end apart: 15, of which 5 were waited for; matrix products, arithmetic and copies ran while one was open for 0% of the time, Pallas kernels for 36%

profile of v10, /device:TPU:0, one launch (start us, length us, event | category | flops | bytes accessed | tf_op | source)
XLA Modules:
  0.0 46.3 jit_solution(3569807951854196536)
XLA Ops:
  0.0 0.5 collective-permute-start
  0.5 3.0 %prefix_scores.1 = (bf16[256,128]{1,0:T(8,128)(2,1)S(1)}, f32[8192,256]{1,0:T(8,128)S(1)}, f32[8,256]{1,0:T(8,128)S(1)}, bf16[32,256,128]{2,1,0:T(8,128)(2,1)S(1)}) custom-call(bf16[32,1024]{1,0:T(8,128)(2,1)} %q_ref.1, bf16[1,2,8192,128]{3,2,1,0:T(8,128)(2,1)} %rest_1_.2, bf16[32,1,2,256,128]{4,3,2,1,0:T(8,128)(2,1)} %suffix_ref.3), custom_call_target="tpu_custom_call" | custom-call | flops 536870912 | bytes 6291456 | tf_op jit(solution)/shard_map/prefix_scores/pallas_call | solution.py:262
  3.5 0.0 copy-start.1
  3.5 3.6 %suffix_scores.1 = (f32[256,256]{1,0:T(8,128)S(1)}, f32[256,128]{1,0:T(8,128)S(1)}, f32[8,256]{1,0:T(8,128)S(1)}, bf16[144,8192]{1,0:T(8,128)(2,1)S(1)}, bf16[2,...) custom-call(s32[32]{0:T(128)S(1)} %collective-permute-done.ids_ref, s32[128]{0:T(128)S(1)} %copy-done, ...), custom_call_target="tpu_custom_call" | custom-call | flops 536870912 | bytes 7340032 | tf_op jit(solution)/shard_map/suffix_scores/pallas_call | solution.py:262
  7.1 0.2 collective-permute-start.1
  7.3 4.8 %values.1 = (bf16[32,1024]{1,0:T(8,128)(2,1)S(1)}, bf16[8,64,1024]{2,1,0:T(8,128)(2,1)S(1)}, bf16[8,64,1024]{2,1,0:T(8,128)(2,1)S(1)}, s32[32,128]{1,0:T(8,128)S...) custom-call(s32[32]{0:T(128)S(1)} %copy-done.1, ...), custom_call_target="tpu_custom_call" | custom-call | flops 536870912 | bytes 14680064 | tf_op jit(solution)/shard_map/values/pallas_call | solution.py:262
  12.2 1.2 %far_blocks.1 = (bf16[32,2176]{1,0:T(8,128)(2,1)S(1)}, f32[32,128]{1,0:T(8,128)S(1)}) custom-call(bf16[32,1024]{1,0:T(8,128)(2,1)S(1)} %get-tuple-element.38.att_ref, s32[32,128]{1,0:T(8,128)S(1)} %get-tuple-element.43.row_slot_ref.refs_2_, s32[8,128]{1,0:T(8,128)S(1)} %get-tuple-element.40.slot_mine_ref, ...), custom_call_target="tpu_custom_call" | custom-call | flops 134217728 | bytes 2097152 | tf_op jit(solution)/shard_map/far_blocks/pallas_call | solution.py:372
  13.3 3.0 %collective-permute-start.2 = (bf16[32,2176]{1,0:T(8,128)(2,1)S(1)}, bf16[32,2176]{1,0:T(8,128)(2,1)S(1)}, u32[]{:S(2)}, u32[]{:S(2)}) collective-permute-start(bf16[32,2176]{1,0:T(8,128)(2,1)S(1)} %get-tuple-element.49), channel_id=1, source_target_pairs={{0,1},{1,0},{2,3},{3,2},{4,5},{5,4},{6,7},{7,6},{8,9},{9,8},{10,11... | collective-permute-start | bytes 417800 | tf_op jit(solution)/shard_map/ppermute | solution.py:553
  16.3 2.7 %near_blocks.3 = (bf16[32,1152]{1,0:T(8,128)(2,1)S(1)}, bf16[32,1152]{1,0:T(8,128)(2,1)S(1)}) custom-call(bf16[32,1024]{1,0:T(8,128)(2,1)S(1)} %get-tuple-element.38.att_ref, f32[32,128]{1,0:T(8,128)S(1)} %get-tuple-element.47.rank_ref.refs_3_, bf16[1024,8192]{1,0:T(8,128)(2,1)} %weight_ref.5), custom_call_target="tpu_custom_call" | custom-call | flops 134217728 | bytes 4194304 | tf_op jit(solution)/shard_map/near_blocks/pallas_call | solution.py:262
  19.1 1.6 %collective-permute-start.4 = (bf16[32,1152]{1,0:T(8,128)(2,1)S(1)}, bf16[32,1152]{1,0:T(8,128)(2,1)S(1)}, u32[]{:S(2)}, u32[]{:S(2)}) collective-permute-start(bf16[32,1152]{1,0:T(8,128)(2,1)S(1)} %get-tuple-element.53), channel_id=1, source_target_pairs={{0,2},{1,3},{2,0},{3,1},{4,6},{5,7},{6,4},{7,5},{8,10},{9,11},{10,... | collective-permute-start | bytes 221192 | tf_op jit(solution)/shard_map/ppermute | solution.py:556
  20.7 0.0 collective-permute-start.5
  20.7 0.5 %add_block.2.rest_0_ = bf16[32,1152]{1,0:T(8,128)(2,1)S(1)} custom-call(bf16[32,1024]{1,0:T(8,128)(2,1)S(1)} %get-tuple-element.38.att_ref, bf16[1024,1024]{1,0:T(8,128)(2,1)S(1)} %get-tuple-element.50.w_ref, bf16[32,2176]{1,0:T(8,128)(2,1)S(1)} %collective-permute-done.2.from_ref.refs_4_, f32[32,128]{1,0:T(8,128)S(1)} %get-tuple-element.47.rank_ref.refs_3_), custom_call_target="tpu_custom_call" | custom-call | flops 134217728 | bytes 2097152 | tf_op jit(solution)/shard_map/add_block/pallas_call | solution.py:372
  21.2 4.0 %collective-permute-start.6 = (bf16[32,1152]{1,0:T(8,128)(2,1)S(1)}, bf16[32,1152]{1,0:T(8,128)(2,1)S(1)}, u32[]{:S(2)}, u32[]{:S(2)}) collective-permute-start(bf16[32,1152]{1,0:T(8,128)(2,1)S(1)} %add_block.2.rest_0_), channel_id=1, source_target_pairs={{0,6},{1,7},{2,4},{3,5},{4,2},{5,3},{6,0},{7,1},{8,14},{9,15},{10,... | collective-permute-start | bytes 221192 | tf_op jit(solution)/shard_map/ppermute | solution.py:556
  25.2 0.5 %add_block.3.rest_0_ = bf16[32,1152]{1,0:T(8,128)(2,1)S(1)} custom-call(bf16[32,1024]{1,0:T(8,128)(2,1)S(1)} %get-tuple-element.38.att_ref, bf16[1024,1024]{1,0:T(8,128)(2,1)S(1)} %get-tuple-element.48.w_ref, bf16[32,2176]{1,0:T(8,128)(2,1)S(1)} %collective-permute-done.2.from_ref.refs_4_, f32[32,128]{1,0:T(8,128)S(1)} %get-tuple-element.47.rank_ref.refs_3_, ...), custom_call_target="tpu_custom_call" | custom-call | flops 134217728 | bytes 2097152 | tf_op jit(solution)/shard_map/add_block/pallas_call | solution.py:372
  25.6 0.0 collective-permute-start.7
  25.7 2.1 %near_blocks.2.after_ref = bf16[32,1024]{1,0:T(8,128)(2,1)S(1)} custom-call(bf16[32,1024]{1,0:T(8,128)(2,1)S(1)} %get-tuple-element.38.att_ref, f32[32,128]{1,0:T(8,128)S(1)} %get-tuple-element.47.rank_ref.refs_3_, bf16[1024,8192]{1,0:T(8,128)(2,1)} %weight_ref.5, bf16[32,1152]{1,0:T(8,128)(2,1)S(1)} %add_block.3.rest_0_), custom_call_target="tpu_custom_call" | custom-call | flops 134217728 | bytes 2097152 | tf_op jit(solution)/shard_map/near_blocks/pallas_call | solution.py:262
  27.8 1.6 %collective-permute-start.3 = (bf16[32,1024]{1,0:T(8,128)(2,1)S(1)}, bf16[32,1024]{1,0:T(8,128)(2,1)S(1)}, u32[]{:S(2)}, u32[]{:S(2)}) collective-permute-start(bf16[32,1024]{1,0:T(8,128)(2,1)S(1)} %near_blocks.2.after_ref), channel_id=1, source_target_pairs={{0,1},{1,0},{2,3},{3,2},{4,5},{5,4},{6,7},{7,6},{8,9},{9,8},{10,11... | collective-permute-start | bytes 196616 | tf_op jit(solution)/shard_map/ppermute | solution.py:553
  29.3 2.1 %own_block.1 = (f32[32,1024]{1,0:T(8,128)S(1)}, bf16[512,1024]{1,0:T(8,128)(2,1)S(1)}) custom-call(bf16[32,1024]{1,0:T(8,128)(2,1)S(1)} %get-tuple-element.38.att_ref, bf16[32,1024]{1,0:T(8,128)(2,1)S(1)} %get-tuple-element.39.res_ref, s32[8,128]{1,0:T(8,128)S(1)} %get-tuple-element.40.slot_mine_ref, bf16[8,64,1024]{2,1,0:T(8,128)(2,1)S(1)} %get-tuple-element.41.own_ref, ...), custom_call_target="tpu_custom_call" | custom-call | bytes 2097152 | tf_op jit(solution)/shard_map/own_block/pallas_call | solution.py:262
  31.5 0.6 %collective-permute-done.3.refs_5_ = bf16[32,1024]{1,0:T(8,128)(2,1)S(1)} collective-permute-done((bf16[32,1024]{1,0:T(8,128)(2,1)S(1)}, bf16[32,1024]{1,0:T(8,128)(2,1)S(1)}, u32[]{:S(2)}, u32[]{:S(2)}) %collective-permute-start.3) | collective-permute-done | bytes 65568 | tf_op jit(solution)/shard_map/ppermute | solution.py:553
  32.1 0.3 finish.1.refs_0_
  32.4 2.0 %collective-permute-start.10 = (bf16[32,1024]{1,0:T(8,128)(2,1)S(1)}, bf16[32,1024]{1,0:T(8,128)(2,1)S(1)}, u32[]{:S(2)}, u32[]{:S(2)}) collective-permute-start(bf16[32,1024]{1,0:T(8,128)(2,1)S(1)} %finish.1.refs_0_), channel_id=1, source_target_pairs={{0,6},{1,7},{2,4},{3,5},{4,2},{5,3},{6,0},{7,1},{8,14},{9,15},{10,... | collective-permute-start | bytes 196616 | tf_op jit(solution)/shard_map/ppermute | solution.py:556
  34.4 1.1 %collective-permute-start.8 = (bf16[32,1024]{1,0:T(8,128)(2,1)S(1)}, bf16[32,1024]{1,0:T(8,128)(2,1)S(1)}, u32[]{:S(2)}, u32[]{:S(2)}) collective-permute-start(bf16[32,1024]{1,0:T(8,128)(2,1)S(1)} %finish.1.refs_0_), channel_id=1, source_target_pairs={{0,4},{1,5},{2,6},{3,7},{4,0},{5,1},{6,2},{7,3},{8,12},{9,13},{10,... | collective-permute-start | bytes 196616 | tf_op jit(solution)/shard_map/ppermute | solution.py:556
  35.5 1.5 %collective-permute-start.14 = (bf16[32,1024]{1,0:T(8,128)(2,1)S(1)}, bf16[32,1024]{1,0:T(8,128)(2,1)S(1)}, u32[]{:S(2)}, u32[]{:S(2)}) collective-permute-start(bf16[32,1024]{1,0:T(8,128)(2,1)S(1)} %finish.1.refs_0_), channel_id=1, source_target_pairs={{0,1},{1,0},{2,3},{3,2},{4,5},{5,4},{6,7},{7,6},{8,9},{9,8},{10,11... | collective-permute-start | bytes 196616 | tf_op jit(solution)/shard_map/ppermute | solution.py:559
  37.0 1.4 %collective-permute-start.13 = (bf16[32,1024]{1,0:T(8,128)(2,1)S(1)}, bf16[32,1024]{1,0:T(8,128)(2,1)S(1)}, u32[]{:S(2)}, u32[]{:S(2)}) collective-permute-start(bf16[32,1024]{1,0:T(8,128)(2,1)S(1)} %finish.1.refs_0_), channel_id=1, source_target_pairs={{0,2},{1,3},{2,0},{3,1},{4,6},{5,7},{6,4},{7,5},{8,10},{9,11},{10,... | collective-permute-start | bytes 196616 | tf_op jit(solution)/shard_map/ppermute | solution.py:556
  38.4 0.6 %collective-permute-start.12 = (bf16[32,1024]{1,0:T(8,128)(2,1)S(1)}, bf16[32,1024]{1,0:T(8,128)(2,1)S(1)}, u32[]{:S(2)}, u32[]{:S(2)}) collective-permute-start(bf16[32,1024]{1,0:T(8,128)(2,1)S(1)} %finish.1.refs_0_), channel_id=1, source_target_pairs={{0,3},{1,2},{2,1},{3,0},{4,7},{5,6},{6,5},{7,4},{8,11},{9,10},{10,... | collective-permute-start | bytes 196616 | tf_op jit(solution)/shard_map/ppermute | solution.py:559
  39.0 1.8 %collective-permute-start.11 = (bf16[32,1024]{1,0:T(8,128)(2,1)S(1)}, bf16[32,1024]{1,0:T(8,128)(2,1)S(1)}, u32[]{:S(2)}, u32[]{:S(2)}) collective-permute-start(bf16[32,1024]{1,0:T(8,128)(2,1)S(1)} %collective-permute-done.10.refs_5_), channel_id=1, source_target_pairs={{0,1},{1,0},{2,3},{3,2},{4,5},{5,4},{6,7},{7,6},{8,9},{9,8},{10,11... | collective-permute-start | bytes 196616 | tf_op jit(solution)/shard_map/ppermute | solution.py:553
  40.8 0.5 %collective-permute-done.8.refs_3_ = bf16[32,1024]{1,0:T(8,128)(2,1)S(1)} collective-permute-done((bf16[32,1024]{1,0:T(8,128)(2,1)S(1)}, bf16[32,1024]{1,0:T(8,128)(2,1)S(1)}, u32[]{:S(2)}, u32[]{:S(2)}) %collective-permute-start.8) | collective-permute-done | bytes 65568 | tf_op jit(solution)/shard_map/ppermute | solution.py:556
  41.3 0.3 collective-permute-done.13.refs_2_
  41.7 2.0 %collective-permute-done.12.refs_1_ = bf16[32,1024]{1,0:T(8,128)(2,1)S(1)} collective-permute-done((bf16[32,1024]{1,0:T(8,128)(2,1)S(1)}, bf16[32,1024]{1,0:T(8,128)(2,1)S(1)}, u32[]{:S(2)}, u32[]{:S(2)}) %collective-permute-start.12) | collective-permute-done | bytes 65568 | tf_op jit(solution)/shard_map/ppermute | solution.py:559
  43.7 0.8 %place.2.refs_2_ = bf16[32,8192]{1,0:T(8,128)(2,1)} custom-call(bf16[32,1024]{1,0:T(8,128)(2,1)S(1)} %finish.1.refs_0_, bf16[32,1024]{1,0:T(8,128)(2,1)S(1)} %collective-permute-done.12.refs_1_, bf16[32,1024]{1,0:T(8,128)(2,1)S(1)} %collective-permute-done.13.refs_2_, bf16[32,1024]{1,0:T(8,128)(2,1)S(1)} %collective-permute-done.8.refs_3_, ...), custom_call_target="tpu_custom_call" | custom-call | bytes 1048576 | tf_op jit(solution)/shard_map/place/pallas_call | solution.py:525
  44.5 1.1 %collective-permute-done.9.refs_0_ = bf16[32,1024]{1,0:T(8,128)(2,1)S(1)} collective-permute-done((bf16[32,1024]{1,0:T(8,128)(2,1)S(1)}, bf16[32,1024]{1,0:T(8,128)(2,1)S(1)}, u32[]{:S(2)}, u32[]{:S(2)}) %collective-permute-start.9) | collective-permute-done | bytes 65568 | tf_op jit(solution)/shard_map/ppermute | solution.py:553
  45.6 0.7 %place.3 = bf16[32,8192]{1,0:T(8,128)(2,1)} custom-call(bf16[32,1024]{1,0:T(8,128)(2,1)S(1)} %collective-permute-done.9.refs_0_, bf16[32,1024]{1,0:T(8,128)(2,1)S(1)} %collective-permute-done.11.refs_1_, bf16[32,8192]{1,0:T(8,128)(2,1)} %place.2.refs_2_), custom_call_target="tpu_custom_call", output_to_operand_aliasing={{}: (2, {})} | custom-call | bytes 1048576 | tf_op jit(solution)/shard_map/place/pallas_call | solution.py:525
  (14 shorter events, 0.0 us)
Async XLA Ops:
  0.0 3.5 %copy-start = (s32[128]{0:T(128)S(1)}, s32[128]{0:T(128)}, u32[]{:S(2)}) copy-start(s32[128]{0:T(128)} %slot_ref.3) | copy-start | bytes 1540
  0.0 3.4 %collective-permute-start = (s32[32]{0:T(128)}, s32[32]{0:T(128)S(1)}, u32[]{:S(2)}, u32[]{:S(2)}) collective-permute-start(s32[32]{0:T(128)} %ids_ref.1), channel_id=1, source_target_pairs={{0,8},{8,0},{1,9},{9,1},{2,10},{10,2},{3,11},{11,3},{4,12},{12,4},... | collective-permute-start | bytes 392 | tf_op jit(solution)/shard_map/ppermute | solution.py:562
  3.5 3.8 %copy-start.1 = (s32[32]{0:T(128)S(1)}, s32[32]{0:T(128)}, u32[]{:S(2)}) copy-start(s32[32]{0:T(128)} %ids_ref.1) | copy-start | bytes 388
  7.1 5.1 %collective-permute-start.1 = (bf16[2,8,64,1024]{3,2,1,0:T(8,128)(2,1)S(1)}, bf16[2,8,64,1024]{3,2,1,0:T(8,128)(2,1)S(1)}, u32[]{:S(2)}, u32[]{:S(2)}) collective-permute-start(bf16[2,8,64,1024]{3,2,1,0:T(8,128)(2,1)S(1)} %get-tuple-element.42), channel_id=1, source_target_pairs={{0,8},{8,0},{1,9},{9,1},{2,10},{10,2},{3,11},{11,3},{4,12},{12,4},... | collective-permute-start | bytes 6291464 | tf_op jit(solution)/shard_map/ppermute | solution.py:562
  13.3 7.4 %collective-permute-start.2 = (bf16[32,2176]{1,0:T(8,128)(2,1)S(1)}, bf16[32,2176]{1,0:T(8,128)(2,1)S(1)}, u32[]{:S(2)}, u32[]{:S(2)}) collective-permute-start(bf16[32,2176]{1,0:T(8,128)(2,1)S(1)} %get-tuple-element.49), channel_id=1, source_target_pairs={{0,1},{1,0},{2,3},{3,2},{4,5},{5,4},{6,7},{7,6},{8,9},{9,8},{10,11... | collective-permute-start | bytes 417800 | tf_op jit(solution)/shard_map/ppermute | solution.py:553
  19.1 12.4 %collective-permute-start.4 = (bf16[32,1152]{1,0:T(8,128)(2,1)S(1)}, bf16[32,1152]{1,0:T(8,128)(2,1)S(1)}, u32[]{:S(2)}, u32[]{:S(2)}) collective-permute-start(bf16[32,1152]{1,0:T(8,128)(2,1)S(1)} %get-tuple-element.53), channel_id=1, source_target_pairs={{0,2},{1,3},{2,0},{3,1},{4,6},{5,7},{6,4},{7,5},{8,10},{9,11},{10,... | collective-permute-start | bytes 221192 | tf_op jit(solution)/shard_map/ppermute | solution.py:556
  20.7 10.7 %collective-permute-start.5 = (bf16[32,1152]{1,0:T(8,128)(2,1)S(1)}, bf16[32,1152]{1,0:T(8,128)(2,1)S(1)}, u32[]{:S(2)}, u32[]{:S(2)}) collective-permute-start(bf16[32,1152]{1,0:T(8,128)(2,1)S(1)} %get-tuple-element.54), channel_id=1, source_target_pairs={{0,3},{1,2},{2,1},{3,0},{4,7},{5,6},{6,5},{7,4},{8,11},{9,10},{10,... | collective-permute-start | bytes 221192 | tf_op jit(solution)/shard_map/ppermute | solution.py:559
  21.2 10.9 %collective-permute-start.6 = (bf16[32,1152]{1,0:T(8,128)(2,1)S(1)}, bf16[32,1152]{1,0:T(8,128)(2,1)S(1)}, u32[]{:S(2)}, u32[]{:S(2)}) collective-permute-start(bf16[32,1152]{1,0:T(8,128)(2,1)S(1)} %add_block.2.rest_0_), channel_id=1, source_target_pairs={{0,6},{1,7},{2,4},{3,5},{4,2},{5,3},{6,0},{7,1},{8,14},{9,15},{10,... | collective-permute-start | bytes 221192 | tf_op jit(solution)/shard_map/ppermute | solution.py:556
  25.6 6.4 %collective-permute-start.7 = (bf16[32,1152]{1,0:T(8,128)(2,1)S(1)}, bf16[32,1152]{1,0:T(8,128)(2,1)S(1)}, u32[]{:S(2)}, u32[]{:S(2)}) collective-permute-start(bf16[32,1152]{1,0:T(8,128)(2,1)S(1)} %add_block.3.rest_0_), channel_id=1, source_target_pairs={{0,4},{1,5},{2,6},{3,7},{4,0},{5,1},{6,2},{7,3},{8,12},{9,13},{10,... | collective-permute-start | bytes 221192 | tf_op jit(solution)/shard_map/ppermute | solution.py:556
  27.8 4.3 %collective-permute-start.3 = (bf16[32,1024]{1,0:T(8,128)(2,1)S(1)}, bf16[32,1024]{1,0:T(8,128)(2,1)S(1)}, u32[]{:S(2)}, u32[]{:S(2)}) collective-permute-start(bf16[32,1024]{1,0:T(8,128)(2,1)S(1)} %near_blocks.2.after_ref), channel_id=1, source_target_pairs={{0,1},{1,0},{2,3},{3,2},{4,5},{5,4},{6,7},{7,6},{8,9},{9,8},{10,11... | collective-permute-start | bytes 196616 | tf_op jit(solution)/shard_map/ppermute | solution.py:553
  32.4 6.5 %collective-permute-start.10 = (bf16[32,1024]{1,0:T(8,128)(2,1)S(1)}, bf16[32,1024]{1,0:T(8,128)(2,1)S(1)}, u32[]{:S(2)}, u32[]{:S(2)}) collective-permute-start(bf16[32,1024]{1,0:T(8,128)(2,1)S(1)} %finish.1.refs_0_), channel_id=1, source_target_pairs={{0,6},{1,7},{2,4},{3,5},{4,2},{5,3},{6,0},{7,1},{8,14},{9,15},{10,... | collective-permute-start | bytes 196616 | tf_op jit(solution)/shard_map/ppermute | solution.py:556
  34.4 6.9 %collective-permute-start.8 = (bf16[32,1024]{1,0:T(8,128)(2,1)S(1)}, bf16[32,1024]{1,0:T(8,128)(2,1)S(1)}, u32[]{:S(2)}, u32[]{:S(2)}) collective-permute-start(bf16[32,1024]{1,0:T(8,128)(2,1)S(1)} %finish.1.refs_0_), channel_id=1, source_target_pairs={{0,4},{1,5},{2,6},{3,7},{4,0},{5,1},{6,2},{7,3},{8,12},{9,13},{10,... | collective-permute-start | bytes 196616 | tf_op jit(solution)/shard_map/ppermute | solution.py:556
  35.5 5.9 %collective-permute-start.14 = (bf16[32,1024]{1,0:T(8,128)(2,1)S(1)}, bf16[32,1024]{1,0:T(8,128)(2,1)S(1)}, u32[]{:S(2)}, u32[]{:S(2)}) collective-permute-start(bf16[32,1024]{1,0:T(8,128)(2,1)S(1)} %finish.1.refs_0_), channel_id=1, source_target_pairs={{0,1},{1,0},{2,3},{3,2},{4,5},{5,4},{6,7},{7,6},{8,9},{9,8},{10,11... | collective-permute-start | bytes 196616 | tf_op jit(solution)/shard_map/ppermute | solution.py:559
  37.0 4.7 %collective-permute-start.13 = (bf16[32,1024]{1,0:T(8,128)(2,1)S(1)}, bf16[32,1024]{1,0:T(8,128)(2,1)S(1)}, u32[]{:S(2)}, u32[]{:S(2)}) collective-permute-start(bf16[32,1024]{1,0:T(8,128)(2,1)S(1)} %finish.1.refs_0_), channel_id=1, source_target_pairs={{0,2},{1,3},{2,0},{3,1},{4,6},{5,7},{6,4},{7,5},{8,10},{9,11},{10,... | collective-permute-start | bytes 196616 | tf_op jit(solution)/shard_map/ppermute | solution.py:556
  38.4 5.3 %collective-permute-start.12 = (bf16[32,1024]{1,0:T(8,128)(2,1)S(1)}, bf16[32,1024]{1,0:T(8,128)(2,1)S(1)}, u32[]{:S(2)}, u32[]{:S(2)}) collective-permute-start(bf16[32,1024]{1,0:T(8,128)(2,1)S(1)} %finish.1.refs_0_), channel_id=1, source_target_pairs={{0,3},{1,2},{2,1},{3,0},{4,7},{5,6},{6,5},{7,4},{8,11},{9,10},{10,... | collective-permute-start | bytes 196616 | tf_op jit(solution)/shard_map/ppermute | solution.py:559
  39.0 5.5 %collective-permute-start.11 = (bf16[32,1024]{1,0:T(8,128)(2,1)S(1)}, bf16[32,1024]{1,0:T(8,128)(2,1)S(1)}, u32[]{:S(2)}, u32[]{:S(2)}) collective-permute-start(bf16[32,1024]{1,0:T(8,128)(2,1)S(1)} %collective-permute-done.10.refs_5_), channel_id=1, source_target_pairs={{0,1},{1,0},{2,3},{3,2},{4,5},{5,4},{6,7},{7,6},{8,9},{9,8},{10,11... | collective-permute-start | bytes 196616 | tf_op jit(solution)/shard_map/ppermute | solution.py:553
  41.3 4.3 %collective-permute-start.9 = (bf16[32,1024]{1,0:T(8,128)(2,1)S(1)}, bf16[32,1024]{1,0:T(8,128)(2,1)S(1)}, u32[]{:S(2)}, u32[]{:S(2)}) collective-permute-start(bf16[32,1024]{1,0:T(8,128)(2,1)S(1)} %collective-permute-done.8.refs_3_), channel_id=1, source_target_pairs={{0,1},{1,0},{2,3},{3,2},{4,5},{5,4},{6,7},{7,6},{8,9},{9,8},{10,11... | collective-permute-start | bytes 196616 | tf_op jit(solution)/shard_map/ppermute | solution.py:553

commit v11 on v10

--- a/solution.py
+++ b/solution.py
@@ -76,7 +76,7 @@
 
 
 def prefix_scores_kernel(
-    q_ref, prefix_ref, suffix_ref, query_ref, scores_ref, peak_ref, suf_keys_ref, qbuf, keys, rowbuf, sem, sem_keys
+    q_ref, prefix_ref, suffix_ref, query_ref, scores_ref, peak_ref, vals_ref, suf_keys_ref, qbuf, keys, rowbuf, sem, sem_keys
 ):
     rows = q_ref.shape[0]
     tokens, head_dim = keys.shape
@@ -90,7 +90,10 @@
         for j in range(parts)
     ]
     fetch_q = pltpu.make_async_copy(q_ref, qbuf, sem.at[0])
-    fetch = [pltpu.make_async_copy(suffix_ref.at[:, 0, 0], suf_keys_ref, sem.at[1])]
+    fetch = [
+        pltpu.make_async_copy(suffix_ref.at[:, 0, 0], suf_keys_ref, sem.at[1]),
+        pltpu.make_async_copy(prefix_ref.at[0, 1], vals_ref, sem.at[2]),
+    ]
     for c in [fetch_q] + key_copies + fetch:
         c.start()
     fetch_q.wait()
@@ -122,27 +125,18 @@
     return copies
 
 
-def suffix_scores_kernel(spots, ids_ref, slot_ref, query_ref, suf_keys_ref, peak_ref, *rest):
-    len_ref, prefix_ref, pages_ref, weight_ref = rest[:4]
-    tail_ref, high_ref, high_row_ref, vals_t_ref, out_pages_ref = rest[4:9]
-    w_refs = rest[9 : 9 + len(spots)]
-    lens, vals_ref, seen, list_id, list_pos, sem, sem_page, sem_w = rest[9 + len(spots) :]
+def suffix_scores_kernel(spots, ids_ref, slot_ref, query_ref, suf_keys_ref, vals_ref, peak_ref, *rest):
+    len_ref, suffix_ref, pages_ref, weight_ref = rest[:4]
+    tail_ref, high_ref, high_row_ref, vals_t_ref, out_pages_ref, suf_vals_ref = rest[4:10]
+    w_refs = rest[10 : 10 + len(spots)]
+    lens, seen, list_id, list_pos, sem, sem_page, sem_w = rest[10 + len(spots) :]
     rows, span, head_dim = suf_keys_ref.shape
     tokens = vals_ref.shape[0]
-    parts = sem.shape[0] - 1
-    size = tokens // parts
     heads = query_ref.shape[0] // rows
-    fetch_len = pltpu.make_async_copy(len_ref, lens, sem.at[parts])
+    fetch_len = pltpu.make_async_copy(len_ref, lens, sem.at[1])
     fetch_len.start()
-    val_copies = [
-        pltpu.make_async_copy(
-            prefix_ref.at[0, 1, pl.ds(j * size, size)], vals_ref.at[pl.ds(j * size, size)], sem.at[j]
-        )
-        for j in range(parts)
-    ]
-    for c in val_copies:
-        c.start()
-    fetch = weight_copies(weight_ref, w_refs, spots, sem_w)
+    fetch = [pltpu.make_async_copy(suffix_ref.at[:, 0, 1], suf_vals_ref, sem.at[0])]
+    fetch += weight_copies(weight_ref, w_refs, spots, sem_w)
     distinct_list(ids_ref, slot_ref, seen, list_id, list_pos)
     outs = (out_pages_ref.at[0], out_pages_ref.at[1])
     page_copies(pages_ref, outs, list_pos, sem_page, False)
@@ -159,11 +153,9 @@
             row = 2 * i + a
             tail_ref[row * heads : (row + 1) * heads, :] = jnp.where(lanes < lens[row], mine, -1.0e30)
     vals_t_ref[head_dim:, :] = jnp.ones((vals_t_ref.shape[0] - head_dim, tokens), BF16)
-    step = min(1024, size)
-    for j in range(parts):
-        val_copies[j].wait()
-        for base in range(j * size, (j + 1) * size, step):
-            vals_t_ref[:head_dim, base : base + step] = vals_ref[base : base + step, :].astype(F32).T.astype(BF16)
+    step = min(1024, tokens)
+    for base in range(0, tokens, step):
+        vals_t_ref[:head_dim, base : base + step] = vals_ref[base : base + step, :].astype(F32).T.astype(BF16)
     best = jnp.maximum(tail_ref[:, :128], tail_ref[:, 128:256])
     for b in range(2, span // 128):
         best = jnp.maximum(best, tail_ref[:, b * 128 : (b + 1) * 128])
@@ -176,14 +168,12 @@
         c.wait()
 
 
-def values_kernel(spots, ids_ref, slot_ref, scores, tail, peak, peak_row, vals_t_ref, suffix_ref, *rest):
+def values_kernel(spots, ids_ref, slot_ref, scores, tail, peak, peak_row, vals_t_ref, suf_vals_ref, *rest):
     pages_ref, weight_ref, residual_ref = rest[:3]
     att_ref, shrink_ref, expand_ref, row_slot_ref, slot_mine_ref, res_ref = rest[3:9]
     w_refs = rest[9 : 9 + len(spots)]
-    suf_vals_ref, rowbuf, total, acc, acc_t, seen, list_id, list_pos, sem, sem_page, sem_w = rest[9 + len(spots) :]
+    rowbuf, total, acc, acc_t, seen, list_id, list_pos, sem, sem_page, sem_w = rest[9 + len(spots) :]
     rows, span, head_dim = suf_vals_ref.shape
-    fetch_vals = pltpu.make_async_copy(suffix_ref.at[:, 0, 1], suf_vals_ref, sem.at[1])
-    fetch_vals.start()
     tokens = vals_t_ref.shape[1]
     heads = att_ref.shape[1] // head_dim
     width = res_ref.shape[1]
@@ -229,7 +219,6 @@
 
     across_rows = jnp.broadcast_to(acc_t[head_dim : head_dim + 1, :], (128, n_q))
     acc[...] = acc_t[:head_dim, :].T
-    fetch_vals.wait()
     zeros = jnp.zeros((heads, span), F32)
     for i in range(rows // 2):
         lo = 2 * heads * i
@@ -283,13 +272,14 @@
     span = suffix_kv.shape[3]
     prefix_kv, suffix_kv, out_weight = in_hbm(prefix_kv), in_hbm(suffix_kv), in_hbm(out_weight)
     pages, residual = in_hbm(pages), in_hbm(residual)
-    query, scores, peak, suf_keys = kernel_call(
+    query, scores, peak, vals, suf_keys = kernel_call(
         prefix_scores_kernel,
         "prefix_scores",
         [
             pltpu.VMEM((n_q, head_dim), BF16),
             pltpu.VMEM((tokens, n_q), F32),
             pltpu.VMEM((8, n_q), F32),
+            pltpu.VMEM((tokens, head_dim), BF16),
             pltpu.VMEM((rows, span, head_dim), BF16),
         ],
         [ANY, ANY, ANY],
@@ -297,7 +287,7 @@
             pltpu.VMEM(queries.shape, BF16),
             pltpu.VMEM((tokens, head_dim), BF16),
             pltpu.VMEM((n_q, head_dim), F32),
-            pltpu.SemaphoreType.DMA((2,)),
+            pltpu.SemaphoreType.DMA((3,)),
             pltpu.SemaphoreType.DMA((4,)),
         ],
         [in_hbm(queries), prefix_kv, suffix_kv],
@@ -308,7 +298,7 @@
     far = list(range(n_z - 1, -1, -1))
     early = [(0, k) for k in far[: n_z // 4]]
     late = [(1, k) for k in far if k > 1] + [(0, k) for k in far[n_z // 4 :] if k > 1]
-    tail, high, high_row, vals_t, out_pages, *early_w = kernel_call(
+    tail, high, high_row, vals_t, out_pages, suf_vals, *early_w = kernel_call(
         functools.partial(suffix_scores_kernel, early),
         "suffix_scores",
         [
@@ -317,17 +307,18 @@
             pltpu.VMEM((8, n_q), F32),
             pltpu.VMEM((head_dim + 16, tokens), BF16),
             pltpu.VMEM((2, DISTINCT) + pages.shape[2:], BF16),
+            pltpu.VMEM((rows, span, head_dim), BF16),
         ]
         + [pltpu.VMEM((in_rows, width), BF16)] * len(early),
-        [SMEM, SMEM, VMEM, VMEM, VMEM, ANY, ANY, ANY, ANY],
-        [pltpu.SMEM((rows,), jnp.int32), pltpu.VMEM((tokens, head_dim), BF16)]
+        [SMEM, SMEM, VMEM, VMEM, VMEM, VMEM, ANY, ANY, ANY, ANY],
+        [pltpu.SMEM((rows,), jnp.int32)]
         + list_scratch(pool_slot)
         + [
-            pltpu.SemaphoreType.DMA((5,)),
+            pltpu.SemaphoreType.DMA((2,)),
             pltpu.SemaphoreType.DMA((2, DISTINCT)),
             pltpu.SemaphoreType.DMA((len(early),)),
         ],
-        [other_ids, pool_slot, query, suf_keys, peak, in_hbm(suffix_len), prefix_kv, pages, out_weight],
+        [other_ids, pool_slot, query, suf_keys, vals, peak, in_hbm(suffix_len), suffix_kv, pages, out_weight],
         8,
         1 << 29,
         7 * MIB,
@@ -345,9 +336,8 @@
             pltpu.VMEM((rows, width), BF16),
         ]
         + [pltpu.VMEM((in_rows, width), BF16)] * len(late),
-        [SMEM, SMEM, VMEM, VMEM, VMEM, VMEM, VMEM, ANY, ANY, ANY, ANY],
+        [SMEM, SMEM, VMEM, VMEM, VMEM, VMEM, VMEM, VMEM, ANY, ANY, ANY],
         [
-            pltpu.VMEM((rows, span, head_dim), BF16),
             pltpu.VMEM((n_q, head_dim), F32),
             pltpu.VMEM((n_q, 128), F32),
             pltpu.VMEM((n_q, head_dim), F32),
@@ -359,7 +349,7 @@
             pltpu.SemaphoreType.DMA((2, DISTINCT)),
             pltpu.SemaphoreType.DMA((len(late),)),
         ],
-        [ids, pool_slot, scores, tail, high, high_row, vals_t, suffix_kv, pages, out_weight, residual],
+        [ids, pool_slot, scores, tail, high, high_row, vals_t, suf_vals, pages, out_weight, residual],
         8,
         2 * n_q * tokens * head_dim,
         14 * MIB,
@@ -613,7 +603,7 @@
     crossed = [along_both(result, k) if k < 2 else along_y(held[k]) for k in range(n_z)]
     spots = [(0, 0), (1, 1), (1, 0)] + [(k, side) for k in range(2, n_z) for side in (0, 1)]
     spots.insert(len(spots) - 2, (0, 1))
-    forwarded = [(k, side) for k, side in spots if k > 1 and side]
+    forwarded = [(k, side) for k, side in spots if k and side]
     placed = None
     for group in ([p for p in spots if p not in forwarded], forwarded):
         placed = place([(crossed if side else held)[k] for k, side in group], group, n_tensor, placed)

time: 46.5 us -> 45.7 us (0.983)
    ppermute x3, waiting for transfers between devices: 2.01 us -> 1.24 us  [along_both(): lax.ppermute(x, 'tensor', [(t, t ^ 2 * k ^ 1) for t in range(n_tensor)])]
    ppermute x4, waiting for transfers between devices: 1.76 us -> 2.39 us  [along_y(): return lax.ppermute(x, 'tensor', [(t, t ^ 1) for t in range(n_tensor)])]
  transfers between devices with their start and end apart: 15 -> 15, of which waited for: 5 -> 6; matrix products, arithmetic and copies ran while one was open for 0% -> 0% of each run, Pallas kernels for 36% -> 35%
where the time goes in v11:
time: 45.7 us; the launch traced here: 45.4 us
  Pallas kernels  21.8 us (48%)
  starting transfers between devices  19.1 us (42%)
  waiting for transfers between devices  4.42 us (10%)
    pallas_call x6, Pallas kernels, kernel_call(): pl.pallas_call(kernel, out_shape=out_shape, in_specs=specs, out_specs=[VM...  17.9 us
    ppermute x6, starting transfers between devices, along_z(): return lax.ppermute(x, 'tensor', [(t, t ^ 2 * k) for t in range(n_tensor)])  10.1 us
    ppermute x4, starting transfers between devices, along_y(): return lax.ppermute(x, 'tensor', [(t, t ^ 1) for t in range(n_tensor)])  6.37 us
    ppermute x4, waiting for transfers between devices, along_y(): return lax.ppermute(x, 'tensor', [(t, t ^ 1) for t in range(n_tensor)])  2.39 us
    pallas_call x4, Pallas kernels, small_call(): pl.pallas_call(kernel, out_shape=out_shape, in_specs=[VMEM] * len(operand...  2.38 us
    ppermute x3, starting transfers between devices, along_both(): lax.ppermute(x, 'tensor', [(t, t ^ 2 * k ^ 1) for t in range(n_tensor)])  2.11 us
    pallas_call x2, Pallas kernels, place(): pl.pallas_call(functools.partial(place_kernel, spots), out_shape=pltpu.HB...  1.45 us
    ppermute x3, waiting for transfers between devices, along_both(): lax.ppermute(x, 'tensor', [(t, t ^ 2 * k ^ 1) for t in range(n_tensor)])  1.24 us
  transfers between devices with their start and end apart: 15, of which 6 were waited for; matrix products, arithmetic and copies ran while one was open for 0% of the time, Pallas kernels for 35%

profile of v11, /device:TPU:0, one launch (start us, length us, event | category | flops | bytes accessed | tf_op | source)
XLA Modules:
  0.0 45.4 jit_solution(16697518990567676184)
XLA Ops:
  0.0 0.5 collective-permute-start
  0.5 3.0 %prefix_scores.1 = (bf16[256,128]{1,0:T(8,128)(2,1)S(1)}, f32[8192,256]{1,0:T(8,128)S(1)}, f32[8,256]{1,0:T(8,128)S(1)}, bf16[8192,128]{1,0:T(8,128)(2,1)S(1)}, bf16[32,256,128]{2,1,0:T(8,128)(2,1)S(1)}) custom-call(bf16[32,1024]{1,0:T(8,128)(2,1)} %q_ref.1, bf16[1,2,8192,128]{3,2,1,0:T(8,128)(2,1)} %prefix_ref.1, bf16[32,1,2,256,128]{4,3,2,1,0:T(8,128)(2,1)} %rest_1_.2), custom_call_target="tpu_custom_call" | custom-call | flops 536870912 | bytes 6291456 | tf_op jit(solution)/shard_map/prefix_scores/pallas_call | solution.py:251
  3.5 3.6 %suffix_scores.1 = (f32[256,256]{1,0:T(8,128)S(1)}, f32[256,128]{1,0:T(8,128)S(1)}, f32[8,256]{1,0:T(8,128)S(1)}, bf16[144,8192]{1,0:T(8,128)(2,1)S(1)}, bf16[2,...) custom-call(s32[32]{0:T(128)S(1)} %collective-permute-done.ids_ref, ...), custom_call_target="tpu_custom_call" | custom-call | flops 536870912 | bytes 7340032 | tf_op jit(solution)/shard_map/suffix_scores/pallas_call | solution.py:251
  7.0 0.1 collective-permute-start.1
  7.1 4.5 %values.1 = (bf16[32,1024]{1,0:T(8,128)(2,1)S(1)}, bf16[8,64,1024]{2,1,0:T(8,128)(2,1)S(1)}, bf16[8,64,1024]{2,1,0:T(8,128)(2,1)S(1)}, s32[32,128]{1,0:T(8,128)S...) custom-call(s32[32]{0:T(128)S(1)} %copy-done.1, ...), custom_call_target="tpu_custom_call" | custom-call | flops 536870912 | bytes 14680064 | tf_op jit(solution)/shard_map/values/pallas_call | solution.py:251
  11.6 1.1 %far_blocks.1 = (bf16[32,2176]{1,0:T(8,128)(2,1)S(1)}, f32[32,128]{1,0:T(8,128)S(1)}) custom-call(bf16[32,1024]{1,0:T(8,128)(2,1)S(1)} %get-tuple-element.42.att_ref, s32[32,128]{1,0:T(8,128)S(1)} %get-tuple-element.47.row_slot_ref.refs_2_, s32[8,128]{1,0:T(8,128)S(1)} %get-tuple-element.44.slot_mine_ref, ...), custom_call_target="tpu_custom_call" | custom-call | flops 134217728 | bytes 2097152 | tf_op jit(solution)/shard_map/far_blocks/pallas_call | solution.py:362
  12.8 2.9 %collective-permute-start.2 = (bf16[32,2176]{1,0:T(8,128)(2,1)S(1)}, bf16[32,2176]{1,0:T(8,128)(2,1)S(1)}, u32[]{:S(2)}, u32[]{:S(2)}) collective-permute-start(bf16[32,2176]{1,0:T(8,128)(2,1)S(1)} %get-tuple-element.53), channel_id=1, source_target_pairs={{0,1},{1,0},{2,3},{3,2},{4,5},{5,4},{6,7},{7,6},{8,9},{9,8},{10,11... | collective-permute-start | bytes 417800 | tf_op jit(solution)/shard_map/ppermute | solution.py:543
  15.6 2.7 %near_blocks.3 = (bf16[32,1152]{1,0:T(8,128)(2,1)S(1)}, bf16[32,1152]{1,0:T(8,128)(2,1)S(1)}) custom-call(bf16[32,1024]{1,0:T(8,128)(2,1)S(1)} %get-tuple-element.42.att_ref, f32[32,128]{1,0:T(8,128)S(1)} %get-tuple-element.51.rank_ref.refs_3_, bf16[1024,8192]{1,0:T(8,128)(2,1)} %weight_ref.5), custom_call_target="tpu_custom_call" | custom-call | flops 134217728 | bytes 4194304 | tf_op jit(solution)/shard_map/near_blocks/pallas_call | solution.py:251
  18.4 1.6 %collective-permute-start.4 = (bf16[32,1152]{1,0:T(8,128)(2,1)S(1)}, bf16[32,1152]{1,0:T(8,128)(2,1)S(1)}, u32[]{:S(2)}, u32[]{:S(2)}) collective-permute-start(bf16[32,1152]{1,0:T(8,128)(2,1)S(1)} %get-tuple-element.57), channel_id=1, source_target_pairs={{0,2},{1,3},{2,0},{3,1},{4,6},{5,7},{6,4},{7,5},{8,10},{9,11},{10,... | collective-permute-start | bytes 221192 | tf_op jit(solution)/shard_map/ppermute | solution.py:546
  20.0 0.0 collective-permute-start.5
  20.0 0.5 %add_block.2.rest_0_ = bf16[32,1152]{1,0:T(8,128)(2,1)S(1)} custom-call(bf16[32,1024]{1,0:T(8,128)(2,1)S(1)} %get-tuple-element.42.att_ref, bf16[1024,1024]{1,0:T(8,128)(2,1)S(1)} %get-tuple-element.54.w_ref, bf16[32,2176]{1,0:T(8,128)(2,1)S(1)} %collective-permute-done.2.from_ref.refs_4_, f32[32,128]{1,0:T(8,128)S(1)} %get-tuple-element.51.rank_ref.refs_3_), custom_call_target="tpu_custom_call" | custom-call | flops 134217728 | bytes 2097152 | tf_op jit(solution)/shard_map/add_block/pallas_call | solution.py:362
  20.5 4.0 %collective-permute-start.6 = (bf16[32,1152]{1,0:T(8,128)(2,1)S(1)}, bf16[32,1152]{1,0:T(8,128)(2,1)S(1)}, u32[]{:S(2)}, u32[]{:S(2)}) collective-permute-start(bf16[32,1152]{1,0:T(8,128)(2,1)S(1)} %add_block.2.rest_0_), channel_id=1, source_target_pairs={{0,6},{1,7},{2,4},{3,5},{4,2},{5,3},{6,0},{7,1},{8,14},{9,15},{10,... | collective-permute-start | bytes 221192 | tf_op jit(solution)/shard_map/ppermute | solution.py:546
  24.5 0.5 %add_block.3.rest_0_ = bf16[32,1152]{1,0:T(8,128)(2,1)S(1)} custom-call(bf16[32,1024]{1,0:T(8,128)(2,1)S(1)} %get-tuple-element.42.att_ref, bf16[1024,1024]{1,0:T(8,128)(2,1)S(1)} %get-tuple-element.52.w_ref, bf16[32,2176]{1,0:T(8,128)(2,1)S(1)} %collective-permute-done.2.from_ref.refs_4_, f32[32,128]{1,0:T(8,128)S(1)} %get-tuple-element.51.rank_ref.refs_3_, ...), custom_call_target="tpu_custom_call" | custom-call | flops 134217728 | bytes 2097152 | tf_op jit(solution)/shard_map/add_block/pallas_call | solution.py:362
  25.0 2.1 %near_blocks.2.after_ref = bf16[32,1024]{1,0:T(8,128)(2,1)S(1)} custom-call(bf16[32,1024]{1,0:T(8,128)(2,1)S(1)} %get-tuple-element.42.att_ref, f32[32,128]{1,0:T(8,128)S(1)} %get-tuple-element.51.rank_ref.refs_3_, bf16[1024,8192]{1,0:T(8,128)(2,1)} %weight_ref.5, bf16[32,1152]{1,0:T(8,128)(2,1)S(1)} %add_block.3.rest_0_), custom_call_target="tpu_custom_call" | custom-call | flops 134217728 | bytes 2097152 | tf_op jit(solution)/shard_map/near_blocks/pallas_call | solution.py:251
  27.1 1.6 %collective-permute-start.3 = (bf16[32,1024]{1,0:T(8,128)(2,1)S(1)}, bf16[32,1024]{1,0:T(8,128)(2,1)S(1)}, u32[]{:S(2)}, u32[]{:S(2)}) collective-permute-start(bf16[32,1024]{1,0:T(8,128)(2,1)S(1)} %near_blocks.2.after_ref), channel_id=1, source_target_pairs={{0,1},{1,0},{2,3},{3,2},{4,5},{5,4},{6,7},{7,6},{8,9},{9,8},{10,11... | collective-permute-start | bytes 196616 | tf_op jit(solution)/shard_map/ppermute | solution.py:543
  28.6 2.1 %own_block.1 = (f32[32,1024]{1,0:T(8,128)S(1)}, bf16[512,1024]{1,0:T(8,128)(2,1)S(1)}) custom-call(bf16[32,1024]{1,0:T(8,128)(2,1)S(1)} %get-tuple-element.42.att_ref, bf16[32,1024]{1,0:T(8,128)(2,1)S(1)} %get-tuple-element.43.res_ref, s32[8,128]{1,0:T(8,128)S(1)} %get-tuple-element.44.slot_mine_ref, bf16[8,64,1024]{2,1,0:T(8,128)(2,1)S(1)} %get-tuple-element.45.own_ref, ...), custom_call_target="tpu_custom_call" | custom-call | bytes 2097152 | tf_op jit(solution)/shard_map/own_block/pallas_call | solution.py:251
  30.8 0.6 %collective-permute-done.3.refs_5_ = bf16[32,1024]{1,0:T(8,128)(2,1)S(1)} collective-permute-done((bf16[32,1024]{1,0:T(8,128)(2,1)S(1)}, bf16[32,1024]{1,0:T(8,128)(2,1)S(1)}, u32[]{:S(2)}, u32[]{:S(2)}) %collective-permute-start.3) | collective-permute-done | bytes 65568 | tf_op jit(solution)/shard_map/ppermute | solution.py:543
  31.4 0.3 finish.1.refs_0_
  31.7 2.0 %collective-permute-start.11 = (bf16[32,1024]{1,0:T(8,128)(2,1)S(1)}, bf16[32,1024]{1,0:T(8,128)(2,1)S(1)}, u32[]{:S(2)}, u32[]{:S(2)}) collective-permute-start(bf16[32,1024]{1,0:T(8,128)(2,1)S(1)} %finish.1.refs_0_), channel_id=1, source_target_pairs={{0,6},{1,7},{2,4},{3,5},{4,2},{5,3},{6,0},{7,1},{8,14},{9,15},{10,... | collective-permute-start | bytes 196616 | tf_op jit(solution)/shard_map/ppermute | solution.py:546
  33.7 1.1 %collective-permute-start.9 = (bf16[32,1024]{1,0:T(8,128)(2,1)S(1)}, bf16[32,1024]{1,0:T(8,128)(2,1)S(1)}, u32[]{:S(2)}, u32[]{:S(2)}) collective-permute-start(bf16[32,1024]{1,0:T(8,128)(2,1)S(1)} %finish.1.refs_0_), channel_id=1, source_target_pairs={{0,4},{1,5},{2,6},{3,7},{4,0},{5,1},{6,2},{7,3},{8,12},{9,13},{10,... | collective-permute-start | bytes 196616 | tf_op jit(solution)/shard_map/ppermute | solution.py:546
  34.8 1.5 %collective-permute-start.14 = (bf16[32,1024]{1,0:T(8,128)(2,1)S(1)}, bf16[32,1024]{1,0:T(8,128)(2,1)S(1)}, u32[]{:S(2)}, u32[]{:S(2)}) collective-permute-start(bf16[32,1024]{1,0:T(8,128)(2,1)S(1)} %finish.1.refs_0_), channel_id=1, source_target_pairs={{0,1},{1,0},{2,3},{3,2},{4,5},{5,4},{6,7},{7,6},{8,9},{9,8},{10,11... | collective-permute-start | bytes 196616 | tf_op jit(solution)/shard_map/ppermute | solution.py:549
  36.3 1.4 %collective-permute-start.13 = (bf16[32,1024]{1,0:T(8,128)(2,1)S(1)}, bf16[32,1024]{1,0:T(8,128)(2,1)S(1)}, u32[]{:S(2)}, u32[]{:S(2)}) collective-permute-start(bf16[32,1024]{1,0:T(8,128)(2,1)S(1)} %finish.1.refs_0_), channel_id=1, source_target_pairs={{0,2},{1,3},{2,0},{3,1},{4,6},{5,7},{6,4},{7,5},{8,10},{9,11},{10,... | collective-permute-start | bytes 196616 | tf_op jit(solution)/shard_map/ppermute | solution.py:546
  37.7 0.6 %collective-permute-start.8 = (bf16[32,1024]{1,0:T(8,128)(2,1)S(1)}, bf16[32,1024]{1,0:T(8,128)(2,1)S(1)}, u32[]{:S(2)}, u32[]{:S(2)}) collective-permute-start(bf16[32,1024]{1,0:T(8,128)(2,1)S(1)} %finish.1.refs_0_), channel_id=1, source_target_pairs={{0,3},{1,2},{2,1},{3,0},{4,7},{5,6},{6,5},{7,4},{8,11},{9,10},{10,... | collective-permute-start | bytes 196616 | tf_op jit(solution)/shard_map/ppermute | solution.py:549
  38.3 1.8 %collective-permute-start.12 = (bf16[32,1024]{1,0:T(8,128)(2,1)S(1)}, bf16[32,1024]{1,0:T(8,128)(2,1)S(1)}, u32[]{:S(2)}, u32[]{:S(2)}) collective-permute-start(bf16[32,1024]{1,0:T(8,128)(2,1)S(1)} %collective-permute-done.11.refs_4_), channel_id=1, source_target_pairs={{0,1},{1,0},{2,3},{3,2},{4,5},{5,4},{6,7},{7,6},{8,9},{9,8},{10,11... | collective-permute-start | bytes 196616 | tf_op jit(solution)/shard_map/ppermute | solution.py:543
  40.1 0.4 collective-permute-done.9.refs_2_
  40.5 0.1 collective-permute-start.10
  40.6 0.4 collective-permute-done.13.refs_1_
  41.0 0.8 %place.2.refs_3_ = bf16[32,8192]{1,0:T(8,128)(2,1)} custom-call(bf16[32,1024]{1,0:T(8,128)(2,1)S(1)} %finish.1.refs_0_, bf16[32,1024]{1,0:T(8,128)(2,1)S(1)} %collective-permute-done.13.refs_1_, bf16[32,1024]{1,0:T(8,128)(2,1)S(1)} %collective-permute-done.9.refs_2_, bf16[32,1024]{1,0:T(8,128)(2,1)S(1)} %collective-permute-done.14.refs_3_, ...), custom_call_target="tpu_custom_call" | custom-call | bytes 1048576 | tf_op jit(solution)/shard_map/place/pallas_call | solution.py:515
  41.7 1.2 %collective-permute-done.8.refs_0_ = bf16[32,1024]{1,0:T(8,128)(2,1)S(1)} collective-permute-done((bf16[32,1024]{1,0:T(8,128)(2,1)S(1)}, bf16[32,1024]{1,0:T(8,128)(2,1)S(1)}, u32[]{:S(2)}, u32[]{:S(2)}) %collective-permute-start.8) | collective-permute-done | bytes 65568 | tf_op jit(solution)/shard_map/ppermute | solution.py:549
  43.0 0.3 collective-permute-done.12.refs_2_
  43.2 1.5 %collective-permute-done.10.refs_1_ = bf16[32,1024]{1,0:T(8,128)(2,1)S(1)} collective-permute-done((bf16[32,1024]{1,0:T(8,128)(2,1)S(1)}, bf16[32,1024]{1,0:T(8,128)(2,1)S(1)}, u32[]{:S(2)}, u32[]{:S(2)}) %collective-permute-start.10) | collective-permute-done | bytes 65568 | tf_op jit(solution)/shard_map/ppermute | solution.py:543
  44.7 0.7 %place.3 = bf16[32,8192]{1,0:T(8,128)(2,1)} custom-call(bf16[32,1024]{1,0:T(8,128)(2,1)S(1)} %collective-permute-done.8.refs_0_, bf16[32,1024]{1,0:T(8,128)(2,1)S(1)} %collective-permute-done.10.refs_1_, bf16[32,1024]{1,0:T(8,128)(2,1)S(1)} %collective-permute-done.12.refs_2_, bf16[32,8192]{1,0:T(8,128)(2,1)} %place.2.refs_3_), custom_call_target="tpu_custom_call", output_to_operand_aliasing={{}: (3, {})} | custom-call | bytes 1048576 | tf_op jit(solution)/shard_map/place/pallas_call | solution.py:515
  (14 shorter events, 0.0 us)
Async XLA Ops:
  0.0 3.4 %copy-start = (s32[128]{0:T(128)S(1)}, s32[128]{0:T(128)}, u32[]{:S(2)}) copy-start(s32[128]{0:T(128)} %slot_ref.3) | copy-start | bytes 1540
  0.0 3.4 %collective-permute-start = (s32[32]{0:T(128)}, s32[32]{0:T(128)S(1)}, u32[]{:S(2)}, u32[]{:S(2)}) collective-permute-start(s32[32]{0:T(128)} %ids_ref.1), channel_id=1, source_target_pairs={{0,8},{8,0},{1,9},{9,1},{2,10},{10,2},{3,11},{11,3},{4,12},{12,4},... | collective-permute-start | bytes 392 | tf_op jit(solution)/shard_map/ppermute | solution.py:552
  3.4 3.7 %copy-start.1 = (s32[32]{0:T(128)S(1)}, s32[32]{0:T(128)}, u32[]{:S(2)}) copy-start(s32[32]{0:T(128)} %ids_ref.1) | copy-start | bytes 388
  7.0 4.6 %collective-permute-start.1 = (bf16[2,8,64,1024]{3,2,1,0:T(8,128)(2,1)S(1)}, bf16[2,8,64,1024]{3,2,1,0:T(8,128)(2,1)S(1)}, u32[]{:S(2)}, u32[]{:S(2)}) collective-permute-start(bf16[2,8,64,1024]{3,2,1,0:T(8,128)(2,1)S(1)} %get-tuple-element.46), channel_id=1, source_target_pairs={{0,8},{8,0},{1,9},{9,1},{2,10},{10,2},{3,11},{11,3},{4,12},{12,4},... | collective-permute-start | bytes 6291464 | tf_op jit(solution)/shard_map/ppermute | solution.py:552
  12.8 7.2 %collective-permute-start.2 = (bf16[32,2176]{1,0:T(8,128)(2,1)S(1)}, bf16[32,2176]{1,0:T(8,128)(2,1)S(1)}, u32[]{:S(2)}, u32[]{:S(2)}) collective-permute-start(bf16[32,2176]{1,0:T(8,128)(2,1)S(1)} %get-tuple-element.53), channel_id=1, source_target_pairs={{0,1},{1,0},{2,3},{3,2},{4,5},{5,4},{6,7},{7,6},{8,9},{9,8},{10,11... | collective-permute-start | bytes 417800 | tf_op jit(solution)/shard_map/ppermute | solution.py:543
  18.4 12.4 %collective-permute-start.4 = (bf16[32,1152]{1,0:T(8,128)(2,1)S(1)}, bf16[32,1152]{1,0:T(8,128)(2,1)S(1)}, u32[]{:S(2)}, u32[]{:S(2)}) collective-permute-start(bf16[32,1152]{1,0:T(8,128)(2,1)S(1)} %get-tuple-element.57), channel_id=1, source_target_pairs={{0,2},{1,3},{2,0},{3,1},{4,6},{5,7},{6,4},{7,5},{8,10},{9,11},{10,... | collective-permute-start | bytes 221192 | tf_op jit(solution)/shard_map/ppermute | solution.py:546
  20.0 10.7 %collective-permute-start.5 = (bf16[32,1152]{1,0:T(8,128)(2,1)S(1)}, bf16[32,1152]{1,0:T(8,128)(2,1)S(1)}, u32[]{:S(2)}, u32[]{:S(2)}) collective-permute-start(bf16[32,1152]{1,0:T(8,128)(2,1)S(1)} %get-tuple-element.58), channel_id=1, source_target_pairs={{0,3},{1,2},{2,1},{3,0},{4,7},{5,6},{6,5},{7,4},{8,11},{9,10},{10,... | collective-permute-start | bytes 221192 | tf_op jit(solution)/shard_map/ppermute | solution.py:549
  20.5 10.9 %collective-permute-start.6 = (bf16[32,1152]{1,0:T(8,128)(2,1)S(1)}, bf16[32,1152]{1,0:T(8,128)(2,1)S(1)}, u32[]{:S(2)}, u32[]{:S(2)}) collective-permute-start(bf16[32,1152]{1,0:T(8,128)(2,1)S(1)} %add_block.2.rest_0_), channel_id=1, source_target_pairs={{0,6},{1,7},{2,4},{3,5},{4,2},{5,3},{6,0},{7,1},{8,14},{9,15},{10,... | collective-permute-start | bytes 221192 | tf_op jit(solution)/shard_map/ppermute | solution.py:546
  24.9 6.4 %collective-permute-start.7 = (bf16[32,1152]{1,0:T(8,128)(2,1)S(1)}, bf16[32,1152]{1,0:T(8,128)(2,1)S(1)}, u32[]{:S(2)}, u32[]{:S(2)}) collective-permute-start(bf16[32,1152]{1,0:T(8,128)(2,1)S(1)} %add_block.3.rest_0_), channel_id=1, source_target_pairs={{0,4},{1,5},{2,6},{3,7},{4,0},{5,1},{6,2},{7,3},{8,12},{9,13},{10,... | collective-permute-start | bytes 221192 | tf_op jit(solution)/shard_map/ppermute | solution.py:546
  27.1 4.3 %collective-permute-start.3 = (bf16[32,1024]{1,0:T(8,128)(2,1)S(1)}, bf16[32,1024]{1,0:T(8,128)(2,1)S(1)}, u32[]{:S(2)}, u32[]{:S(2)}) collective-permute-start(bf16[32,1024]{1,0:T(8,128)(2,1)S(1)} %near_blocks.2.after_ref), channel_id=1, source_target_pairs={{0,1},{1,0},{2,3},{3,2},{4,5},{5,4},{6,7},{7,6},{8,9},{9,8},{10,11... | collective-permute-start | bytes 196616 | tf_op jit(solution)/shard_map/ppermute | solution.py:543
  31.7 6.5 %collective-permute-start.11 = (bf16[32,1024]{1,0:T(8,128)(2,1)S(1)}, bf16[32,1024]{1,0:T(8,128)(2,1)S(1)}, u32[]{:S(2)}, u32[]{:S(2)}) collective-permute-start(bf16[32,1024]{1,0:T(8,128)(2,1)S(1)} %finish.1.refs_0_), channel_id=1, source_target_pairs={{0,6},{1,7},{2,4},{3,5},{4,2},{5,3},{6,0},{7,1},{8,14},{9,15},{10,... | collective-permute-start | bytes 196616 | tf_op jit(solution)/shard_map/ppermute | solution.py:546
  33.7 6.8 %collective-permute-start.9 = (bf16[32,1024]{1,0:T(8,128)(2,1)S(1)}, bf16[32,1024]{1,0:T(8,128)(2,1)S(1)}, u32[]{:S(2)}, u32[]{:S(2)}) collective-permute-start(bf16[32,1024]{1,0:T(8,128)(2,1)S(1)} %finish.1.refs_0_), channel_id=1, source_target_pairs={{0,4},{1,5},{2,6},{3,7},{4,0},{5,1},{6,2},{7,3},{8,12},{9,13},{10,... | collective-permute-start | bytes 196616 | tf_op jit(solution)/shard_map/ppermute | solution.py:546
  34.8 5.8 %collective-permute-start.14 = (bf16[32,1024]{1,0:T(8,128)(2,1)S(1)}, bf16[32,1024]{1,0:T(8,128)(2,1)S(1)}, u32[]{:S(2)}, u32[]{:S(2)}) collective-permute-start(bf16[32,1024]{1,0:T(8,128)(2,1)S(1)} %finish.1.refs_0_), channel_id=1, source_target_pairs={{0,1},{1,0},{2,3},{3,2},{4,5},{5,4},{6,7},{7,6},{8,9},{9,8},{10,11... | collective-permute-start | bytes 196616 | tf_op jit(solution)/shard_map/ppermute | solution.py:549
  36.3 4.7 %collective-permute-start.13 = (bf16[32,1024]{1,0:T(8,128)(2,1)S(1)}, bf16[32,1024]{1,0:T(8,128)(2,1)S(1)}, u32[]{:S(2)}, u32[]{:S(2)}) collective-permute-start(bf16[32,1024]{1,0:T(8,128)(2,1)S(1)} %finish.1.refs_0_), channel_id=1, source_target_pairs={{0,2},{1,3},{2,0},{3,1},{4,6},{5,7},{6,4},{7,5},{8,10},{9,11},{10,... | collective-permute-start | bytes 196616 | tf_op jit(solution)/shard_map/ppermute | solution.py:546
  37.7 5.3 %collective-permute-start.8 = (bf16[32,1024]{1,0:T(8,128)(2,1)S(1)}, bf16[32,1024]{1,0:T(8,128)(2,1)S(1)}, u32[]{:S(2)}, u32[]{:S(2)}) collective-permute-start(bf16[32,1024]{1,0:T(8,128)(2,1)S(1)} %finish.1.refs_0_), channel_id=1, source_target_pairs={{0,3},{1,2},{2,1},{3,0},{4,7},{5,6},{6,5},{7,4},{8,11},{9,10},{10,... | collective-permute-start | bytes 196616 | tf_op jit(solution)/shard_map/ppermute | solution.py:549
  38.3 5.0 %collective-permute-start.12 = (bf16[32,1024]{1,0:T(8,128)(2,1)S(1)}, bf16[32,1024]{1,0:T(8,128)(2,1)S(1)}, u32[]{:S(2)}, u32[]{:S(2)}) collective-permute-start(bf16[32,1024]{1,0:T(8,128)(2,1)S(1)} %collective-permute-done.11.refs_4_), channel_id=1, source_target_pairs={{0,1},{1,0},{2,3},{3,2},{4,5},{5,4},{6,7},{7,6},{8,9},{9,8},{10,11... | collective-permute-start | bytes 196616 | tf_op jit(solution)/shard_map/ppermute | solution.py:543
  40.5 4.3 %collective-permute-start.10 = (bf16[32,1024]{1,0:T(8,128)(2,1)S(1)}, bf16[32,1024]{1,0:T(8,128)(2,1)S(1)}, u32[]{:S(2)}, u32[]{:S(2)}) collective-permute-start(bf16[32,1024]{1,0:T(8,128)(2,1)S(1)} %collective-permute-done.9.refs_2_), channel_id=1, source_target_pairs={{0,1},{1,0},{2,3},{3,2},{4,5},{5,4},{6,7},{7,6},{8,9},{9,8},{10,11... | collective-permute-start | bytes 196616 | tf_op jit(solution)/shard_map/ppermute | solution.py:543

commit v12 on v11

--- a/solution.py
+++ b/solution.py
@@ -600,8 +600,8 @@
         [own, expand_pages, row_slot, rank_own, from_far, from_own] + moved,
     )
     held = [result] + [along_z(result, k) for k in range(1, n_z)]
-    crossed = [along_both(result, k) if k < 2 else along_y(held[k]) for k in range(n_z)]
-    spots = [(0, 0), (1, 1), (1, 0)] + [(k, side) for k in range(2, n_z) for side in (0, 1)]
+    crossed = [along_y(held[k]) for k in range(n_z)]
+    spots = [(k, side) for k in range(n_z) for side in (0, 1) if (k, side) != (0, 1)]
     spots.insert(len(spots) - 2, (0, 1))
     forwarded = [(k, side) for k, side in spots if k and side]
     placed = None

time: 45.7 us -> 46.4 us (1.015)
  starting transfers between devices: 19.1 us -> 19.7 us
    ppermute x4 -> x6, starting transfers between devices: 6.37 us -> 9.03 us  [along_y(): return lax.ppermute(x, 'tensor', [(t, t ^ 1) for t in range(n_tensor)])]
    ppermute x3 -> x1, starting transfers between devices: 2.11 us -> 0.02 us  [along_both(): lax.ppermute(x, 'tensor', [(t, t ^ 2 * k ^ 1) for t in range(n_tensor)])]
    ppermute x3 -> x1, waiting for transfers between devices: 1.24 us -> 0.01 us  [along_both(): lax.ppermute(x, 'tensor', [(t, t ^ 2 * k ^ 1) for t in range(n_tensor)])]
    ppermute x6, waiting for transfers between devices: 0.79 us -> 1.68 us  [along_z(): return lax.ppermute(x, 'tensor', [(t, t ^ 2 * k) for t in range(n_tensor)])]
    ppermute x4 -> x6, waiting for transfers between devices: 2.39 us -> 2.8 us  [along_y(): return lax.ppermute(x, 'tensor', [(t, t ^ 1) for t in range(n_tensor)])]
  transfers between devices with their start and end apart: 15 -> 15, of which waited for: 6 -> 5; matrix products, arithmetic and copies ran while one was open for 0% -> 0% of each run, Pallas kernels for 35% -> 34%
where the time goes in v12:
time: 46.4 us; the launch traced here: 46.1 us
  Pallas kernels  21.8 us (47%)
  starting transfers between devices  19.7 us (42%)
  waiting for transfers between devices  4.49 us (10%)
    pallas_call x6, Pallas kernels, kernel_call(): pl.pallas_call(kernel, out_shape=out_shape, in_specs=specs, out_specs=[VM...  17.9 us
    ppermute x6, starting transfers between devices, along_z(): return lax.ppermute(x, 'tensor', [(t, t ^ 2 * k) for t in range(n_tensor)])  10.1 us
    ppermute x6, starting transfers between devices, along_y(): return lax.ppermute(x, 'tensor', [(t, t ^ 1) for t in range(n_tensor)])  9.03 us
    ppermute x6, waiting for transfers between devices, along_y(): return lax.ppermute(x, 'tensor', [(t, t ^ 1) for t in range(n_tensor)])  2.8 us
    pallas_call x4, Pallas kernels, small_call(): pl.pallas_call(kernel, out_shape=out_shape, in_specs=[VMEM] * len(operand...  2.38 us
    ppermute x6, waiting for transfers between devices, along_z(): return lax.ppermute(x, 'tensor', [(t, t ^ 2 * k) for t in range(n_tensor)])  1.68 us
    pallas_call x2, Pallas kernels, place(): pl.pallas_call(functools.partial(place_kernel, spots), out_shape=pltpu.HB...  1.45 us
  transfers between devices with their start and end apart: 15, of which 5 were waited for; matrix products, arithmetic and copies ran while one was open for 0% of the time, Pallas kernels for 34%

profile of v12, /device:TPU:0, one launch (start us, length us, event | category | flops | bytes accessed | tf_op | source)
XLA Modules:
  0.0 46.1 jit_solution(17326830511679816304)
XLA Ops:
  0.0 0.5 collective-permute-start
  0.5 3.0 %prefix_scores.1 = (bf16[256,128]{1,0:T(8,128)(2,1)S(1)}, f32[8192,256]{1,0:T(8,128)S(1)}, f32[8,256]{1,0:T(8,128)S(1)}, bf16[8192,128]{1,0:T(8,128)(2,1)S(1)}, bf16[32,256,128]{2,1,0:T(8,128)(2,1)S(1)}) custom-call(bf16[32,1024]{1,0:T(8,128)(2,1)} %q_ref.1, bf16[1,2,8192,128]{3,2,1,0:T(8,128)(2,1)} %prefix_ref.1, bf16[32,1,2,256,128]{4,3,2,1,0:T(8,128)(2,1)} %rest_1_.2), custom_call_target="tpu_custom_call" | custom-call | flops 536870912 | bytes 6291456 | tf_op jit(solution)/shard_map/prefix_scores/pallas_call | solution.py:251
  3.5 3.8 %suffix_scores.1 = (f32[256,256]{1,0:T(8,128)S(1)}, f32[256,128]{1,0:T(8,128)S(1)}, f32[8,256]{1,0:T(8,128)S(1)}, bf16[144,8192]{1,0:T(8,128)(2,1)S(1)}, bf16[2,...) custom-call(s32[32]{0:T(128)S(1)} %collective-permute-done.ids_ref, ...), custom_call_target="tpu_custom_call" | custom-call | flops 536870912 | bytes 7340032 | tf_op jit(solution)/shard_map/suffix_scores/pallas_call | solution.py:251
  7.3 0.1 collective-permute-start.1
  7.4 4.3 %values.1 = (bf16[32,1024]{1,0:T(8,128)(2,1)S(1)}, bf16[8,64,1024]{2,1,0:T(8,128)(2,1)S(1)}, bf16[8,64,1024]{2,1,0:T(8,128)(2,1)S(1)}, s32[32,128]{1,0:T(8,128)S...) custom-call(s32[32]{0:T(128)S(1)} %copy-done.1, ...), custom_call_target="tpu_custom_call" | custom-call | flops 536870912 | bytes 14680064 | tf_op jit(solution)/shard_map/values/pallas_call | solution.py:251
  11.7 1.1 %far_blocks.1 = (bf16[32,2176]{1,0:T(8,128)(2,1)S(1)}, f32[32,128]{1,0:T(8,128)S(1)}) custom-call(bf16[32,1024]{1,0:T(8,128)(2,1)S(1)} %get-tuple-element.42.att_ref, s32[32,128]{1,0:T(8,128)S(1)} %get-tuple-element.47.row_slot_ref.refs_2_, s32[8,128]{1,0:T(8,128)S(1)} %get-tuple-element.44.slot_mine_ref, ...), custom_call_target="tpu_custom_call" | custom-call | flops 134217728 | bytes 2097152 | tf_op jit(solution)/shard_map/far_blocks/pallas_call | solution.py:362
  12.8 2.9 %collective-permute-start.2 = (bf16[32,2176]{1,0:T(8,128)(2,1)S(1)}, bf16[32,2176]{1,0:T(8,128)(2,1)S(1)}, u32[]{:S(2)}, u32[]{:S(2)}) collective-permute-start(bf16[32,2176]{1,0:T(8,128)(2,1)S(1)} %get-tuple-element.53), channel_id=1, source_target_pairs={{0,1},{1,0},{2,3},{3,2},{4,5},{5,4},{6,7},{7,6},{8,9},{9,8},{10,11... | collective-permute-start | bytes 417800 | tf_op jit(solution)/shard_map/ppermute | solution.py:543
  15.7 2.7 %near_blocks.3 = (bf16[32,1152]{1,0:T(8,128)(2,1)S(1)}, bf16[32,1152]{1,0:T(8,128)(2,1)S(1)}) custom-call(bf16[32,1024]{1,0:T(8,128)(2,1)S(1)} %get-tuple-element.42.att_ref, f32[32,128]{1,0:T(8,128)S(1)} %get-tuple-element.51.rank_ref.refs_3_, bf16[1024,8192]{1,0:T(8,128)(2,1)} %weight_ref.5), custom_call_target="tpu_custom_call" | custom-call | flops 134217728 | bytes 4194304 | tf_op jit(solution)/shard_map/near_blocks/pallas_call | solution.py:251
  18.4 1.6 %collective-permute-start.4 = (bf16[32,1152]{1,0:T(8,128)(2,1)S(1)}, bf16[32,1152]{1,0:T(8,128)(2,1)S(1)}, u32[]{:S(2)}, u32[]{:S(2)}) collective-permute-start(bf16[32,1152]{1,0:T(8,128)(2,1)S(1)} %get-tuple-element.57), channel_id=1, source_target_pairs={{0,2},{1,3},{2,0},{3,1},{4,6},{5,7},{6,4},{7,5},{8,10},{9,11},{10,... | collective-permute-start | bytes 221192 | tf_op jit(solution)/shard_map/ppermute | solution.py:546
  20.0 0.0 collective-permute-start.5
  20.1 0.5 %add_block.2.rest_0_ = bf16[32,1152]{1,0:T(8,128)(2,1)S(1)} custom-call(bf16[32,1024]{1,0:T(8,128)(2,1)S(1)} %get-tuple-element.42.att_ref, bf16[1024,1024]{1,0:T(8,128)(2,1)S(1)} %get-tuple-element.54.w_ref, bf16[32,2176]{1,0:T(8,128)(2,1)S(1)} %collective-permute-done.2.from_ref.refs_4_, f32[32,128]{1,0:T(8,128)S(1)} %get-tuple-element.51.rank_ref.refs_3_), custom_call_target="tpu_custom_call" | custom-call | flops 134217728 | bytes 2097152 | tf_op jit(solution)/shard_map/add_block/pallas_call | solution.py:362
  20.5 4.0 %collective-permute-start.6 = (bf16[32,1152]{1,0:T(8,128)(2,1)S(1)}, bf16[32,1152]{1,0:T(8,128)(2,1)S(1)}, u32[]{:S(2)}, u32[]{:S(2)}) collective-permute-start(bf16[32,1152]{1,0:T(8,128)(2,1)S(1)} %add_block.2.rest_0_), channel_id=1, source_target_pairs={{0,6},{1,7},{2,4},{3,5},{4,2},{5,3},{6,0},{7,1},{8,14},{9,15},{10,... | collective-permute-start | bytes 221192 | tf_op jit(solution)/shard_map/ppermute | solution.py:546
  24.5 0.5 %add_block.3.rest_0_ = bf16[32,1152]{1,0:T(8,128)(2,1)S(1)} custom-call(bf16[32,1024]{1,0:T(8,128)(2,1)S(1)} %get-tuple-element.42.att_ref, bf16[1024,1024]{1,0:T(8,128)(2,1)S(1)} %get-tuple-element.52.w_ref, bf16[32,2176]{1,0:T(8,128)(2,1)S(1)} %collective-permute-done.2.from_ref.refs_4_, f32[32,128]{1,0:T(8,128)S(1)} %get-tuple-element.51.rank_ref.refs_3_, ...), custom_call_target="tpu_custom_call" | custom-call | flops 134217728 | bytes 2097152 | tf_op jit(solution)/shard_map/add_block/pallas_call | solution.py:362
  25.0 2.1 %near_blocks.2.after_ref = bf16[32,1024]{1,0:T(8,128)(2,1)S(1)} custom-call(bf16[32,1024]{1,0:T(8,128)(2,1)S(1)} %get-tuple-element.42.att_ref, f32[32,128]{1,0:T(8,128)S(1)} %get-tuple-element.51.rank_ref.refs_3_, bf16[1024,8192]{1,0:T(8,128)(2,1)} %weight_ref.5, bf16[32,1152]{1,0:T(8,128)(2,1)S(1)} %add_block.3.rest_0_), custom_call_target="tpu_custom_call" | custom-call | flops 134217728 | bytes 2097152 | tf_op jit(solution)/shard_map/near_blocks/pallas_call | solution.py:251
  27.1 1.6 %collective-permute-start.3 = (bf16[32,1024]{1,0:T(8,128)(2,1)S(1)}, bf16[32,1024]{1,0:T(8,128)(2,1)S(1)}, u32[]{:S(2)}, u32[]{:S(2)}) collective-permute-start(bf16[32,1024]{1,0:T(8,128)(2,1)S(1)} %near_blocks.2.after_ref), channel_id=1, source_target_pairs={{0,1},{1,0},{2,3},{3,2},{4,5},{5,4},{6,7},{7,6},{8,9},{9,8},{10,11... | collective-permute-start | bytes 196616 | tf_op jit(solution)/shard_map/ppermute | solution.py:543
  28.7 2.1 %own_block.1 = (f32[32,1024]{1,0:T(8,128)S(1)}, bf16[512,1024]{1,0:T(8,128)(2,1)S(1)}) custom-call(bf16[32,1024]{1,0:T(8,128)(2,1)S(1)} %get-tuple-element.42.att_ref, bf16[32,1024]{1,0:T(8,128)(2,1)S(1)} %get-tuple-element.43.res_ref, s32[8,128]{1,0:T(8,128)S(1)} %get-tuple-element.44.slot_mine_ref, bf16[8,64,1024]{2,1,0:T(8,128)(2,1)S(1)} %get-tuple-element.45.own_ref, ...), custom_call_target="tpu_custom_call" | custom-call | bytes 2097152 | tf_op jit(solution)/shard_map/own_block/pallas_call | solution.py:251
  30.8 0.6 %collective-permute-done.3.refs_5_ = bf16[32,1024]{1,0:T(8,128)(2,1)S(1)} collective-permute-done((bf16[32,1024]{1,0:T(8,128)(2,1)S(1)}, bf16[32,1024]{1,0:T(8,128)(2,1)S(1)}, u32[]{:S(2)}, u32[]{:S(2)}) %collective-permute-start.3) | collective-permute-done | bytes 65568 | tf_op jit(solution)/shard_map/ppermute | solution.py:543
  31.4 0.3 finish.1.refs_0_
  31.8 2.0 %collective-permute-start.12 = (bf16[32,1024]{1,0:T(8,128)(2,1)S(1)}, bf16[32,1024]{1,0:T(8,128)(2,1)S(1)}, u32[]{:S(2)}, u32[]{:S(2)}) collective-permute-start(bf16[32,1024]{1,0:T(8,128)(2,1)S(1)} %finish.1.refs_0_), channel_id=1, source_target_pairs={{0,6},{1,7},{2,4},{3,5},{4,2},{5,3},{6,0},{7,1},{8,14},{9,15},{10,... | collective-permute-start | bytes 196616 | tf_op jit(solution)/shard_map/ppermute | solution.py:546
  33.7 1.1 %collective-permute-start.10 = (bf16[32,1024]{1,0:T(8,128)(2,1)S(1)}, bf16[32,1024]{1,0:T(8,128)(2,1)S(1)}, u32[]{:S(2)}, u32[]{:S(2)}) collective-permute-start(bf16[32,1024]{1,0:T(8,128)(2,1)S(1)} %finish.1.refs_0_), channel_id=1, source_target_pairs={{0,4},{1,5},{2,6},{3,7},{4,0},{5,1},{6,2},{7,3},{8,12},{9,13},{10,... | collective-permute-start | bytes 196616 | tf_op jit(solution)/shard_map/ppermute | solution.py:546
  34.8 1.4 %collective-permute-start.8 = (bf16[32,1024]{1,0:T(8,128)(2,1)S(1)}, bf16[32,1024]{1,0:T(8,128)(2,1)S(1)}, u32[]{:S(2)}, u32[]{:S(2)}) collective-permute-start(bf16[32,1024]{1,0:T(8,128)(2,1)S(1)} %finish.1.refs_0_), channel_id=1, source_target_pairs={{0,2},{1,3},{2,0},{3,1},{4,6},{5,7},{6,4},{7,5},{8,10},{9,11},{10,... | collective-permute-start | bytes 196616 | tf_op jit(solution)/shard_map/ppermute | solution.py:546
  36.2 1.5 %collective-permute-start.14 = (bf16[32,1024]{1,0:T(8,128)(2,1)S(1)}, bf16[32,1024]{1,0:T(8,128)(2,1)S(1)}, u32[]{:S(2)}, u32[]{:S(2)}) collective-permute-start(bf16[32,1024]{1,0:T(8,128)(2,1)S(1)} %finish.1.refs_0_), channel_id=1, source_target_pairs={{0,1},{1,0},{2,3},{3,2},{4,5},{5,4},{6,7},{7,6},{8,9},{9,8},{10,11... | collective-permute-start | bytes 196616 | tf_op jit(solution)/shard_map/ppermute | solution.py:543
  37.7 0.9 %collective-permute-done.12.refs_4_ = bf16[32,1024]{1,0:T(8,128)(2,1)S(1)} collective-permute-done((bf16[32,1024]{1,0:T(8,128)(2,1)S(1)}, bf16[32,1024]{1,0:T(8,128)(2,1)S(1)}, u32[]{:S(2)}, u32[]{:S(2)}) %collective-permute-start.12) | collective-permute-done | bytes 65568 | tf_op jit(solution)/shard_map/ppermute | solution.py:546
  38.6 1.0 %collective-permute-start.13 = (bf16[32,1024]{1,0:T(8,128)(2,1)S(1)}, bf16[32,1024]{1,0:T(8,128)(2,1)S(1)}, u32[]{:S(2)}, u32[]{:S(2)}) collective-permute-start(bf16[32,1024]{1,0:T(8,128)(2,1)S(1)} %collective-permute-done.12.refs_4_), channel_id=1, source_target_pairs={{0,1},{1,0},{2,3},{3,2},{4,5},{5,4},{6,7},{7,6},{8,9},{9,8},{10,11... | collective-permute-start | bytes 196616 | tf_op jit(solution)/shard_map/ppermute | solution.py:543
  39.7 0.8 %collective-permute-done.10.refs_2_ = bf16[32,1024]{1,0:T(8,128)(2,1)S(1)} collective-permute-done((bf16[32,1024]{1,0:T(8,128)(2,1)S(1)}, bf16[32,1024]{1,0:T(8,128)(2,1)S(1)}, u32[]{:S(2)}, u32[]{:S(2)}) %collective-permute-start.10) | collective-permute-done | bytes 65568 | tf_op jit(solution)/shard_map/ppermute | solution.py:546
  40.4 0.2 collective-permute-start.11
  40.7 1.8 %collective-permute-start.9 = (bf16[32,1024]{1,0:T(8,128)(2,1)S(1)}, bf16[32,1024]{1,0:T(8,128)(2,1)S(1)}, u32[]{:S(2)}, u32[]{:S(2)}) collective-permute-start(bf16[32,1024]{1,0:T(8,128)(2,1)S(1)} %collective-permute-done.8.refs_1_), channel_id=1, source_target_pairs={{0,1},{1,0},{2,3},{3,2},{4,5},{5,4},{6,7},{7,6},{8,9},{9,8},{10,11... | collective-permute-start | bytes 196616 | tf_op jit(solution)/shard_map/ppermute | solution.py:543
  42.4 0.8 %place.2.refs_3_ = bf16[32,8192]{1,0:T(8,128)(2,1)} custom-call(bf16[32,1024]{1,0:T(8,128)(2,1)S(1)} %finish.1.refs_0_, bf16[32,1024]{1,0:T(8,128)(2,1)S(1)} %collective-permute-done.8.refs_1_, bf16[32,1024]{1,0:T(8,128)(2,1)S(1)} %collective-permute-done.10.refs_2_, bf16[32,1024]{1,0:T(8,128)(2,1)S(1)} %collective-permute-done.14.refs_3_, ...), custom_call_target="tpu_custom_call" | custom-call | bytes 1048576 | tf_op jit(solution)/shard_map/place/pallas_call | solution.py:515
  43.2 0.0 collective-permute-done.13.refs_2_
  43.3 1.4 %collective-permute-done.11.refs_1_ = bf16[32,1024]{1,0:T(8,128)(2,1)S(1)} collective-permute-done((bf16[32,1024]{1,0:T(8,128)(2,1)S(1)}, bf16[32,1024]{1,0:T(8,128)(2,1)S(1)}, u32[]{:S(2)}, u32[]{:S(2)}) %collective-permute-start.11) | collective-permute-done | bytes 65568 | tf_op jit(solution)/shard_map/ppermute | solution.py:543
  44.7 0.7 %collective-permute-done.9.refs_0_ = bf16[32,1024]{1,0:T(8,128)(2,1)S(1)} collective-permute-done((bf16[32,1024]{1,0:T(8,128)(2,1)S(1)}, bf16[32,1024]{1,0:T(8,128)(2,1)S(1)}, u32[]{:S(2)}, u32[]{:S(2)}) %collective-permute-start.9) | collective-permute-done | bytes 65568 | tf_op jit(solution)/shard_map/ppermute | solution.py:543
  45.4 0.7 %place.3 = bf16[32,8192]{1,0:T(8,128)(2,1)} custom-call(bf16[32,1024]{1,0:T(8,128)(2,1)S(1)} %collective-permute-done.9.refs_0_, bf16[32,1024]{1,0:T(8,128)(2,1)S(1)} %collective-permute-done.11.refs_1_, bf16[32,1024]{1,0:T(8,128)(2,1)S(1)} %collective-permute-done.13.refs_2_, bf16[32,8192]{1,0:T(8,128)(2,1)} %place.2.refs_3_), custom_call_target="tpu_custom_call", output_to_operand_aliasing={{}: (3, {})} | custom-call | bytes 1048576 | tf_op jit(solution)/shard_map/place/pallas_call | solution.py:515
  (14 shorter events, 0.0 us)
Async XLA Ops:
  0.0 3.4 %copy-start = (s32[128]{0:T(128)S(1)}, s32[128]{0:T(128)}, u32[]{:S(2)}) copy-start(s32[128]{0:T(128)} %slot_ref.3) | copy-start | bytes 1540
  0.0 3.4 %collective-permute-start = (s32[32]{0:T(128)}, s32[32]{0:T(128)S(1)}, u32[]{:S(2)}, u32[]{:S(2)}) collective-permute-start(s32[32]{0:T(128)} %ids_ref.1), channel_id=1, source_target_pairs={{0,8},{8,0},{1,9},{9,1},{2,10},{10,2},{3,11},{11,3},{4,12},{12,4},... | collective-permute-start | bytes 392 | tf_op jit(solution)/shard_map/ppermute | solution.py:552
  3.4 3.9 %copy-start.1 = (s32[32]{0:T(128)S(1)}, s32[32]{0:T(128)}, u32[]{:S(2)}) copy-start(s32[32]{0:T(128)} %ids_ref.1) | copy-start | bytes 388
  7.3 4.4 %collective-permute-start.1 = (bf16[2,8,64,1024]{3,2,1,0:T(8,128)(2,1)S(1)}, bf16[2,8,64,1024]{3,2,1,0:T(8,128)(2,1)S(1)}, u32[]{:S(2)}, u32[]{:S(2)}) collective-permute-start(bf16[2,8,64,1024]{3,2,1,0:T(8,128)(2,1)S(1)} %get-tuple-element.46), channel_id=1, source_target_pairs={{0,8},{8,0},{1,9},{9,1},{2,10},{10,2},{3,11},{11,3},{4,12},{12,4},... | collective-permute-start | bytes 6291464 | tf_op jit(solution)/shard_map/ppermute | solution.py:552
  12.8 7.3 %collective-permute-start.2 = (bf16[32,2176]{1,0:T(8,128)(2,1)S(1)}, bf16[32,2176]{1,0:T(8,128)(2,1)S(1)}, u32[]{:S(2)}, u32[]{:S(2)}) collective-permute-start(bf16[32,2176]{1,0:T(8,128)(2,1)S(1)} %get-tuple-element.53), channel_id=1, source_target_pairs={{0,1},{1,0},{2,3},{3,2},{4,5},{5,4},{6,7},{7,6},{8,9},{9,8},{10,11... | collective-permute-start | bytes 417800 | tf_op jit(solution)/shard_map/ppermute | solution.py:543
  18.4 12.4 %collective-permute-start.4 = (bf16[32,1152]{1,0:T(8,128)(2,1)S(1)}, bf16[32,1152]{1,0:T(8,128)(2,1)S(1)}, u32[]{:S(2)}, u32[]{:S(2)}) collective-permute-start(bf16[32,1152]{1,0:T(8,128)(2,1)S(1)} %get-tuple-element.57), channel_id=1, source_target_pairs={{0,2},{1,3},{2,0},{3,1},{4,6},{5,7},{6,4},{7,5},{8,10},{9,11},{10,... | collective-permute-start | bytes 221192 | tf_op jit(solution)/shard_map/ppermute | solution.py:546
  20.0 10.7 %collective-permute-start.5 = (bf16[32,1152]{1,0:T(8,128)(2,1)S(1)}, bf16[32,1152]{1,0:T(8,128)(2,1)S(1)}, u32[]{:S(2)}, u32[]{:S(2)}) collective-permute-start(bf16[32,1152]{1,0:T(8,128)(2,1)S(1)} %get-tuple-element.58), channel_id=1, source_target_pairs={{0,3},{1,2},{2,1},{3,0},{4,7},{5,6},{6,5},{7,4},{8,11},{9,10},{10,... | collective-permute-start | bytes 221192 | tf_op jit(solution)/shard_map/ppermute | solution.py:549
  20.5 10.9 %collective-permute-start.6 = (bf16[32,1152]{1,0:T(8,128)(2,1)S(1)}, bf16[32,1152]{1,0:T(8,128)(2,1)S(1)}, u32[]{:S(2)}, u32[]{:S(2)}) collective-permute-start(bf16[32,1152]{1,0:T(8,128)(2,1)S(1)} %add_block.2.rest_0_), channel_id=1, source_target_pairs={{0,6},{1,7},{2,4},{3,5},{4,2},{5,3},{6,0},{7,1},{8,14},{9,15},{10,... | collective-permute-start | bytes 221192 | tf_op jit(solution)/shard_map/ppermute | solution.py:546
  25.0 6.4 %collective-permute-start.7 = (bf16[32,1152]{1,0:T(8,128)(2,1)S(1)}, bf16[32,1152]{1,0:T(8,128)(2,1)S(1)}, u32[]{:S(2)}, u32[]{:S(2)}) collective-permute-start(bf16[32,1152]{1,0:T(8,128)(2,1)S(1)} %add_block.3.rest_0_), channel_id=1, source_target_pairs={{0,4},{1,5},{2,6},{3,7},{4,0},{5,1},{6,2},{7,3},{8,12},{9,13},{10,... | collective-permute-start | bytes 221192 | tf_op jit(solution)/shard_map/ppermute | solution.py:546
  27.1 4.3 %collective-permute-start.3 = (bf16[32,1024]{1,0:T(8,128)(2,1)S(1)}, bf16[32,1024]{1,0:T(8,128)(2,1)S(1)}, u32[]{:S(2)}, u32[]{:S(2)}) collective-permute-start(bf16[32,1024]{1,0:T(8,128)(2,1)S(1)} %near_blocks.2.after_ref), channel_id=1, source_target_pairs={{0,1},{1,0},{2,3},{3,2},{4,5},{5,4},{6,7},{7,6},{8,9},{9,8},{10,11... | collective-permute-start | bytes 196616 | tf_op jit(solution)/shard_map/ppermute | solution.py:543
  31.8 6.9 %collective-permute-start.12 = (bf16[32,1024]{1,0:T(8,128)(2,1)S(1)}, bf16[32,1024]{1,0:T(8,128)(2,1)S(1)}, u32[]{:S(2)}, u32[]{:S(2)}) collective-permute-start(bf16[32,1024]{1,0:T(8,128)(2,1)S(1)} %finish.1.refs_0_), channel_id=1, source_target_pairs={{0,6},{1,7},{2,4},{3,5},{4,2},{5,3},{6,0},{7,1},{8,14},{9,15},{10,... | collective-permute-start | bytes 196616 | tf_op jit(solution)/shard_map/ppermute | solution.py:546
  33.7 6.7 %collective-permute-start.10 = (bf16[32,1024]{1,0:T(8,128)(2,1)S(1)}, bf16[32,1024]{1,0:T(8,128)(2,1)S(1)}, u32[]{:S(2)}, u32[]{:S(2)}) collective-permute-start(bf16[32,1024]{1,0:T(8,128)(2,1)S(1)} %finish.1.refs_0_), channel_id=1, source_target_pairs={{0,4},{1,5},{2,6},{3,7},{4,0},{5,1},{6,2},{7,3},{8,12},{9,13},{10,... | collective-permute-start | bytes 196616 | tf_op jit(solution)/shard_map/ppermute | solution.py:546
  34.8 5.9 %collective-permute-start.8 = (bf16[32,1024]{1,0:T(8,128)(2,1)S(1)}, bf16[32,1024]{1,0:T(8,128)(2,1)S(1)}, u32[]{:S(2)}, u32[]{:S(2)}) collective-permute-start(bf16[32,1024]{1,0:T(8,128)(2,1)S(1)} %finish.1.refs_0_), channel_id=1, source_target_pairs={{0,2},{1,3},{2,0},{3,1},{4,6},{5,7},{6,4},{7,5},{8,10},{9,11},{10,... | collective-permute-start | bytes 196616 | tf_op jit(solution)/shard_map/ppermute | solution.py:546
  36.2 6.2 %collective-permute-start.14 = (bf16[32,1024]{1,0:T(8,128)(2,1)S(1)}, bf16[32,1024]{1,0:T(8,128)(2,1)S(1)}, u32[]{:S(2)}, u32[]{:S(2)}) collective-permute-start(bf16[32,1024]{1,0:T(8,128)(2,1)S(1)} %finish.1.refs_0_), channel_id=1, source_target_pairs={{0,1},{1,0},{2,3},{3,2},{4,5},{5,4},{6,7},{7,6},{8,9},{9,8},{10,11... | collective-permute-start | bytes 196616 | tf_op jit(solution)/shard_map/ppermute | solution.py:543
  38.6 4.6 %collective-permute-start.13 = (bf16[32,1024]{1,0:T(8,128)(2,1)S(1)}, bf16[32,1024]{1,0:T(8,128)(2,1)S(1)}, u32[]{:S(2)}, u32[]{:S(2)}) collective-permute-start(bf16[32,1024]{1,0:T(8,128)(2,1)S(1)} %collective-permute-done.12.refs_4_), channel_id=1, source_target_pairs={{0,1},{1,0},{2,3},{3,2},{4,5},{5,4},{6,7},{7,6},{8,9},{9,8},{10,11... | collective-permute-start | bytes 196616 | tf_op jit(solution)/shard_map/ppermute | solution.py:543
  40.4 4.3 %collective-permute-start.11 = (bf16[32,1024]{1,0:T(8,128)(2,1)S(1)}, bf16[32,1024]{1,0:T(8,128)(2,1)S(1)}, u32[]{:S(2)}, u32[]{:S(2)}) collective-permute-start(bf16[32,1024]{1,0:T(8,128)(2,1)S(1)} %collective-permute-done.10.refs_2_), channel_id=1, source_target_pairs={{0,1},{1,0},{2,3},{3,2},{4,5},{5,4},{6,7},{7,6},{8,9},{9,8},{10,11... | collective-permute-start | bytes 196616 | tf_op jit(solution)/shard_map/ppermute | solution.py:543
  40.7 4.7 %collective-permute-start.9 = (bf16[32,1024]{1,0:T(8,128)(2,1)S(1)}, bf16[32,1024]{1,0:T(8,128)(2,1)S(1)}, u32[]{:S(2)}, u32[]{:S(2)}) collective-permute-start(bf16[32,1024]{1,0:T(8,128)(2,1)S(1)} %collective-permute-done.8.refs_1_), channel_id=1, source_target_pairs={{0,1},{1,0},{2,3},{3,2},{4,5},{5,4},{6,7},{7,6},{8,9},{9,8},{10,11... | collective-permute-start | bytes 196616 | tf_op jit(solution)/shard_map/ppermute | solution.py:543

commit v13 on v11

--- a/solution.py
+++ b/solution.py
@@ -155,7 +155,7 @@
     vals_t_ref[head_dim:, :] = jnp.ones((vals_t_ref.shape[0] - head_dim, tokens), BF16)
     step = min(1024, tokens)
     for base in range(0, tokens, step):
-        vals_t_ref[:head_dim, base : base + step] = vals_ref[base : base + step, :].astype(F32).T.astype(BF16)
+        vals_t_ref[:head_dim, base : base + step] = vals_ref[base : base + step, :].T
     best = jnp.maximum(tail_ref[:, :128], tail_ref[:, 128:256])
     for b in range(2, span // 128):
         best = jnp.maximum(best, tail_ref[:, b * 128 : (b + 1) * 128])

time: 45.7 us -> 45.6 us (level)
  no operation moved by 1% of the time
where the time goes in v13:
time: 45.6 us; the launch traced here: 45.5 us
  Pallas kernels  21.9 us (48%)
  starting transfers between devices  18.9 us (41%)
  waiting for transfers between devices  4.48 us (10%)
    pallas_call x6, Pallas kernels, kernel_call(): pl.pallas_call(kernel, out_shape=out_shape, in_specs=specs, out_specs=[VM...  18.1 us
    ppermute x6, starting transfers between devices, along_z(): return lax.ppermute(x, 'tensor', [(t, t ^ 2 * k) for t in range(n_tensor)])  10.1 us
    ppermute x4, starting transfers between devices, along_y(): return lax.ppermute(x, 'tensor', [(t, t ^ 1) for t in range(n_tensor)])  6.18 us
    ppermute x4, waiting for transfers between devices, along_y(): return lax.ppermute(x, 'tensor', [(t, t ^ 1) for t in range(n_tensor)])  2.42 us
    pallas_call x4, Pallas kernels, small_call(): pl.pallas_call(kernel, out_shape=out_shape, in_specs=[VMEM] * len(operand...  2.38 us
    ppermute x3, starting transfers between devices, along_both(): lax.ppermute(x, 'tensor', [(t, t ^ 2 * k ^ 1) for t in range(n_tensor)])  2.11 us
    pallas_call x2, Pallas kernels, place(): pl.pallas_call(functools.partial(place_kernel, spots), out_shape=pltpu.HB...  1.45 us
    ppermute x3, waiting for transfers between devices, along_both(): lax.ppermute(x, 'tensor', [(t, t ^ 2 * k ^ 1) for t in range(n_tensor)])  1.24 us
  transfers between devices with their start and end apart: 15, of which 6 were waited for; matrix products, arithmetic and copies ran while one was open for 0% of the time, Pallas kernels for 35%

profile of v13, /device:TPU:0, one launch (start us, length us, event | category | flops | bytes accessed | tf_op | source)
XLA Modules:
  0.0 45.5 jit_solution(13234291461460782441)
XLA Ops:
  0.0 0.5 collective-permute-start
  0.5 3.0 %prefix_scores.1 = (bf16[256,128]{1,0:T(8,128)(2,1)S(1)}, f32[8192,256]{1,0:T(8,128)S(1)}, f32[8,256]{1,0:T(8,128)S(1)}, bf16[8192,128]{1,0:T(8,128)(2,1)S(1)}, bf16[32,256,128]{2,1,0:T(8,128)(2,1)S(1)}) custom-call(bf16[32,1024]{1,0:T(8,128)(2,1)} %q_ref.1, bf16[1,2,8192,128]{3,2,1,0:T(8,128)(2,1)} %prefix_ref.1, bf16[32,1,2,256,128]{4,3,2,1,0:T(8,128)(2,1)} %rest_1_.2), custom_call_target="tpu_custom_call" | custom-call | flops 536870912 | bytes 6291456 | tf_op jit(solution)/shard_map/prefix_scores/pallas_call | solution.py:251
  3.5 3.7 %suffix_scores.1 = (f32[256,256]{1,0:T(8,128)S(1)}, f32[256,128]{1,0:T(8,128)S(1)}, f32[8,256]{1,0:T(8,128)S(1)}, bf16[144,8192]{1,0:T(8,128)(2,1)S(1)}, bf16[2,...) custom-call(s32[32]{0:T(128)S(1)} %collective-permute-done.ids_ref, ...), custom_call_target="tpu_custom_call" | custom-call | flops 536870912 | bytes 7340032 | tf_op jit(solution)/shard_map/suffix_scores/pallas_call | solution.py:251
  7.2 0.1 collective-permute-start.1
  7.3 4.5 %values.1 = (bf16[32,1024]{1,0:T(8,128)(2,1)S(1)}, bf16[8,64,1024]{2,1,0:T(8,128)(2,1)S(1)}, bf16[8,64,1024]{2,1,0:T(8,128)(2,1)S(1)}, s32[32,128]{1,0:T(8,128)S...) custom-call(s32[32]{0:T(128)S(1)} %copy-done.1, ...), custom_call_target="tpu_custom_call" | custom-call | flops 536870912 | bytes 14680064 | tf_op jit(solution)/shard_map/values/pallas_call | solution.py:251
  11.8 1.1 %far_blocks.1 = (bf16[32,2176]{1,0:T(8,128)(2,1)S(1)}, f32[32,128]{1,0:T(8,128)S(1)}) custom-call(bf16[32,1024]{1,0:T(8,128)(2,1)S(1)} %get-tuple-element.42.att_ref, s32[32,128]{1,0:T(8,128)S(1)} %get-tuple-element.47.row_slot_ref.refs_2_, s32[8,128]{1,0:T(8,128)S(1)} %get-tuple-element.44.slot_mine_ref, ...), custom_call_target="tpu_custom_call" | custom-call | flops 134217728 | bytes 2097152 | tf_op jit(solution)/shard_map/far_blocks/pallas_call | solution.py:362
  12.9 2.7 %collective-permute-start.2 = (bf16[32,2176]{1,0:T(8,128)(2,1)S(1)}, bf16[32,2176]{1,0:T(8,128)(2,1)S(1)}, u32[]{:S(2)}, u32[]{:S(2)}) collective-permute-start(bf16[32,2176]{1,0:T(8,128)(2,1)S(1)} %get-tuple-element.53), channel_id=1, source_target_pairs={{0,1},{1,0},{2,3},{3,2},{4,5},{5,4},{6,7},{7,6},{8,9},{9,8},{10,11... | collective-permute-start | bytes 417800 | tf_op jit(solution)/shard_map/ppermute | solution.py:543
  15.6 2.7 %near_blocks.3 = (bf16[32,1152]{1,0:T(8,128)(2,1)S(1)}, bf16[32,1152]{1,0:T(8,128)(2,1)S(1)}) custom-call(bf16[32,1024]{1,0:T(8,128)(2,1)S(1)} %get-tuple-element.42.att_ref, f32[32,128]{1,0:T(8,128)S(1)} %get-tuple-element.51.rank_ref.refs_3_, bf16[1024,8192]{1,0:T(8,128)(2,1)} %weight_ref.5), custom_call_target="tpu_custom_call" | custom-call | flops 134217728 | bytes 4194304 | tf_op jit(solution)/shard_map/near_blocks/pallas_call | solution.py:251
  18.4 1.6 %collective-permute-start.4 = (bf16[32,1152]{1,0:T(8,128)(2,1)S(1)}, bf16[32,1152]{1,0:T(8,128)(2,1)S(1)}, u32[]{:S(2)}, u32[]{:S(2)}) collective-permute-start(bf16[32,1152]{1,0:T(8,128)(2,1)S(1)} %get-tuple-element.57), channel_id=1, source_target_pairs={{0,2},{1,3},{2,0},{3,1},{4,6},{5,7},{6,4},{7,5},{8,10},{9,11},{10,... | collective-permute-start | bytes 221192 | tf_op jit(solution)/shard_map/ppermute | solution.py:546
  20.0 0.0 collective-permute-start.5
  20.0 0.5 %add_block.2.rest_0_ = bf16[32,1152]{1,0:T(8,128)(2,1)S(1)} custom-call(bf16[32,1024]{1,0:T(8,128)(2,1)S(1)} %get-tuple-element.42.att_ref, bf16[1024,1024]{1,0:T(8,128)(2,1)S(1)} %get-tuple-element.54.w_ref, bf16[32,2176]{1,0:T(8,128)(2,1)S(1)} %collective-permute-done.2.from_ref.refs_4_, f32[32,128]{1,0:T(8,128)S(1)} %get-tuple-element.51.rank_ref.refs_3_), custom_call_target="tpu_custom_call" | custom-call | flops 134217728 | bytes 2097152 | tf_op jit(solution)/shard_map/add_block/pallas_call | solution.py:362
  20.5 4.0 %collective-permute-start.6 = (bf16[32,1152]{1,0:T(8,128)(2,1)S(1)}, bf16[32,1152]{1,0:T(8,128)(2,1)S(1)}, u32[]{:S(2)}, u32[]{:S(2)}) collective-permute-start(bf16[32,1152]{1,0:T(8,128)(2,1)S(1)} %add_block.2.rest_0_), channel_id=1, source_target_pairs={{0,6},{1,7},{2,4},{3,5},{4,2},{5,3},{6,0},{7,1},{8,14},{9,15},{10,... | collective-permute-start | bytes 221192 | tf_op jit(solution)/shard_map/ppermute | solution.py:546
  24.5 0.5 %add_block.3.rest_0_ = bf16[32,1152]{1,0:T(8,128)(2,1)S(1)} custom-call(bf16[32,1024]{1,0:T(8,128)(2,1)S(1)} %get-tuple-element.42.att_ref, bf16[1024,1024]{1,0:T(8,128)(2,1)S(1)} %get-tuple-element.52.w_ref, bf16[32,2176]{1,0:T(8,128)(2,1)S(1)} %collective-permute-done.2.from_ref.refs_4_, f32[32,128]{1,0:T(8,128)S(1)} %get-tuple-element.51.rank_ref.refs_3_, ...), custom_call_target="tpu_custom_call" | custom-call | flops 134217728 | bytes 2097152 | tf_op jit(solution)/shard_map/add_block/pallas_call | solution.py:362
  25.0 2.1 %near_blocks.2.after_ref = bf16[32,1024]{1,0:T(8,128)(2,1)S(1)} custom-call(bf16[32,1024]{1,0:T(8,128)(2,1)S(1)} %get-tuple-element.42.att_ref, f32[32,128]{1,0:T(8,128)S(1)} %get-tuple-element.51.rank_ref.refs_3_, bf16[1024,8192]{1,0:T(8,128)(2,1)} %weight_ref.5, bf16[32,1152]{1,0:T(8,128)(2,1)S(1)} %add_block.3.rest_0_), custom_call_target="tpu_custom_call" | custom-call | flops 134217728 | bytes 2097152 | tf_op jit(solution)/shard_map/near_blocks/pallas_call | solution.py:251
  27.1 1.6 %collective-permute-start.3 = (bf16[32,1024]{1,0:T(8,128)(2,1)S(1)}, bf16[32,1024]{1,0:T(8,128)(2,1)S(1)}, u32[]{:S(2)}, u32[]{:S(2)}) collective-permute-start(bf16[32,1024]{1,0:T(8,128)(2,1)S(1)} %near_blocks.2.after_ref), channel_id=1, source_target_pairs={{0,1},{1,0},{2,3},{3,2},{4,5},{5,4},{6,7},{7,6},{8,9},{9,8},{10,11... | collective-permute-start | bytes 196616 | tf_op jit(solution)/shard_map/ppermute | solution.py:543
  28.7 2.1 %own_block.1 = (f32[32,1024]{1,0:T(8,128)S(1)}, bf16[512,1024]{1,0:T(8,128)(2,1)S(1)}) custom-call(bf16[32,1024]{1,0:T(8,128)(2,1)S(1)} %get-tuple-element.42.att_ref, bf16[32,1024]{1,0:T(8,128)(2,1)S(1)} %get-tuple-element.43.res_ref, s32[8,128]{1,0:T(8,128)S(1)} %get-tuple-element.44.slot_mine_ref, bf16[8,64,1024]{2,1,0:T(8,128)(2,1)S(1)} %get-tuple-element.45.own_ref, ...), custom_call_target="tpu_custom_call" | custom-call | bytes 2097152 | tf_op jit(solution)/shard_map/own_block/pallas_call | solution.py:251
  30.8 0.6 %collective-permute-done.3.refs_5_ = bf16[32,1024]{1,0:T(8,128)(2,1)S(1)} collective-permute-done((bf16[32,1024]{1,0:T(8,128)(2,1)S(1)}, bf16[32,1024]{1,0:T(8,128)(2,1)S(1)}, u32[]{:S(2)}, u32[]{:S(2)}) %collective-permute-start.3) | collective-permute-done | bytes 65568 | tf_op jit(solution)/shard_map/ppermute | solution.py:543
  31.4 0.3 finish.1.refs_0_
  31.7 2.0 %collective-permute-start.11 = (bf16[32,1024]{1,0:T(8,128)(2,1)S(1)}, bf16[32,1024]{1,0:T(8,128)(2,1)S(1)}, u32[]{:S(2)}, u32[]{:S(2)}) collective-permute-start(bf16[32,1024]{1,0:T(8,128)(2,1)S(1)} %finish.1.refs_0_), channel_id=1, source_target_pairs={{0,6},{1,7},{2,4},{3,5},{4,2},{5,3},{6,0},{7,1},{8,14},{9,15},{10,... | collective-permute-start | bytes 196616 | tf_op jit(solution)/shard_map/ppermute | solution.py:546
  33.7 1.1 %collective-permute-start.9 = (bf16[32,1024]{1,0:T(8,128)(2,1)S(1)}, bf16[32,1024]{1,0:T(8,128)(2,1)S(1)}, u32[]{:S(2)}, u32[]{:S(2)}) collective-permute-start(bf16[32,1024]{1,0:T(8,128)(2,1)S(1)} %finish.1.refs_0_), channel_id=1, source_target_pairs={{0,4},{1,5},{2,6},{3,7},{4,0},{5,1},{6,2},{7,3},{8,12},{9,13},{10,... | collective-permute-start | bytes 196616 | tf_op jit(solution)/shard_map/ppermute | solution.py:546
  34.8 1.5 %collective-permute-start.14 = (bf16[32,1024]{1,0:T(8,128)(2,1)S(1)}, bf16[32,1024]{1,0:T(8,128)(2,1)S(1)}, u32[]{:S(2)}, u32[]{:S(2)}) collective-permute-start(bf16[32,1024]{1,0:T(8,128)(2,1)S(1)} %finish.1.refs_0_), channel_id=1, source_target_pairs={{0,1},{1,0},{2,3},{3,2},{4,5},{5,4},{6,7},{7,6},{8,9},{9,8},{10,11... | collective-permute-start | bytes 196616 | tf_op jit(solution)/shard_map/ppermute | solution.py:549
  36.3 1.4 %collective-permute-start.13 = (bf16[32,1024]{1,0:T(8,128)(2,1)S(1)}, bf16[32,1024]{1,0:T(8,128)(2,1)S(1)}, u32[]{:S(2)}, u32[]{:S(2)}) collective-permute-start(bf16[32,1024]{1,0:T(8,128)(2,1)S(1)} %finish.1.refs_0_), channel_id=1, source_target_pairs={{0,2},{1,3},{2,0},{3,1},{4,6},{5,7},{6,4},{7,5},{8,10},{9,11},{10,... | collective-permute-start | bytes 196616 | tf_op jit(solution)/shard_map/ppermute | solution.py:546
  37.7 0.6 %collective-permute-start.8 = (bf16[32,1024]{1,0:T(8,128)(2,1)S(1)}, bf16[32,1024]{1,0:T(8,128)(2,1)S(1)}, u32[]{:S(2)}, u32[]{:S(2)}) collective-permute-start(bf16[32,1024]{1,0:T(8,128)(2,1)S(1)} %finish.1.refs_0_), channel_id=1, source_target_pairs={{0,3},{1,2},{2,1},{3,0},{4,7},{5,6},{6,5},{7,4},{8,11},{9,10},{10,... | collective-permute-start | bytes 196616 | tf_op jit(solution)/shard_map/ppermute | solution.py:549
  38.3 1.8 %collective-permute-start.12 = (bf16[32,1024]{1,0:T(8,128)(2,1)S(1)}, bf16[32,1024]{1,0:T(8,128)(2,1)S(1)}, u32[]{:S(2)}, u32[]{:S(2)}) collective-permute-start(bf16[32,1024]{1,0:T(8,128)(2,1)S(1)} %collective-permute-done.11.refs_4_), channel_id=1, source_target_pairs={{0,1},{1,0},{2,3},{3,2},{4,5},{5,4},{6,7},{7,6},{8,9},{9,8},{10,11... | collective-permute-start | bytes 196616 | tf_op jit(solution)/shard_map/ppermute | solution.py:543
  40.1 0.4 collective-permute-done.9.refs_2_
  40.5 0.1 collective-permute-start.10
  40.6 0.4 collective-permute-done.13.refs_1_
  41.0 0.8 %place.2.refs_3_ = bf16[32,8192]{1,0:T(8,128)(2,1)} custom-call(bf16[32,1024]{1,0:T(8,128)(2,1)S(1)} %finish.1.refs_0_, bf16[32,1024]{1,0:T(8,128)(2,1)S(1)} %collective-permute-done.13.refs_1_, bf16[32,1024]{1,0:T(8,128)(2,1)S(1)} %collective-permute-done.9.refs_2_, bf16[32,1024]{1,0:T(8,128)(2,1)S(1)} %collective-permute-done.14.refs_3_, ...), custom_call_target="tpu_custom_call" | custom-call | bytes 1048576 | tf_op jit(solution)/shard_map/place/pallas_call | solution.py:515
  41.7 1.2 %collective-permute-done.8.refs_0_ = bf16[32,1024]{1,0:T(8,128)(2,1)S(1)} collective-permute-done((bf16[32,1024]{1,0:T(8,128)(2,1)S(1)}, bf16[32,1024]{1,0:T(8,128)(2,1)S(1)}, u32[]{:S(2)}, u32[]{:S(2)}) %collective-permute-start.8) | collective-permute-done | bytes 65568 | tf_op jit(solution)/shard_map/ppermute | solution.py:549
  43.0 0.3 collective-permute-done.12.refs_2_
  43.3 1.5 %collective-permute-done.10.refs_1_ = bf16[32,1024]{1,0:T(8,128)(2,1)S(1)} collective-permute-done((bf16[32,1024]{1,0:T(8,128)(2,1)S(1)}, bf16[32,1024]{1,0:T(8,128)(2,1)S(1)}, u32[]{:S(2)}, u32[]{:S(2)}) %collective-permute-start.10) | collective-permute-done | bytes 65568 | tf_op jit(solution)/shard_map/ppermute | solution.py:543
  44.8 0.7 %place.3 = bf16[32,8192]{1,0:T(8,128)(2,1)} custom-call(bf16[32,1024]{1,0:T(8,128)(2,1)S(1)} %collective-permute-done.8.refs_0_, bf16[32,1024]{1,0:T(8,128)(2,1)S(1)} %collective-permute-done.10.refs_1_, bf16[32,1024]{1,0:T(8,128)(2,1)S(1)} %collective-permute-done.12.refs_2_, bf16[32,8192]{1,0:T(8,128)(2,1)} %place.2.refs_3_), custom_call_target="tpu_custom_call", output_to_operand_aliasing={{}: (3, {})} | custom-call | bytes 1048576 | tf_op jit(solution)/shard_map/place/pallas_call | solution.py:515
  (14 shorter events, 0.0 us)
Async XLA Ops:
  0.0 3.4 %copy-start = (s32[128]{0:T(128)S(1)}, s32[128]{0:T(128)}, u32[]{:S(2)}) copy-start(s32[128]{0:T(128)} %slot_ref.3) | copy-start | bytes 1540
  0.0 3.4 %collective-permute-start = (s32[32]{0:T(128)}, s32[32]{0:T(128)S(1)}, u32[]{:S(2)}, u32[]{:S(2)}) collective-permute-start(s32[32]{0:T(128)} %ids_ref.1), channel_id=1, source_target_pairs={{0,8},{8,0},{1,9},{9,1},{2,10},{10,2},{3,11},{11,3},{4,12},{12,4},... | collective-permute-start | bytes 392 | tf_op jit(solution)/shard_map/ppermute | solution.py:552
  3.4 3.8 %copy-start.1 = (s32[32]{0:T(128)S(1)}, s32[32]{0:T(128)}, u32[]{:S(2)}) copy-start(s32[32]{0:T(128)} %ids_ref.1) | copy-start | bytes 388
  7.2 4.6 %collective-permute-start.1 = (bf16[2,8,64,1024]{3,2,1,0:T(8,128)(2,1)S(1)}, bf16[2,8,64,1024]{3,2,1,0:T(8,128)(2,1)S(1)}, u32[]{:S(2)}, u32[]{:S(2)}) collective-permute-start(bf16[2,8,64,1024]{3,2,1,0:T(8,128)(2,1)S(1)} %get-tuple-element.46), channel_id=1, source_target_pairs={{0,8},{8,0},{1,9},{9,1},{2,10},{10,2},{3,11},{11,3},{4,12},{12,4},... | collective-permute-start | bytes 6291464 | tf_op jit(solution)/shard_map/ppermute | solution.py:552
  12.9 7.1 %collective-permute-start.2 = (bf16[32,2176]{1,0:T(8,128)(2,1)S(1)}, bf16[32,2176]{1,0:T(8,128)(2,1)S(1)}, u32[]{:S(2)}, u32[]{:S(2)}) collective-permute-start(bf16[32,2176]{1,0:T(8,128)(2,1)S(1)} %get-tuple-element.53), channel_id=1, source_target_pairs={{0,1},{1,0},{2,3},{3,2},{4,5},{5,4},{6,7},{7,6},{8,9},{9,8},{10,11... | collective-permute-start | bytes 417800 | tf_op jit(solution)/shard_map/ppermute | solution.py:543
  18.4 12.4 %collective-permute-start.4 = (bf16[32,1152]{1,0:T(8,128)(2,1)S(1)}, bf16[32,1152]{1,0:T(8,128)(2,1)S(1)}, u32[]{:S(2)}, u32[]{:S(2)}) collective-permute-start(bf16[32,1152]{1,0:T(8,128)(2,1)S(1)} %get-tuple-element.57), channel_id=1, source_target_pairs={{0,2},{1,3},{2,0},{3,1},{4,6},{5,7},{6,4},{7,5},{8,10},{9,11},{10,... | collective-permute-start | bytes 221192 | tf_op jit(solution)/shard_map/ppermute | solution.py:546
  20.0 10.7 %collective-permute-start.5 = (bf16[32,1152]{1,0:T(8,128)(2,1)S(1)}, bf16[32,1152]{1,0:T(8,128)(2,1)S(1)}, u32[]{:S(2)}, u32[]{:S(2)}) collective-permute-start(bf16[32,1152]{1,0:T(8,128)(2,1)S(1)} %get-tuple-element.58), channel_id=1, source_target_pairs={{0,3},{1,2},{2,1},{3,0},{4,7},{5,6},{6,5},{7,4},{8,11},{9,10},{10,... | collective-permute-start | bytes 221192 | tf_op jit(solution)/shard_map/ppermute | solution.py:549
  20.5 10.9 %collective-permute-start.6 = (bf16[32,1152]{1,0:T(8,128)(2,1)S(1)}, bf16[32,1152]{1,0:T(8,128)(2,1)S(1)}, u32[]{:S(2)}, u32[]{:S(2)}) collective-permute-start(bf16[32,1152]{1,0:T(8,128)(2,1)S(1)} %add_block.2.rest_0_), channel_id=1, source_target_pairs={{0,6},{1,7},{2,4},{3,5},{4,2},{5,3},{6,0},{7,1},{8,14},{9,15},{10,... | collective-permute-start | bytes 221192 | tf_op jit(solution)/shard_map/ppermute | solution.py:546
  25.0 6.4 %collective-permute-start.7 = (bf16[32,1152]{1,0:T(8,128)(2,1)S(1)}, bf16[32,1152]{1,0:T(8,128)(2,1)S(1)}, u32[]{:S(2)}, u32[]{:S(2)}) collective-permute-start(bf16[32,1152]{1,0:T(8,128)(2,1)S(1)} %add_block.3.rest_0_), channel_id=1, source_target_pairs={{0,4},{1,5},{2,6},{3,7},{4,0},{5,1},{6,2},{7,3},{8,12},{9,13},{10,... | collective-permute-start | bytes 221192 | tf_op jit(solution)/shard_map/ppermute | solution.py:546
  27.1 4.3 %collective-permute-start.3 = (bf16[32,1024]{1,0:T(8,128)(2,1)S(1)}, bf16[32,1024]{1,0:T(8,128)(2,1)S(1)}, u32[]{:S(2)}, u32[]{:S(2)}) collective-permute-start(bf16[32,1024]{1,0:T(8,128)(2,1)S(1)} %near_blocks.2.after_ref), channel_id=1, source_target_pairs={{0,1},{1,0},{2,3},{3,2},{4,5},{5,4},{6,7},{7,6},{8,9},{9,8},{10,11... | collective-permute-start | bytes 196616 | tf_op jit(solution)/shard_map/ppermute | solution.py:543
  31.7 6.5 %collective-permute-start.11 = (bf16[32,1024]{1,0:T(8,128)(2,1)S(1)}, bf16[32,1024]{1,0:T(8,128)(2,1)S(1)}, u32[]{:S(2)}, u32[]{:S(2)}) collective-permute-start(bf16[32,1024]{1,0:T(8,128)(2,1)S(1)} %finish.1.refs_0_), channel_id=1, source_target_pairs={{0,6},{1,7},{2,4},{3,5},{4,2},{5,3},{6,0},{7,1},{8,14},{9,15},{10,... | collective-permute-start | bytes 196616 | tf_op jit(solution)/shard_map/ppermute | solution.py:546
  33.7 6.8 %collective-permute-start.9 = (bf16[32,1024]{1,0:T(8,128)(2,1)S(1)}, bf16[32,1024]{1,0:T(8,128)(2,1)S(1)}, u32[]{:S(2)}, u32[]{:S(2)}) collective-permute-start(bf16[32,1024]{1,0:T(8,128)(2,1)S(1)} %finish.1.refs_0_), channel_id=1, source_target_pairs={{0,4},{1,5},{2,6},{3,7},{4,0},{5,1},{6,2},{7,3},{8,12},{9,13},{10,... | collective-permute-start | bytes 196616 | tf_op jit(solution)/shard_map/ppermute | solution.py:546
  34.8 5.8 %collective-permute-start.14 = (bf16[32,1024]{1,0:T(8,128)(2,1)S(1)}, bf16[32,1024]{1,0:T(8,128)(2,1)S(1)}, u32[]{:S(2)}, u32[]{:S(2)}) collective-permute-start(bf16[32,1024]{1,0:T(8,128)(2,1)S(1)} %finish.1.refs_0_), channel_id=1, source_target_pairs={{0,1},{1,0},{2,3},{3,2},{4,5},{5,4},{6,7},{7,6},{8,9},{9,8},{10,11... | collective-permute-start | bytes 196616 | tf_op jit(solution)/shard_map/ppermute | solution.py:549
  36.3 4.7 %collective-permute-start.13 = (bf16[32,1024]{1,0:T(8,128)(2,1)S(1)}, bf16[32,1024]{1,0:T(8,128)(2,1)S(1)}, u32[]{:S(2)}, u32[]{:S(2)}) collective-permute-start(bf16[32,1024]{1,0:T(8,128)(2,1)S(1)} %finish.1.refs_0_), channel_id=1, source_target_pairs={{0,2},{1,3},{2,0},{3,1},{4,6},{5,7},{6,4},{7,5},{8,10},{9,11},{10,... | collective-permute-start | bytes 196616 | tf_op jit(solution)/shard_map/ppermute | solution.py:546
  37.7 5.3 %collective-permute-start.8 = (bf16[32,1024]{1,0:T(8,128)(2,1)S(1)}, bf16[32,1024]{1,0:T(8,128)(2,1)S(1)}, u32[]{:S(2)}, u32[]{:S(2)}) collective-permute-start(bf16[32,1024]{1,0:T(8,128)(2,1)S(1)} %finish.1.refs_0_), channel_id=1, source_target_pairs={{0,3},{1,2},{2,1},{3,0},{4,7},{5,6},{6,5},{7,4},{8,11},{9,10},{10,... | collective-permute-start | bytes 196616 | tf_op jit(solution)/shard_map/ppermute | solution.py:549
  38.3 5.0 %collective-permute-start.12 = (bf16[32,1024]{1,0:T(8,128)(2,1)S(1)}, bf16[32,1024]{1,0:T(8,128)(2,1)S(1)}, u32[]{:S(2)}, u32[]{:S(2)}) collective-permute-start(bf16[32,1024]{1,0:T(8,128)(2,1)S(1)} %collective-permute-done.11.refs_4_), channel_id=1, source_target_pairs={{0,1},{1,0},{2,3},{3,2},{4,5},{5,4},{6,7},{7,6},{8,9},{9,8},{10,11... | collective-permute-start | bytes 196616 | tf_op jit(solution)/shard_map/ppermute | solution.py:543
  40.5 4.3 %collective-permute-start.10 = (bf16[32,1024]{1,0:T(8,128)(2,1)S(1)}, bf16[32,1024]{1,0:T(8,128)(2,1)S(1)}, u32[]{:S(2)}, u32[]{:S(2)}) collective-permute-start(bf16[32,1024]{1,0:T(8,128)(2,1)S(1)} %collective-permute-done.9.refs_2_), channel_id=1, source_target_pairs={{0,1},{1,0},{2,3},{3,2},{4,5},{5,4},{6,7},{7,6},{8,9},{9,8},{10,11... | collective-permute-start | bytes 196616 | tf_op jit(solution)/shard_map/ppermute | solution.py:543

commit v14 on v11

--- a/solution.py
+++ b/solution.py
@@ -76,7 +76,22 @@
 
 
 def prefix_scores_kernel(
-    q_ref, prefix_ref, suffix_ref, query_ref, scores_ref, peak_ref, vals_ref, suf_keys_ref, qbuf, keys, rowbuf, sem, sem_keys
+    q_ref,
+    prefix_ref,
+    suffix_ref,
+    weight_ref,
+    query_ref,
+    scores_ref,
+    peak_ref,
+    vals_ref,
+    suf_keys_ref,
+    w_ref,
+    qbuf,
+    keys,
+    rowbuf,
+    sem,
+    sem_keys,
+    sem_w,
 ):
     rows = q_ref.shape[0]
     tokens, head_dim = keys.shape
@@ -93,7 +108,7 @@
     fetch = [
         pltpu.make_async_copy(suffix_ref.at[:, 0, 0], suf_keys_ref, sem.at[1]),
         pltpu.make_async_copy(prefix_ref.at[0, 1], vals_ref, sem.at[2]),
-    ]
+    ] + weight_copies(weight_ref, [w_ref], [(1, 0)], sem_w)
     for c in [fetch_q] + key_copies + fetch:
         c.start()
     fetch_q.wait()
@@ -272,7 +287,7 @@
     span = suffix_kv.shape[3]
     prefix_kv, suffix_kv, out_weight = in_hbm(prefix_kv), in_hbm(suffix_kv), in_hbm(out_weight)
     pages, residual = in_hbm(pages), in_hbm(residual)
-    query, scores, peak, vals, suf_keys = kernel_call(
+    query, scores, peak, vals, suf_keys, own_far_w = kernel_call(
         prefix_scores_kernel,
         "prefix_scores",
         [
@@ -281,16 +296,18 @@
             pltpu.VMEM((8, n_q), F32),
             pltpu.VMEM((tokens, head_dim), BF16),
             pltpu.VMEM((rows, span, head_dim), BF16),
+            pltpu.VMEM((in_rows, width), BF16),
         ],
-        [ANY, ANY, ANY],
+        [ANY, ANY, ANY, ANY],
         [
             pltpu.VMEM(queries.shape, BF16),
             pltpu.VMEM((tokens, head_dim), BF16),
             pltpu.VMEM((n_q, head_dim), F32),
             pltpu.SemaphoreType.DMA((3,)),
             pltpu.SemaphoreType.DMA((4,)),
+            pltpu.SemaphoreType.DMA((1,)),
         ],
-        [in_hbm(queries), prefix_kv, suffix_kv],
+        [in_hbm(queries), prefix_kv, suffix_kv, out_weight],
         8,
         2 * n_q * tokens * head_dim,
         6 * MIB,
@@ -355,6 +372,7 @@
         14 * MIB,
     )
     weights = dict(zip(early + late, list(early_w) + list(late_w)))
+    weights[1, 0] = own_far_w
     return attended, own_shrink, own_expand, other_pages, row_slot, slot_mine, res, weights
 
 
@@ -401,6 +419,10 @@
         picked = jnp.where(hit, low[:, tile * 128 : (tile + 1) * 128], picked)
     rank_ref[...] = picked
     out_ref[:, n * width :] = picked.astype(BF16)
+
+
+def block_kernel(att_ref, w_ref, after_ref, out_ref):
+    out_ref[...] = nn_dot(att_ref[...], w_ref[...]).astype(BF16)
 
 
 def near_kernel(spots, att_ref, rank_ref, weight_ref, *rest):
@@ -590,7 +612,9 @@
         )
         moved.append(along_z(piece, k))
         after = [piece]
-    (own_far,) = near_blocks([(1, 0)], width, attended, rank_own, out_weight, [piece], n_tensor)
+    own_far = small_call(
+        block_kernel, "own_far_block", pltpu.VMEM((rows, width), BF16), [attended, weights[1, 0], piece]
+    )
     from_own = along_y(own_far)
     own, expand_pages = own_block(attended, res, slot_mine, own_expand, other_pages, out_weight, own_far)
     result = small_call(

time: 45.7 us -> 45.5 us (level)
  waiting for transfers between devices: 4.42 us -> 6.6 us
  starting transfers between devices: 19.1 us -> 17.8 us
  Pallas kernels: 21.8 us -> 20.8 us
    ppermute x6, waiting for transfers between devices: 0.79 us -> 3.37 us  [along_z(): return lax.ppermute(x, 'tensor', [(t, t ^ 2 * k) for t in range(n_tensor)])]
    pallas_call x6 -> x5, Pallas kernels: 17.9 us -> 16.5 us  [kernel_call(): pl.pallas_call(kernel, out_shape=out_shape, in_specs=specs, out_specs=[VM...]
    ppermute x6, starting transfers between devices: 10.1 us -> 9.32 us  [along_z(): return lax.ppermute(x, 'tensor', [(t, t ^ 2 * k) for t in range(n_tensor)])]
    ppermute x3, waiting for transfers between devices: 1.24 us -> 0.51 us  [along_both(): lax.ppermute(x, 'tensor', [(t, t ^ 2 * k ^ 1) for t in range(n_tensor)])]
    ppermute x4, starting transfers between devices: 6.37 us -> 5.72 us  [along_y(): return lax.ppermute(x, 'tensor', [(t, t ^ 1) for t in range(n_tensor)])]
    pallas_call x4 -> x5, Pallas kernels: 2.38 us -> 2.84 us  [small_call(): pl.pallas_call(kernel, out_shape=out_shape, in_specs=[VMEM] * len(operand...]
  transfers between devices with their start and end apart: 15 -> 15, of which waited for: 6 -> 7; matrix products, arithmetic and copies ran while one was open for 0% -> 0% of each run, Pallas kernels for 35% -> 33%
where the time goes in v14:
time: 45.5 us; the launch traced here: 45.3 us
  Pallas kernels  20.8 us (46%)
  starting transfers between devices  17.8 us (39%)
  waiting for transfers between devices  6.6 us (15%)
    pallas_call x5, Pallas kernels, kernel_call(): pl.pallas_call(kernel, out_shape=out_shape, in_specs=specs, out_specs=[VM...  16.5 us
    ppermute x6, starting transfers between devices, along_z(): return lax.ppermute(x, 'tensor', [(t, t ^ 2 * k) for t in range(n_tensor)])  9.32 us
    ppermute x4, starting transfers between devices, along_y(): return lax.ppermute(x, 'tensor', [(t, t ^ 1) for t in range(n_tensor)])  5.72 us
    ppermute x6, waiting for transfers between devices, along_z(): return lax.ppermute(x, 'tensor', [(t, t ^ 2 * k) for t in range(n_tensor)])  3.37 us
    pallas_call x5, Pallas kernels, small_call(): pl.pallas_call(kernel, out_shape=out_shape, in_specs=[VMEM] * len(operand...  2.84 us
    ppermute x4, waiting for transfers between devices, along_y(): return lax.ppermute(x, 'tensor', [(t, t ^ 1) for t in range(n_tensor)])  2.71 us
    ppermute x3, starting transfers between devices, along_both(): lax.ppermute(x, 'tensor', [(t, t ^ 2 * k ^ 1) for t in range(n_tensor)])  2.26 us
    pallas_call x2, Pallas kernels, place(): pl.pallas_call(functools.partial(place_kernel, spots), out_shape=pltpu.HB...  1.46 us
  transfers between devices with their start and end apart: 15, of which 7 were waited for; matrix products, arithmetic and copies ran while one was open for 0% of the time, Pallas kernels for 33%

profile of v14, /device:TPU:0, one launch (start us, length us, event | category | flops | bytes accessed | tf_op | source)
XLA Modules:
  0.0 45.3 jit_solution(11321064721292494760)
XLA Ops:
  0.0 0.5 collective-permute-start
  0.5 3.6 %prefix_scores.1 = (bf16[256,128]{1,0:T(8,128)(2,1)S(1)}, f32[8192,256]{1,0:T(8,128)S(1)}, f32[8,256]{1,0:T(8,128)S(1)}, bf16[8192,128]{1,0:T(8,128)(2,1)S(1)}, ...) custom-call(bf16[32,1024]{1,0:T(8,128)(2,1)} %q_ref.1, bf16[1,2,8192,128]{3,2,1,0:T(8,128)(2,1)} %prefix_ref.1, ...), custom_call_target="tpu_custom_call" | custom-call | flops 536870912 | bytes 6291456 | tf_op jit(solution)/shard_map/prefix_scores/pallas_call | solution.py:266
  4.1 3.6 %suffix_scores.1 = (f32[256,256]{1,0:T(8,128)S(1)}, f32[256,128]{1,0:T(8,128)S(1)}, f32[8,256]{1,0:T(8,128)S(1)}, bf16[144,8192]{1,0:T(8,128)(2,1)S(1)}, bf16[2,...) custom-call(s32[32]{0:T(128)S(1)} %collective-permute-done.ids_ref, ...), custom_call_target="tpu_custom_call" | custom-call | flops 536870912 | bytes 7340032 | tf_op jit(solution)/shard_map/suffix_scores/pallas_call | solution.py:266
  7.7 0.1 collective-permute-start.1
  7.8 4.5 %values.1 = (bf16[32,1024]{1,0:T(8,128)(2,1)S(1)}, bf16[8,64,1024]{2,1,0:T(8,128)(2,1)S(1)}, bf16[8,64,1024]{2,1,0:T(8,128)(2,1)S(1)}, s32[32,128]{1,0:T(8,128)S...) custom-call(s32[32]{0:T(128)S(1)} %copy-done.1, ...), custom_call_target="tpu_custom_call" | custom-call | flops 536870912 | bytes 14680064 | tf_op jit(solution)/shard_map/values/pallas_call | solution.py:266
  12.3 1.1 %far_blocks.1 = (bf16[32,2176]{1,0:T(8,128)(2,1)S(1)}, f32[32,128]{1,0:T(8,128)S(1)}) custom-call(bf16[32,1024]{1,0:T(8,128)(2,1)S(1)} %get-tuple-element.43.att_ref, s32[32,128]{1,0:T(8,128)S(1)} %get-tuple-element.50.row_slot_ref.refs_2_, s32[8,128]{1,0:T(8,128)S(1)} %get-tuple-element.45.slot_mine_ref, ...), custom_call_target="tpu_custom_call" | custom-call | flops 134217728 | bytes 2097152 | tf_op jit(solution)/shard_map/far_blocks/pallas_call | solution.py:380
  13.4 3.0 %collective-permute-start.2 = (bf16[32,2176]{1,0:T(8,128)(2,1)S(1)}, bf16[32,2176]{1,0:T(8,128)(2,1)S(1)}, u32[]{:S(2)}, u32[]{:S(2)}) collective-permute-start(bf16[32,2176]{1,0:T(8,128)(2,1)S(1)} %get-tuple-element.54), channel_id=1, source_target_pairs={{0,1},{1,0},{2,3},{3,2},{4,5},{5,4},{6,7},{7,6},{8,9},{9,8},{10,11... | collective-permute-start | bytes 417800 | tf_op jit(solution)/shard_map/ppermute | solution.py:565
  16.4 2.7 %near_blocks.1 = (bf16[32,1152]{1,0:T(8,128)(2,1)S(1)}, bf16[32,1152]{1,0:T(8,128)(2,1)S(1)}) custom-call(bf16[32,1024]{1,0:T(8,128)(2,1)S(1)} %get-tuple-element.43.att_ref, f32[32,128]{1,0:T(8,128)S(1)} %get-tuple-element.55.rank_ref.refs_3_, bf16[1024,8192]{1,0:T(8,128)(2,1)} %weight_ref.5), custom_call_target="tpu_custom_call" | custom-call | flops 134217728 | bytes 4194304 | tf_op jit(solution)/shard_map/near_blocks/pallas_call | solution.py:266
  19.1 1.6 %collective-permute-start.4 = (bf16[32,1152]{1,0:T(8,128)(2,1)S(1)}, bf16[32,1152]{1,0:T(8,128)(2,1)S(1)}, u32[]{:S(2)}, u32[]{:S(2)}) collective-permute-start(bf16[32,1152]{1,0:T(8,128)(2,1)S(1)} %get-tuple-element.59), channel_id=1, source_target_pairs={{0,2},{1,3},{2,0},{3,1},{4,6},{5,7},{6,4},{7,5},{8,10},{9,11},{10,... | collective-permute-start | bytes 221192 | tf_op jit(solution)/shard_map/ppermute | solution.py:568
  20.8 0.0 collective-permute-start.5
  20.8 0.5 %add_block.2.rest_0_ = bf16[32,1152]{1,0:T(8,128)(2,1)S(1)} custom-call(bf16[32,1024]{1,0:T(8,128)(2,1)S(1)} %get-tuple-element.43.att_ref, bf16[1024,1024]{1,0:T(8,128)(2,1)S(1)} %get-tuple-element.56.w_ref, bf16[32,2176]{1,0:T(8,128)(2,1)S(1)} %collective-permute-done.2.from_ref.refs_4_, f32[32,128]{1,0:T(8,128)S(1)} %get-tuple-element.55.rank_ref.refs_3_), custom_call_target="tpu_custom_call" | custom-call | flops 134217728 | bytes 2097152 | tf_op jit(solution)/shard_map/add_block/pallas_call | solution.py:380
  21.2 4.0 %collective-permute-start.6 = (bf16[32,1152]{1,0:T(8,128)(2,1)S(1)}, bf16[32,1152]{1,0:T(8,128)(2,1)S(1)}, u32[]{:S(2)}, u32[]{:S(2)}) collective-permute-start(bf16[32,1152]{1,0:T(8,128)(2,1)S(1)} %add_block.2.rest_0_), channel_id=1, source_target_pairs={{0,6},{1,7},{2,4},{3,5},{4,2},{5,3},{6,0},{7,1},{8,14},{9,15},{10,... | collective-permute-start | bytes 221192 | tf_op jit(solution)/shard_map/ppermute | solution.py:568
  25.2 0.5 %add_block.3.after_ref = bf16[32,1152]{1,0:T(8,128)(2,1)S(1)} custom-call(bf16[32,1024]{1,0:T(8,128)(2,1)S(1)} %get-tuple-element.43.att_ref, bf16[1024,1024]{1,0:T(8,128)(2,1)S(1)} %get-tuple-element.49.w_ref, bf16[32,2176]{1,0:T(8,128)(2,1)S(1)} %collective-permute-done.2.from_ref.refs_4_, f32[32,128]{1,0:T(8,128)S(1)} %get-tuple-element.55.rank_ref.refs_3_, ...), custom_call_target="tpu_custom_call" | custom-call | flops 134217728 | bytes 2097152 | tf_op jit(solution)/shard_map/add_block/pallas_call | solution.py:380
  25.7 0.5 %own_far_block.1.after_ref = bf16[32,1024]{1,0:T(8,128)(2,1)S(1)} custom-call(bf16[32,1024]{1,0:T(8,128)(2,1)S(1)} %get-tuple-element.43.att_ref, bf16[1024,1024]{1,0:T(8,128)(2,1)S(1)} %get-tuple-element.48.w_ref, bf16[32,1152]{1,0:T(8,128)(2,1)S(1)} %add_block.3.after_ref), custom_call_target="tpu_custom_call" | custom-call | flops 134217728 | bytes 2097152 | tf_op jit(solution)/shard_map/own_far_block/pallas_call | solution.py:380
  26.2 1.5 %collective-permute-start.3 = (bf16[32,1024]{1,0:T(8,128)(2,1)S(1)}, bf16[32,1024]{1,0:T(8,128)(2,1)S(1)}, u32[]{:S(2)}, u32[]{:S(2)}) collective-permute-start(bf16[32,1024]{1,0:T(8,128)(2,1)S(1)} %own_far_block.1.after_ref), channel_id=1, source_target_pairs={{0,1},{1,0},{2,3},{3,2},{4,5},{5,4},{6,7},{7,6},{8,9},{9,8},{10,11... | collective-permute-start | bytes 196616 | tf_op jit(solution)/shard_map/ppermute | solution.py:565
  27.7 2.1 %own_block.1 = (f32[32,1024]{1,0:T(8,128)S(1)}, bf16[512,1024]{1,0:T(8,128)(2,1)S(1)}) custom-call(bf16[32,1024]{1,0:T(8,128)(2,1)S(1)} %get-tuple-element.43.att_ref, bf16[32,1024]{1,0:T(8,128)(2,1)S(1)} %get-tuple-element.44.res_ref, s32[8,128]{1,0:T(8,128)S(1)} %get-tuple-element.45.slot_mine_ref, bf16[8,64,1024]{2,1,0:T(8,128)(2,1)S(1)} %get-tuple-element.46.own_ref, ...), custom_call_target="tpu_custom_call" | custom-call | bytes 2097152 | tf_op jit(solution)/shard_map/own_block/pallas_call | solution.py:266
  29.8 0.6 %collective-permute-done.3.refs_5_ = bf16[32,1024]{1,0:T(8,128)(2,1)S(1)} collective-permute-done((bf16[32,1024]{1,0:T(8,128)(2,1)S(1)}, bf16[32,1024]{1,0:T(8,128)(2,1)S(1)}, u32[]{:S(2)}, u32[]{:S(2)}) %collective-permute-start.3) | collective-permute-done | bytes 65568 | tf_op jit(solution)/shard_map/ppermute | solution.py:565
  30.5 1.3 %collective-permute-done.7.refs_9_ = bf16[32,1152]{1,0:T(8,128)(2,1)S(1)} collective-permute-done((bf16[32,1152]{1,0:T(8,128)(2,1)S(1)}, bf16[32,1152]{1,0:T(8,128)(2,1)S(1)}, u32[]{:S(2)}, u32[]{:S(2)}) %collective-permute-start.7) | collective-permute-done | bytes 73760 | tf_op jit(solution)/shard_map/ppermute | solution.py:568
  31.8 0.3 finish.1.refs_0_
  32.1 2.1 %collective-permute-start.11 = (bf16[32,1024]{1,0:T(8,128)(2,1)S(1)}, bf16[32,1024]{1,0:T(8,128)(2,1)S(1)}, u32[]{:S(2)}, u32[]{:S(2)}) collective-permute-start(bf16[32,1024]{1,0:T(8,128)(2,1)S(1)} %finish.1.refs_0_), channel_id=1, source_target_pairs={{0,6},{1,7},{2,4},{3,5},{4,2},{5,3},{6,0},{7,1},{8,14},{9,15},{10,... | collective-permute-start | bytes 196616 | tf_op jit(solution)/shard_map/ppermute | solution.py:568
  34.2 1.5 %collective-permute-start.14 = (bf16[32,1024]{1,0:T(8,128)(2,1)S(1)}, bf16[32,1024]{1,0:T(8,128)(2,1)S(1)}, u32[]{:S(2)}, u32[]{:S(2)}) collective-permute-start(bf16[32,1024]{1,0:T(8,128)(2,1)S(1)} %finish.1.refs_0_), channel_id=1, source_target_pairs={{0,1},{1,0},{2,3},{3,2},{4,5},{5,4},{6,7},{7,6},{8,9},{9,8},{10,11... | collective-permute-start | bytes 196616 | tf_op jit(solution)/shard_map/ppermute | solution.py:571
  35.7 1.6 %collective-permute-start.13 = (bf16[32,1024]{1,0:T(8,128)(2,1)S(1)}, bf16[32,1024]{1,0:T(8,128)(2,1)S(1)}, u32[]{:S(2)}, u32[]{:S(2)}) collective-permute-start(bf16[32,1024]{1,0:T(8,128)(2,1)S(1)} %finish.1.refs_0_), channel_id=1, source_target_pairs={{0,2},{1,3},{2,0},{3,1},{4,6},{5,7},{6,4},{7,5},{8,10},{9,11},{10,... | collective-permute-start | bytes 196616 | tf_op jit(solution)/shard_map/ppermute | solution.py:568
  37.3 0.7 %collective-permute-start.8 = (bf16[32,1024]{1,0:T(8,128)(2,1)S(1)}, bf16[32,1024]{1,0:T(8,128)(2,1)S(1)}, u32[]{:S(2)}, u32[]{:S(2)}) collective-permute-start(bf16[32,1024]{1,0:T(8,128)(2,1)S(1)} %finish.1.refs_0_), channel_id=1, source_target_pairs={{0,3},{1,2},{2,1},{3,0},{4,7},{5,6},{6,5},{7,4},{8,11},{9,10},{10,... | collective-permute-start | bytes 196616 | tf_op jit(solution)/shard_map/ppermute | solution.py:571
  38.0 0.9 %collective-permute-done.11.refs_4_ = bf16[32,1024]{1,0:T(8,128)(2,1)S(1)} collective-permute-done((bf16[32,1024]{1,0:T(8,128)(2,1)S(1)}, bf16[32,1024]{1,0:T(8,128)(2,1)S(1)}, u32[]{:S(2)}, u32[]{:S(2)}) %collective-permute-start.11) | collective-permute-done | bytes 65568 | tf_op jit(solution)/shard_map/ppermute | solution.py:568
  38.9 0.3 collective-permute-start.12
  39.2 1.1 %collective-permute-done.9.refs_2_ = bf16[32,1024]{1,0:T(8,128)(2,1)S(1)} collective-permute-done((bf16[32,1024]{1,0:T(8,128)(2,1)S(1)}, bf16[32,1024]{1,0:T(8,128)(2,1)S(1)}, u32[]{:S(2)}, u32[]{:S(2)}) %collective-permute-start.9) | collective-permute-done | bytes 65568 | tf_op jit(solution)/shard_map/ppermute | solution.py:568
  40.4 0.9 %collective-permute-start.10 = (bf16[32,1024]{1,0:T(8,128)(2,1)S(1)}, bf16[32,1024]{1,0:T(8,128)(2,1)S(1)}, u32[]{:S(2)}, u32[]{:S(2)}) collective-permute-start(bf16[32,1024]{1,0:T(8,128)(2,1)S(1)} %collective-permute-done.9.refs_2_), channel_id=1, source_target_pairs={{0,1},{1,0},{2,3},{3,2},{4,5},{5,4},{6,7},{7,6},{8,9},{9,8},{10,11... | collective-permute-start | bytes 196616 | tf_op jit(solution)/shard_map/ppermute | solution.py:565
  41.3 0.8 %place.2.refs_3_ = bf16[32,8192]{1,0:T(8,128)(2,1)} custom-call(bf16[32,1024]{1,0:T(8,128)(2,1)S(1)} %finish.1.refs_0_, bf16[32,1024]{1,0:T(8,128)(2,1)S(1)} %collective-permute-done.13.refs_1_, bf16[32,1024]{1,0:T(8,128)(2,1)S(1)} %collective-permute-done.9.refs_2_, bf16[32,1024]{1,0:T(8,128)(2,1)S(1)} %collective-permute-done.14.refs_3_, ...), custom_call_target="tpu_custom_call" | custom-call | bytes 1048576 | tf_op jit(solution)/shard_map/place/pallas_call | solution.py:537
  42.0 0.5 %collective-permute-done.8.refs_0_ = bf16[32,1024]{1,0:T(8,128)(2,1)S(1)} collective-permute-done((bf16[32,1024]{1,0:T(8,128)(2,1)S(1)}, bf16[32,1024]{1,0:T(8,128)(2,1)S(1)}, u32[]{:S(2)}, u32[]{:S(2)}) %collective-permute-start.8) | collective-permute-done | bytes 65568 | tf_op jit(solution)/shard_map/ppermute | solution.py:571
  42.5 1.3 %collective-permute-done.12.refs_2_ = bf16[32,1024]{1,0:T(8,128)(2,1)S(1)} collective-permute-done((bf16[32,1024]{1,0:T(8,128)(2,1)S(1)}, bf16[32,1024]{1,0:T(8,128)(2,1)S(1)}, u32[]{:S(2)}, u32[]{:S(2)}) %collective-permute-start.12) | collective-permute-done | bytes 65568 | tf_op jit(solution)/shard_map/ppermute | solution.py:565
  43.9 0.7 %collective-permute-done.10.refs_1_ = bf16[32,1024]{1,0:T(8,128)(2,1)S(1)} collective-permute-done((bf16[32,1024]{1,0:T(8,128)(2,1)S(1)}, bf16[32,1024]{1,0:T(8,128)(2,1)S(1)}, u32[]{:S(2)}, u32[]{:S(2)}) %collective-permute-start.10) | collective-permute-done | bytes 65568 | tf_op jit(solution)/shard_map/ppermute | solution.py:565
  44.6 0.7 %place.3 = bf16[32,8192]{1,0:T(8,128)(2,1)} custom-call(bf16[32,1024]{1,0:T(8,128)(2,1)S(1)} %collective-permute-done.8.refs_0_, bf16[32,1024]{1,0:T(8,128)(2,1)S(1)} %collective-permute-done.10.refs_1_, bf16[32,1024]{1,0:T(8,128)(2,1)S(1)} %collective-permute-done.12.refs_2_, bf16[32,8192]{1,0:T(8,128)(2,1)} %place.2.refs_3_), custom_call_target="tpu_custom_call", output_to_operand_aliasing={{}: (3, {})} | custom-call | bytes 1048576 | tf_op jit(solution)/shard_map/place/pallas_call | solution.py:537
  (14 shorter events, 0.0 us)
Async XLA Ops:
  0.0 4.0 %copy-start = (s32[128]{0:T(128)S(1)}, s32[128]{0:T(128)}, u32[]{:S(2)}) copy-start(s32[128]{0:T(128)} %slot_ref.3) | copy-start | bytes 1540
  0.0 4.0 %collective-permute-start = (s32[32]{0:T(128)}, s32[32]{0:T(128)S(1)}, u32[]{:S(2)}, u32[]{:S(2)}) collective-permute-start(s32[32]{0:T(128)} %ids_ref.1), channel_id=1, source_target_pairs={{0,8},{8,0},{1,9},{9,1},{2,10},{10,2},{3,11},{11,3},{4,12},{12,4},... | collective-permute-start | bytes 392 | tf_op jit(solution)/shard_map/ppermute | solution.py:574
  4.1 3.7 %copy-start.1 = (s32[32]{0:T(128)S(1)}, s32[32]{0:T(128)}, u32[]{:S(2)}) copy-start(s32[32]{0:T(128)} %ids_ref.1) | copy-start | bytes 388
  7.7 4.6 %collective-permute-start.1 = (bf16[2,8,64,1024]{3,2,1,0:T(8,128)(2,1)S(1)}, bf16[2,8,64,1024]{3,2,1,0:T(8,128)(2,1)S(1)}, u32[]{:S(2)}, u32[]{:S(2)}) collective-permute-start(bf16[2,8,64,1024]{3,2,1,0:T(8,128)(2,1)S(1)} %get-tuple-element.47), channel_id=1, source_target_pairs={{0,8},{8,0},{1,9},{9,1},{2,10},{10,2},{3,11},{11,3},{4,12},{12,4},... | collective-permute-start | bytes 6291464 | tf_op jit(solution)/shard_map/ppermute | solution.py:574
  13.4 7.4 %collective-permute-start.2 = (bf16[32,2176]{1,0:T(8,128)(2,1)S(1)}, bf16[32,2176]{1,0:T(8,128)(2,1)S(1)}, u32[]{:S(2)}, u32[]{:S(2)}) collective-permute-start(bf16[32,2176]{1,0:T(8,128)(2,1)S(1)} %get-tuple-element.54), channel_id=1, source_target_pairs={{0,1},{1,0},{2,3},{3,2},{4,5},{5,4},{6,7},{7,6},{8,9},{9,8},{10,11... | collective-permute-start | bytes 417800 | tf_op jit(solution)/shard_map/ppermute | solution.py:565
  19.1 10.7 %collective-permute-start.4 = (bf16[32,1152]{1,0:T(8,128)(2,1)S(1)}, bf16[32,1152]{1,0:T(8,128)(2,1)S(1)}, u32[]{:S(2)}, u32[]{:S(2)}) collective-permute-start(bf16[32,1152]{1,0:T(8,128)(2,1)S(1)} %get-tuple-element.59), channel_id=1, source_target_pairs={{0,2},{1,3},{2,0},{3,1},{4,6},{5,7},{6,4},{7,5},{8,10},{9,11},{10,... | collective-permute-start | bytes 221192 | tf_op jit(solution)/shard_map/ppermute | solution.py:568
  20.8 9.1 %collective-permute-start.5 = (bf16[32,1152]{1,0:T(8,128)(2,1)S(1)}, bf16[32,1152]{1,0:T(8,128)(2,1)S(1)}, u32[]{:S(2)}, u32[]{:S(2)}) collective-permute-start(bf16[32,1152]{1,0:T(8,128)(2,1)S(1)} %get-tuple-element.60), channel_id=1, source_target_pairs={{0,3},{1,2},{2,1},{3,0},{4,7},{5,6},{6,5},{7,4},{8,11},{9,10},{10,... | collective-permute-start | bytes 221192 | tf_op jit(solution)/shard_map/ppermute | solution.py:571
  21.2 10.6 %collective-permute-start.6 = (bf16[32,1152]{1,0:T(8,128)(2,1)S(1)}, bf16[32,1152]{1,0:T(8,128)(2,1)S(1)}, u32[]{:S(2)}, u32[]{:S(2)}) collective-permute-start(bf16[32,1152]{1,0:T(8,128)(2,1)S(1)} %add_block.2.rest_0_), channel_id=1, source_target_pairs={{0,6},{1,7},{2,4},{3,5},{4,2},{5,3},{6,0},{7,1},{8,14},{9,15},{10,... | collective-permute-start | bytes 221192 | tf_op jit(solution)/shard_map/ppermute | solution.py:568
  25.7 6.1 %collective-permute-start.7 = (bf16[32,1152]{1,0:T(8,128)(2,1)S(1)}, bf16[32,1152]{1,0:T(8,128)(2,1)S(1)}, u32[]{:S(2)}, u32[]{:S(2)}) collective-permute-start(bf16[32,1152]{1,0:T(8,128)(2,1)S(1)} %add_block.3.after_ref), channel_id=1, source_target_pairs={{0,4},{1,5},{2,6},{3,7},{4,0},{5,1},{6,2},{7,3},{8,12},{9,13},{10,... | collective-permute-start | bytes 221192 | tf_op jit(solution)/shard_map/ppermute | solution.py:568
  26.2 4.3 %collective-permute-start.3 = (bf16[32,1024]{1,0:T(8,128)(2,1)S(1)}, bf16[32,1024]{1,0:T(8,128)(2,1)S(1)}, u32[]{:S(2)}, u32[]{:S(2)}) collective-permute-start(bf16[32,1024]{1,0:T(8,128)(2,1)S(1)} %own_far_block.1.after_ref), channel_id=1, source_target_pairs={{0,1},{1,0},{2,3},{3,2},{4,5},{5,4},{6,7},{7,6},{8,9},{9,8},{10,11... | collective-permute-start | bytes 196616 | tf_op jit(solution)/shard_map/ppermute | solution.py:565
  32.1 6.8 %collective-permute-start.11 = (bf16[32,1024]{1,0:T(8,128)(2,1)S(1)}, bf16[32,1024]{1,0:T(8,128)(2,1)S(1)}, u32[]{:S(2)}, u32[]{:S(2)}) collective-permute-start(bf16[32,1024]{1,0:T(8,128)(2,1)S(1)} %finish.1.refs_0_), channel_id=1, source_target_pairs={{0,6},{1,7},{2,4},{3,5},{4,2},{5,3},{6,0},{7,1},{8,14},{9,15},{10,... | collective-permute-start | bytes 196616 | tf_op jit(solution)/shard_map/ppermute | solution.py:568
  34.2 6.2 %collective-permute-start.9 = (bf16[32,1024]{1,0:T(8,128)(2,1)S(1)}, bf16[32,1024]{1,0:T(8,128)(2,1)S(1)}, u32[]{:S(2)}, u32[]{:S(2)}) collective-permute-start(bf16[32,1024]{1,0:T(8,128)(2,1)S(1)} %finish.1.refs_0_), channel_id=1, source_target_pairs={{0,4},{1,5},{2,6},{3,7},{4,0},{5,1},{6,2},{7,3},{8,12},{9,13},{10,... | collective-permute-start | bytes 196616 | tf_op jit(solution)/shard_map/ppermute | solution.py:568
  34.2 7.1 %collective-permute-start.14 = (bf16[32,1024]{1,0:T(8,128)(2,1)S(1)}, bf16[32,1024]{1,0:T(8,128)(2,1)S(1)}, u32[]{:S(2)}, u32[]{:S(2)}) collective-permute-start(bf16[32,1024]{1,0:T(8,128)(2,1)S(1)} %finish.1.refs_0_), channel_id=1, source_target_pairs={{0,1},{1,0},{2,3},{3,2},{4,5},{5,4},{6,7},{7,6},{8,9},{9,8},{10,11... | collective-permute-start | bytes 196616 | tf_op jit(solution)/shard_map/ppermute | solution.py:571
  35.7 5.5 %collective-permute-start.13 = (bf16[32,1024]{1,0:T(8,128)(2,1)S(1)}, bf16[32,1024]{1,0:T(8,128)(2,1)S(1)}, u32[]{:S(2)}, u32[]{:S(2)}) collective-permute-start(bf16[32,1024]{1,0:T(8,128)(2,1)S(1)} %finish.1.refs_0_), channel_id=1, source_target_pairs={{0,2},{1,3},{2,0},{3,1},{4,6},{5,7},{6,4},{7,5},{8,10},{9,11},{10,... | collective-permute-start | bytes 196616 | tf_op jit(solution)/shard_map/ppermute | solution.py:568
  37.3 5.2 %collective-permute-start.8 = (bf16[32,1024]{1,0:T(8,128)(2,1)S(1)}, bf16[32,1024]{1,0:T(8,128)(2,1)S(1)}, u32[]{:S(2)}, u32[]{:S(2)}) collective-permute-start(bf16[32,1024]{1,0:T(8,128)(2,1)S(1)} %finish.1.refs_0_), channel_id=1, source_target_pairs={{0,3},{1,2},{2,1},{3,0},{4,7},{5,6},{6,5},{7,4},{8,11},{9,10},{10,... | collective-permute-start | bytes 196616 | tf_op jit(solution)/shard_map/ppermute | solution.py:571
  38.9 5.0 %collective-permute-start.12 = (bf16[32,1024]{1,0:T(8,128)(2,1)S(1)}, bf16[32,1024]{1,0:T(8,128)(2,1)S(1)}, u32[]{:S(2)}, u32[]{:S(2)}) collective-permute-start(bf16[32,1024]{1,0:T(8,128)(2,1)S(1)} %collective-permute-done.11.refs_4_), channel_id=1, source_target_pairs={{0,1},{1,0},{2,3},{3,2},{4,5},{5,4},{6,7},{7,6},{8,9},{9,8},{10,11... | collective-permute-start | bytes 196616 | tf_op jit(solution)/shard_map/ppermute | solution.py:565
  40.4 4.3 %collective-permute-start.10 = (bf16[32,1024]{1,0:T(8,128)(2,1)S(1)}, bf16[32,1024]{1,0:T(8,128)(2,1)S(1)}, u32[]{:S(2)}, u32[]{:S(2)}) collective-permute-start(bf16[32,1024]{1,0:T(8,128)(2,1)S(1)} %collective-permute-done.9.refs_2_), channel_id=1, source_target_pairs={{0,1},{1,0},{2,3},{3,2},{4,5},{5,4},{6,7},{7,6},{8,9},{9,8},{10,11... | collective-permute-start | bytes 196616 | tf_op jit(solution)/shard_map/ppermute | solution.py:565

commit v15 on v11

--- a/solution.py
+++ b/solution.py
@@ -206,7 +206,7 @@
 
     acc_t[...] = jnp.zeros(acc_t.shape, F32)
     n_q = acc_t.shape[1]
-    chunk = min(2048, tokens)
+    chunk = min(4096, tokens)
 
     @pl.loop(0, tokens // chunk)
     def _(i):

time: 45.7 us -> 45.6 us (level)
  no operation moved by 1% of the time
where the time goes in v15:
time: 45.6 us; the launch traced here: 45.5 us
  Pallas kernels  22.1 us (48%)
  starting transfers between devices  18.9 us (41%)
  waiting for transfers between devices  4.41 us (10%)
    pallas_call x6, Pallas kernels, kernel_call(): pl.pallas_call(kernel, out_shape=out_shape, in_specs=specs, out_specs=[VM...  18.2 us
    ppermute x6, starting transfers between devices, along_z(): return lax.ppermute(x, 'tensor', [(t, t ^ 2 * k) for t in range(n_tensor)])  10.1 us
    ppermute x4, starting transfers between devices, along_y(): return lax.ppermute(x, 'tensor', [(t, t ^ 1) for t in range(n_tensor)])  6.14 us
    ppermute x4, waiting for transfers between devices, along_y(): return lax.ppermute(x, 'tensor', [(t, t ^ 1) for t in range(n_tensor)])  2.39 us
    pallas_call x4, Pallas kernels, small_call(): pl.pallas_call(kernel, out_shape=out_shape, in_specs=[VMEM] * len(operand...  2.38 us
    ppermute x3, starting transfers between devices, along_both(): lax.ppermute(x, 'tensor', [(t, t ^ 2 * k ^ 1) for t in range(n_tensor)])  2.11 us
    pallas_call x2, Pallas kernels, place(): pl.pallas_call(functools.partial(place_kernel, spots), out_shape=pltpu.HB...  1.45 us
    ppermute x3, waiting for transfers between devices, along_both(): lax.ppermute(x, 'tensor', [(t, t ^ 2 * k ^ 1) for t in range(n_tensor)])  1.23 us
  transfers between devices with their start and end apart: 15, of which 6 were waited for; matrix products, arithmetic and copies ran while one was open for 0% of the time, Pallas kernels for 35%

profile of v15, /device:TPU:0, one launch (start us, length us, event | category | flops | bytes accessed | tf_op | source)
XLA Modules:
  0.0 45.5 jit_solution(17987244837794537905)
XLA Ops:
  0.0 0.5 collective-permute-start
  0.5 3.0 %prefix_scores.1 = (bf16[256,128]{1,0:T(8,128)(2,1)S(1)}, f32[8192,256]{1,0:T(8,128)S(1)}, f32[8,256]{1,0:T(8,128)S(1)}, bf16[8192,128]{1,0:T(8,128)(2,1)S(1)}, bf16[32,256,128]{2,1,0:T(8,128)(2,1)S(1)}) custom-call(bf16[32,1024]{1,0:T(8,128)(2,1)} %q_ref.1, bf16[1,2,8192,128]{3,2,1,0:T(8,128)(2,1)} %prefix_ref.1, bf16[32,1,2,256,128]{4,3,2,1,0:T(8,128)(2,1)} %rest_1_.2), custom_call_target="tpu_custom_call" | custom-call | flops 536870912 | bytes 6291456 | tf_op jit(solution)/shard_map/prefix_scores/pallas_call | solution.py:251
  3.5 3.8 %suffix_scores.1 = (f32[256,256]{1,0:T(8,128)S(1)}, f32[256,128]{1,0:T(8,128)S(1)}, f32[8,256]{1,0:T(8,128)S(1)}, bf16[144,8192]{1,0:T(8,128)(2,1)S(1)}, bf16[2,...) custom-call(s32[32]{0:T(128)S(1)} %collective-permute-done.ids_ref, ...), custom_call_target="tpu_custom_call" | custom-call | flops 536870912 | bytes 7340032 | tf_op jit(solution)/shard_map/suffix_scores/pallas_call | solution.py:251
  7.3 0.1 collective-permute-start.1
  7.4 4.6 %values.1 = (bf16[32,1024]{1,0:T(8,128)(2,1)S(1)}, bf16[8,64,1024]{2,1,0:T(8,128)(2,1)S(1)}, bf16[8,64,1024]{2,1,0:T(8,128)(2,1)S(1)}, s32[32,128]{1,0:T(8,128)S...) custom-call(s32[32]{0:T(128)S(1)} %copy-done.1, ...), custom_call_target="tpu_custom_call" | custom-call | flops 536870912 | bytes 14680064 | tf_op jit(solution)/shard_map/values/pallas_call | solution.py:251
  12.0 1.1 %far_blocks.1 = (bf16[32,2176]{1,0:T(8,128)(2,1)S(1)}, f32[32,128]{1,0:T(8,128)S(1)}) custom-call(bf16[32,1024]{1,0:T(8,128)(2,1)S(1)} %get-tuple-element.42.att_ref, s32[32,128]{1,0:T(8,128)S(1)} %get-tuple-element.47.row_slot_ref.refs_2_, s32[8,128]{1,0:T(8,128)S(1)} %get-tuple-element.44.slot_mine_ref, ...), custom_call_target="tpu_custom_call" | custom-call | flops 134217728 | bytes 2097152 | tf_op jit(solution)/shard_map/far_blocks/pallas_call | solution.py:362
  13.1 2.6 %collective-permute-start.2 = (bf16[32,2176]{1,0:T(8,128)(2,1)S(1)}, bf16[32,2176]{1,0:T(8,128)(2,1)S(1)}, u32[]{:S(2)}, u32[]{:S(2)}) collective-permute-start(bf16[32,2176]{1,0:T(8,128)(2,1)S(1)} %get-tuple-element.53), channel_id=1, source_target_pairs={{0,1},{1,0},{2,3},{3,2},{4,5},{5,4},{6,7},{7,6},{8,9},{9,8},{10,11... | collective-permute-start | bytes 417800 | tf_op jit(solution)/shard_map/ppermute | solution.py:543
  15.7 2.7 %near_blocks.3 = (bf16[32,1152]{1,0:T(8,128)(2,1)S(1)}, bf16[32,1152]{1,0:T(8,128)(2,1)S(1)}) custom-call(bf16[32,1024]{1,0:T(8,128)(2,1)S(1)} %get-tuple-element.42.att_ref, f32[32,128]{1,0:T(8,128)S(1)} %get-tuple-element.51.rank_ref.refs_3_, bf16[1024,8192]{1,0:T(8,128)(2,1)} %weight_ref.5), custom_call_target="tpu_custom_call" | custom-call | flops 134217728 | bytes 4194304 | tf_op jit(solution)/shard_map/near_blocks/pallas_call | solution.py:251
  18.5 1.6 %collective-permute-start.4 = (bf16[32,1152]{1,0:T(8,128)(2,1)S(1)}, bf16[32,1152]{1,0:T(8,128)(2,1)S(1)}, u32[]{:S(2)}, u32[]{:S(2)}) collective-permute-start(bf16[32,1152]{1,0:T(8,128)(2,1)S(1)} %get-tuple-element.57), channel_id=1, source_target_pairs={{0,2},{1,3},{2,0},{3,1},{4,6},{5,7},{6,4},{7,5},{8,10},{9,11},{10,... | collective-permute-start | bytes 221192 | tf_op jit(solution)/shard_map/ppermute | solution.py:546
  20.1 0.0 collective-permute-start.5
  20.1 0.5 %add_block.2.rest_0_ = bf16[32,1152]{1,0:T(8,128)(2,1)S(1)} custom-call(bf16[32,1024]{1,0:T(8,128)(2,1)S(1)} %get-tuple-element.42.att_ref, bf16[1024,1024]{1,0:T(8,128)(2,1)S(1)} %get-tuple-element.54.w_ref, bf16[32,2176]{1,0:T(8,128)(2,1)S(1)} %collective-permute-done.2.from_ref.refs_4_, f32[32,128]{1,0:T(8,128)S(1)} %get-tuple-element.51.rank_ref.refs_3_), custom_call_target="tpu_custom_call" | custom-call | flops 134217728 | bytes 2097152 | tf_op jit(solution)/shard_map/add_block/pallas_call | solution.py:362
  20.6 4.0 %collective-permute-start.6 = (bf16[32,1152]{1,0:T(8,128)(2,1)S(1)}, bf16[32,1152]{1,0:T(8,128)(2,1)S(1)}, u32[]{:S(2)}, u32[]{:S(2)}) collective-permute-start(bf16[32,1152]{1,0:T(8,128)(2,1)S(1)} %add_block.2.rest_0_), channel_id=1, source_target_pairs={{0,6},{1,7},{2,4},{3,5},{4,2},{5,3},{6,0},{7,1},{8,14},{9,15},{10,... | collective-permute-start | bytes 221192 | tf_op jit(solution)/shard_map/ppermute | solution.py:546
  24.6 0.5 %add_block.3.rest_0_ = bf16[32,1152]{1,0:T(8,128)(2,1)S(1)} custom-call(bf16[32,1024]{1,0:T(8,128)(2,1)S(1)} %get-tuple-element.42.att_ref, bf16[1024,1024]{1,0:T(8,128)(2,1)S(1)} %get-tuple-element.52.w_ref, bf16[32,2176]{1,0:T(8,128)(2,1)S(1)} %collective-permute-done.2.from_ref.refs_4_, f32[32,128]{1,0:T(8,128)S(1)} %get-tuple-element.51.rank_ref.refs_3_, ...), custom_call_target="tpu_custom_call" | custom-call | flops 134217728 | bytes 2097152 | tf_op jit(solution)/shard_map/add_block/pallas_call | solution.py:362
  25.1 2.1 %near_blocks.2.after_ref = bf16[32,1024]{1,0:T(8,128)(2,1)S(1)} custom-call(bf16[32,1024]{1,0:T(8,128)(2,1)S(1)} %get-tuple-element.42.att_ref, f32[32,128]{1,0:T(8,128)S(1)} %get-tuple-element.51.rank_ref.refs_3_, bf16[1024,8192]{1,0:T(8,128)(2,1)} %weight_ref.5, bf16[32,1152]{1,0:T(8,128)(2,1)S(1)} %add_block.3.rest_0_), custom_call_target="tpu_custom_call" | custom-call | flops 134217728 | bytes 2097152 | tf_op jit(solution)/shard_map/near_blocks/pallas_call | solution.py:251
  27.2 1.6 %collective-permute-start.3 = (bf16[32,1024]{1,0:T(8,128)(2,1)S(1)}, bf16[32,1024]{1,0:T(8,128)(2,1)S(1)}, u32[]{:S(2)}, u32[]{:S(2)}) collective-permute-start(bf16[32,1024]{1,0:T(8,128)(2,1)S(1)} %near_blocks.2.after_ref), channel_id=1, source_target_pairs={{0,1},{1,0},{2,3},{3,2},{4,5},{5,4},{6,7},{7,6},{8,9},{9,8},{10,11... | collective-permute-start | bytes 196616 | tf_op jit(solution)/shard_map/ppermute | solution.py:543
  28.7 2.1 %own_block.1 = (f32[32,1024]{1,0:T(8,128)S(1)}, bf16[512,1024]{1,0:T(8,128)(2,1)S(1)}) custom-call(bf16[32,1024]{1,0:T(8,128)(2,1)S(1)} %get-tuple-element.42.att_ref, bf16[32,1024]{1,0:T(8,128)(2,1)S(1)} %get-tuple-element.43.res_ref, s32[8,128]{1,0:T(8,128)S(1)} %get-tuple-element.44.slot_mine_ref, bf16[8,64,1024]{2,1,0:T(8,128)(2,1)S(1)} %get-tuple-element.45.own_ref, ...), custom_call_target="tpu_custom_call" | custom-call | bytes 2097152 | tf_op jit(solution)/shard_map/own_block/pallas_call | solution.py:251
  30.9 0.6 %collective-permute-done.3.refs_5_ = bf16[32,1024]{1,0:T(8,128)(2,1)S(1)} collective-permute-done((bf16[32,1024]{1,0:T(8,128)(2,1)S(1)}, bf16[32,1024]{1,0:T(8,128)(2,1)S(1)}, u32[]{:S(2)}, u32[]{:S(2)}) %collective-permute-start.3) | collective-permute-done | bytes 65568 | tf_op jit(solution)/shard_map/ppermute | solution.py:543
  31.5 0.3 finish.1.refs_0_
  31.8 2.0 %collective-permute-start.11 = (bf16[32,1024]{1,0:T(8,128)(2,1)S(1)}, bf16[32,1024]{1,0:T(8,128)(2,1)S(1)}, u32[]{:S(2)}, u32[]{:S(2)}) collective-permute-start(bf16[32,1024]{1,0:T(8,128)(2,1)S(1)} %finish.1.refs_0_), channel_id=1, source_target_pairs={{0,6},{1,7},{2,4},{3,5},{4,2},{5,3},{6,0},{7,1},{8,14},{9,15},{10,... | collective-permute-start | bytes 196616 | tf_op jit(solution)/shard_map/ppermute | solution.py:546
  33.8 1.1 %collective-permute-start.9 = (bf16[32,1024]{1,0:T(8,128)(2,1)S(1)}, bf16[32,1024]{1,0:T(8,128)(2,1)S(1)}, u32[]{:S(2)}, u32[]{:S(2)}) collective-permute-start(bf16[32,1024]{1,0:T(8,128)(2,1)S(1)} %finish.1.refs_0_), channel_id=1, source_target_pairs={{0,4},{1,5},{2,6},{3,7},{4,0},{5,1},{6,2},{7,3},{8,12},{9,13},{10,... | collective-permute-start | bytes 196616 | tf_op jit(solution)/shard_map/ppermute | solution.py:546
  34.9 1.5 %collective-permute-start.14 = (bf16[32,1024]{1,0:T(8,128)(2,1)S(1)}, bf16[32,1024]{1,0:T(8,128)(2,1)S(1)}, u32[]{:S(2)}, u32[]{:S(2)}) collective-permute-start(bf16[32,1024]{1,0:T(8,128)(2,1)S(1)} %finish.1.refs_0_), channel_id=1, source_target_pairs={{0,1},{1,0},{2,3},{3,2},{4,5},{5,4},{6,7},{7,6},{8,9},{9,8},{10,11... | collective-permute-start | bytes 196616 | tf_op jit(solution)/shard_map/ppermute | solution.py:549
  36.4 1.4 %collective-permute-start.13 = (bf16[32,1024]{1,0:T(8,128)(2,1)S(1)}, bf16[32,1024]{1,0:T(8,128)(2,1)S(1)}, u32[]{:S(2)}, u32[]{:S(2)}) collective-permute-start(bf16[32,1024]{1,0:T(8,128)(2,1)S(1)} %finish.1.refs_0_), channel_id=1, source_target_pairs={{0,2},{1,3},{2,0},{3,1},{4,6},{5,7},{6,4},{7,5},{8,10},{9,11},{10,... | collective-permute-start | bytes 196616 | tf_op jit(solution)/shard_map/ppermute | solution.py:546
  37.8 0.6 %collective-permute-start.8 = (bf16[32,1024]{1,0:T(8,128)(2,1)S(1)}, bf16[32,1024]{1,0:T(8,128)(2,1)S(1)}, u32[]{:S(2)}, u32[]{:S(2)}) collective-permute-start(bf16[32,1024]{1,0:T(8,128)(2,1)S(1)} %finish.1.refs_0_), channel_id=1, source_target_pairs={{0,3},{1,2},{2,1},{3,0},{4,7},{5,6},{6,5},{7,4},{8,11},{9,10},{10,... | collective-permute-start | bytes 196616 | tf_op jit(solution)/shard_map/ppermute | solution.py:549
  38.3 1.8 %collective-permute-start.12 = (bf16[32,1024]{1,0:T(8,128)(2,1)S(1)}, bf16[32,1024]{1,0:T(8,128)(2,1)S(1)}, u32[]{:S(2)}, u32[]{:S(2)}) collective-permute-start(bf16[32,1024]{1,0:T(8,128)(2,1)S(1)} %collective-permute-done.11.refs_4_), channel_id=1, source_target_pairs={{0,1},{1,0},{2,3},{3,2},{4,5},{5,4},{6,7},{7,6},{8,9},{9,8},{10,11... | collective-permute-start | bytes 196616 | tf_op jit(solution)/shard_map/ppermute | solution.py:543
  40.2 0.4 collective-permute-done.9.refs_2_
  40.5 0.1 collective-permute-start.10
  40.7 0.4 collective-permute-done.13.refs_1_
  41.1 0.8 %place.2.refs_3_ = bf16[32,8192]{1,0:T(8,128)(2,1)} custom-call(bf16[32,1024]{1,0:T(8,128)(2,1)S(1)} %finish.1.refs_0_, bf16[32,1024]{1,0:T(8,128)(2,1)S(1)} %collective-permute-done.13.refs_1_, bf16[32,1024]{1,0:T(8,128)(2,1)S(1)} %collective-permute-done.9.refs_2_, bf16[32,1024]{1,0:T(8,128)(2,1)S(1)} %collective-permute-done.14.refs_3_, ...), custom_call_target="tpu_custom_call" | custom-call | bytes 1048576 | tf_op jit(solution)/shard_map/place/pallas_call | solution.py:515
  41.8 1.2 %collective-permute-done.8.refs_0_ = bf16[32,1024]{1,0:T(8,128)(2,1)S(1)} collective-permute-done((bf16[32,1024]{1,0:T(8,128)(2,1)S(1)}, bf16[32,1024]{1,0:T(8,128)(2,1)S(1)}, u32[]{:S(2)}, u32[]{:S(2)}) %collective-permute-start.8) | collective-permute-done | bytes 65568 | tf_op jit(solution)/shard_map/ppermute | solution.py:549
  43.1 0.3 collective-permute-done.12.refs_2_
  43.3 1.5 %collective-permute-done.10.refs_1_ = bf16[32,1024]{1,0:T(8,128)(2,1)S(1)} collective-permute-done((bf16[32,1024]{1,0:T(8,128)(2,1)S(1)}, bf16[32,1024]{1,0:T(8,128)(2,1)S(1)}, u32[]{:S(2)}, u32[]{:S(2)}) %collective-permute-start.10) | collective-permute-done | bytes 65568 | tf_op jit(solution)/shard_map/ppermute | solution.py:543
  44.8 0.7 %place.3 = bf16[32,8192]{1,0:T(8,128)(2,1)} custom-call(bf16[32,1024]{1,0:T(8,128)(2,1)S(1)} %collective-permute-done.8.refs_0_, bf16[32,1024]{1,0:T(8,128)(2,1)S(1)} %collective-permute-done.10.refs_1_, bf16[32,1024]{1,0:T(8,128)(2,1)S(1)} %collective-permute-done.12.refs_2_, bf16[32,8192]{1,0:T(8,128)(2,1)} %place.2.refs_3_), custom_call_target="tpu_custom_call", output_to_operand_aliasing={{}: (3, {})} | custom-call | bytes 1048576 | tf_op jit(solution)/shard_map/place/pallas_call | solution.py:515
  (14 shorter events, 0.0 us)
Async XLA Ops:
  0.0 3.4 %copy-start = (s32[128]{0:T(128)S(1)}, s32[128]{0:T(128)}, u32[]{:S(2)}) copy-start(s32[128]{0:T(128)} %slot_ref.3) | copy-start | bytes 1540
  0.0 3.4 %collective-permute-start = (s32[32]{0:T(128)}, s32[32]{0:T(128)S(1)}, u32[]{:S(2)}, u32[]{:S(2)}) collective-permute-start(s32[32]{0:T(128)} %ids_ref.1), channel_id=1, source_target_pairs={{0,8},{8,0},{1,9},{9,1},{2,10},{10,2},{3,11},{11,3},{4,12},{12,4},... | collective-permute-start | bytes 392 | tf_op jit(solution)/shard_map/ppermute | solution.py:552
  3.4 3.9 %copy-start.1 = (s32[32]{0:T(128)S(1)}, s32[32]{0:T(128)}, u32[]{:S(2)}) copy-start(s32[32]{0:T(128)} %ids_ref.1) | copy-start | bytes 388
  7.3 4.7 %collective-permute-start.1 = (bf16[2,8,64,1024]{3,2,1,0:T(8,128)(2,1)S(1)}, bf16[2,8,64,1024]{3,2,1,0:T(8,128)(2,1)S(1)}, u32[]{:S(2)}, u32[]{:S(2)}) collective-permute-start(bf16[2,8,64,1024]{3,2,1,0:T(8,128)(2,1)S(1)} %get-tuple-element.46), channel_id=1, source_target_pairs={{0,8},{8,0},{1,9},{9,1},{2,10},{10,2},{3,11},{11,3},{4,12},{12,4},... | collective-permute-start | bytes 6291464 | tf_op jit(solution)/shard_map/ppermute | solution.py:552
  13.1 7.0 %collective-permute-start.2 = (bf16[32,2176]{1,0:T(8,128)(2,1)S(1)}, bf16[32,2176]{1,0:T(8,128)(2,1)S(1)}, u32[]{:S(2)}, u32[]{:S(2)}) collective-permute-start(bf16[32,2176]{1,0:T(8,128)(2,1)S(1)} %get-tuple-element.53), channel_id=1, source_target_pairs={{0,1},{1,0},{2,3},{3,2},{4,5},{5,4},{6,7},{7,6},{8,9},{9,8},{10,11... | collective-permute-start | bytes 417800 | tf_op jit(solution)/shard_map/ppermute | solution.py:543
  18.5 12.4 %collective-permute-start.4 = (bf16[32,1152]{1,0:T(8,128)(2,1)S(1)}, bf16[32,1152]{1,0:T(8,128)(2,1)S(1)}, u32[]{:S(2)}, u32[]{:S(2)}) collective-permute-start(bf16[32,1152]{1,0:T(8,128)(2,1)S(1)} %get-tuple-element.57), channel_id=1, source_target_pairs={{0,2},{1,3},{2,0},{3,1},{4,6},{5,7},{6,4},{7,5},{8,10},{9,11},{10,... | collective-permute-start | bytes 221192 | tf_op jit(solution)/shard_map/ppermute | solution.py:546
  20.1 10.7 %collective-permute-start.5 = (bf16[32,1152]{1,0:T(8,128)(2,1)S(1)}, bf16[32,1152]{1,0:T(8,128)(2,1)S(1)}, u32[]{:S(2)}, u32[]{:S(2)}) collective-permute-start(bf16[32,1152]{1,0:T(8,128)(2,1)S(1)} %get-tuple-element.58), channel_id=1, source_target_pairs={{0,3},{1,2},{2,1},{3,0},{4,7},{5,6},{6,5},{7,4},{8,11},{9,10},{10,... | collective-permute-start | bytes 221192 | tf_op jit(solution)/shard_map/ppermute | solution.py:549
  20.6 10.9 %collective-permute-start.6 = (bf16[32,1152]{1,0:T(8,128)(2,1)S(1)}, bf16[32,1152]{1,0:T(8,128)(2,1)S(1)}, u32[]{:S(2)}, u32[]{:S(2)}) collective-permute-start(bf16[32,1152]{1,0:T(8,128)(2,1)S(1)} %add_block.2.rest_0_), channel_id=1, source_target_pairs={{0,6},{1,7},{2,4},{3,5},{4,2},{5,3},{6,0},{7,1},{8,14},{9,15},{10,... | collective-permute-start | bytes 221192 | tf_op jit(solution)/shard_map/ppermute | solution.py:546
  25.0 6.4 %collective-permute-start.7 = (bf16[32,1152]{1,0:T(8,128)(2,1)S(1)}, bf16[32,1152]{1,0:T(8,128)(2,1)S(1)}, u32[]{:S(2)}, u32[]{:S(2)}) collective-permute-start(bf16[32,1152]{1,0:T(8,128)(2,1)S(1)} %add_block.3.rest_0_), channel_id=1, source_target_pairs={{0,4},{1,5},{2,6},{3,7},{4,0},{5,1},{6,2},{7,3},{8,12},{9,13},{10,... | collective-permute-start | bytes 221192 | tf_op jit(solution)/shard_map/ppermute | solution.py:546
  27.2 4.3 %collective-permute-start.3 = (bf16[32,1024]{1,0:T(8,128)(2,1)S(1)}, bf16[32,1024]{1,0:T(8,128)(2,1)S(1)}, u32[]{:S(2)}, u32[]{:S(2)}) collective-permute-start(bf16[32,1024]{1,0:T(8,128)(2,1)S(1)} %near_blocks.2.after_ref), channel_id=1, source_target_pairs={{0,1},{1,0},{2,3},{3,2},{4,5},{5,4},{6,7},{7,6},{8,9},{9,8},{10,11... | collective-permute-start | bytes 196616 | tf_op jit(solution)/shard_map/ppermute | solution.py:543
  31.8 6.5 %collective-permute-start.11 = (bf16[32,1024]{1,0:T(8,128)(2,1)S(1)}, bf16[32,1024]{1,0:T(8,128)(2,1)S(1)}, u32[]{:S(2)}, u32[]{:S(2)}) collective-permute-start(bf16[32,1024]{1,0:T(8,128)(2,1)S(1)} %finish.1.refs_0_), channel_id=1, source_target_pairs={{0,6},{1,7},{2,4},{3,5},{4,2},{5,3},{6,0},{7,1},{8,14},{9,15},{10,... | collective-permute-start | bytes 196616 | tf_op jit(solution)/shard_map/ppermute | solution.py:546
  33.8 6.8 %collective-permute-start.9 = (bf16[32,1024]{1,0:T(8,128)(2,1)S(1)}, bf16[32,1024]{1,0:T(8,128)(2,1)S(1)}, u32[]{:S(2)}, u32[]{:S(2)}) collective-permute-start(bf16[32,1024]{1,0:T(8,128)(2,1)S(1)} %finish.1.refs_0_), channel_id=1, source_target_pairs={{0,4},{1,5},{2,6},{3,7},{4,0},{5,1},{6,2},{7,3},{8,12},{9,13},{10,... | collective-permute-start | bytes 196616 | tf_op jit(solution)/shard_map/ppermute | solution.py:546
  34.9 5.8 %collective-permute-start.14 = (bf16[32,1024]{1,0:T(8,128)(2,1)S(1)}, bf16[32,1024]{1,0:T(8,128)(2,1)S(1)}, u32[]{:S(2)}, u32[]{:S(2)}) collective-permute-start(bf16[32,1024]{1,0:T(8,128)(2,1)S(1)} %finish.1.refs_0_), channel_id=1, source_target_pairs={{0,1},{1,0},{2,3},{3,2},{4,5},{5,4},{6,7},{7,6},{8,9},{9,8},{10,11... | collective-permute-start | bytes 196616 | tf_op jit(solution)/shard_map/ppermute | solution.py:549
  36.4 4.7 %collective-permute-start.13 = (bf16[32,1024]{1,0:T(8,128)(2,1)S(1)}, bf16[32,1024]{1,0:T(8,128)(2,1)S(1)}, u32[]{:S(2)}, u32[]{:S(2)}) collective-permute-start(bf16[32,1024]{1,0:T(8,128)(2,1)S(1)} %finish.1.refs_0_), channel_id=1, source_target_pairs={{0,2},{1,3},{2,0},{3,1},{4,6},{5,7},{6,4},{7,5},{8,10},{9,11},{10,... | collective-permute-start | bytes 196616 | tf_op jit(solution)/shard_map/ppermute | solution.py:546
  37.8 5.3 %collective-permute-start.8 = (bf16[32,1024]{1,0:T(8,128)(2,1)S(1)}, bf16[32,1024]{1,0:T(8,128)(2,1)S(1)}, u32[]{:S(2)}, u32[]{:S(2)}) collective-permute-start(bf16[32,1024]{1,0:T(8,128)(2,1)S(1)} %finish.1.refs_0_), channel_id=1, source_target_pairs={{0,3},{1,2},{2,1},{3,0},{4,7},{5,6},{6,5},{7,4},{8,11},{9,10},{10,... | collective-permute-start | bytes 196616 | tf_op jit(solution)/shard_map/ppermute | solution.py:549
  38.3 5.0 %collective-permute-start.12 = (bf16[32,1024]{1,0:T(8,128)(2,1)S(1)}, bf16[32,1024]{1,0:T(8,128)(2,1)S(1)}, u32[]{:S(2)}, u32[]{:S(2)}) collective-permute-start(bf16[32,1024]{1,0:T(8,128)(2,1)S(1)} %collective-permute-done.11.refs_4_), channel_id=1, source_target_pairs={{0,1},{1,0},{2,3},{3,2},{4,5},{5,4},{6,7},{7,6},{8,9},{9,8},{10,11... | collective-permute-start | bytes 196616 | tf_op jit(solution)/shard_map/ppermute | solution.py:543
  40.5 4.3 %collective-permute-start.10 = (bf16[32,1024]{1,0:T(8,128)(2,1)S(1)}, bf16[32,1024]{1,0:T(8,128)(2,1)S(1)}, u32[]{:S(2)}, u32[]{:S(2)}) collective-permute-start(bf16[32,1024]{1,0:T(8,128)(2,1)S(1)} %collective-permute-done.9.refs_2_), channel_id=1, source_target_pairs={{0,1},{1,0},{2,3},{3,2},{4,5},{5,4},{6,7},{7,6},{8,9},{9,8},{10,11... | collective-permute-start | bytes 196616 | tf_op jit(solution)/shard_map/ppermute | solution.py:543
